TPU v7x, 512 devices: a whole 4x4x16 slice. The times are simulated.
512 devices in a mesh: grp: 16 (over x, z_lo), ep: 32 (over z_hi, y, core).
Axes of the slice: x: 4, y: 4, z: 16 (z_hi: 4, z_lo: 4; z = z_hi * 4 + z_lo), core: 2. Of those that a mesh axis runs over, the one named last changes fastest.
Arguments:
- tokens: bfloat16 [8192, 2048], P('ep'), may hold values from -6 to 6
- routes: int32 [8192, 8], P('ep'), may hold values from 0 to 63, all different within a row; in each aligned block of 256 rows (0 to 255, 256 to 511, ...) at most 48 rows name the same one
- gate_values: float32 [8192, 8], P('ep'), may hold values from 0.05 to 0.3
- old_group: int32 [64], replicated, may hold values from 0 to 15, as said below
- move_mask: int32 [4], replicated, may hold values from 0 to 15
- pair_index: int32 [8192], replicated, may hold values from 0 to 8191, each once
- reward_head: bfloat16 [2048], replicated, may hold values from -0.125 to 0.125
- w_up: bfloat16 [16, 2048, 4096], P('grp', None, 'ep'), may hold values from -0.125 to 0.125
- w_down: bfloat16 [16, 4096, 2048], P('grp', 'ep'), may hold values from -0.1875 to 0.1875
- acc_up: bfloat16 [16, 2048, 4096], P('grp', None, 'ep'), may hold values from -6 to 6
- acc_down: bfloat16 [16, 4096, 2048], P('grp', 'ep'), may hold values from -6 to 6
Outputs:
- new_acc_up: bfloat16 [16, 2048, 4096], P('grp', None, 'ep')
- new_acc_down: bfloat16 [16, 4096, 2048], P('grp', 'ep')
- pair_loss: float32 [], replicated
Inputs may be any that keep to these rules, and one draw needn't show every extreme that they name: `routes`: in the rows of one device (aligned blocks of 256 rows), no expert is named by more than 48 rows, a bound that some block reaches. `old_group`: for each l, the experts e with e % 4 == l lie in 16 different groups. `pair_index`: every token appears once.
All inputs are finite; a program needn't handle non-finite values.
Results may differ from a plain program's by a relative error of at most 0.0048.
Values may be sent and summed in bfloat16 or wider, within the bound.
No kernel may reach another device: no remote copies, remote signals or barrier semaphores. Data moves between devices by JAX's collectives and lax.ppermute only.
A program may use at most 64 MiB of HBM per device.

v0:
```python
import jax
import jax.numpy as jnp
from jax import lax
from jax.sharding import PartitionSpec as P

EXP_GRP = 4


loss_scale = 64.0
highest = lax.Precision.HIGHEST


def from_partner(block, axis, apart):
    count = lax.axis_size(axis)
    route = []
    for low in range(count):
        high = low | 1 << apart
        if high != low and high < count:
            route += [(low, high), (high, low)]
    return lax.ppermute(block, axis, route)


def silu_slope(pre_act):
    sigmoid_value = jax.nn.sigmoid(pre_act)
    return sigmoid_value * (1.0 + pre_act * (1.0 - sigmoid_value))


def relocate_accums(acc_up, acc_down, slot_mask, bit_count):
    for bit_index in range(bit_count):
        partner = from_partner((acc_up, acc_down), "grp", bit_index)
        take_partner = jnp.bitwise_and(jnp.right_shift(slot_mask, bit_index), 1) == 1
        acc_up = jnp.where(take_partner, partner[0], acc_up)
        acc_down = jnp.where(take_partner, partner[1], acc_down)
    return (acc_up, acc_down)


def body(
    tokens,
    routes,
    gate_values,
    old_group,
    move_mask,
    pair_index,
    reward_head,
    w_up,
    w_down,
    acc_up,
    acc_down,
):
    group_count = lax.axis_size("grp")
    rank_count = lax.axis_size("ep")
    token_count, top_count = routes.shape
    experts = old_group.shape[0]
    shards = rank_count // EXP_GRP
    capacity = 3 * token_count * top_count // (2 * experts)
    bit_count = group_count.bit_length() - 1
    group_rank = lax.axis_index("grp")
    member_rank = lax.axis_index("ep")
    slot_rank = member_rank // shards
    slot_range = jnp.arange(EXP_GRP, dtype=jnp.int32)
    slot_mask = jnp.sum(jnp.where(slot_range == slot_rank, move_mask, 0))
    expert_ids = jnp.arange(experts, dtype=jnp.int32)
    route_hits = routes[:, :, None] == expert_ids
    owner_of = jnp.sum(jnp.where(route_hits, old_group, 0), axis=2)
    selected = (owner_of == group_rank)[:, :, None] & ((routes % EXP_GRP)[:, :, None] == slot_range)
    selected = selected.reshape(token_count * top_count, EXP_GRP).astype(jnp.int32)
    position = jnp.cumsum(selected, axis=0) - 1
    cap_range = jnp.arange(capacity, dtype=jnp.int32)
    placed = (selected[:, :, None] == 1) & (position[:, :, None] == cap_range)
    placed = placed.astype(jnp.float32).reshape(token_count, top_count, EXP_GRP * capacity)
    dispatch = jnp.sum(placed, axis=1)
    slot_gate = jnp.sum(placed * gate_values[:, :, None], axis=(0, 1))
    outgoing = lax.dot_general(
        dispatch.astype(jnp.bfloat16),
        tokens,
        (((0,), (0,)), ((), ())),
        preferred_element_type=jnp.float32,
    ).astype(jnp.bfloat16)
    width = tokens.shape[1]
    outgoing = jnp.broadcast_to(
        outgoing.reshape(EXP_GRP, 1, capacity, width), (EXP_GRP, shards, capacity, width)
    ).reshape(rank_count, capacity, width)
    arrived = lax.all_to_all(outgoing, "ep", split_axis=0, concat_axis=0, tiled=True)
    rows_in = arrived.reshape(rank_count * capacity, width)
    pre_act = jnp.dot(rows_in, w_up[0], preferred_element_type=jnp.float32)
    hidden = jax.nn.silu(pre_act).astype(jnp.bfloat16)
    hidden_wide = hidden.astype(jnp.float32)
    head_proj = jnp.dot(w_down[0], reward_head, preferred_element_type=jnp.float32)
    partial_value = jnp.dot(hidden_wide, head_proj, precision=highest)
    returned = lax.all_to_all(
        partial_value.reshape(rank_count, capacity), "ep", split_axis=0, concat_axis=0, tiled=True
    )
    per_slot = jnp.sum(returned.reshape(EXP_GRP, shards, capacity), axis=1).reshape(-1) * slot_gate
    reward_part = jnp.dot(dispatch, per_slot, precision=highest)
    base_reward = jnp.dot(tokens, reward_head, preferred_element_type=jnp.float32)
    summed = lax.psum(reward_part, "grp")
    rewards = lax.all_gather(base_reward + summed, "ep", axis=0, tiled=True)
    pair_count = pair_index.shape[0] // 2
    chosen = pair_index[:pair_count]
    rejected = pair_index[pair_count:]
    margin = rewards[chosen] - rewards[rejected]
    pair_loss = jnp.mean(jax.nn.softplus(-margin))
    weight_grad = loss_scale * jax.nn.sigmoid(-margin)
    token_grad = jnp.zeros_like(rewards).at[chosen].set(-weight_grad).at[rejected].set(weight_grad)
    local_grad = lax.dynamic_slice_in_dim(token_grad, member_rank * token_count, token_count)
    slot_grad = jnp.dot(local_grad, dispatch, precision=highest) * slot_gate
    slot_grad = jnp.broadcast_to(
        slot_grad.reshape(EXP_GRP, 1, capacity), (EXP_GRP, shards, capacity)
    ).reshape(rank_count, capacity)
    grad_in = lax.all_to_all(slot_grad, "ep", split_axis=0, concat_axis=0, tiled=True).reshape(-1)
    hidden_grad = jnp.dot(grad_in, hidden_wide, precision=highest)
    grad_down = hidden_grad[:, None] * reward_head.astype(jnp.float32)[None, :]
    new_down = (acc_down[0].astype(jnp.float32) + grad_down).astype(jnp.bfloat16)
    pre_grad = (grad_in[:, None] * head_proj[None, :] * silu_slope(pre_act)).astype(jnp.bfloat16)
    grad_up = lax.dot_general(
        rows_in, pre_grad, (((0,), (0,)), ((), ())), preferred_element_type=jnp.float32
    )
    new_up = (acc_up[0].astype(jnp.float32) + grad_up).astype(jnp.bfloat16)
    new_up, new_down = relocate_accums(new_up, new_down, slot_mask, bit_count)
    return (new_up[None], new_down[None], pair_loss)


def solution(mesh):
    placed = (
        P("ep", None),
        P("ep", None),
        P("ep", None),
        P(),
        P(),
        P(),
        P(),
        P("grp", None, "ep"),
        P("grp", "ep", None),
        P("grp", None, "ep"),
        P("grp", "ep", None),
    )
    return jax.shard_map(
        body,
        mesh=mesh,
        in_specs=placed,
        out_specs=(P("grp", None, "ep"), P("grp", "ep", None), P()),
        check_vma=False,
    )
```

profile of v0, /device:TPU:1, one launch (start us, length us, event | category | flops | bytes accessed | tf_op | source)
XLA Modules:
  0.0 650.3 jit_solution(10994232681551592793)
XLA Ops:
  0.7 0.8 add_select_fusion
  1.4 0.9 select_reduce_fusion.1
  2.3 0.2 copy.38
  3.2 1.2 reduce-window.6
  4.4 0.2 slice_reduce_fusion
  4.6 0.2 reduce-window.9
  4.9 0.5 copy.40
  5.4 0.4 copy.43
  5.8 6.4 and.65
  12.2 2.2 and.66
  14.3 6.8 %eq.139 = s32[2048,4,48]{2,1,0:T(4,128)} broadcast(s32[2048,4]{1,0:T(8,128)S(1)} %copy.43), dimensions={0,1} | broadcast | bytes 1605632 | tf_op jit(solution)/shard_map/eq | solution.py:69
  21.1 5.2 eq.140
  26.3 2.5 convert_reduce_fusion
  28.8 0.4 convolution_convert_fusion
  29.2 3.5 broadcast_in_dim.59
  32.7 19.6 %all-to-all-start = ((bf16[32,48,2048]{2,1,0:T(8,128)(2,1)}), bf16[32,48,2048]{2,1,0:T(8,128)(2,1)}, u32[]{:S(2)}, u32[]{:S(2)}) async-start(bf16[32,48,2048]{2,1,0:T(8,128)(2,1)} %bitcast.67), calls=%async_computation | async-start | bytes 12582912 | tf_op jit(solution)/shard_map/all_to_all | solution.py:83
  52.6 0.2 fusion.3
  52.8 0.4 fusion.22
  53.2 7.7 %select_reduce_fusion = f32[4,48]{1,0:T(4,128)S(1)} fusion(f32[2048]{0:T(1024)S(1)} %mul.68, s32[2048,4]{1,0:T(8,128)S(1)} %copy.43, pred[2048,4]{1,0:T(8,128)(4,1)S(1)} %copy.40), kind=kLoop, calls=%fused_computation.4 | loop fusion | flops 1572672 | bytes 49920 | tf_op jit(solution)/shard_map/reduce_sum | solution.py:72
  60.9 270.0 %all-to-all-done = bf16[32,48,2048]{2,1,0:T(8,128)(2,1)} async-done(((bf16[32,48,2048]{2,1,0:T(8,128)(2,1)}), bf16[32,48,2048]{2,1,0:T(8,128)(2,1)}, u32[]{:S(2)}, u32[]{:S(2)}) %all-to-all-start) | async-done | bytes 6291488 | tf_op jit(solution)/shard_map/all_to_all | solution.py:83
  331.0 5.6 multiply_convert_fusion.1
  336.5 0.4 convolution_reduce_fusion
  337.0 0.7 all_to_all.16
  337.7 8.8 %all-to-all-start.1 = ((f32[32,1,48]{2,1,0:T(1,128)}), f32[32,1,48]{2,1,0:T(1,128)S(1)}, u32[]{:S(2)}, u32[]{:S(2)}) async-start(f32[32,1,48]{2,1,0:T(1,128)} %all_to_all.16), calls=%async_computation.1 | async-start | bytes 32768 | tf_op jit(solution)/shard_map/all_to_all | solution.py:90
  346.6 14.0 %all-to-all-done.1 = f32[32,1,48]{2,1,0:T(1,128)S(1)} async-done(((f32[32,1,48]{2,1,0:T(1,128)}), f32[32,1,48]{2,1,0:T(1,128)S(1)}, u32[]{:S(2)}, u32[]{:S(2)}) %all-to-all-start.1) | async-done | bytes 6176 | tf_op jit(solution)/shard_map/all_to_all | solution.py:90
  360.7 0.3 fusion.23
  361.0 32.8 %psum.7 = f32[256]{0:T(256)S(1)} all-reduce(f32[256]{0:T(256)S(1)} %bitcast.77), channel_id=1, replica_groups=mesh['grp'=16,'ep'=32] {'grp'}, use_global_device_ids=true, to_apply=%region_7.8 | all-reduce | flops 256 | bytes 2048 | tf_op jit(solution)/shard_map/psum | solution.py:96
  393.8 55.0 %all-gather = f32[32,1,256]{2,1,0:T(1,128)S(1)} all-gather(f32[1,1,256]{2,1,0:T(1,128)S(1)} %bitcast.78), channel_id=1, replica_groups=mesh['grp'=16,'ep'=32] {'ep'}, dimensions={0}, use_global_device_ids=true | all-gather | bytes 33792 | tf_op jit(solution)/shard_map/all_gather | solution.py:97
  448.8 23.0 %gather_fusion.1 = f32[4096]{0:T(1024)S(1)} fusion(f32[8192]{0:T(1024)S(1)} %bitcast.65, s32[4096]{0:T(1024)S(1)} %get-tuple-element.7), kind=kCustom, calls=%fused_computation.1 | custom fusion | bytes 49152 | tf_op jit(solution)/shard_map/gather | solution.py:101
  471.9 23.0 %gather_fusion = f32[4096]{0:T(1024)S(1)} fusion(f32[8192]{0:T(1024)S(1)} %bitcast.66, s32[4096]{0:T(1024)S(1)} %get-tuple-element.8), kind=kCustom, calls=%fused_computation | custom fusion | bytes 49152 | tf_op jit(solution)/shard_map/gather | solution.py:101
  494.9 0.6 fusion.21
  495.5 15.5 %scatter_custom_fusion = f32[8192]{0:T(1024)S(1)} fusion(s32[4096]{0:T(1024)S(1)} %get-tuple-element.9, f32[4096]{0:T(1024)S(1)} %get-tuple-element.3, f32[]{:T(128)} %constant.65.clone.1), kind=kCustom, calls=%fused_computation.51 | custom fusion | bytes 32772 | tf_op jit(solution)/shard_map/scatter | solution.py:104
  511.1 15.6 %scatter_fusion = f32[8192]{0:T(1024)S(1)} fusion(f32[8192]{0:T(1024)S(1)} %scatter_custom_fusion, s32[4096]{0:T(1024)S(1)} %get-tuple-element.6, f32[4096]{0:T(1024)S(1)} %get-tuple-element.4), kind=kCustom, calls=%fused_computation.3 | custom fusion | bytes 65536 | tf_op jit(solution)/shard_map/scatter | solution.py:104
  526.8 0.2 fusion.24
  527.1 0.6 broadcast_in_dim.64
  527.7 7.0 %all-to-all-start.2 = ((f32[32,1,48]{2,1,0:T(1,128)}), f32[32,1,48]{2,1,0:T(1,128)S(1)}, u32[]{:S(2)}, u32[]{:S(2)}) async-start(f32[32,1,48]{2,1,0:T(1,128)} %bitcast.17), calls=%async_computation.2 | async-start | bytes 32768 | tf_op jit(solution)/shard_map/all_to_all | solution.py:110
  534.8 14.1 %all-to-all-done.2 = f32[32,1,48]{2,1,0:T(1,128)S(1)} async-done(((f32[32,1,48]{2,1,0:T(1,128)}), f32[32,1,48]{2,1,0:T(1,128)S(1)}, u32[]{:S(2)}, u32[]{:S(2)}) %all-to-all-start.2) | async-done | bytes 6176 | tf_op jit(solution)/shard_map/all_to_all | solution.py:110
  548.9 0.3 convolution_bitcast_fusion
  549.2 0.5 broadcast.131
  549.7 0.7 reduce.10
  550.5 0.2 fusion.2
  550.7 2.9 collective-permute-start.4
  553.6 5.2 fusion.1
  558.9 2.4 collective-permute-start
  561.2 0.6 fusion.18
  562.5 3.0 collective-permute-done.4
  565.5 0.3 broadcast_select_fusion
  565.8 1.9 collective-permute-start.5
  567.7 12.5 %collective-permute-done = bf16[2048,128]{1,0:T(8,128)(2,1)} collective-permute-done((bf16[2048,128]{1,0:T(8,128)(2,1)S(1)}, bf16[2048,128]{1,0:T(8,128)(2,1)}, u32[]{:S(2)}, u32[]{:S(2)}) %collective-permute-start) | collective-permute-done | bytes 524320 | tf_op jit(solution)/shard_map/ppermute | solution.py:20
  580.3 3.0 collective-permute-start.1
  583.9 18.5 %collective-permute-done.5 = bf16[128,2048]{1,0:T(8,128)(2,1)} collective-permute-done((bf16[128,2048]{1,0:T(8,128)(2,1)S(1)}, bf16[128,2048]{1,0:T(8,128)(2,1)}, u32[]{:S(2)}, u32[]{:S(2)}) %collective-permute-start.5) | collective-permute-done | bytes 524320 | tf_op jit(solution)/shard_map/ppermute | solution.py:20
  602.4 1.1 broadcast_select_fusion.1
  603.5 1.9 collective-permute-start.6
  605.5 8.2 %collective-permute-done.1 = bf16[2048,128]{1,0:T(8,128)(2,1)} collective-permute-done((bf16[2048,128]{1,0:T(8,128)(2,1)S(1)}, bf16[2048,128]{1,0:T(8,128)(2,1)}, u32[]{:S(2)}, u32[]{:S(2)}) %collective-permute-start.1) | collective-permute-done | bytes 524320 | tf_op jit(solution)/shard_map/ppermute | solution.py:20
  613.7 1.1 broadcast_select_fusion.4
  614.8 1.9 collective-permute-start.2
  617.4 1.9 collective-permute-start.7
  619.3 9.1 %collective-permute-done.2 = bf16[2048,128]{1,0:T(8,128)(2,1)} collective-permute-done((bf16[2048,128]{1,0:T(8,128)(2,1)S(1)}, bf16[2048,128]{1,0:T(8,128)(2,1)}, u32[]{:S(2)}, u32[]{:S(2)}) %collective-permute-start.2) | collective-permute-done | bytes 524320 | tf_op jit(solution)/shard_map/ppermute | solution.py:20
  628.5 1.1 broadcast_select_fusion.5
  629.6 1.9 collective-permute-start.3
  632.8 4.3 collective-permute-done.7
  637.1 0.8 select_bitcast_fusion
  638.0 10.4 %collective-permute-done.3 = bf16[2048,128]{1,0:T(8,128)(2,1)S(1)} collective-permute-done((bf16[2048,128]{1,0:T(8,128)(2,1)S(1)}, bf16[2048,128]{1,0:T(8,128)(2,1)S(1)}, u32[]{:S(2)}, u32[]{:S(2)}) %collective-permute-start.3) | collective-permute-done | bytes 524320 | tf_op jit(solution)/shard_map/ppermute | solution.py:20
  648.3 0.8 select_bitcast_fusion.1
  (46 shorter events, 1.8 us)
Async XLA Ops:
  0.6 28.2 %copy-start = (bf16[256,2048]{1,0:T(8,128)(2,1)S(1)}, bf16[256,2048]{1,0:T(8,128)(2,1)}, u32[]{:S(2)}) copy-start(bf16[256,2048]{1,0:T(8,128)(2,1)} %param.11) | copy-start | bytes 3145732
  21.1 5.2 copy-start.1
  32.7 19.6 %copy-start.5 = (bf16[2048]{0:T(1024)(128)(2,1)S(1)}, bf16[2048]{0:T(1024)(128)(2,1)}, u32[]{:S(2)}) copy-start(bf16[2048]{0:T(1024)(128)(2,1)} %param.17) | copy-start | bytes 12292
  32.7 19.6 %copy-start.6 = (f32[256,8]{0,1:T(8,128)S(1)}, f32[256,8]{0,1:T(8,128)}, u32[]{:S(2)}) copy-start(f32[256,8]{0,1:T(8,128)} %param.13) | copy-start | bytes 24580
  32.7 19.8 %copy-start.3 = (bf16[1,128,2048]{2,1,0:T(8,128)(2,1)S(1)}, bf16[1,128,2048]{2,1,0:T(8,128)(2,1)}, u32[]{:S(2)}) copy-start(bf16[1,128,2048]{2,1,0:T(8,128)(2,1)} %param.19) | copy-start | bytes 1572868
  32.7 298.2 %all-to-all-start = ((bf16[32,48,2048]{2,1,0:T(8,128)(2,1)}), bf16[32,48,2048]{2,1,0:T(8,128)(2,1)}, u32[]{:S(2)}, u32[]{:S(2)}) async-start(bf16[32,48,2048]{2,1,0:T(8,128)(2,1)} %bitcast.67), calls=%async_computation | async-start | bytes 12582912 | tf_op jit(solution)/shard_map/all_to_all | solution.py:83
  331.0 15.5 %copy-start.4 = (s32[8192]{0:T(1024)S(1)}, s32[8192]{0:T(1024)}, u32[]{:S(2)}) copy-start(s32[8192]{0:T(1024)} %param.16) | copy-start | bytes 98308
  337.7 22.9 %all-to-all-start.1 = ((f32[32,1,48]{2,1,0:T(1,128)}), f32[32,1,48]{2,1,0:T(1,128)S(1)}, u32[]{:S(2)}, u32[]{:S(2)}) async-start(f32[32,1,48]{2,1,0:T(1,128)} %all_to_all.16), calls=%async_computation.1 | async-start | bytes 32768 | tf_op jit(solution)/shard_map/all_to_all | solution.py:90
  511.1 39.4 %copy-start.2 = (bf16[1,128,2048]{2,1,0:T(8,128)(2,1)S(1)}, bf16[1,128,2048]{2,1,0:T(8,128)(2,1)}, u32[]{:S(2)}) copy-start(bf16[1,128,2048]{2,1,0:T(8,128)(2,1)} %param.21) | copy-start | bytes 1572868
  527.7 21.2 %all-to-all-start.2 = ((f32[32,1,48]{2,1,0:T(1,128)}), f32[32,1,48]{2,1,0:T(1,128)S(1)}, u32[]{:S(2)}, u32[]{:S(2)}) async-start(f32[32,1,48]{2,1,0:T(1,128)} %bitcast.17), calls=%async_computation.2 | async-start | bytes 32768 | tf_op jit(solution)/shard_map/all_to_all | solution.py:110
  550.7 14.8 %collective-permute-start.4 = (bf16[128,2048]{1,0:T(8,128)(2,1)S(1)}, bf16[128,2048]{1,0:T(8,128)(2,1)}, u32[]{:S(2)}, u32[]{:S(2)}) collective-permute-start(bf16[128,2048]{1,0:T(8,128)(2,1)S(1)} %fusion.2), channel_id=1, source_target_pairs={{0,32},{32,0},{64,96},{96,64},{128,160},{160,128},{192,224},{224,1... | collective-permute-start | bytes 1572872 | tf_op jit(solution)/shard_map/ppermute | solution.py:20
  553.6 7.6 %copy-start.7 = (s32[4]{0:T(128)S(1)}, s32[4]{0:T(128)}, u32[]{:S(2)}) copy-start(s32[4]{0:T(128)} %param.15) | copy-start | bytes 52
  558.9 21.4 %collective-permute-start = (bf16[2048,128]{1,0:T(8,128)(2,1)S(1)}, bf16[2048,128]{1,0:T(8,128)(2,1)}, u32[]{:S(2)}, u32[]{:S(2)}) collective-permute-start(bf16[2048,128]{1,0:T(8,128)(2,1)S(1)} %fusion.1), channel_id=1, source_target_pairs={{0,32},{32,0},{64,96},{96,64},{128,160},{160,128},{192,224},{224,1... | collective-permute-start | bytes 1572872 | tf_op jit(solution)/shard_map/ppermute | solution.py:20
  565.8 36.6 %collective-permute-start.5 = (bf16[128,2048]{1,0:T(8,128)(2,1)S(1)}, bf16[128,2048]{1,0:T(8,128)(2,1)}, u32[]{:S(2)}, u32[]{:S(2)}) collective-permute-start(bf16[128,2048]{1,0:T(8,128)(2,1)S(1)} %broadcast_select_fusion), channel_id=1, source_target_pairs={{0,64},{64,0},{32,96},{96,32},{128,192},{192,128},{160,224},{224,1... | collective-permute-start | bytes 1572872 | tf_op jit(solution)/shard_map/ppermute | solution.py:20
  580.3 33.3 %collective-permute-start.1 = (bf16[2048,128]{1,0:T(8,128)(2,1)S(1)}, bf16[2048,128]{1,0:T(8,128)(2,1)}, u32[]{:S(2)}, u32[]{:S(2)}) collective-permute-start(bf16[2048,128]{1,0:T(8,128)(2,1)S(1)} %broadcast_select_fusion.3), channel_id=1, source_target_pairs={{0,64},{64,0},{32,96},{96,32},{128,192},{192,128},{160,224},{224,1... | collective-permute-start | bytes 1572872 | tf_op jit(solution)/shard_map/ppermute | solution.py:20
  603.5 13.8 %collective-permute-start.6 = (bf16[128,2048]{1,0:T(8,128)(2,1)S(1)}, bf16[128,2048]{1,0:T(8,128)(2,1)S(1)}, u32[]{:S(2)}, u32[]{:S(2)}) collective-permute-start(bf16[128,2048]{1,0:T(8,128)(2,1)S(1)} %broadcast_select_fusion.1), channel_id=1, source_target_pairs={{0,128},{128,0},{32,160},{160,32},{64,192},{192,64},{96,224},{224,... | collective-permute-start | bytes 1572872 | tf_op jit(solution)/shard_map/ppermute | solution.py:20
  614.8 13.7 %collective-permute-start.2 = (bf16[2048,128]{1,0:T(8,128)(2,1)S(1)}, bf16[2048,128]{1,0:T(8,128)(2,1)}, u32[]{:S(2)}, u32[]{:S(2)}) collective-permute-start(bf16[2048,128]{1,0:T(8,128)(2,1)S(1)} %broadcast_select_fusion.4), channel_id=1, source_target_pairs={{0,128},{128,0},{32,160},{160,32},{64,192},{192,64},{96,224},{224,... | collective-permute-start | bytes 1572872 | tf_op jit(solution)/shard_map/ppermute | solution.py:20
  617.4 19.7 %collective-permute-start.7 = (bf16[128,2048]{1,0:T(8,128)(2,1)S(1)}, bf16[128,2048]{1,0:T(8,128)(2,1)S(1)}, u32[]{:S(2)}, u32[]{:S(2)}) collective-permute-start(bf16[128,2048]{1,0:T(8,128)(2,1)S(1)} %broadcast_select_fusion.2), channel_id=1, source_target_pairs={{0,256},{256,0},{32,288},{288,32},{64,320},{320,64},{96,352},{352,... | collective-permute-start | bytes 1572872 | tf_op jit(solution)/shard_map/ppermute | solution.py:20
  629.6 18.8 %collective-permute-start.3 = (bf16[2048,128]{1,0:T(8,128)(2,1)S(1)}, bf16[2048,128]{1,0:T(8,128)(2,1)S(1)}, u32[]{:S(2)}, u32[]{:S(2)}) collective-permute-start(bf16[2048,128]{1,0:T(8,128)(2,1)S(1)} %broadcast_select_fusion.5), channel_id=1, source_target_pairs={{0,256},{256,0},{32,288},{288,32},{64,320},{320,64},{96,352},{352,... | collective-permute-start | bytes 1572872 | tf_op jit(solution)/shard_map/ppermute | solution.py:20
where the time goes:
time: 655 us; the launch traced here: 650 us
  waiting for transfers between devices  364 us (56%)
  local copies, waits for them, and re-layouts  106 us (16%)
  blocking collectives  87.8 us (13%)
  starting transfers between devices  53.3 us (8%)
  other arithmetic  20.9 us (3%)
  matrix products  12.9 us (2%)
    all_to_all x1, waiting for transfers between devices, body(): lax.all_to_all(outgoing, 'ep', split_axis=0, concat_axis=0, tiled=True)  270 us
    ppermute x8, waiting for transfers between devices, from_partner(): return lax.ppermute(block, axis, route)  66.1 us
    all_gather x1, blocking collectives, body(): rewards = lax.all_gather(base_reward + summed, 'ep', axis=0, tiled=True)  55 us
    gather x2, local copies, waits for them, and re-layouts, body(): margin = rewards[chosen] - rewards[rejected]  46.1 us
    psum x1, blocking collectives, body(): summed = lax.psum(reward_part, 'grp')  32.8 us
    scatter x2, local copies, waits for them, and re-layouts, body(): jnp.zeros_like(rewards).at[chosen].set(-weight_grad).at[rejected]  31.1 us
    all_to_all x1, starting transfers between devices, body(): lax.all_to_all(outgoing, 'ep', split_axis=0, concat_axis=0, tiled=True)  19.6 us
    ppermute x8, starting transfers between devices, from_partner(): return lax.ppermute(block, axis, route)  17.8 us
  transfers between devices with their start and end apart: 11, of which 10 were waited for; matrix products, arithmetic and copies ran while one was open for 3% of the time, Pallas kernels for 0%

commit v1 on v0

v1 whole, which is shorter than its diff:
```python
import jax
import jax.numpy as jnp
from jax import lax
from jax.experimental import pallas as pl
from jax.experimental.pallas import tpu as pltpu
from jax.sharding import Mesh
from jax.sharding import PartitionSpec as P

D = 2048
HID_DEV = 128
EXP_GRP = 4
TOK_DEV = 256
CAP = 48
WIDE = D + 128
ROWS = 16 * CAP
PAIRS = 4096

f32 = jnp.float32
bf16 = jnp.bfloat16
VMEM = pl.BlockSpec(memory_space=pltpu.VMEM)
SMEM = pl.BlockSpec(memory_space=pltpu.SMEM)
PARAMS = pltpu.CompilerParams(vmem_limit_bytes=48 * 1024 * 1024)
NT = (((1,), (1,)), ((), ()))

BLOCKS = (
    [(CAP * d, 0, d) for d in range(4)]
    + [(4 * CAP + 2 * CAP * d + CAP * i, k, d) for d in range(4) for i, k in enumerate((1, 3))]
    + [(12 * CAP + CAP * d, 2, d) for d in range(4)]
)


def shape(dims, kind):
    return jax.ShapeDtypeStruct(dims, kind)


def iota(dims, axis):
    return lax.broadcasted_iota(jnp.int32, dims, axis)


def thirds(value):
    first = value.astype(bf16).astype(f32)
    second = (value - first).astype(bf16).astype(f32)
    third = (value - first - second).astype(bf16).astype(f32)
    return first, second, third


def weights_kernel(up_ref, down_ref, head_ref, out_ref):
    out_ref[:D, :] = up_ref[...]
    head = jnp.broadcast_to(head_ref[...], (16, D))
    proj = lax.dot_general(head, down_ref[...], NT, preferred_element_type=f32)
    first, second, third = thirds(proj)
    row = iota((16, HID_DEV), 0)
    packed = jnp.where(row == 0, first, jnp.where(row == 1, second, jnp.where(row == 2, third, 0.0)))
    out_ref[D:, :] = packed.astype(bf16)


def dispatch_kernel(group_ref, mask_ref, info_ref, tok_ref, routes_ref, gates_ref, pair_ref, head_ref, *outs):
    out_refs, base_ref = outs[:4], outs[4]
    grp, zh, member = info_ref[0], info_ref[1], info_ref[2]
    routes = routes_ref[...]
    gates = gates_ref[...]
    sel, gate = [], []
    for k in range(EXP_GRP):
        slot = zh ^ k
        mask = mask_ref[slot]
        expert = jnp.int32(0)
        for j in range(16):
            found = (group_ref[4 * j + slot] ^ mask) == grp
            expert = jnp.where(found, 4 * j + slot, expert)
        hit = routes == expert
        sel.append(jnp.sum(jnp.where(hit, 1.0, 0.0), axis=0, keepdims=True))
        gate.append(jnp.sum(jnp.where(hit, gates, 0.0), axis=0, keepdims=True))
    row8 = iota((8, TOK_DEV), 0)
    chosen = jnp.zeros((8, TOK_DEV), f32)
    for k in range(EXP_GRP):
        chosen = jnp.where(row8 == k, sel[k], chosen)
    tri = jnp.where(iota((TOK_DEV, TOK_DEV), 0) <= iota((TOK_DEV, TOK_DEV), 1), 1.0, 0.0).astype(bf16)
    place = jnp.dot(chosen.astype(bf16), tri, preferred_element_type=f32) - 1.0
    own = (iota((TOK_DEV, 1), 0) + member * TOK_DEV).astype(f32)

    def look(r, code):
        first = pair_ref[pl.ds(r, 1), :]
        second = pair_ref[pl.ds(r + 32, 1), :]
        return jnp.where(first == own, second + 1.0, jnp.where(second == own, -1.0 - first, code))

    code = lax.fori_loop(0, 32, look, jnp.zeros((TOK_DEV, 128), f32), unroll=4)
    code = jnp.sum(code, axis=1, keepdims=True)
    partner = jnp.abs(code) - 1.0
    high = jnp.floor(partner * (1.0 / TOK_DEV))
    low = partner - high * TOK_DEV
    lane = iota((TOK_DEV, 128), 1)
    by_token = jnp.where(lane == 13, high, jnp.where(lane == 14, low, jnp.where(lane == 15, jnp.where(code > 0, 1.0, -1.0), 0.0)))
    by_token = jnp.where(lane == 0, iota((TOK_DEV, 128), 0).astype(f32), by_token).astype(bf16)
    rows = iota((128, TOK_DEV), 0)
    by_slot = jnp.zeros((128, TOK_DEV), f32)
    for k in range(EXP_GRP):
        for j, part in enumerate(thirds(gate[k])):
            by_slot = jnp.where(rows == 1 + 3 * k + j, part, by_slot)
    by_slot = by_slot.astype(bf16)
    base_ref[...] = lax.dot_general(
        jnp.broadcast_to(head_ref[...], (16, D)), tok_ref[...], NT, preferred_element_type=f32
    )[:8]
    height = iota((CAP, TOK_DEV), 0).astype(f32)
    picks = [
        jnp.where((place[k : k + 1] == height) & (sel[k] > 0.5), 1.0, 0.0).astype(bf16) for k in range(EXP_GRP)
    ]
    pick = jnp.concatenate(picks, axis=0)
    notes = jnp.dot(pick, by_token, preferred_element_type=f32) + lax.dot_general(
        pick, by_slot, NT, preferred_element_type=f32
    )
    wide = jnp.dot(pick, tok_ref[...], preferred_element_type=f32)
    for k in range(EXP_GRP):
        out_refs[k][:, :D] = wide[CAP * k : CAP * (k + 1)].astype(bf16)
        out_refs[k][:, D:] = notes[CAP * k : CAP * (k + 1)].astype(bf16)


def forward_kernel(info_ref, base_ref, own_w_ref, other_w_ref, *refs):
    groups, (x_ref, slope_ref, hid_ref, note_ref, part_ref, u_ref) = refs[:12], refs[12:]
    grp, zh, y = info_ref[0], info_ref[1], info_ref[3]
    u_ref[:, :HID_DEV] = own_w_ref[:D, :]
    u_ref[:, HID_DEV:] = other_w_ref[:D, :]
    start = 0
    for ref in groups:
        count = ref.shape[0]
        x_ref[start : start + count, :] = ref[:, :D]
        note_ref[start : start + count, :] = ref[:, D:].astype(f32)
        start += count
    pieces = jnp.concatenate([own_w_ref[D:, :], other_w_ref[D:, :]], axis=1).astype(f32)
    proj = pieces[0:1] + pieces[1:2] + pieces[2:3]
    pre = jnp.dot(x_ref[...], u_ref[...], preferred_element_type=f32)
    sig = jax.nn.sigmoid(pre)
    hidden = (pre * sig).astype(bf16)
    hid_ref[...] = hidden
    slope_ref[...] = proj * (sig * (1.0 + pre * (1.0 - sig)))
    value = jnp.sum(hidden.astype(f32) * proj, axis=1, keepdims=True)
    lane = iota((CAP, 128), 1)
    token = iota((CAP, TOK_DEV), 1).astype(f32)
    row = iota((16, TOK_DEV), 0)
    total = jnp.where((row == zh * 4 + y) & (grp == 0), base_ref[0:1, :], 0.0)
    for at, k, d in BLOCKS:
        note = note_ref[at : at + CAP, :]
        gate = jnp.sum(jnp.where((lane >= 1 + 3 * k) & (lane < 4 + 3 * k), note, 0.0), axis=1, keepdims=True)
        term = gate * value[at : at + CAP]
        spread = jnp.sum(jnp.where(note[:, 0:1] == token, term, 0.0), axis=0, keepdims=True)
        total = total + jnp.where(row == (zh ^ k) * 4 + (y ^ d), spread, 0.0)
    part_ref[...] = total


def backward_kernel(info_ref, table_ref, x_ref, slope_ref, hid_ref, note_ref, own_ref, send_ref, own_head_ref):
    zh, c, y = info_ref[1], info_ref[4], info_ref[3]
    table = table_ref[...]
    note = note_ref[...]
    token = iota((CAP, TOK_DEV), 1).astype(f32)
    lane = iota((CAP, 128), 1)
    mine, gates = [], []
    for at, k, d in BLOCKS:
        block = ((zh ^ k) * 4 + (y ^ d)) * 2 + c
        values = table_ref[pl.ds(block, 1), :]
        part = note_ref[at : at + CAP, :]
        mine.append(jnp.sum(jnp.where(part[:, 0:1] == token, values, 0.0), axis=1, keepdims=True))
        gates.append(
            jnp.sum(jnp.where((lane >= 1 + 3 * k) & (lane < 4 + 3 * k), part, 0.0), axis=1, keepdims=True)
        )
    mine = jnp.concatenate(mine, axis=0)
    gate = jnp.concatenate(gates, axis=0)
    hot = jnp.where(iota((ROWS, 32), 1).astype(f32) == note[:, 13:14], 1.0, 0.0).astype(bf16)
    found = jnp.zeros((ROWS, TOK_DEV), f32)
    for part in thirds(table):
        found = found + jnp.dot(hot, part.astype(bf16), preferred_element_type=f32)
    places = iota((ROWS, TOK_DEV), 1).astype(f32)
    theirs = jnp.sum(jnp.where(places == note[:, 14:15], found, 0.0), axis=1, keepdims=True)
    side = note[:, 15:16]
    margin = side * (mine - theirs)
    grad = -side * (64.0 * jax.nn.sigmoid(-margin)) * gate
    hid_grad = jnp.sum(grad * hid_ref[...].astype(f32), axis=0, keepdims=True)
    pre_grad = (grad * slope_ref[...]).astype(bf16)
    out = lax.dot_general(x_ref[...], pre_grad, (((0,), (0,)), ((), ())), preferred_element_type=f32)
    own_ref[...] = out[:, :HID_DEV]
    send_ref[:D, :] = out[:, HID_DEV:]
    own_head_ref[...] = jnp.broadcast_to(hid_grad[:, :HID_DEV], (8, HID_DEV))
    send_ref[D:, :] = jnp.broadcast_to(hid_grad[:, HID_DEV:], (8, HID_DEV))


def loss_kernel(table_ref, pair_ref, out_ref):
    parts = jnp.concatenate([p.astype(bf16) for p in thirds(table_ref[...])], axis=0)

    def rewards_of(index):
        high = jnp.floor(index * (1.0 / TOK_DEV))
        low = index - high * TOK_DEV
        count = index.shape[1]
        row = iota((96, count), 0) & 31
        hot = jnp.where(row.astype(f32) == high, 1.0, 0.0).astype(bf16)
        found = lax.dot_general(parts, hot, (((0,), (0,)), ((), ())), preferred_element_type=f32)
        return jnp.sum(jnp.where(iota((TOK_DEV, count), 0).astype(f32) == low, found, 0.0), axis=0, keepdims=True)

    def step(r, total):
        margin = rewards_of(pair_ref[pl.ds(r, 1), :]) - rewards_of(pair_ref[pl.ds(r + 8, 1), :])
        return total + jnp.maximum(-margin, 0.0) + jnp.log1p(jnp.exp(-jnp.abs(margin)))

    total = lax.fori_loop(0, 8, step, jnp.zeros((1, 512), f32))
    out_ref[...] = jnp.broadcast_to(jnp.sum(total, axis=1, keepdims=True) * (1.0 / PAIRS), (1, 128))


def final_kernel(up_ref, down_ref, own_ref, recv_ref, own_head_ref, head_ref, new_up_ref, new_down_ref):
    new_up_ref[...] = (up_ref[...].astype(f32) + (own_ref[...] + recv_ref[:D, :])).astype(bf16)
    grad = own_head_ref[0:1] + recv_ref[D : D + 1, :]
    square = (HID_DEV, HID_DEV)
    column = jnp.sum(jnp.where(iota(square, 0) == iota(square, 1), grad, 0.0), axis=1, keepdims=True)
    new_down_ref[...] = (down_ref[...].astype(f32) + column * head_ref[...].astype(f32)).astype(bf16)


def swap(block, axis, mask):
    count = lax.axis_size(axis)
    return lax.ppermute(block, axis, [(i, i ^ mask) for i in range(count)])


def relocate(block, stages):
    for axis, mask, take in stages:
        block = jnp.where(take, swap(block, axis, mask), block)
    return block


def body(tokens, routes, gate_values, old_group, move_mask, pair_index, reward_head, w_up, w_down, acc_up, acc_down):
    x, zl, zh, y, c = (lax.axis_index(a) for a in ("x", "zl", "zh", "y", "c"))
    info = jnp.stack([x * 4 + zl, zh, zh * 8 + y * 2 + c, y, c]).astype(jnp.int32)
    head = reward_head.reshape(1, D)
    mask = jnp.sum(jnp.where(jnp.arange(EXP_GRP) == zh, move_mask, 0))
    bit = [jnp.bitwise_and(jnp.right_shift(mask, i), 1) for i in range(4)]
    by_x = [("x", 1, jnp.bitwise_xor(bit[2], bit[3]) == 1), ("x", 3, bit[3] == 1)]
    by_z = [("zl", 1, bit[0] == 1), ("zl", 2, bit[1] == 1)]

    weights = pl.pallas_call(
        weights_kernel,
        out_shape=shape((D + 16, HID_DEV), bf16),
        in_specs=[VMEM] * 3,
        out_specs=VMEM,
        compiler_params=PARAMS,
        name="weights",
    )(w_up[0], w_down[0], head)
    weights = relocate(weights, by_x + by_z)
    other_weights = swap(weights, "c", 1)

    pairs = pair_index.astype(f32)
    *sent, base = pl.pallas_call(
        dispatch_kernel,
        out_shape=[shape((CAP, WIDE), bf16)] * 4 + [shape((8, TOK_DEV), f32)],
        in_specs=[SMEM] * 3 + [VMEM] * 5,
        out_specs=[VMEM] * 5,
        compiler_params=PARAMS,
        name="dispatch",
    )(old_group, move_mask, info, tokens, routes.T, gate_values.T, pairs.reshape(64, 128), head)
    far = swap(sent[2], "zh", 2)
    near = jnp.concatenate([swap(sent[1], "zh", 1), swap(sent[3], "zh", 3)], axis=0)
    held = []
    for group in (sent[0], near, far):
        held += [group] + [swap(group, "y", d) for d in (1, 2, 3)]

    xs, slope, hidden, notes, part = pl.pallas_call(
        forward_kernel,
        out_shape=[
            shape((ROWS, D), bf16),
            shape((ROWS, 2 * HID_DEV), f32),
            shape((ROWS, 2 * HID_DEV), bf16),
            shape((ROWS, 128), f32),
            shape((16, TOK_DEV), f32),
        ],
        in_specs=[SMEM] + [VMEM] * 15,
        out_specs=[VMEM] * 5,
        scratch_shapes=[pltpu.VMEM((D, 2 * HID_DEV), bf16)],
        compiler_params=PARAMS,
        name="forward",
    )(info, base, weights, other_weights, *held)

    mine = lax.all_to_all(part, ("x", "y"), 0, 0, tiled=True)
    mine = jnp.broadcast_to(jnp.sum(mine, axis=0, keepdims=True), (16, TOK_DEV))
    mine = lax.all_to_all(mine, ("zl", "zh"), 0, 0, tiled=True)
    mine = jnp.broadcast_to(jnp.sum(mine, axis=0, keepdims=True), (32, TOK_DEV))
    table = lax.all_to_all(mine, ("x", "y", "c"), 0, 0, tiled=True)

    own, send, own_head = pl.pallas_call(
        backward_kernel,
        out_shape=[shape((D, HID_DEV), f32), shape((D + 8, HID_DEV), f32), shape((8, HID_DEV), f32)],
        in_specs=[SMEM] + [VMEM] * 5,
        out_specs=[VMEM] * 3,
        compiler_params=PARAMS,
        name="backward",
    )(info, table, xs, slope, hidden, notes)
    recv = swap(send, "c", 1)
    loss = pl.pallas_call(
        loss_kernel,
        out_shape=shape((1, 128), f32),
        in_specs=[VMEM] * 2,
        out_specs=VMEM,
        compiler_params=PARAMS,
        name="loss",
    )(table, pairs.reshape(16, 512))
    up = relocate(acc_up[0], by_x + by_z)
    down = relocate(acc_down[0], by_z + by_x)
    new_up, new_down = pl.pallas_call(
        final_kernel,
        out_shape=[shape((D, HID_DEV), bf16), shape((HID_DEV, D), bf16)],
        in_specs=[VMEM] * 6,
        out_specs=[VMEM] * 2,
        compiler_params=PARAMS,
        name="final",
    )(up, down, own, recv, own_head, head)
    return new_up[None], new_down[None], loss[0, 0]


def solution(mesh):
    fine = Mesh(mesh.devices.reshape(4, 4, 4, 4, 2), ("x", "zl", "zh", "y", "c"))
    grp, ep = ("x", "zl"), ("zh", "y", "c")
    return jax.shard_map(
        body,
        mesh=fine,
        in_specs=(P(ep, None), P(ep, None), P(ep, None), P(), P(), P(), P())
        + (P(grp, None, ep), P(grp, ep, None)) * 2,
        out_specs=(P(grp, None, ep), P(grp, ep, None), P()),
        check_vma=False,
    )
```

time: 655 us -> 271 us (0.41)
  waiting for transfers between devices: 364 us -> 121 us
  local copies, waits for them, and re-layouts: 106 us -> 4.84 us
  blocking collectives: 87.8 us -> 0 us
  starting transfers between devices: 53.3 us -> 117 us
  Pallas kernels: 0 us -> 17.2 us
  other arithmetic: 20.9 us -> 5.42 us
  matrix products: 12.9 us -> 0 us
    all_to_all x3, waiting for transfers between devices: 298 us -> 10.8 us  [the longest x1 6.87 us: body(): mine = lax.all_to_all(mine, ('zl', 'zh'), 0, 0, tiled=True)]
    ppermute x8 -> x26, starting transfers between devices: 17.8 us -> 96.8 us  [swap(): return lax.ppermute(block, axis, [(i, i ^ mask) for i in range(count)])]
    all_gather x1 -> x0, blocking collectives: 55 us -> none  [body(): rewards = lax.all_gather(base_reward + summed, 'ep', axis=0, tiled=True)]
    gather x2 -> x0, local copies, waits for them, and re-layouts: 46.1 us -> none  [body(): margin = rewards[chosen] - rewards[rejected]]
    ppermute x8 -> x26, waiting for transfers between devices: 66.1 us -> 110 us  [swap(): return lax.ppermute(block, axis, [(i, i ^ mask) for i in range(count)])]
    psum x1 -> x0, blocking collectives: 32.8 us -> none  [body(): summed = lax.psum(reward_part, 'grp')]
    scatter x2 -> x0, local copies, waits for them, and re-layouts: 31.1 us -> none  [body(): jnp.zeros_like(rewards).at[chosen].set(-weight_grad).at[rejected]]
    pallas_call x0 -> x6, Pallas kernels: none -> 17.2 us  [the longest x1 6.57 us: body(): pl.pallas_call(backward_kernel, out_shape=[shape((D, HID_DEV), f32), shap...]
  transfers between devices with their start and end apart: 11 -> 29, of which waited for: 10 -> 13; matrix products, arithmetic and copies ran while one was open for 3% -> 3% of each run, Pallas kernels for 0% -> 6%
where the time goes in v1:
time: 271 us; the launch traced here: 270 us
  waiting for transfers between devices  121 us (45%)
  starting transfers between devices  117 us (43%)
  Pallas kernels  17.2 us (6%)
  other arithmetic  5.42 us (2%)
  local copies, waits for them, and re-layouts  4.84 us (2%)
  between operations  3.79 us (1%)
    ppermute x26, waiting for transfers between devices, swap(): return lax.ppermute(block, axis, [(i, i ^ mask) for i in range(count)])  110 us
    ppermute x26, starting transfers between devices, swap(): return lax.ppermute(block, axis, [(i, i ^ mask) for i in range(count)])  96.8 us
    all_to_all x1, starting transfers between devices, body(): table = lax.all_to_all(mine, ('x', 'y', 'c'), 0, 0, tiled=True)  8.39 us
    all_to_all x1, waiting for transfers between devices, body(): mine = lax.all_to_all(mine, ('zl', 'zh'), 0, 0, tiled=True)  6.87 us
    pallas_call x1, Pallas kernels, body(): pl.pallas_call(backward_kernel, out_shape=[shape((D, HID_DEV), f32), shap...  6.57 us
    all_to_all x1, starting transfers between devices, body(): mine = lax.all_to_all(part, ('x', 'y'), 0, 0, tiled=True)  6.19 us
    all_to_all x1, starting transfers between devices, body(): mine = lax.all_to_all(mine, ('zl', 'zh'), 0, 0, tiled=True)  5.9 us
  transfers between devices with their start and end apart: 29, of which 13 were waited for; matrix products, arithmetic and copies ran while one was open for 3% of the time, Pallas kernels for 6%

profile of v1, /device:TPU:1, one launch (start us, length us, event | category | flops | bytes accessed | tf_op | source)
XLA Modules:
  0.0 269.7 jit_solution(18288366992935170742)
XLA Ops:
  0.6 0.7 reshape.30.head_ref
  1.3 1.0 copy-done.1
  2.4 1.0 copy-done.2
  3.4 0.3 weights.1
  3.7 3.9 %collective-permute-start.8 = (bf16[2064,128]{1,0:T(8,128)(2,1)S(1)}, bf16[2064,128]{1,0:T(8,128)(2,1)S(1)}, u32[]{:S(2)}, u32[]{:S(2)}) collective-permute-start(bf16[2064,128]{1,0:T(8,128)(2,1)S(1)} %weights.1), channel_id=1, source_target_pairs={{0,128},{128,0},{256,384},{384,256},{1,129},{129,1},{257,385},{385... | collective-permute-start | bytes 1585160 | tf_op jit(solution)/shard_map/ppermute | solution.py:214
  7.6 0.6 fusion
  9.6 4.8 %collective-permute-done.8 = bf16[2064,128]{1,0:T(8,128)(2,1)S(1)} collective-permute-done((bf16[2064,128]{1,0:T(8,128)(2,1)S(1)}, bf16[2064,128]{1,0:T(8,128)(2,1)S(1)}, u32[]{:S(2)}, u32[]{:S(2)}) %collective-permute-start.8) | collective-permute-done | bytes 528416 | tf_op jit(solution)/shard_map/ppermute | solution.py:214
  14.5 9.5 %collective-permute-start.9 = (bf16[2064,128]{1,0:T(8,128)(2,1)S(1)}, bf16[2064,128]{1,0:T(8,128)(2,1)S(1)}, u32[]{:S(2)}, u32[]{:S(2)}) collective-permute-start(bf16[2064,128]{1,0:T(8,128)(2,1)S(1)} %broadcast_select_fusion), channel_id=1, source_target_pairs={{0,384},{128,256},{256,128},{384,0},{1,385},{129,257},{257,129},{3... | collective-permute-start | bytes 1585160 | tf_op jit(solution)/shard_map/ppermute | solution.py:214
  23.9 9.7 %collective-permute-done.9 = bf16[2064,128]{1,0:T(8,128)(2,1)S(1)} collective-permute-done((bf16[2064,128]{1,0:T(8,128)(2,1)S(1)}, bf16[2064,128]{1,0:T(8,128)(2,1)S(1)}, u32[]{:S(2)}, u32[]{:S(2)}) %collective-permute-start.9) | collective-permute-done | bytes 528416 | tf_op jit(solution)/shard_map/ppermute | solution.py:214
  33.7 4.5 %collective-permute-start.10 = (bf16[2064,128]{1,0:T(8,128)(2,1)S(1)}, bf16[2064,128]{1,0:T(8,128)(2,1)S(1)}, u32[]{:S(2)}, u32[]{:S(2)}) collective-permute-start(bf16[2064,128]{1,0:T(8,128)(2,1)S(1)} %broadcast_select_fusion.1), channel_id=1, source_target_pairs={{0,32},{32,0},{64,96},{96,64},{1,33},{33,1},{65,97},{97,65},{2,34}... | collective-permute-start | bytes 1585160 | tf_op jit(solution)/shard_map/ppermute | solution.py:214
  38.2 0.1 stack.23.info_ref
  38.4 2.2 dispatch.1
  40.6 3.3 %collective-permute-start.13 = (bf16[48,2176]{1,0:T(8,128)(2,1)S(1)}, bf16[48,2176]{1,0:T(8,128)(2,1)S(1)}, u32[]{:S(2)}, u32[]{:S(2)}) collective-permute-start(bf16[48,2176]{1,0:T(8,128)(2,1)S(1)} %get-tuple-element.19.refs_0_), channel_id=1, source_target_pairs={{0,2},{2,0},{4,6},{6,4},{1,3},{3,1},{5,7},{7,5},{8,10},{10,8},{12,... | collective-permute-start | bytes 626696 | tf_op jit(solution)/shard_map/ppermute | solution.py:214
  43.9 4.5 %collective-permute-start.14 = (bf16[48,2176]{1,0:T(8,128)(2,1)S(1)}, bf16[48,2176]{1,0:T(8,128)(2,1)S(1)}, u32[]{:S(2)}, u32[]{:S(2)}) collective-permute-start(bf16[48,2176]{1,0:T(8,128)(2,1)S(1)} %get-tuple-element.19.refs_0_), channel_id=1, source_target_pairs={{0,4},{2,6},{4,0},{6,2},{1,5},{3,7},{5,1},{7,3},{8,12},{10,14},{12... | collective-permute-start | bytes 626696 | tf_op jit(solution)/shard_map/ppermute | solution.py:214
  48.5 8.8 %collective-permute-start.16 = (bf16[48,2176]{1,0:T(8,128)(2,1)S(1)}, bf16[48,2176]{1,0:T(8,128)(2,1)S(1)}, u32[]{:S(2)}, u32[]{:S(2)}) collective-permute-start(bf16[48,2176]{1,0:T(8,128)(2,1)S(1)} %get-tuple-element.20), channel_id=1, source_target_pairs={{0,8},{8,0},{16,24},{24,16},{1,9},{9,1},{17,25},{25,17},{2,10},{10... | collective-permute-start | bytes 626696 | tf_op jit(solution)/shard_map/ppermute | solution.py:214
  57.3 7.9 %collective-permute-start.17 = (bf16[48,2176]{1,0:T(8,128)(2,1)S(1)}, bf16[48,2176]{1,0:T(8,128)(2,1)S(1)}, u32[]{:S(2)}, u32[]{:S(2)}) collective-permute-start(bf16[48,2176]{1,0:T(8,128)(2,1)S(1)} %get-tuple-element.21), channel_id=1, source_target_pairs={{0,24},{8,16},{16,8},{24,0},{1,25},{9,17},{17,9},{25,1},{2,26},{10... | collective-permute-start | bytes 626696 | tf_op jit(solution)/shard_map/ppermute | solution.py:214
  66.5 2.6 collective-permute-start.4
  69.2 0.1 broadcast_select_fusion.2
  69.2 6.5 %collective-permute-done.16 = bf16[48,2176]{1,0:T(8,128)(2,1)S(1)} collective-permute-done((bf16[48,2176]{1,0:T(8,128)(2,1)S(1)}, bf16[48,2176]{1,0:T(8,128)(2,1)S(1)}, u32[]{:S(2)}, u32[]{:S(2)}) %collective-permute-start.16) | collective-permute-done | bytes 208928 | tf_op jit(solution)/shard_map/ppermute | solution.py:214
  75.7 1.9 collective-permute-start.11
  77.6 28.0 %collective-permute-done.4 = bf16[128,2048]{1,0:T(8,128)(2,1)S(1)} collective-permute-done((bf16[128,2048]{1,0:T(8,128)(2,1)}, bf16[128,2048]{1,0:T(8,128)(2,1)S(1)}, u32[]{:S(2)}, u32[]{:S(2)}) %collective-permute-start.4) | collective-permute-done | bytes 524320 | tf_op jit(solution)/shard_map/ppermute | solution.py:214
  105.6 1.9 collective-permute-start.21
  107.6 0.1 broadcast_select_fusion.4
  107.6 1.9 collective-permute-start.15
  109.6 21.6 %collective-permute-done.21.refs_8_ = bf16[48,2176]{1,0:T(8,128)(2,1)S(1)} collective-permute-done((bf16[48,2176]{1,0:T(8,128)(2,1)S(1)}, bf16[48,2176]{1,0:T(8,128)(2,1)S(1)}, u32[]{:S(2)}, u32[]{:S(2)}) %collective-permute-start.21) | collective-permute-done | bytes 208928 | tf_op jit(solution)/shard_map/ppermute | solution.py:214
  131.2 1.9 collective-permute-start
  133.1 1.9 collective-permute-start.22
  135.1 0.1 broadcast_select_fusion.3.own_w_ref
  135.1 3.0 %collective-permute-start.23 = (bf16[48,2176]{1,0:T(8,128)(2,1)S(1)}, bf16[48,2176]{1,0:T(8,128)(2,1)S(1)}, u32[]{:S(2)}, u32[]{:S(2)}) collective-permute-start(bf16[48,2176]{1,0:T(8,128)(2,1)S(1)} %collective-permute-done.21.refs_8_), channel_id=1, source_target_pairs={{0,4},{2,6},{4,0},{6,2},{1,5},{3,7},{5,1},{7,3},{8,12},{10,14},{12... | collective-permute-start | bytes 626696 | tf_op jit(solution)/shard_map/ppermute | solution.py:214
  138.2 4.7 %collective-permute-start.24 = (bf16[48,2176]{1,0:T(8,128)(2,1)S(1)}, bf16[48,2176]{1,0:T(8,128)(2,1)S(1)}, u32[]{:S(2)}, u32[]{:S(2)}) collective-permute-start(bf16[48,2176]{1,0:T(8,128)(2,1)S(1)} %collective-permute-done.21.refs_8_), channel_id=1, source_target_pairs={{0,6},{2,4},{4,2},{6,0},{1,7},{3,5},{5,3},{7,1},{8,14},{10,12},{12... | collective-permute-start | bytes 626696 | tf_op jit(solution)/shard_map/ppermute | solution.py:214
  142.8 1.9 collective-permute-start.5
  144.8 3.5 %collective-permute-start.12 = (bf16[2064,128]{1,0:T(8,128)(2,1)S(1)}, bf16[2064,128]{1,0:T(8,128)(2,1)S(1)}, u32[]{:S(2)}, u32[]{:S(2)}) collective-permute-start(bf16[2064,128]{1,0:T(8,128)(2,1)S(1)} %broadcast_select_fusion.3.own_w_ref), channel_id=1, source_target_pairs={{0,1},{1,0},{2,3},{3,2},{4,5},{5,4},{6,7},{7,6},{8,9},{9,8},{10,11... | collective-permute-start | bytes 1585160 | tf_op jit(solution)/shard_map/ppermute | solution.py:214
  148.3 1.9 collective-permute-start.18
  150.3 0.4 collective-permute-done.24.refs_11_
  150.7 3.6 %collective-permute-start.19 = (bf16[96,2176]{1,0:T(8,128)(2,1)S(1)}, bf16[96,2176]{1,0:T(8,128)(2,1)S(1)}, u32[]{:S(2)}, u32[]{:S(2)}) collective-permute-start(bf16[96,2176]{1,0:T(8,128)(2,1)S(1)} %constant_dynamic-update-slice_fusion.refs_4_), channel_id=1, source_target_pairs={{0,4},{2,6},{4,0},{6,2},{1,5},{3,7},{5,1},{7,3},{8,12},{10,14},{12... | collective-permute-start | bytes 1253384 | tf_op jit(solution)/shard_map/ppermute | solution.py:214
  154.3 3.6 %collective-permute-start.20 = (bf16[96,2176]{1,0:T(8,128)(2,1)S(1)}, bf16[96,2176]{1,0:T(8,128)(2,1)S(1)}, u32[]{:S(2)}, u32[]{:S(2)}) collective-permute-start(bf16[96,2176]{1,0:T(8,128)(2,1)S(1)} %constant_dynamic-update-slice_fusion.refs_4_), channel_id=1, source_target_pairs={{0,6},{2,4},{4,2},{6,0},{1,7},{3,5},{5,3},{7,1},{8,14},{10,12},{12... | collective-permute-start | bytes 1253384 | tf_op jit(solution)/shard_map/ppermute | solution.py:214
  158.0 3.6 %collective-permute-done.18.refs_5_ = bf16[96,2176]{1,0:T(8,128)(2,1)S(1)} collective-permute-done((bf16[96,2176]{1,0:T(8,128)(2,1)S(1)}, bf16[96,2176]{1,0:T(8,128)(2,1)S(1)}, u32[]{:S(2)}, u32[]{:S(2)}) %collective-permute-start.18) | collective-permute-done | bytes 417824 | tf_op jit(solution)/shard_map/ppermute | solution.py:214
  161.6 4.1 %collective-permute-start.1 = (bf16[2048,128]{1,0:T(8,128)(2,1)S(1)}, bf16[2048,128]{1,0:T(8,128)(2,1)}, u32[]{:S(2)}, u32[]{:S(2)}) collective-permute-start(bf16[2048,128]{1,0:T(8,128)(2,1)S(1)} %broadcast_select_fusion.8), channel_id=1, source_target_pairs={{0,384},{128,256},{256,128},{384,0},{1,385},{129,257},{257,129},{3... | collective-permute-start | bytes 1572872 | tf_op jit(solution)/shard_map/ppermute | solution.py:214
  165.7 3.1 %collective-permute-done.19.refs_6_ = bf16[96,2176]{1,0:T(8,128)(2,1)S(1)} collective-permute-done((bf16[96,2176]{1,0:T(8,128)(2,1)S(1)}, bf16[96,2176]{1,0:T(8,128)(2,1)S(1)}, u32[]{:S(2)}, u32[]{:S(2)}) %collective-permute-start.19) | collective-permute-done | bytes 417824 | tf_op jit(solution)/shard_map/ppermute | solution.py:214
  168.8 8.5 %collective-permute-done.20.refs_7_ = bf16[96,2176]{1,0:T(8,128)(2,1)S(1)} collective-permute-done((bf16[96,2176]{1,0:T(8,128)(2,1)S(1)}, bf16[96,2176]{1,0:T(8,128)(2,1)S(1)}, u32[]{:S(2)}, u32[]{:S(2)}) %collective-permute-start.20) | collective-permute-done | bytes 417824 | tf_op jit(solution)/shard_map/ppermute | solution.py:214
  177.3 3.5 %forward.1 = (bf16[768,2048]{1,0:T(8,128)(2,1)}, f32[768,256]{1,0:T(8,128)S(1)}, bf16[768,256]{1,0:T(8,128)(2,1)S(1)}, f32[768,128]{1,0:T(8,128)S(1)}, f32[16,256]{1,0:T(8,128)S(1)}) custom-call(s32[5]{0:T(128)S(1)} %stack.23.info_ref, f32[8,256]{1,0:T(8,128)S(1)} %get-tuple-element.18.base_ref, bf16[2064,128]{1,0:T(8,128)(2,1)S(1)} %broadcast_select_fusion.3.own_w_ref, ...), custom_call_target="tpu_custom_call" | custom-call | tf_op jit(solution)/shard_map/forward/pallas_call | solution.py:258
  180.8 0.6 copy.16
  181.4 6.2 %all-to-all-start = ((f32[16,1,256]{2,1,0:T(1,128)}), f32[16,1,256]{2,1,0:T(1,128)S(1)}, u32[]{:S(2)}, u32[]{:S(2)}) async-start(f32[16,1,256]{2,1,0:T(1,128)} %copy.16), calls=%async_computation | async-start | bytes 32768 | tf_op jit(solution)/shard_map/all_to_all | solution.py:274
  187.7 1.1 broadcast_select_fusion.5
  188.8 3.3 %collective-permute-start.6 = (bf16[128,2048]{1,0:T(8,128)(2,1)S(1)}, bf16[128,2048]{1,0:T(8,128)(2,1)}, u32[]{:S(2)}, u32[]{:S(2)}) collective-permute-start(bf16[128,2048]{1,0:T(8,128)(2,1)S(1)} %broadcast_select_fusion.5), channel_id=1, source_target_pairs={{0,128},{128,0},{256,384},{384,256},{1,129},{129,1},{257,385},{385... | collective-permute-start | bytes 1572872 | tf_op jit(solution)/shard_map/ppermute | solution.py:214
  192.0 2.0 all-to-all-done
  194.1 0.6 broadcast_in_dim.23
  194.7 5.9 %all-to-all-start.1 = ((f32[16,1,256]{2,1,0:T(1,128)}), f32[16,1,256]{2,1,0:T(1,128)S(1)}, u32[]{:S(2)}, u32[]{:S(2)}) async-start(f32[16,1,256]{2,1,0:T(1,128)} %broadcast_in_dim.23), calls=%async_computation.1 | async-start | bytes 32768 | tf_op jit(solution)/shard_map/all_to_all | solution.py:276
  200.7 1.1 broadcast_select_fusion.9
  201.8 3.3 %collective-permute-start.2 = (bf16[2048,128]{1,0:T(8,128)(2,1)S(1)}, bf16[2048,128]{1,0:T(8,128)(2,1)}, u32[]{:S(2)}, u32[]{:S(2)}) collective-permute-start(bf16[2048,128]{1,0:T(8,128)(2,1)S(1)} %broadcast_select_fusion.9), channel_id=1, source_target_pairs={{0,32},{32,0},{64,96},{96,64},{1,33},{33,1},{65,97},{97,65},{2,34}... | collective-permute-start | bytes 1572872 | tf_op jit(solution)/shard_map/ppermute | solution.py:214
  205.1 6.9 %all-to-all-done.1 = f32[16,1,256]{2,1,0:T(1,128)S(1)} async-done(((f32[16,1,256]{2,1,0:T(1,128)}), f32[16,1,256]{2,1,0:T(1,128)S(1)}, u32[]{:S(2)}, u32[]{:S(2)}) %all-to-all-start.1) | async-done | bytes 16416 | tf_op jit(solution)/shard_map/all_to_all | solution.py:276
  212.0 0.6 broadcast_in_dim.24
  212.6 8.4 %all-to-all-start.2 = ((f32[32,1,256]{2,1,0:T(1,128)}), f32[32,1,256]{2,1,0:T(1,128)S(1)}, u32[]{:S(2)}, u32[]{:S(2)}) async-start(f32[32,1,256]{2,1,0:T(1,128)} %broadcast_in_dim.24), calls=%async_computation.2 | async-start | bytes 65536 | tf_op jit(solution)/shard_map/all_to_all | solution.py:278
  221.0 0.9 broadcast_select_fusion.6
  221.9 4.5 %collective-permute-start.7 = (bf16[128,2048]{1,0:T(8,128)(2,1)}, bf16[128,2048]{1,0:T(8,128)(2,1)}, u32[]{:S(2)}, u32[]{:S(2)}) collective-permute-start(bf16[128,2048]{1,0:T(8,128)(2,1)} %broadcast_select_fusion.6), channel_id=1, source_target_pairs={{0,384},{128,256},{256,128},{384,0},{1,385},{129,257},{257,129},{3... | collective-permute-start | bytes 1572872 | tf_op jit(solution)/shard_map/ppermute | solution.py:214
  226.4 1.9 all-to-all-done.2
  228.3 6.6 %backward.1 = (f32[2048,128]{1,0:T(8,128)S(1)}, f32[2056,128]{1,0:T(8,128)}, f32[8,128]{1,0:T(8,128)S(1)}) custom-call(s32[5]{0:T(128)S(1)} %stack.23.info_ref, f32[32,256]{1,0:T(8,128)S(1)} %bitcast.25, bf16[768,2048]{1,0:T(8,128)(2,1)} %get-tuple-element.24.x_ref, f32[768,256]{1,0:T(8,128)S(1)} %get-tuple-element.25.slope_ref, ...), custom_call_target="tpu_custom_call" | custom-call | tf_op jit(solution)/shard_map/backward/pallas_call | solution.py:280
  234.9 2.3 collective-permute-start.25
  237.2 0.1 broadcast_select_fusion.10
  237.2 2.4 collective-permute-start.3
  239.7 1.1 broadcast_select_fusion.7.down_ref
  240.8 24.2 %collective-permute-done.3 = bf16[2048,128]{1,0:T(8,128)(2,1)S(1)} collective-permute-done((bf16[2048,128]{1,0:T(8,128)(2,1)S(1)}, bf16[2048,128]{1,0:T(8,128)(2,1)S(1)}, u32[]{:S(2)}, u32[]{:S(2)}) %collective-permute-start.3) | collective-permute-done | bytes 524320 | tf_op jit(solution)/shard_map/ppermute | solution.py:214
  265.1 3.4 %loss.1 = f32[1,128]{1,0:T(1,128)} custom-call(f32[32,256]{1,0:T(8,128)S(1)} %bitcast.26, f32[16,512]{1,0:T(8,128)S(1)} %reshape.31.pair_ref), custom_call_target="tpu_custom_call" | custom-call | tf_op jit(solution)/shard_map/loss/pallas_call | solution.py:289
  268.4 1.3 final.1
  (45 shorter events, 0.4 us)
Async XLA Ops:
  0.6 7.0 %copy-start.5 = (s32[4]{0:T(128)S(1)}, s32[4]{0:T(128)}, u32[]{:S(2)}) copy-start(s32[4]{0:T(128)} %mask_ref.1) | copy-start | bytes 52
  1.3 1.0 copy-start.1
  2.4 1.0 copy-start.2
  3.7 10.7 %collective-permute-start.8 = (bf16[2064,128]{1,0:T(8,128)(2,1)S(1)}, bf16[2064,128]{1,0:T(8,128)(2,1)S(1)}, u32[]{:S(2)}, u32[]{:S(2)}) collective-permute-start(bf16[2064,128]{1,0:T(8,128)(2,1)S(1)} %weights.1), channel_id=1, source_target_pairs={{0,128},{128,0},{256,384},{384,256},{1,129},{129,1},{257,385},{385... | collective-permute-start | bytes 1585160 | tf_op jit(solution)/shard_map/ppermute | solution.py:214
  14.4 23.9 %copy-start.9 = (s32[8192]{0:T(1024)S(1)}, s32[8192]{0:T(1024)}, u32[]{:S(2)}) copy-start(s32[8192]{0:T(1024)} %param.16) | copy-start | bytes 98308
  14.4 23.9 %copy-start = (bf16[256,2048]{1,0:T(8,128)(2,1)S(1)}, bf16[256,2048]{1,0:T(8,128)(2,1)}, u32[]{:S(2)}) copy-start(bf16[256,2048]{1,0:T(8,128)(2,1)} %tok_ref.1) | copy-start | bytes 3145732
  14.4 23.9 %copy-start.3 = (s32[256,8]{0,1:T(8,128)S(1)}, s32[256,8]{0,1:T(8,128)}, u32[]{:S(2)}) copy-start(s32[256,8]{0,1:T(8,128)} %param.12) | copy-start | bytes 24580
  14.4 23.9 %copy-start.4 = (f32[256,8]{0,1:T(8,128)S(1)}, f32[256,8]{0,1:T(8,128)}, u32[]{:S(2)}) copy-start(f32[256,8]{0,1:T(8,128)} %param.13) | copy-start | bytes 24580
  14.5 23.9 %copy-start.6 = (s32[64]{0:T(128)S(1)}, s32[64]{0:T(128)}, u32[]{:S(2)}) copy-start(s32[64]{0:T(128)} %group_ref.1) | copy-start | bytes 772
  14.5 19.2 %collective-permute-start.9 = (bf16[2064,128]{1,0:T(8,128)(2,1)S(1)}, bf16[2064,128]{1,0:T(8,128)(2,1)S(1)}, u32[]{:S(2)}, u32[]{:S(2)}) collective-permute-start(bf16[2064,128]{1,0:T(8,128)(2,1)S(1)} %broadcast_select_fusion), channel_id=1, source_target_pairs={{0,384},{128,256},{256,128},{384,0},{1,385},{129,257},{257,129},{3... | collective-permute-start | bytes 1585160 | tf_op jit(solution)/shard_map/ppermute | solution.py:214
  33.7 32.8 %collective-permute-start.10 = (bf16[2064,128]{1,0:T(8,128)(2,1)S(1)}, bf16[2064,128]{1,0:T(8,128)(2,1)S(1)}, u32[]{:S(2)}, u32[]{:S(2)}) collective-permute-start(bf16[2064,128]{1,0:T(8,128)(2,1)S(1)} %broadcast_select_fusion.1), channel_id=1, source_target_pairs={{0,32},{32,0},{64,96},{96,64},{1,33},{33,1},{65,97},{97,65},{2,34}... | collective-permute-start | bytes 1585160 | tf_op jit(solution)/shard_map/ppermute | solution.py:214
  40.6 67.0 %copy-start.7 = (bf16[1,128,2048]{2,1,0:T(8,128)(2,1)S(1)}, bf16[1,128,2048]{2,1,0:T(8,128)(2,1)}, u32[]{:S(2)}) copy-start(bf16[1,128,2048]{2,1,0:T(8,128)(2,1)} %param.21) | copy-start | bytes 1572868
  40.6 94.6 %collective-permute-start.13 = (bf16[48,2176]{1,0:T(8,128)(2,1)S(1)}, bf16[48,2176]{1,0:T(8,128)(2,1)S(1)}, u32[]{:S(2)}, u32[]{:S(2)}) collective-permute-start(bf16[48,2176]{1,0:T(8,128)(2,1)S(1)} %get-tuple-element.19.refs_0_), channel_id=1, source_target_pairs={{0,2},{2,0},{4,6},{6,4},{1,3},{3,1},{5,7},{7,5},{8,10},{10,8},{12,... | collective-permute-start | bytes 626696 | tf_op jit(solution)/shard_map/ppermute | solution.py:214
  43.9 94.3 %collective-permute-start.14 = (bf16[48,2176]{1,0:T(8,128)(2,1)S(1)}, bf16[48,2176]{1,0:T(8,128)(2,1)S(1)}, u32[]{:S(2)}, u32[]{:S(2)}) collective-permute-start(bf16[48,2176]{1,0:T(8,128)(2,1)S(1)} %get-tuple-element.19.refs_0_), channel_id=1, source_target_pairs={{0,4},{2,6},{4,0},{6,2},{1,5},{3,7},{5,1},{7,3},{8,12},{10,14},{12... | collective-permute-start | bytes 626696 | tf_op jit(solution)/shard_map/ppermute | solution.py:214
  48.5 27.2 %collective-permute-start.16 = (bf16[48,2176]{1,0:T(8,128)(2,1)S(1)}, bf16[48,2176]{1,0:T(8,128)(2,1)S(1)}, u32[]{:S(2)}, u32[]{:S(2)}) collective-permute-start(bf16[48,2176]{1,0:T(8,128)(2,1)S(1)} %get-tuple-element.20), channel_id=1, source_target_pairs={{0,8},{8,0},{16,24},{24,16},{1,9},{9,1},{17,25},{25,17},{2,10},{10... | collective-permute-start | bytes 626696 | tf_op jit(solution)/shard_map/ppermute | solution.py:214
  57.3 50.4 %collective-permute-start.17 = (bf16[48,2176]{1,0:T(8,128)(2,1)S(1)}, bf16[48,2176]{1,0:T(8,128)(2,1)S(1)}, u32[]{:S(2)}, u32[]{:S(2)}) collective-permute-start(bf16[48,2176]{1,0:T(8,128)(2,1)S(1)} %get-tuple-element.21), channel_id=1, source_target_pairs={{0,24},{8,16},{16,8},{24,0},{1,25},{9,17},{17,9},{25,1},{2,26},{10... | collective-permute-start | bytes 626696 | tf_op jit(solution)/shard_map/ppermute | solution.py:214
  66.5 39.1 %collective-permute-start.4 = (bf16[128,2048]{1,0:T(8,128)(2,1)}, bf16[128,2048]{1,0:T(8,128)(2,1)S(1)}, u32[]{:S(2)}, u32[]{:S(2)}) collective-permute-start(bf16[128,2048]{1,0:T(8,128)(2,1)} %bitcast.30), channel_id=1, source_target_pairs={{0,32},{32,0},{64,96},{96,64},{1,33},{33,1},{65,97},{97,65},{2,34}... | collective-permute-start | bytes 1572872 | tf_op jit(solution)/shard_map/ppermute | solution.py:214
  69.2 62.0 %copy-start.8 = (bf16[1,2048,128]{2,1,0:T(8,128)(2,1)S(1)}, bf16[1,2048,128]{2,1,0:T(8,128)(2,1)}, u32[]{:S(2)}) copy-start(bf16[1,2048,128]{2,1,0:T(8,128)(2,1)} %param.20) | copy-start | bytes 1572868
  75.7 57.4 %collective-permute-start.11 = (bf16[2064,128]{1,0:T(8,128)(2,1)S(1)}, bf16[2064,128]{1,0:T(8,128)(2,1)S(1)}, u32[]{:S(2)}, u32[]{:S(2)}) collective-permute-start(bf16[2064,128]{1,0:T(8,128)(2,1)S(1)} %broadcast_select_fusion.2), channel_id=1, source_target_pairs={{0,64},{32,96},{64,0},{96,32},{1,65},{33,97},{65,1},{97,33},{2,66}... | collective-permute-start | bytes 1585160 | tf_op jit(solution)/shard_map/ppermute | solution.py:214
  105.6 25.6 %collective-permute-start.21 = (bf16[48,2176]{1,0:T(8,128)(2,1)S(1)}, bf16[48,2176]{1,0:T(8,128)(2,1)S(1)}, u32[]{:S(2)}, u32[]{:S(2)}) collective-permute-start(bf16[48,2176]{1,0:T(8,128)(2,1)S(1)} %get-tuple-element.22), channel_id=1, source_target_pairs={{0,16},{8,24},{16,0},{24,8},{1,17},{9,25},{17,1},{25,9},{2,18},{10... | collective-permute-start | bytes 626696 | tf_op jit(solution)/shard_map/ppermute | solution.py:214
  107.6 35.2 %collective-permute-start.15 = (bf16[48,2176]{1,0:T(8,128)(2,1)S(1)}, bf16[48,2176]{1,0:T(8,128)(2,1)S(1)}, u32[]{:S(2)}, u32[]{:S(2)}) collective-permute-start(bf16[48,2176]{1,0:T(8,128)(2,1)S(1)} %get-tuple-element.19.refs_0_), channel_id=1, source_target_pairs={{0,6},{2,4},{4,2},{6,0},{1,7},{3,5},{5,3},{7,1},{8,14},{10,12},{12... | collective-permute-start | bytes 626696 | tf_op jit(solution)/shard_map/ppermute | solution.py:214
  131.2 23.1 %collective-permute-start = (bf16[2048,128]{1,0:T(8,128)(2,1)S(1)}, bf16[2048,128]{1,0:T(8,128)(2,1)S(1)}, u32[]{:S(2)}, u32[]{:S(2)}) collective-permute-start(bf16[2048,128]{1,0:T(8,128)(2,1)S(1)} %bitcast.31), channel_id=1, source_target_pairs={{0,128},{128,0},{256,384},{384,256},{1,129},{129,1},{257,385},{385... | collective-permute-start | bytes 1572872 | tf_op jit(solution)/shard_map/ppermute | solution.py:214
  133.1 11.6 %collective-permute-start.22 = (bf16[48,2176]{1,0:T(8,128)(2,1)S(1)}, bf16[48,2176]{1,0:T(8,128)(2,1)S(1)}, u32[]{:S(2)}, u32[]{:S(2)}) collective-permute-start(bf16[48,2176]{1,0:T(8,128)(2,1)S(1)} %collective-permute-done.21.refs_8_), channel_id=1, source_target_pairs={{0,2},{2,0},{4,6},{6,4},{1,3},{3,1},{5,7},{7,5},{8,10},{10,8},{12,... | collective-permute-start | bytes 626696 | tf_op jit(solution)/shard_map/ppermute | solution.py:214
  135.1 13.2 %collective-permute-start.23 = (bf16[48,2176]{1,0:T(8,128)(2,1)S(1)}, bf16[48,2176]{1,0:T(8,128)(2,1)S(1)}, u32[]{:S(2)}, u32[]{:S(2)}) collective-permute-start(bf16[48,2176]{1,0:T(8,128)(2,1)S(1)} %collective-permute-done.21.refs_8_), channel_id=1, source_target_pairs={{0,4},{2,6},{4,0},{6,2},{1,5},{3,7},{5,1},{7,3},{8,12},{10,14},{12... | collective-permute-start | bytes 626696 | tf_op jit(solution)/shard_map/ppermute | solution.py:214
  138.2 12.5 %collective-permute-start.24 = (bf16[48,2176]{1,0:T(8,128)(2,1)S(1)}, bf16[48,2176]{1,0:T(8,128)(2,1)S(1)}, u32[]{:S(2)}, u32[]{:S(2)}) collective-permute-start(bf16[48,2176]{1,0:T(8,128)(2,1)S(1)} %collective-permute-done.21.refs_8_), channel_id=1, source_target_pairs={{0,6},{2,4},{4,2},{6,0},{1,7},{3,5},{5,3},{7,1},{8,14},{10,12},{12... | collective-permute-start | bytes 626696 | tf_op jit(solution)/shard_map/ppermute | solution.py:214
  142.8 44.8 %collective-permute-start.5 = (bf16[128,2048]{1,0:T(8,128)(2,1)S(1)}, bf16[128,2048]{1,0:T(8,128)(2,1)}, u32[]{:S(2)}, u32[]{:S(2)}) collective-permute-start(bf16[128,2048]{1,0:T(8,128)(2,1)S(1)} %broadcast_select_fusion.4), channel_id=1, source_target_pairs={{0,64},{32,96},{64,0},{96,32},{1,65},{33,97},{65,1},{97,33},{2,66}... | collective-permute-start | bytes 1572872 | tf_op jit(solution)/shard_map/ppermute | solution.py:214
  144.8 32.5 %collective-permute-start.12 = (bf16[2064,128]{1,0:T(8,128)(2,1)S(1)}, bf16[2064,128]{1,0:T(8,128)(2,1)S(1)}, u32[]{:S(2)}, u32[]{:S(2)}) collective-permute-start(bf16[2064,128]{1,0:T(8,128)(2,1)S(1)} %broadcast_select_fusion.3.own_w_ref), channel_id=1, source_target_pairs={{0,1},{1,0},{2,3},{3,2},{4,5},{5,4},{6,7},{7,6},{8,9},{9,8},{10,11... | collective-permute-start | bytes 1585160 | tf_op jit(solution)/shard_map/ppermute | solution.py:214
  148.3 13.3 %collective-permute-start.18 = (bf16[96,2176]{1,0:T(8,128)(2,1)S(1)}, bf16[96,2176]{1,0:T(8,128)(2,1)S(1)}, u32[]{:S(2)}, u32[]{:S(2)}) collective-permute-start(bf16[96,2176]{1,0:T(8,128)(2,1)S(1)} %constant_dynamic-update-slice_fusion.refs_4_), channel_id=1, source_target_pairs={{0,2},{2,0},{4,6},{6,4},{1,3},{3,1},{5,7},{7,5},{8,10},{10,8},{12,... | collective-permute-start | bytes 1253384 | tf_op jit(solution)/shard_map/ppermute | solution.py:214
  150.7 18.1 %collective-permute-start.19 = (bf16[96,2176]{1,0:T(8,128)(2,1)S(1)}, bf16[96,2176]{1,0:T(8,128)(2,1)S(1)}, u32[]{:S(2)}, u32[]{:S(2)}) collective-permute-start(bf16[96,2176]{1,0:T(8,128)(2,1)S(1)} %constant_dynamic-update-slice_fusion.refs_4_), channel_id=1, source_target_pairs={{0,4},{2,6},{4,0},{6,2},{1,5},{3,7},{5,1},{7,3},{8,12},{10,14},{12... | collective-permute-start | bytes 1253384 | tf_op jit(solution)/shard_map/ppermute | solution.py:214
  154.3 23.0 %collective-permute-start.20 = (bf16[96,2176]{1,0:T(8,128)(2,1)S(1)}, bf16[96,2176]{1,0:T(8,128)(2,1)S(1)}, u32[]{:S(2)}, u32[]{:S(2)}) collective-permute-start(bf16[96,2176]{1,0:T(8,128)(2,1)S(1)} %constant_dynamic-update-slice_fusion.refs_4_), channel_id=1, source_target_pairs={{0,6},{2,4},{4,2},{6,0},{1,7},{3,5},{5,3},{7,1},{8,14},{10,12},{12... | collective-permute-start | bytes 1253384 | tf_op jit(solution)/shard_map/ppermute | solution.py:214
  161.6 39.0 %collective-permute-start.1 = (bf16[2048,128]{1,0:T(8,128)(2,1)S(1)}, bf16[2048,128]{1,0:T(8,128)(2,1)}, u32[]{:S(2)}, u32[]{:S(2)}) collective-permute-start(bf16[2048,128]{1,0:T(8,128)(2,1)S(1)} %broadcast_select_fusion.8), channel_id=1, source_target_pairs={{0,384},{128,256},{256,128},{384,0},{1,385},{129,257},{257,129},{3... | collective-permute-start | bytes 1572872 | tf_op jit(solution)/shard_map/ppermute | solution.py:214
  181.4 12.6 %all-to-all-start = ((f32[16,1,256]{2,1,0:T(1,128)}), f32[16,1,256]{2,1,0:T(1,128)S(1)}, u32[]{:S(2)}, u32[]{:S(2)}) async-start(f32[16,1,256]{2,1,0:T(1,128)} %copy.16), calls=%async_computation | async-start | bytes 32768 | tf_op jit(solution)/shard_map/all_to_all | solution.py:274
  188.8 32.2 %collective-permute-start.6 = (bf16[128,2048]{1,0:T(8,128)(2,1)S(1)}, bf16[128,2048]{1,0:T(8,128)(2,1)}, u32[]{:S(2)}, u32[]{:S(2)}) collective-permute-start(bf16[128,2048]{1,0:T(8,128)(2,1)S(1)} %broadcast_select_fusion.5), channel_id=1, source_target_pairs={{0,128},{128,0},{256,384},{384,256},{1,129},{129,1},{257,385},{385... | collective-permute-start | bytes 1572872 | tf_op jit(solution)/shard_map/ppermute | solution.py:214
  194.7 17.2 %all-to-all-start.1 = ((f32[16,1,256]{2,1,0:T(1,128)}), f32[16,1,256]{2,1,0:T(1,128)S(1)}, u32[]{:S(2)}, u32[]{:S(2)}) async-start(f32[16,1,256]{2,1,0:T(1,128)} %broadcast_in_dim.23), calls=%async_computation.1 | async-start | bytes 32768 | tf_op jit(solution)/shard_map/all_to_all | solution.py:276
  201.8 35.4 %collective-permute-start.2 = (bf16[2048,128]{1,0:T(8,128)(2,1)S(1)}, bf16[2048,128]{1,0:T(8,128)(2,1)}, u32[]{:S(2)}, u32[]{:S(2)}) collective-permute-start(bf16[2048,128]{1,0:T(8,128)(2,1)S(1)} %broadcast_select_fusion.9), channel_id=1, source_target_pairs={{0,32},{32,0},{64,96},{96,64},{1,33},{33,1},{65,97},{97,65},{2,34}... | collective-permute-start | bytes 1572872 | tf_op jit(solution)/shard_map/ppermute | solution.py:214
  212.6 15.7 %all-to-all-start.2 = ((f32[32,1,256]{2,1,0:T(1,128)}), f32[32,1,256]{2,1,0:T(1,128)S(1)}, u32[]{:S(2)}, u32[]{:S(2)}) async-start(f32[32,1,256]{2,1,0:T(1,128)} %broadcast_in_dim.24), calls=%async_computation.2 | async-start | bytes 65536 | tf_op jit(solution)/shard_map/all_to_all | solution.py:278
  221.9 17.8 %collective-permute-start.7 = (bf16[128,2048]{1,0:T(8,128)(2,1)}, bf16[128,2048]{1,0:T(8,128)(2,1)}, u32[]{:S(2)}, u32[]{:S(2)}) collective-permute-start(bf16[128,2048]{1,0:T(8,128)(2,1)} %broadcast_select_fusion.6), channel_id=1, source_target_pairs={{0,384},{128,256},{256,128},{384,0},{1,385},{129,257},{257,129},{3... | collective-permute-start | bytes 1572872 | tf_op jit(solution)/shard_map/ppermute | solution.py:214
  234.9 33.6 %collective-permute-start.25 = (f32[2056,128]{1,0:T(8,128)}, f32[2056,128]{1,0:T(8,128)S(1)}, u32[]{:S(2)}, u32[]{:S(2)}) collective-permute-start(f32[2056,128]{1,0:T(8,128)} %get-tuple-element.29), channel_id=1, source_target_pairs={{0,1},{1,0},{2,3},{3,2},{4,5},{5,4},{6,7},{7,6},{8,9},{9,8},{10,11... | collective-permute-start | bytes 3158024 | tf_op jit(solution)/shard_map/ppermute | solution.py:214
  237.2 27.8 %collective-permute-start.3 = (bf16[2048,128]{1,0:T(8,128)(2,1)S(1)}, bf16[2048,128]{1,0:T(8,128)(2,1)S(1)}, u32[]{:S(2)}, u32[]{:S(2)}) collective-permute-start(bf16[2048,128]{1,0:T(8,128)(2,1)S(1)} %broadcast_select_fusion.10), channel_id=1, source_target_pairs={{0,64},{32,96},{64,0},{96,32},{1,65},{33,97},{65,1},{97,33},{2,66}... | collective-permute-start | bytes 1572872 | tf_op jit(solution)/shard_map/ppermute | solution.py:214

commit v2 on v1

--- a/solution.py
+++ b/solution.py
@@ -1,3 +1,5 @@
+import functools
+
 import jax
 import jax.numpy as jnp
 from jax import lax
@@ -22,11 +24,9 @@
 PARAMS = pltpu.CompilerParams(vmem_limit_bytes=48 * 1024 * 1024)
 NT = (((1,), (1,)), ((), ()))
 
-BLOCKS = (
-    [(CAP * d, 0, d) for d in range(4)]
-    + [(4 * CAP + 2 * CAP * d + CAP * i, k, d) for d in range(4) for i, k in enumerate((1, 3))]
-    + [(12 * CAP + CAP * d, 2, d) for d in range(4)]
-)
+BLOCKS = [(EXP_GRP * CAP * d + CAP * k, k, d) for d in range(4) for k in range(EXP_GRP)]
+SPACED = pl.CostEstimate(flops=10**11, bytes_accessed=0, transcendentals=0)
+ANY = pl.BlockSpec(memory_space=pl.ANY)
 
 
 def shape(dims, kind):
@@ -115,7 +115,7 @@
 
 
 def forward_kernel(info_ref, base_ref, own_w_ref, other_w_ref, *refs):
-    groups, (x_ref, slope_ref, hid_ref, note_ref, part_ref, u_ref) = refs[:12], refs[12:]
+    groups, (x_ref, slope_ref, hid_ref, note_ref, part_ref, u_ref) = refs[:4], refs[-6:]
     grp, zh, y = info_ref[0], info_ref[1], info_ref[3]
     u_ref[:, :HID_DEV] = own_w_ref[:D, :]
     u_ref[:, HID_DEV:] = other_w_ref[:D, :]
@@ -146,7 +146,8 @@
     part_ref[...] = total
 
 
-def backward_kernel(info_ref, table_ref, x_ref, slope_ref, hid_ref, note_ref, own_ref, send_ref, own_head_ref):
+def backward_kernel(info_ref, table_ref, x_ref, slope_ref, hid_ref, note_ref, *refs):
+    own_ref, send_ref, own_head_ref = refs[-3:]
     zh, c, y = info_ref[1], info_ref[4], info_ref[3]
     table = table_ref[...]
     note = note_ref[...]
@@ -206,7 +207,35 @@
     grad = own_head_ref[0:1] + recv_ref[D : D + 1, :]
     square = (HID_DEV, HID_DEV)
     column = jnp.sum(jnp.where(iota(square, 0) == iota(square, 1), grad, 0.0), axis=1, keepdims=True)
-    new_down_ref[...] = (down_ref[...].astype(f32) + column * head_ref[...].astype(f32)).astype(bf16)
+    for j in range(D // HID_DEV):
+        at = j * HID_DEV
+        old = down_ref[at : at + HID_DEV, :].astype(f32)
+        step = column * head_ref[:, at : at + HID_DEV].astype(f32)
+        new_down_ref[:, at : at + HID_DEV] = (old + step).astype(bf16)
+
+
+def pack_kernel(up_ref, down_ref, earlier_ref, out_ref):
+    out_ref[:D, :] = up_ref[...]
+    for j in range(D // HID_DEV):
+        at = j * HID_DEV
+        out_ref[D + at : D + at + HID_DEV, :] = down_ref[:, at : at + HID_DEV]
+
+
+def pick_kernel(outs, take_ref, got_ref, own_ref, *refs):
+    for wanted, ref in ((1, got_ref), (0, own_ref)):
+
+        @pl.when(take_ref[0] == wanted)
+        def _(ref=ref):
+            at = 0
+            for out_ref in refs[-outs:]:
+                count = out_ref.shape[0]
+                out_ref[...] = ref[at : at + count, :]
+                at += count
+
+
+def join_kernel(*refs):
+    for k in range(EXP_GRP):
+        refs[-1][CAP * k : CAP * (k + 1), :] = refs[k][...]
 
 
 def swap(block, axis, mask):
@@ -214,10 +243,30 @@
     return lax.ppermute(block, axis, [(i, i ^ mask) for i in range(count)])
 
 
-def relocate(block, stages):
-    for axis, mask, take in stages:
-        block = jnp.where(take, swap(block, axis, mask), block)
-    return block
+def pick(stage, got, own, *earlier, outs=1):
+    out = shape((own.shape[0] // outs, own.shape[1]), own.dtype)
+    picked = pl.pallas_call(
+        functools.partial(pick_kernel, outs),
+        out_shape=[out] * outs,
+        in_specs=[SMEM, VMEM, VMEM] + [ANY] * len(earlier),
+        out_specs=[VMEM] * outs,
+        compiler_params=PARAMS,
+        cost_estimate=SPACED,
+        name="pick",
+    )(stage[2], got, own, *earlier)
+    return picked if outs > 1 else picked[0]
+
+
+def join(blocks, *earlier):
+    return pl.pallas_call(
+        join_kernel,
+        out_shape=shape((EXP_GRP * CAP, WIDE), bf16),
+        in_specs=[VMEM] * EXP_GRP + [ANY] * len(earlier),
+        out_specs=VMEM,
+        compiler_params=PARAMS,
+        cost_estimate=SPACED,
+        name="join",
+    )(*blocks, *earlier)
 
 
 def body(tokens, routes, gate_values, old_group, move_mask, pair_index, reward_head, w_up, w_down, acc_up, acc_down):
@@ -226,8 +275,10 @@
     head = reward_head.reshape(1, D)
     mask = jnp.sum(jnp.where(jnp.arange(EXP_GRP) == zh, move_mask, 0))
     bit = [jnp.bitwise_and(jnp.right_shift(mask, i), 1) for i in range(4)]
-    by_x = [("x", 1, jnp.bitwise_xor(bit[2], bit[3]) == 1), ("x", 3, bit[3] == 1)]
-    by_z = [("zl", 1, bit[0] == 1), ("zl", 2, bit[1] == 1)]
+    x1 = ("x", 1, jnp.bitwise_xor(bit[2], bit[3]).reshape(1))
+    x3 = ("x", 3, bit[3].reshape(1))
+    z1 = ("zl", 1, bit[0].reshape(1))
+    z2 = ("zl", 2, bit[1].reshape(1))
 
     weights = pl.pallas_call(
         weights_kernel,
@@ -237,8 +288,7 @@
         compiler_params=PARAMS,
         name="weights",
     )(w_up[0], w_down[0], head)
-    weights = relocate(weights, by_x + by_z)
-    other_weights = swap(weights, "c", 1)
+    got = swap(weights, *z1[:2])
 
     pairs = pair_index.astype(f32)
     *sent, base = pl.pallas_call(
@@ -249,11 +299,33 @@
         compiler_params=PARAMS,
         name="dispatch",
     )(old_group, move_mask, info, tokens, routes.T, gate_values.T, pairs.reshape(64, 128), head)
-    far = swap(sent[2], "zh", 2)
-    near = jnp.concatenate([swap(sent[1], "zh", 1), swap(sent[3], "zh", 3)], axis=0)
-    held = []
-    for group in (sent[0], near, far):
-        held += [group] + [swap(group, "y", d) for d in (1, 2, 3)]
+    blocks = [sent[0], swap(sent[1], "zh", 1), swap(sent[2], "zh", 2), swap(sent[3], "zh", 3)]
+    accums = pl.pallas_call(
+        pack_kernel,
+        out_shape=shape((2 * D, HID_DEV), bf16),
+        in_specs=[VMEM, VMEM, ANY],
+        out_specs=VMEM,
+        compiler_params=PARAMS,
+        cost_estimate=SPACED,
+        name="pack",
+    )(acc_up[0], acc_down[0], sent[0])
+    acc_got = swap(accums, *x1[:2])
+
+    weights = pick(z1, got, weights, accums)
+    got = swap(weights, *x1[:2])
+    weights = pick(x1, got, weights)
+    got = swap(weights, *x3[:2])
+    rows = join(blocks, weights)
+    held = [rows] + [swap(rows, "y", d) for d in (1, 2, 3)]
+    accums = pick(x1, acc_got, accums, rows)
+    acc_got = swap(accums, *x3[:2])
+    weights = pick(x3, got, weights, accums)
+    got = swap(weights, *z2[:2])
+    up, down = pick(x3, acc_got, accums, weights, outs=2)
+    up_got = swap(up, *z1[:2])
+    down_got = swap(down, *z2[:2])
+    weights = pick(z2, got, weights, up)
+    other_weights = swap(weights, "c", 1)
 
     xs, slope, hidden, notes, part = pl.pallas_call(
         forward_kernel,
@@ -264,7 +336,7 @@
             shape((ROWS, 128), f32),
             shape((16, TOK_DEV), f32),
         ],
-        in_specs=[SMEM] + [VMEM] * 15,
+        in_specs=[SMEM] + [VMEM] * 7,
         out_specs=[VMEM] * 5,
         scratch_shapes=[pltpu.VMEM((D, 2 * HID_DEV), bf16)],
         compiler_params=PARAMS,
@@ -275,16 +347,20 @@
     mine = jnp.broadcast_to(jnp.sum(mine, axis=0, keepdims=True), (16, TOK_DEV))
     mine = lax.all_to_all(mine, ("zl", "zh"), 0, 0, tiled=True)
     mine = jnp.broadcast_to(jnp.sum(mine, axis=0, keepdims=True), (32, TOK_DEV))
+    up = pick(z1, up_got, up, mine)
+    up_got = swap(up, *z2[:2])
+    down = pick(z2, down_got, down, mine)
+    down_got = swap(down, *z1[:2])
     table = lax.all_to_all(mine, ("x", "y", "c"), 0, 0, tiled=True)
 
     own, send, own_head = pl.pallas_call(
         backward_kernel,
         out_shape=[shape((D, HID_DEV), f32), shape((D + 8, HID_DEV), f32), shape((8, HID_DEV), f32)],
-        in_specs=[SMEM] + [VMEM] * 5,
+        in_specs=[SMEM] + [VMEM] * 5 + [ANY] * 2,
         out_specs=[VMEM] * 3,
         compiler_params=PARAMS,
         name="backward",
-    )(info, table, xs, slope, hidden, notes)
+    )(info, table, xs, slope, hidden, notes, up, down)
     recv = swap(send, "c", 1)
     loss = pl.pallas_call(
         loss_kernel,
@@ -294,8 +370,8 @@
         compiler_params=PARAMS,
         name="loss",
     )(table, pairs.reshape(16, 512))
-    up = relocate(acc_up[0], by_x + by_z)
-    down = relocate(acc_down[0], by_z + by_x)
+    up = pick(z2, up_got, up)
+    down = pick(z1, down_got, down)
     new_up, new_down = pl.pallas_call(
         final_kernel,
         out_shape=[shape((D, HID_DEV), bf16), shape((HID_DEV, D), bf16)],

time: 271 us -> 214 us (0.79)
  waiting for transfers between devices: 121 us -> 71.2 us
  starting transfers between devices: 117 us -> 88.9 us
  Pallas kernels: 17.2 us -> 28 us
  blocking collectives: 0 us -> 10.5 us
  other arithmetic: 5.42 us -> 2.08 us
  local copies, waits for them, and re-layouts: 4.84 us -> 7.94 us
    ppermute x26 -> x18, waiting for transfers between devices: 110 us -> 63.2 us  [swap(): return lax.ppermute(block, axis, [(i, i ^ mask) for i in range(count)])]
    ppermute x26 -> x18, starting transfers between devices: 96.8 us -> 70.4 us  [swap(): return lax.ppermute(block, axis, [(i, i ^ mask) for i in range(count)])]
    all_to_all x0 -> x1, blocking collectives: none -> 10.5 us  [body(): mine = lax.all_to_all(part, ('x', 'y'), 0, 0, tiled=True)]
    pallas_call x0 -> x12, Pallas kernels: none -> 8.21 us  [the longest x10 6.1 us: pick(): pl.pallas_call(functools.partial(pick_kernel, outs), out_shape=[out] * ou...]
    all_to_all x1 -> x0, starting transfers between devices: 6.19 us -> none  [body(): mine = lax.all_to_all(part, ('x', 'y'), 0, 0, tiled=True)]
    select_n x12 -> x0, other arithmetic: 4.71 us -> none  [relocate(): block = jnp.where(take, swap(block, axis, mask), block)]
    unnamed x22 -> x49, local copies, waits for them, and re-layouts: 2.15 us -> 5.8 us
    all_to_all x1, starting transfers between devices: 5.9 us -> 9.21 us  [body(): mine = lax.all_to_all(mine, ('zl', 'zh'), 0, 0, tiled=True)]
  transfers between devices with their start and end apart: 29 -> 20, of which waited for: 13 -> 8; matrix products, arithmetic and copies ran while one was open for 3% -> 2% of each run, Pallas kernels for 6% -> 12%
where the time goes in v2:
time: 214 us; the launch traced here: 212 us
  starting transfers between devices  88.9 us (42%)
  waiting for transfers between devices  71.2 us (33%)
  Pallas kernels  28 us (13%)
  blocking collectives  10.5 us (5%)
  local copies, waits for them, and re-layouts  7.94 us (4%)
  between operations  3.71 us (2%)
    ppermute x18, starting transfers between devices, swap(): return lax.ppermute(block, axis, [(i, i ^ mask) for i in range(count)])  70.4 us
    ppermute x18, waiting for transfers between devices, swap(): return lax.ppermute(block, axis, [(i, i ^ mask) for i in range(count)])  63.2 us
    all_to_all x1, blocking collectives, body(): mine = lax.all_to_all(part, ('x', 'y'), 0, 0, tiled=True)  10.5 us
    all_to_all x1, starting transfers between devices, body(): table = lax.all_to_all(mine, ('x', 'y', 'c'), 0, 0, tiled=True)  9.26 us
    all_to_all x1, starting transfers between devices, body(): mine = lax.all_to_all(mine, ('zl', 'zh'), 0, 0, tiled=True)  9.21 us
    all_to_all x1, waiting for transfers between devices, body(): mine = lax.all_to_all(mine, ('zl', 'zh'), 0, 0, tiled=True)  7.98 us
    pallas_call x1, Pallas kernels, body(): pl.pallas_call(backward_kernel, out_shape=[shape((D, HID_DEV), f32), shap...  6.56 us
    pallas_call x10, Pallas kernels, pick(): pl.pallas_call(functools.partial(pick_kernel, outs), out_shape=[out] * ou...  6.1 us
  transfers between devices with their start and end apart: 20, of which 8 were waited for; matrix products, arithmetic and copies ran while one was open for 2% of the time, Pallas kernels for 12%

profile of v2, /device:TPU:1, one launch (start us, length us, event | category | flops | bytes accessed | tf_op | source)
XLA Modules:
  0.0 212.3 jit_solution(5928164836149900911)
XLA Ops:
  0.6 0.8 reshape.45.head_ref
  1.4 1.0 copy-done.1
  2.5 1.0 copy-done.2
  3.5 0.0 copy-start.11
  3.5 0.0 copy-start.12
  3.5 0.3 weights.1.own_ref
  3.8 4.5 %collective-permute-start.4 = (bf16[2064,128]{1,0:T(8,128)(2,1)S(1)}, bf16[2064,128]{1,0:T(8,128)(2,1)S(1)}, u32[]{:S(2)}, u32[]{:S(2)}) collective-permute-start(bf16[2064,128]{1,0:T(8,128)(2,1)S(1)} %weights.1.own_ref), channel_id=1, source_target_pairs={{0,32},{32,0},{64,96},{96,64},{1,33},{33,1},{65,97},{97,65},{2,34}... | collective-permute-start | bytes 1585160 | tf_op jit(solution)/shard_map/ppermute | solution.py:243
  8.3 1.4 fusion.1
  9.7 0.1 stack.23.info_ref
  9.8 2.2 %dispatch.1 = (bf16[48,2176]{1,0:T(8,128)(2,1)S(1)}, bf16[48,2176]{1,0:T(8,128)(2,1)S(1)}, bf16[48,2176]{1,0:T(8,128)(2,1)S(1)}, bf16[48,2176]{1,0:T(8,128)(2,1)S(1)}, f32[8,256]{1,0:T(8,128)S(1)}) custom-call(s32[64]{0:T(128)S(1)} %copy-done.9, s32[4]{0:T(128)S(1)} %copy-done.10, s32[5]{0:T(128)S(1)} %stack.23.info_ref, bf16[256,2048]{1,0:T(8,128)(2,1)S(1)} %copy-done, ...), custom_call_target="tpu_custom_call" | custom-call | tf_op jit(solution)/shard_map/dispatch/pallas_call | solution.py:294
  12.0 0.0 copy-start.17
  12.0 0.0 copy-start.21
  12.1 1.1 pack.1.refs_0_.own_ref
  13.2 0.6 fusion
  14.5 0.9 collective-permute-done.4.got_ref
  15.5 7.7 %collective-permute-start.5 = (bf16[2064,128]{1,0:T(8,128)(2,1)S(1)}, bf16[2064,128]{1,0:T(8,128)(2,1)S(1)}, u32[]{:S(2)}, u32[]{:S(2)}) collective-permute-start(bf16[2064,128]{1,0:T(8,128)(2,1)S(1)} %pick.10.own_ref), channel_id=1, source_target_pairs={{0,128},{128,0},{256,384},{384,256},{1,129},{129,1},{257,385},{385... | collective-permute-start | bytes 1585160 | tf_op jit(solution)/shard_map/ppermute | solution.py:243
  23.2 1.9 collective-permute-start
  25.2 9.1 %collective-permute-start.1 = (bf16[48,2176]{1,0:T(8,128)(2,1)S(1)}, bf16[48,2176]{1,0:T(8,128)(2,1)S(1)}, u32[]{:S(2)}, u32[]{:S(2)}) collective-permute-start(bf16[48,2176]{1,0:T(8,128)(2,1)S(1)} %copy-done.22), channel_id=1, source_target_pairs={{0,8},{8,0},{16,24},{24,16},{1,9},{9,1},{17,25},{25,17},{2,10},{10... | collective-permute-start | bytes 626696 | tf_op jit(solution)/shard_map/ppermute | solution.py:243
  34.3 10.2 %collective-permute-start.2 = (bf16[48,2176]{1,0:T(8,128)(2,1)S(1)}, bf16[48,2176]{1,0:T(8,128)(2,1)S(1)}, u32[]{:S(2)}, u32[]{:S(2)}) collective-permute-start(bf16[48,2176]{1,0:T(8,128)(2,1)S(1)} %copy-done.20), channel_id=1, source_target_pairs={{0,16},{8,24},{16,0},{24,8},{1,17},{9,25},{17,1},{25,9},{2,18},{10... | collective-permute-start | bytes 626696 | tf_op jit(solution)/shard_map/ppermute | solution.py:243
  44.5 1.9 collective-permute-start.3
  48.3 0.0 copy-start.18
  48.3 0.9 pick.11.refs_4_.own_ref
  49.2 4.4 %collective-permute-start.7 = (bf16[2064,128]{1,0:T(8,128)(2,1)}, bf16[2064,128]{1,0:T(8,128)(2,1)}, u32[]{:S(2)}, u32[]{:S(2)}) collective-permute-start(bf16[2064,128]{1,0:T(8,128)(2,1)} %pick.11.refs_4_.own_ref), channel_id=1, source_target_pairs={{0,384},{128,256},{256,128},{384,0},{1,385},{129,257},{257,129},{3... | collective-permute-start | bytes 1585160 | tf_op jit(solution)/shard_map/ppermute | solution.py:243
  53.6 15.5 %collective-permute-done.1.refs_1_ = bf16[48,2176]{1,0:T(8,128)(2,1)S(1)} collective-permute-done((bf16[48,2176]{1,0:T(8,128)(2,1)S(1)}, bf16[48,2176]{1,0:T(8,128)(2,1)S(1)}, u32[]{:S(2)}, u32[]{:S(2)}) %collective-permute-start.1) | collective-permute-done | bytes 208928 | tf_op jit(solution)/shard_map/ppermute | solution.py:243
  69.1 12.0 %collective-permute-done.3.refs_3_ = bf16[48,2176]{1,0:T(8,128)(2,1)S(1)} collective-permute-done((bf16[48,2176]{1,0:T(8,128)(2,1)S(1)}, bf16[48,2176]{1,0:T(8,128)(2,1)S(1)}, u32[]{:S(2)}, u32[]{:S(2)}) %collective-permute-start.3) | collective-permute-done | bytes 208928 | tf_op jit(solution)/shard_map/ppermute | solution.py:243
  81.1 1.0 join.1.refs_0_
  82.0 3.2 %collective-permute-start.11 = (bf16[192,2176]{1,0:T(8,128)(2,1)}, bf16[192,2176]{1,0:T(8,128)(2,1)}, u32[]{:S(2)}, u32[]{:S(2)}) collective-permute-start(bf16[192,2176]{1,0:T(8,128)(2,1)} %join.1.refs_0_), channel_id=1, source_target_pairs={{0,2},{2,0},{4,6},{6,4},{1,3},{3,1},{5,7},{7,5},{8,10},{10,8},{12,... | collective-permute-start | bytes 2506760 | tf_op jit(solution)/shard_map/ppermute | solution.py:243
  85.2 4.5 %collective-permute-start.12 = (bf16[192,2176]{1,0:T(8,128)(2,1)}, bf16[192,2176]{1,0:T(8,128)(2,1)}, u32[]{:S(2)}, u32[]{:S(2)}) collective-permute-start(bf16[192,2176]{1,0:T(8,128)(2,1)} %join.1.refs_0_), channel_id=1, source_target_pairs={{0,4},{2,6},{4,0},{6,2},{1,5},{3,7},{5,1},{7,3},{8,12},{10,14},{12... | collective-permute-start | bytes 2506760 | tf_op jit(solution)/shard_map/ppermute | solution.py:243
  89.8 1.9 collective-permute-start.13
  91.7 0.0 collective-permute-done.got_ref
  91.7 1.6 pick.12.refs_0_.own_ref
  93.3 4.4 %collective-permute-start.6 = (bf16[4096,128]{1,0:T(8,128)(2,1)S(1)}, bf16[4096,128]{1,0:T(8,128)(2,1)S(1)}, u32[]{:S(2)}, u32[]{:S(2)}) collective-permute-start(bf16[4096,128]{1,0:T(8,128)(2,1)S(1)} %pick.12.refs_0_.own_ref), channel_id=1, source_target_pairs={{0,384},{128,256},{256,128},{384,0},{1,385},{129,257},{257,129},{3... | collective-permute-start | bytes 3145736 | tf_op jit(solution)/shard_map/ppermute | solution.py:243
  97.7 1.2 pick.13.refs_0_.own_ref
  99.0 1.9 collective-permute-start.9
  100.9 18.8 %collective-permute-done.6.got_ref = bf16[4096,128]{1,0:T(8,128)(2,1)S(1)} collective-permute-done((bf16[4096,128]{1,0:T(8,128)(2,1)S(1)}, bf16[4096,128]{1,0:T(8,128)(2,1)S(1)}, u32[]{:S(2)}, u32[]{:S(2)}) %collective-permute-start.6) | collective-permute-done | bytes 1048608 | tf_op jit(solution)/shard_map/ppermute | solution.py:243
  119.7 0.1 pick.14
  119.8 0.0 copy-start.13
  119.8 6.0 %collective-permute-done.9.got_ref = bf16[2064,128]{1,0:T(8,128)(2,1)S(1)} collective-permute-done((bf16[2064,128]{1,0:T(8,128)(2,1)S(1)}, bf16[2064,128]{1,0:T(8,128)(2,1)S(1)}, u32[]{:S(2)}, u32[]{:S(2)}) %collective-permute-start.9) | collective-permute-done | bytes 528416 | tf_op jit(solution)/shard_map/ppermute | solution.py:243
  125.9 2.3 %collective-permute-start.10 = (bf16[2064,128]{1,0:T(8,128)(2,1)S(1)}, bf16[2064,128]{1,0:T(8,128)(2,1)S(1)}, u32[]{:S(2)}, u32[]{:S(2)}) collective-permute-start(bf16[2064,128]{1,0:T(8,128)(2,1)S(1)} %pick.15.own_w_ref), channel_id=1, source_target_pairs={{0,1},{1,0},{2,3},{3,2},{4,5},{5,4},{6,7},{7,6},{8,9},{9,8},{10,11... | collective-permute-start | bytes 1585160 | tf_op jit(solution)/shard_map/ppermute | solution.py:243
  128.2 1.9 collective-permute-start.15
  130.2 4.9 %forward.1 = (bf16[768,2048]{1,0:T(8,128)(2,1)}, f32[768,256]{1,0:T(8,128)S(1)}, bf16[768,256]{1,0:T(8,128)(2,1)S(1)}, f32[768,128]{1,0:T(8,128)S(1)}, f32[16,256]{1,0:T(8,128)S(1)}) custom-call(s32[5]{0:T(128)S(1)} %stack.23.info_ref, f32[8,256]{1,0:T(8,128)S(1)} %get-tuple-element.25.base_ref, bf16[2064,128]{1,0:T(8,128)(2,1)S(1)} %pick.15.own_w_ref, ...), custom_call_target="tpu_custom_call" | custom-call | tf_op jit(solution)/shard_map/forward/pallas_call | solution.py:330
  135.1 10.5 %all_to_all.23 = f32[16,1,256]{2,1,0:T(1,128)S(1)} all-to-all(f32[16,1,256]{2,1,0:T(1,128)S(1)} %copy.16), channel_id=1, replica_groups=mesh['x'=4,'zl'=4,'zh'=4,'y'=4,'c'=2] {'x','y'}, dimensions={0} | all-to-all | bytes 32768 | tf_op jit(solution)/shard_map/all_to_all | solution.py:346
  145.7 0.6 broadcast_in_dim.25
  146.3 9.2 %all-to-all-start.1 = ((f32[16,1,256]{2,1,0:T(1,128)}), f32[16,1,256]{2,1,0:T(1,128)S(1)}, u32[]{:S(2)}, u32[]{:S(2)}) async-start(f32[16,1,256]{2,1,0:T(1,128)} %broadcast_in_dim.25), calls=%async_computation.1 | async-start | bytes 32768 | tf_op jit(solution)/shard_map/all_to_all | solution.py:348
  155.6 3.3 %collective-permute-start.8 = (bf16[2048,128]{1,0:T(8,128)(2,1)S(1)}, bf16[2048,128]{1,0:T(8,128)(2,1)S(1)}, u32[]{:S(2)}, u32[]{:S(2)}) collective-permute-start(bf16[2048,128]{1,0:T(8,128)(2,1)S(1)} %get-tuple-element.24.refs_0_.own_ref), channel_id=1, source_target_pairs={{0,32},{32,0},{64,96},{96,64},{1,33},{33,1},{65,97},{97,65},{2,34}... | collective-permute-start | bytes 1572872 | tf_op jit(solution)/shard_map/ppermute | solution.py:243
  158.8 8.0 %all-to-all-done.1 = f32[16,1,256]{2,1,0:T(1,128)S(1)} async-done(((f32[16,1,256]{2,1,0:T(1,128)}), f32[16,1,256]{2,1,0:T(1,128)S(1)}, u32[]{:S(2)}, u32[]{:S(2)}) %all-to-all-start.1) | async-done | bytes 16416 | tf_op jit(solution)/shard_map/all_to_all | solution.py:348
  166.8 0.6 broadcast_in_dim.27
  167.5 9.3 %all-to-all-start.2 = ((f32[32,1,256]{2,1,0:T(1,128)}), f32[32,1,256]{2,1,0:T(1,128)}, u32[]{:S(2)}, u32[]{:S(2)}) async-start(f32[32,1,256]{2,1,0:T(1,128)} %broadcast_in_dim.27), calls=%async_computation.2 | async-start | bytes 65536 | tf_op jit(solution)/shard_map/all_to_all | solution.py:354
  176.8 0.0 copy-start.14
  176.8 1.0 copy-done.14
  177.8 1.1 pick.18.own_ref.refs_1_
  178.9 2.0 collective-permute-start.16
  180.9 0.0 copy-start.15
  181.0 0.8 copy-done.15
  181.7 1.0 copy-done.16
  182.8 2.3 %collective-permute-start.14 = (bf16[2048,128]{1,0:T(8,128)(2,1)S(1)}, bf16[2048,128]{1,0:T(8,128)(2,1)S(1)}, u32[]{:S(2)}, u32[]{:S(2)}) collective-permute-start(bf16[2048,128]{1,0:T(8,128)(2,1)S(1)} %pick.16.own_ref.refs_0_), channel_id=1, source_target_pairs={{0,64},{32,96},{64,0},{96,32},{1,65},{33,97},{65,1},{97,33},{2,66}... | collective-permute-start | bytes 1572872 | tf_op jit(solution)/shard_map/ppermute | solution.py:243
  185.2 0.8 copy.21
  185.9 6.6 %backward.1 = (f32[2048,128]{1,0:T(8,128)S(1)}, f32[2056,128]{1,0:T(8,128)}, f32[8,128]{1,0:T(8,128)S(1)}) custom-call(s32[5]{0:T(128)S(1)} %copy-done.8, f32[32,256]{1,0:T(8,128)S(1)} %bitcast.27, bf16[768,2048]{1,0:T(8,128)(2,1)} %get-tuple-element.28.x_ref, f32[768,256]{1,0:T(8,128)S(1)} %get-tuple-element.29.slope_ref, ...), custom_call_target="tpu_custom_call" | custom-call | tf_op jit(solution)/shard_map/backward/pallas_call | solution.py:356
  192.5 2.9 %collective-permute-start.17 = (f32[2056,128]{1,0:T(8,128)}, f32[2056,128]{1,0:T(8,128)}, u32[]{:S(2)}, u32[]{:S(2)}) collective-permute-start(f32[2056,128]{1,0:T(8,128)} %get-tuple-element.33), channel_id=1, source_target_pairs={{0,1},{1,0},{2,3},{3,2},{4,5},{5,4},{6,7},{7,6},{8,9},{9,8},{10,11... | collective-permute-start | bytes 3158024 | tf_op jit(solution)/shard_map/ppermute | solution.py:243
  195.4 3.4 %loss.1 = f32[1,128]{1,0:T(1,128)} custom-call(f32[32,256]{1,0:T(8,128)S(1)} %bitcast.28, f32[16,512]{1,0:T(8,128)S(1)} %reshape.46.pair_ref), custom_call_target="tpu_custom_call" | custom-call | tf_op jit(solution)/shard_map/loss/pallas_call | solution.py:365
  198.7 1.8 collective-permute-done.16.got_ref
  200.6 1.1 pick.19.down_ref
  201.7 8.0 %collective-permute-done.14.got_ref = bf16[2048,128]{1,0:T(8,128)(2,1)S(1)} collective-permute-done((bf16[2048,128]{1,0:T(8,128)(2,1)S(1)}, bf16[2048,128]{1,0:T(8,128)(2,1)S(1)}, u32[]{:S(2)}, u32[]{:S(2)}) %collective-permute-start.14) | collective-permute-done | bytes 524320 | tf_op jit(solution)/shard_map/ppermute | solution.py:243
  209.8 2.5 %final.1 = (bf16[2048,128]{1,0:T(8,128)(2,1)}, bf16[128,2048]{1,0:T(8,128)(2,1)}) custom-call(bf16[2048,128]{1,0:T(8,128)(2,1)S(1)} %pick.17.up_ref, bf16[2048,128]{1,0:T(8,128)(2,1)S(1)} %pick.19.down_ref, f32[2048,128]{1,0:T(8,128)S(1)} %get-tuple-element.32.own_ref, f32[2056,128]{1,0:T(8,128)} %collective-permute-done.17.recv_ref, ...), custom_call_target="tpu_custom_call" | custom-call | tf_op jit(solution)/shard_map/final/pallas_call | solution.py:375
  (55 shorter events, 0.4 us)
Async XLA Ops:
  0.6 9.2 %copy-start = (bf16[256,2048]{1,0:T(8,128)(2,1)S(1)}, bf16[256,2048]{1,0:T(8,128)(2,1)}, u32[]{:S(2)}) copy-start(bf16[256,2048]{1,0:T(8,128)(2,1)} %tok_ref.1) | copy-start | bytes 3145732
  1.4 10.6 %copy-start.3 = (bf16[1,2048]{1,0:T(2,128)(2,1)}, bf16[1,2048]{1,0:T(2,128)(2,1)S(1)}, u32[]{:S(2)}) copy-start(bf16[1,2048]{1,0:T(2,128)(2,1)S(1)} %reshape.45.head_ref) | copy-start | bytes 12292
  1.4 1.0 copy-start.1
  2.5 1.0 copy-start.2
  3.5 6.3 %copy-start.5 = (s32[256,8]{0,1:T(8,128)S(1)}, s32[256,8]{0,1:T(8,128)}, u32[]{:S(2)}) copy-start(s32[256,8]{0,1:T(8,128)} %param.12) | copy-start | bytes 24580
  3.5 6.3 %copy-start.6 = (f32[256,8]{0,1:T(8,128)S(1)}, f32[256,8]{0,1:T(8,128)}, u32[]{:S(2)}) copy-start(f32[256,8]{0,1:T(8,128)} %param.13) | copy-start | bytes 24580
  3.5 6.3 %copy-start.9 = (s32[64]{0:T(128)S(1)}, s32[64]{0:T(128)}, u32[]{:S(2)}) copy-start(s32[64]{0:T(128)} %group_ref.1) | copy-start | bytes 772
  3.5 6.3 %copy-start.10 = (s32[4]{0:T(128)S(1)}, s32[4]{0:T(128)}, u32[]{:S(2)}) copy-start(s32[4]{0:T(128)} %mask_ref.1) | copy-start | bytes 52
  3.5 8.5 %copy-start.11 = (bf16[1,2048,128]{2,1,0:T(8,128)(2,1)S(1)}, bf16[1,2048,128]{2,1,0:T(8,128)(2,1)}, u32[]{:S(2)}) copy-start(bf16[1,2048,128]{2,1,0:T(8,128)(2,1)} %param.20) | copy-start | bytes 1572868
  3.5 8.5 %copy-start.12 = (bf16[1,128,2048]{2,1,0:T(8,128)(2,1)S(1)}, bf16[1,128,2048]{2,1,0:T(8,128)(2,1)}, u32[]{:S(2)}) copy-start(bf16[1,128,2048]{2,1,0:T(8,128)(2,1)} %param.21) | copy-start | bytes 1572868
  3.8 11.6 %collective-permute-start.4 = (bf16[2064,128]{1,0:T(8,128)(2,1)S(1)}, bf16[2064,128]{1,0:T(8,128)(2,1)S(1)}, u32[]{:S(2)}, u32[]{:S(2)}) collective-permute-start(bf16[2064,128]{1,0:T(8,128)(2,1)S(1)} %weights.1.own_ref), channel_id=1, source_target_pairs={{0,32},{32,0},{64,96},{96,64},{1,33},{33,1},{65,97},{97,65},{2,34}... | collective-permute-start | bytes 1585160 | tf_op jit(solution)/shard_map/ppermute | solution.py:243
  9.8 120.4 %copy-start.7 = (s32[5]{0:T(128)}, s32[5]{0:T(128)S(1)}, u32[]{:S(2)}) copy-start(s32[5]{0:T(128)S(1)} %stack.23.info_ref) | copy-start | bytes 64
  12.0 1.2 copy-start.17
  12.0 1.2 copy-start.19
  12.0 1.2 copy-start.21
  15.5 9.7 %copy-start.22 = (bf16[48,2176]{1,0:T(8,128)(2,1)S(1)}, bf16[48,2176]{1,0:T(8,128)(2,1)}, u32[]{:S(2)}) copy-start(bf16[48,2176]{1,0:T(8,128)(2,1)} %copy-done.21) | copy-start | bytes 626692
  15.5 18.8 %copy-start.20 = (bf16[48,2176]{1,0:T(8,128)(2,1)S(1)}, bf16[48,2176]{1,0:T(8,128)(2,1)}, u32[]{:S(2)}) copy-start(bf16[48,2176]{1,0:T(8,128)(2,1)} %copy-done.19) | copy-start | bytes 626692
  15.5 32.8 %collective-permute-start.5 = (bf16[2064,128]{1,0:T(8,128)(2,1)S(1)}, bf16[2064,128]{1,0:T(8,128)(2,1)S(1)}, u32[]{:S(2)}, u32[]{:S(2)}) collective-permute-start(bf16[2064,128]{1,0:T(8,128)(2,1)S(1)} %pick.10.own_ref), channel_id=1, source_target_pairs={{0,128},{128,0},{256,384},{384,256},{1,129},{129,1},{257,385},{385... | collective-permute-start | bytes 1585160 | tf_op jit(solution)/shard_map/ppermute | solution.py:243
  23.2 68.5 %collective-permute-start = (bf16[4096,128]{1,0:T(8,128)(2,1)}, bf16[4096,128]{1,0:T(8,128)(2,1)}, u32[]{:S(2)}, u32[]{:S(2)}) collective-permute-start(bf16[4096,128]{1,0:T(8,128)(2,1)} %pack.1.refs_0_.own_ref), channel_id=1, source_target_pairs={{0,128},{128,0},{256,384},{384,256},{1,129},{129,1},{257,385},{385... | collective-permute-start | bytes 3145736 | tf_op jit(solution)/shard_map/ppermute | solution.py:243
  25.2 43.9 %collective-permute-start.1 = (bf16[48,2176]{1,0:T(8,128)(2,1)S(1)}, bf16[48,2176]{1,0:T(8,128)(2,1)S(1)}, u32[]{:S(2)}, u32[]{:S(2)}) collective-permute-start(bf16[48,2176]{1,0:T(8,128)(2,1)S(1)} %copy-done.22), channel_id=1, source_target_pairs={{0,8},{8,0},{16,24},{24,16},{1,9},{9,1},{17,25},{25,17},{2,10},{10... | collective-permute-start | bytes 626696 | tf_op jit(solution)/shard_map/ppermute | solution.py:243
  34.3 34.9 %collective-permute-start.2 = (bf16[48,2176]{1,0:T(8,128)(2,1)S(1)}, bf16[48,2176]{1,0:T(8,128)(2,1)S(1)}, u32[]{:S(2)}, u32[]{:S(2)}) collective-permute-start(bf16[48,2176]{1,0:T(8,128)(2,1)S(1)} %copy-done.20), channel_id=1, source_target_pairs={{0,16},{8,24},{16,0},{24,8},{1,17},{9,25},{17,1},{25,9},{2,18},{10... | collective-permute-start | bytes 626696 | tf_op jit(solution)/shard_map/ppermute | solution.py:243
  44.5 36.6 %collective-permute-start.3 = (bf16[48,2176]{1,0:T(8,128)(2,1)S(1)}, bf16[48,2176]{1,0:T(8,128)(2,1)S(1)}, u32[]{:S(2)}, u32[]{:S(2)}) collective-permute-start(bf16[48,2176]{1,0:T(8,128)(2,1)S(1)} %get-tuple-element.23), channel_id=1, source_target_pairs={{0,24},{8,16},{16,8},{24,0},{1,25},{9,17},{17,9},{25,1},{2,26},{10... | collective-permute-start | bytes 626696 | tf_op jit(solution)/shard_map/ppermute | solution.py:243
  48.3 32.7 %copy-start.18 = (bf16[48,2176]{1,0:T(8,128)(2,1)S(1)}, bf16[48,2176]{1,0:T(8,128)(2,1)}, u32[]{:S(2)}) copy-start(bf16[48,2176]{1,0:T(8,128)(2,1)} %copy-done.17) | copy-start | bytes 626692
  49.2 48.5 %collective-permute-start.7 = (bf16[2064,128]{1,0:T(8,128)(2,1)}, bf16[2064,128]{1,0:T(8,128)(2,1)}, u32[]{:S(2)}, u32[]{:S(2)}) collective-permute-start(bf16[2064,128]{1,0:T(8,128)(2,1)} %pick.11.refs_4_.own_ref), channel_id=1, source_target_pairs={{0,384},{128,256},{256,128},{384,0},{1,385},{129,257},{257,129},{3... | collective-permute-start | bytes 1585160 | tf_op jit(solution)/shard_map/ppermute | solution.py:243
  82.0 48.1 %collective-permute-start.11 = (bf16[192,2176]{1,0:T(8,128)(2,1)}, bf16[192,2176]{1,0:T(8,128)(2,1)}, u32[]{:S(2)}, u32[]{:S(2)}) collective-permute-start(bf16[192,2176]{1,0:T(8,128)(2,1)} %join.1.refs_0_), channel_id=1, source_target_pairs={{0,2},{2,0},{4,6},{6,4},{1,3},{3,1},{5,7},{7,5},{8,10},{10,8},{12,... | collective-permute-start | bytes 2506760 | tf_op jit(solution)/shard_map/ppermute | solution.py:243
  85.2 44.9 %collective-permute-start.12 = (bf16[192,2176]{1,0:T(8,128)(2,1)}, bf16[192,2176]{1,0:T(8,128)(2,1)}, u32[]{:S(2)}, u32[]{:S(2)}) collective-permute-start(bf16[192,2176]{1,0:T(8,128)(2,1)} %join.1.refs_0_), channel_id=1, source_target_pairs={{0,4},{2,6},{4,0},{6,2},{1,5},{3,7},{5,1},{7,3},{8,12},{10,14},{12... | collective-permute-start | bytes 2506760 | tf_op jit(solution)/shard_map/ppermute | solution.py:243
  89.8 40.4 %collective-permute-start.13 = (bf16[192,2176]{1,0:T(8,128)(2,1)}, bf16[192,2176]{1,0:T(8,128)(2,1)}, u32[]{:S(2)}, u32[]{:S(2)}) collective-permute-start(bf16[192,2176]{1,0:T(8,128)(2,1)} %join.1.refs_0_), channel_id=1, source_target_pairs={{0,6},{2,4},{4,2},{6,0},{1,7},{3,5},{5,3},{7,1},{8,14},{10,12},{12... | collective-permute-start | bytes 2506760 | tf_op jit(solution)/shard_map/ppermute | solution.py:243
  93.3 26.4 %collective-permute-start.6 = (bf16[4096,128]{1,0:T(8,128)(2,1)S(1)}, bf16[4096,128]{1,0:T(8,128)(2,1)S(1)}, u32[]{:S(2)}, u32[]{:S(2)}) collective-permute-start(bf16[4096,128]{1,0:T(8,128)(2,1)S(1)} %pick.12.refs_0_.own_ref), channel_id=1, source_target_pairs={{0,384},{128,256},{256,128},{384,0},{1,385},{129,257},{257,129},{3... | collective-permute-start | bytes 3145736 | tf_op jit(solution)/shard_map/ppermute | solution.py:243
  99.0 26.9 %collective-permute-start.9 = (bf16[2064,128]{1,0:T(8,128)(2,1)S(1)}, bf16[2064,128]{1,0:T(8,128)(2,1)S(1)}, u32[]{:S(2)}, u32[]{:S(2)}) collective-permute-start(bf16[2064,128]{1,0:T(8,128)(2,1)S(1)} %pick.13.refs_0_.own_ref), channel_id=1, source_target_pairs={{0,64},{32,96},{64,0},{96,32},{1,65},{33,97},{65,1},{97,33},{2,66}... | collective-permute-start | bytes 1585160 | tf_op jit(solution)/shard_map/ppermute | solution.py:243
  119.8 8.4 %copy-start.13 = (bf16[2048,128]{1,0:T(8,128)(2,1)}, bf16[2048,128]{1,0:T(8,128)(2,1)S(1)}, u32[]{:S(2)}) copy-start(bf16[2048,128]{1,0:T(8,128)(2,1)S(1)} %get-tuple-element.27.own_ref) | copy-start | bytes 1572868
  125.9 4.3 %collective-permute-start.10 = (bf16[2064,128]{1,0:T(8,128)(2,1)S(1)}, bf16[2064,128]{1,0:T(8,128)(2,1)S(1)}, u32[]{:S(2)}, u32[]{:S(2)}) collective-permute-start(bf16[2064,128]{1,0:T(8,128)(2,1)S(1)} %pick.15.own_w_ref), channel_id=1, source_target_pairs={{0,1},{1,0},{2,3},{3,2},{4,5},{5,4},{6,7},{7,6},{8,9},{9,8},{10,11... | collective-permute-start | bytes 1585160 | tf_op jit(solution)/shard_map/ppermute | solution.py:243
  128.2 48.5 %collective-permute-start.15 = (bf16[2048,128]{1,0:T(8,128)(2,1)S(1)}, bf16[2048,128]{1,0:T(8,128)(2,1)}, u32[]{:S(2)}, u32[]{:S(2)}) collective-permute-start(bf16[2048,128]{1,0:T(8,128)(2,1)S(1)} %get-tuple-element.27.own_ref), channel_id=1, source_target_pairs={{0,64},{32,96},{64,0},{96,32},{1,65},{33,97},{65,1},{97,33},{2,66}... | collective-permute-start | bytes 1572872 | tf_op jit(solution)/shard_map/ppermute | solution.py:243
  130.2 25.3 %copy-start.23 = (f32[8192]{0:T(1024)S(1)}, f32[8192]{0:T(1024)}, u32[]{:S(2)}) copy-start(f32[8192]{0:T(1024)} %get-tuple-element.37) | copy-start | bytes 98308
  146.3 20.5 %all-to-all-start.1 = ((f32[16,1,256]{2,1,0:T(1,128)}), f32[16,1,256]{2,1,0:T(1,128)S(1)}, u32[]{:S(2)}, u32[]{:S(2)}) async-start(f32[16,1,256]{2,1,0:T(1,128)} %broadcast_in_dim.25), calls=%async_computation.1 | async-start | bytes 32768 | tf_op jit(solution)/shard_map/all_to_all | solution.py:348
  155.6 25.4 %collective-permute-start.8 = (bf16[2048,128]{1,0:T(8,128)(2,1)S(1)}, bf16[2048,128]{1,0:T(8,128)(2,1)S(1)}, u32[]{:S(2)}, u32[]{:S(2)}) collective-permute-start(bf16[2048,128]{1,0:T(8,128)(2,1)S(1)} %get-tuple-element.24.refs_0_.own_ref), channel_id=1, source_target_pairs={{0,32},{32,0},{64,96},{96,64},{1,33},{33,1},{65,97},{97,65},{2,34}... | collective-permute-start | bytes 1572872 | tf_op jit(solution)/shard_map/ppermute | solution.py:243
  167.5 17.7 %all-to-all-start.2 = ((f32[32,1,256]{2,1,0:T(1,128)}), f32[32,1,256]{2,1,0:T(1,128)}, u32[]{:S(2)}, u32[]{:S(2)}) async-start(f32[32,1,256]{2,1,0:T(1,128)} %broadcast_in_dim.27), calls=%async_computation.2 | async-start | bytes 65536 | tf_op jit(solution)/shard_map/all_to_all | solution.py:354
  176.8 1.0 copy-start.14
  178.9 7.0 %copy-start.8 = (s32[5]{0:T(128)S(1)}, s32[5]{0:T(128)}, u32[]{:S(2)}) copy-start(s32[5]{0:T(128)} %copy-done.7) | copy-start | bytes 64
  178.9 21.6 %collective-permute-start.16 = (bf16[2048,128]{1,0:T(8,128)(2,1)S(1)}, bf16[2048,128]{1,0:T(8,128)(2,1)}, u32[]{:S(2)}, u32[]{:S(2)}) collective-permute-start(bf16[2048,128]{1,0:T(8,128)(2,1)S(1)} %pick.18.own_ref.refs_1_), channel_id=1, source_target_pairs={{0,32},{32,0},{64,96},{96,64},{1,33},{33,1},{65,97},{97,65},{2,34}... | collective-permute-start | bytes 1572872 | tf_op jit(solution)/shard_map/ppermute | solution.py:243
  180.9 0.8 copy-start.15
  181.7 1.0 copy-start.16
  182.8 26.9 %collective-permute-start.14 = (bf16[2048,128]{1,0:T(8,128)(2,1)S(1)}, bf16[2048,128]{1,0:T(8,128)(2,1)S(1)}, u32[]{:S(2)}, u32[]{:S(2)}) collective-permute-start(bf16[2048,128]{1,0:T(8,128)(2,1)S(1)} %pick.16.own_ref.refs_0_), channel_id=1, source_target_pairs={{0,64},{32,96},{64,0},{96,32},{1,65},{33,97},{65,1},{97,33},{2,66}... | collective-permute-start | bytes 1572872 | tf_op jit(solution)/shard_map/ppermute | solution.py:243
  192.5 17.3 %collective-permute-start.17 = (f32[2056,128]{1,0:T(8,128)}, f32[2056,128]{1,0:T(8,128)}, u32[]{:S(2)}, u32[]{:S(2)}) collective-permute-start(f32[2056,128]{1,0:T(8,128)} %get-tuple-element.33), channel_id=1, source_target_pairs={{0,1},{1,0},{2,3},{3,2},{4,5},{5,4},{6,7},{7,6},{8,9},{9,8},{10,11... | collective-permute-start | bytes 3158024 | tf_op jit(solution)/shard_map/ppermute | solution.py:243
  201.7 8.1 %copy-start.4 = (bf16[1,2048]{1,0:T(2,128)(2,1)S(1)}, bf16[1,2048]{1,0:T(2,128)(2,1)}, u32[]{:S(2)}) copy-start(bf16[1,2048]{1,0:T(2,128)(2,1)} %copy-done.3) | copy-start | bytes 12292

commit v3 on v2

v3 whole, which is shorter than its diff:
```python
import functools

import jax
import jax.numpy as jnp
from jax import lax
from jax.experimental import pallas as pl
from jax.experimental.pallas import tpu as pltpu
from jax.sharding import Mesh
from jax.sharding import PartitionSpec as P

D = 2048
HID_DEV = 128
EXP_GRP = 4
TOK_DEV = 256
CAP = 48
WIDE = D + 128
ROWS = 16 * CAP
PAIRS = 4096

f32 = jnp.float32
bf16 = jnp.bfloat16
VMEM = pl.BlockSpec(memory_space=pltpu.VMEM)
SMEM = pl.BlockSpec(memory_space=pltpu.SMEM)
PARAMS = pltpu.CompilerParams(vmem_limit_bytes=24 * 1024 * 1024)
NT = (((1,), (1,)), ((), ()))

BLOCKS = [(EXP_GRP * CAP * d + CAP * k, k, d) for d in range(4) for k in range(EXP_GRP)]
SPACED = pl.CostEstimate(flops=10**11, bytes_accessed=0, transcendentals=0)
ANY = pl.BlockSpec(memory_space=pl.ANY)


def shape(dims, kind):
    return jax.ShapeDtypeStruct(dims, kind)


def iota(dims, axis):
    return lax.broadcasted_iota(jnp.int32, dims, axis)


def thirds(value):
    first = value.astype(bf16).astype(f32)
    second = (value - first).astype(bf16).astype(f32)
    third = (value - first - second).astype(bf16).astype(f32)
    return first, second, third


def dispatch_kernel(
    group_ref,
    mask_ref,
    info_ref,
    tok_ref,
    routes_ref,
    gates_ref,
    pair_ref,
    head_ref,
    up_ref,
    down_ref,
    acc_up_ref,
    acc_down_ref,
    *outs,
):
    out_refs, (base_ref, weights_ref, acc_ref) = outs[:4], outs[4:]
    acc_ref[:D, :] = acc_up_ref[...]
    for j in range(D // HID_DEV):
        at = j * HID_DEV
        acc_ref[D + at : D + at + HID_DEV, :] = acc_down_ref[:, at : at + HID_DEV]
    weights_ref[:D, :] = up_ref[...]
    head = head_ref[...].astype(f32)
    head = jnp.concatenate([head[j : j + 1] for j in range(D // 128)], axis=1)
    head = jnp.broadcast_to(head, (16, D)).astype(bf16)
    proj = lax.dot_general(head, down_ref[...], NT, preferred_element_type=f32)
    first, second, third = thirds(proj)
    row = iota((16, HID_DEV), 0)
    packed = jnp.where(row == 0, first, jnp.where(row == 1, second, jnp.where(row == 2, third, 0.0)))
    weights_ref[D:, :] = packed.astype(bf16)
    grp, zh, member = info_ref[0], info_ref[1], info_ref[2]
    routes = routes_ref[...]
    gates = gates_ref[...]
    sel, gate = [], []
    for k in range(EXP_GRP):
        slot = zh ^ k
        mask = mask_ref[slot]
        expert = jnp.int32(0)
        for j in range(16):
            found = (group_ref[4 * j + slot] ^ mask) == grp
            expert = jnp.where(found, 4 * j + slot, expert)
        hit = routes == expert
        sel.append(jnp.sum(jnp.where(hit, 1.0, 0.0), axis=0, keepdims=True))
        gate.append(jnp.sum(jnp.where(hit, gates, 0.0), axis=0, keepdims=True))
    row8 = iota((8, TOK_DEV), 0)
    chosen = jnp.zeros((8, TOK_DEV), f32)
    for k in range(EXP_GRP):
        chosen = jnp.where(row8 == k, sel[k], chosen)
    tri = jnp.where(iota((TOK_DEV, TOK_DEV), 0) <= iota((TOK_DEV, TOK_DEV), 1), 1.0, 0.0).astype(bf16)
    place = jnp.dot(chosen.astype(bf16), tri, preferred_element_type=f32) - 1.0
    own = (iota((TOK_DEV, 1), 0) + member * TOK_DEV).astype(f32)

    def look(r, code):
        first = pair_ref[pl.ds(r, 1), :].astype(f32)
        second = pair_ref[pl.ds(r + 32, 1), :].astype(f32)
        return jnp.where(first == own, second + 1.0, jnp.where(second == own, -1.0 - first, code))

    code = lax.fori_loop(0, 32, look, jnp.zeros((TOK_DEV, 128), f32), unroll=4)
    code = jnp.sum(code, axis=1, keepdims=True)
    partner = jnp.abs(code) - 1.0
    high = jnp.floor(partner * (1.0 / TOK_DEV))
    low = partner - high * TOK_DEV
    lane = iota((TOK_DEV, 128), 1)
    by_token = jnp.where(lane == 13, high, jnp.where(lane == 14, low, jnp.where(lane == 15, jnp.where(code > 0, 1.0, -1.0), 0.0)))
    by_token = jnp.where(lane == 0, iota((TOK_DEV, 128), 0).astype(f32), by_token).astype(bf16)
    rows = iota((128, TOK_DEV), 0)
    by_slot = jnp.zeros((128, TOK_DEV), f32)
    for k in range(EXP_GRP):
        for j, part in enumerate(thirds(gate[k])):
            by_slot = jnp.where(rows == 1 + 3 * k + j, part, by_slot)
    by_slot = by_slot.astype(bf16)
    base_ref[...] = lax.dot_general(head, tok_ref[...], NT, preferred_element_type=f32)[:8]
    height = iota((CAP, TOK_DEV), 0).astype(f32)
    picks = [
        jnp.where((place[k : k + 1] == height) & (sel[k] > 0.5), 1.0, 0.0).astype(bf16) for k in range(EXP_GRP)
    ]
    pick = jnp.concatenate(picks, axis=0)
    notes = jnp.dot(pick, by_token, preferred_element_type=f32) + lax.dot_general(
        pick, by_slot, NT, preferred_element_type=f32
    )
    wide = jnp.dot(pick, tok_ref[...], preferred_element_type=f32)
    for k in range(EXP_GRP):
        out_refs[k][:, :D] = wide[CAP * k : CAP * (k + 1)].astype(bf16)
        out_refs[k][:, D:] = notes[CAP * k : CAP * (k + 1)].astype(bf16)


def forward_kernel(info_ref, base_ref, own_w_ref, other_w_ref, *refs):
    groups, (x_ref, keep_ref, part_ref, u_ref) = refs[:4], refs[-4:]
    grp, zh, y = info_ref[0], info_ref[1], info_ref[3]
    u_ref[:, :HID_DEV] = own_w_ref[:D, :]
    u_ref[:, HID_DEV:] = other_w_ref[:D, :]
    start = 0
    for ref in groups:
        count = ref.shape[0]
        x_ref[start : start + count, :] = ref[:, :D]
        keep_ref[start : start + count, 2 * HID_DEV :] = ref[:, D:].astype(f32)
        start += count
    pieces = jnp.concatenate([own_w_ref[D:, :], other_w_ref[D:, :]], axis=1).astype(f32)
    proj = pieces[0:1] + pieces[1:2] + pieces[2:3]
    pre = jnp.dot(x_ref[...], u_ref[...], preferred_element_type=f32)
    sig = jax.nn.sigmoid(pre)
    hidden = (pre * sig).astype(bf16)
    keep_ref[:ROWS, : 2 * HID_DEV] = pre
    keep_ref[ROWS:, : 2 * HID_DEV] = jnp.broadcast_to(proj, (8, 2 * HID_DEV))
    value = jnp.sum(hidden.astype(f32) * proj, axis=1, keepdims=True)
    lane = iota((CAP, 128), 1)
    token = iota((CAP, TOK_DEV), 1).astype(f32)
    row = iota((16, TOK_DEV), 0)
    total = jnp.where((row == zh * 4 + y) & (grp == 0), base_ref[0:1, :], 0.0)
    for at, k, d in BLOCKS:
        note = keep_ref[at : at + CAP, 2 * HID_DEV :]
        gate = jnp.sum(jnp.where((lane >= 1 + 3 * k) & (lane < 4 + 3 * k), note, 0.0), axis=1, keepdims=True)
        term = gate * value[at : at + CAP]
        spread = jnp.sum(jnp.where(note[:, 0:1] == token, term, 0.0), axis=0, keepdims=True)
        total = total + jnp.where(row == (zh ^ k) * 4 + (y ^ d), spread, 0.0)
    part_ref[...] = total


def backward_kernel(info_ref, table_ref, x_ref, keep_ref, own_ref, send_ref, own_head_ref):
    zh, c, y = info_ref[1], info_ref[4], info_ref[3]
    table = table_ref[...]
    note = keep_ref[:ROWS, 2 * HID_DEV :]
    token = iota((CAP, TOK_DEV), 1).astype(f32)
    lane = iota((CAP, 128), 1)
    mine, gates = [], []
    for at, k, d in BLOCKS:
        block = ((zh ^ k) * 4 + (y ^ d)) * 2 + c
        values = table_ref[pl.ds(block, 1), :]
        part = keep_ref[at : at + CAP, 2 * HID_DEV :]
        mine.append(jnp.sum(jnp.where(part[:, 0:1] == token, values, 0.0), axis=1, keepdims=True))
        gates.append(
            jnp.sum(jnp.where((lane >= 1 + 3 * k) & (lane < 4 + 3 * k), part, 0.0), axis=1, keepdims=True)
        )
    mine = jnp.concatenate(mine, axis=0)
    gate = jnp.concatenate(gates, axis=0)
    hot = jnp.where(iota((ROWS, 32), 1).astype(f32) == note[:, 13:14], 1.0, 0.0).astype(bf16)
    found = jnp.zeros((ROWS, TOK_DEV), f32)
    for part in thirds(table):
        found = found + jnp.dot(hot, part.astype(bf16), preferred_element_type=f32)
    places = iota((ROWS, TOK_DEV), 1).astype(f32)
    theirs = jnp.sum(jnp.where(places == note[:, 14:15], found, 0.0), axis=1, keepdims=True)
    side = note[:, 15:16]
    margin = side * (mine - theirs)
    grad = -side * (64.0 * jax.nn.sigmoid(-margin)) * gate
    pre = keep_ref[:ROWS, : 2 * HID_DEV]
    proj = keep_ref[ROWS : ROWS + 1, : 2 * HID_DEV]
    sig = jax.nn.sigmoid(pre)
    hidden = (pre * sig).astype(bf16).astype(f32)
    hid_grad = jnp.sum(grad * hidden, axis=0, keepdims=True)
    pre_grad = (grad * proj * (sig * (1.0 + pre * (1.0 - sig)))).astype(bf16)
    out = lax.dot_general(x_ref[...], pre_grad, (((0,), (0,)), ((), ())), preferred_element_type=f32)
    own_ref[...] = out[:, :HID_DEV]
    send_ref[:D, :] = out[:, HID_DEV:]
    own_head_ref[...] = jnp.broadcast_to(hid_grad[:, :HID_DEV], (8, HID_DEV))
    send_ref[D:, :] = jnp.broadcast_to(hid_grad[:, HID_DEV:], (8, HID_DEV))


def loss_kernel(table_ref, pair_ref, out_ref):
    parts = jnp.concatenate([p.astype(bf16) for p in thirds(table_ref[...])], axis=0)

    def rewards_of(index):
        high = jnp.floor(index * (1.0 / TOK_DEV))
        low = index - high * TOK_DEV
        count = index.shape[1]
        row = iota((96, count), 0) & 31
        hot = jnp.where(row.astype(f32) == high, 1.0, 0.0).astype(bf16)
        found = lax.dot_general(parts, hot, (((0,), (0,)), ((), ())), preferred_element_type=f32)
        return jnp.sum(jnp.where(iota((TOK_DEV, count), 0).astype(f32) == low, found, 0.0), axis=0, keepdims=True)

    def step(r, total):
        def line(at):
            rows = [pair_ref[pl.ds(at + i, 1), :].astype(f32) for i in range(4)]
            return jnp.concatenate(rows, axis=1)

        margin = rewards_of(line(4 * r)) - rewards_of(line(4 * r + 32))
        return total + jnp.maximum(-margin, 0.0) + jnp.log1p(jnp.exp(-jnp.abs(margin)))

    total = lax.fori_loop(0, 8, step, jnp.zeros((1, 512), f32))
    out_ref[...] = jnp.broadcast_to(jnp.sum(total, axis=1, keepdims=True) * (1.0 / PAIRS), (1, 128))


def final_kernel(take_ref, acc_ref, got_ref, own_ref, recv_ref, own_head_ref, head_ref, new_up_ref, new_down_ref):
    step = own_ref[...] + recv_ref[:D, :]
    grad = own_head_ref[0:1] + recv_ref[D : D + 1, :]
    square = (HID_DEV, HID_DEV)
    column = jnp.sum(jnp.where(iota(square, 0) == iota(square, 1), grad, 0.0), axis=1, keepdims=True)
    head = head_ref[...].astype(f32)
    for wanted, ref in ((1, got_ref), (0, acc_ref)):

        @pl.when(take_ref[0] == wanted)
        def _(ref=ref):
            new_up_ref[...] = (ref[:D, :].astype(f32) + step).astype(bf16)
            for j in range(D // HID_DEV):
                at = j * HID_DEV
                old = ref[D + at : D + at + HID_DEV, :].astype(f32)
                new_down_ref[:, at : at + HID_DEV] = (old + column * head[j : j + 1]).astype(bf16)


def pick_kernel(count, take_ref, *refs):
    got_refs, own_refs, out_refs = refs[:count], refs[count : 2 * count], refs[-count:]
    for i in range(count):

        @pl.when(take_ref[i] == 1)
        def _(i=i):
            out_refs[i][...] = got_refs[i][...]

        @pl.when(take_ref[i] == 0)
        def _(i=i):
            out_refs[i][...] = own_refs[i][...]


def join_kernel(*refs):
    for k in range(EXP_GRP):
        refs[-1][CAP * k : CAP * (k + 1), :] = refs[k][...]


def swap(block, axis, mask):
    count = lax.axis_size(axis)
    return lax.ppermute(block, axis, [(i, i ^ mask) for i in range(count)])


def picks(stages, got, own, *earlier):
    count = len(stages)
    return pl.pallas_call(
        functools.partial(pick_kernel, count),
        out_shape=[shape(o.shape, o.dtype) for o in own],
        in_specs=[SMEM] + [VMEM] * (2 * count) + [ANY] * len(earlier),
        out_specs=[VMEM] * count,
        compiler_params=PARAMS,
        cost_estimate=SPACED,
        name="pick",
    )(jnp.concatenate([s[2] for s in stages]), *got, *own, *earlier)


def pick(stage, got, own, *earlier):
    return picks([stage], [got], [own], *earlier)[0]


def join(blocks, *earlier):
    return pl.pallas_call(
        join_kernel,
        out_shape=shape((EXP_GRP * CAP, WIDE), bf16),
        in_specs=[VMEM] * EXP_GRP + [ANY] * len(earlier),
        out_specs=VMEM,
        compiler_params=PARAMS,
        cost_estimate=SPACED,
        name="join",
    )(*blocks, *earlier)


def body(tokens, routes, gate_values, old_group, move_mask, pair_index, reward_head, w_up, w_down, acc_up, acc_down):
    x, zl, zh, y, c = (lax.axis_index(a) for a in ("x", "zl", "zh", "y", "c"))
    info = jnp.stack([x * 4 + zl, zh, zh * 8 + y * 2 + c, y, c]).astype(jnp.int32)
    head = reward_head.reshape(D // 128, 128)
    pairs = pair_index.reshape(64, 128)
    mask = jnp.sum(jnp.where(jnp.arange(EXP_GRP) == zh, move_mask, 0))
    bit = [jnp.bitwise_and(jnp.right_shift(mask, i), 1) for i in range(4)]
    x1 = ("x", 1, jnp.bitwise_xor(bit[2], bit[3]).reshape(1))
    x3 = ("x", 3, bit[3].reshape(1))
    z1 = ("zl", 1, bit[0].reshape(1))
    z2 = ("zl", 2, bit[1].reshape(1))

    *sent, base, weights, accums = pl.pallas_call(
        dispatch_kernel,
        out_shape=[shape((CAP, WIDE), bf16)] * 4 + [shape((8, TOK_DEV), f32), shape((D + 16, HID_DEV), bf16), shape((2 * D, HID_DEV), bf16)],
        in_specs=[SMEM] * 3 + [VMEM] * 9,
        out_specs=[VMEM] * 7,
        compiler_params=pltpu.CompilerParams(vmem_limit_bytes=63 * 1024 * 1024),
        name="dispatch",
    )(
        old_group,
        move_mask,
        info,
        tokens,
        routes.T,
        gate_values.T,
        pairs,
        head,
        w_up[0],
        w_down[0],
        acc_up[0],
        acc_down[0],
    )
    blocks = [sent[0], swap(sent[1], "zh", 1), swap(sent[2], "zh", 2), swap(sent[3], "zh", 3)]
    got = swap(weights, *x1[:2])
    acc_got = swap(accums, *x1[:2])
    weights = pick(x1, got, weights)
    got = swap(weights, *x3[:2])
    accums = pick(x1, acc_got, accums, weights)
    acc_got = swap(accums, *x3[:2])
    weights = pick(x3, got, weights, accums)
    got = swap(weights, *z1[:2])
    rows = join(blocks, weights)
    held = [rows] + [swap(rows, "y", d) for d in (1, 2, 3)]
    weights = pick(z1, got, weights, rows)
    got = swap(weights, *z2[:2])
    accums = pick(x3, acc_got, accums, weights)
    acc_got = swap(accums, *z1[:2])
    weights = pick(z2, got, weights, accums)
    other_weights = swap(weights, "c", 1)

    xs, keep, part = pl.pallas_call(
        forward_kernel,
        out_shape=[
            shape((ROWS, D), bf16),
            shape((ROWS + 8, 2 * HID_DEV + 128), f32),
            shape((16, TOK_DEV), f32),
        ],
        in_specs=[SMEM] + [VMEM] * 7,
        out_specs=[VMEM] * 3,
        scratch_shapes=[pltpu.VMEM((D, 2 * HID_DEV), bf16)],
        compiler_params=PARAMS,
        name="forward",
    )(info, base, weights, other_weights, *held)

    accums = pick(z1, acc_got, accums, part)
    part, accums = lax.optimization_barrier((part, accums))
    acc_got = swap(accums, *z2[:2])
    mine = lax.all_to_all(part, ("x", "y"), 0, 0, tiled=True)
    mine = jnp.broadcast_to(jnp.sum(mine, axis=0, keepdims=True), (16, TOK_DEV))
    mine = lax.all_to_all(mine, ("zl", "zh"), 0, 0, tiled=True)
    mine = jnp.broadcast_to(jnp.sum(mine, axis=0, keepdims=True), (32, TOK_DEV))
    table = lax.all_to_all(mine, ("x", "y", "c"), 0, 0, tiled=True)

    table, acc_got = lax.optimization_barrier((table, acc_got))
    own, send, own_head = pl.pallas_call(
        backward_kernel,
        out_shape=[shape((D, HID_DEV), f32), shape((D + 8, HID_DEV), f32), shape((8, HID_DEV), f32)],
        in_specs=[SMEM] + [VMEM] * 3,
        out_specs=[VMEM] * 3,
        compiler_params=PARAMS,
        cost_estimate=SPACED,
        name="backward",
    )(info, table, xs, keep)
    recv = swap(send, "c", 1)
    loss = pl.pallas_call(
        loss_kernel,
        out_shape=shape((1, 128), f32),
        in_specs=[VMEM] * 2,
        out_specs=VMEM,
        compiler_params=PARAMS,
        cost_estimate=SPACED,
        name="loss",
    )(table, pairs)
    new_up, new_down = pl.pallas_call(
        final_kernel,
        out_shape=[shape((D, HID_DEV), bf16), shape((HID_DEV, D), bf16)],
        in_specs=[SMEM] + [VMEM] * 6,
        out_specs=[VMEM] * 2,
        compiler_params=PARAMS,
        name="final",
    )(z2[2], accums, acc_got, own, recv, own_head, head)
    return new_up[None], new_down[None], loss[0, 0]


def solution(mesh):
    fine = Mesh(mesh.devices.reshape(4, 4, 4, 4, 2), ("x", "zl", "zh", "y", "c"))
    grp, ep = ("x", "zl"), ("zh", "y", "c")
    return jax.shard_map(
        body,
        mesh=fine,
        in_specs=(P(ep, None), P(ep, None), P(ep, None), P(), P(), P(), P())
        + (P(grp, None, ep), P(grp, ep, None)) * 2,
        out_specs=(P(grp, None, ep), P(grp, ep, None), P()),
        check_vma=False,
    )
```

time: 214 us -> 205 us (0.958)
  blocking collectives: 10.5 us -> 67.8 us
  starting transfers between devices: 88.9 us -> 58.7 us
  waiting for transfers between devices: 71.2 us -> 47.7 us
  Pallas kernels: 28 us -> 22.2 us
  local copies, waits for them, and re-layouts: 7.94 us -> 3.61 us
    all_to_all x0 -> x2, blocking collectives: none -> 55.7 us  [the longest x1 41.7 us: body(): mine = lax.all_to_all(mine, ('zl', 'zh'), 0, 0, tiled=True)]
    all_to_all x2 -> x0, starting transfers between devices: 18.5 us -> none  [the longest x1 9.26 us: body(): table = lax.all_to_all(mine, ('x', 'y', 'c'), 0, 0, tiled=True)]
    ppermute x18 -> x16, waiting for transfers between devices: 63.2 us -> 47.7 us  [swap(): return lax.ppermute(block, axis, [(i, i ^ mask) for i in range(count)])]
    ppermute x18 -> x16, starting transfers between devices: 70.4 us -> 58.7 us  [swap(): return lax.ppermute(block, axis, [(i, i ^ mask) for i in range(count)])]
    all_to_all x2 -> x0, waiting for transfers between devices: 7.98 us -> none  [the longest x1 7.98 us: body(): mine = lax.all_to_all(mine, ('zl', 'zh'), 0, 0, tiled=True)]
    pallas_call x12 -> x7, Pallas kernels: 7.51 us -> 2.9 us  [picks(): pl.pallas_call(functools.partial(pick_kernel, count), out_shape=[shape(o....]
    unnamed x49 -> x21, local copies, waits for them, and re-layouts: 5.8 us -> 2.96 us
    pallas_call x1, Pallas kernels: 2.19 us -> 4.84 us  [body(): pl.pallas_call(dispatch_kernel, out_shape=[shape((CAP, WIDE), bf16)] * 4...]
  transfers between devices with their start and end apart: 20 -> 16, of which waited for: 8 -> 7; matrix products, arithmetic and copies ran while one was open for 2% -> 0% of each run, Pallas kernels for 12% -> 6%
where the time goes in v3:
time: 205 us; the launch traced here: 204 us
  blocking collectives  67.8 us (33%)
  starting transfers between devices  58.7 us (29%)
  waiting for transfers between devices  47.7 us (23%)
  Pallas kernels  22.2 us (11%)
  local copies, waits for them, and re-layouts  3.61 us (2%)
  between operations  3.49 us (2%)
    ppermute x16, starting transfers between devices, swap(): return lax.ppermute(block, axis, [(i, i ^ mask) for i in range(count)])  58.7 us
    ppermute x16, waiting for transfers between devices, swap(): return lax.ppermute(block, axis, [(i, i ^ mask) for i in range(count)])  47.7 us
    all_to_all x1, blocking collectives, body(): mine = lax.all_to_all(mine, ('zl', 'zh'), 0, 0, tiled=True)  41.7 us
    all_to_all x1, blocking collectives, body(): table = lax.all_to_all(mine, ('x', 'y', 'c'), 0, 0, tiled=True)  14.1 us
    all_to_all x1, blocking collectives, body(): mine = lax.all_to_all(part, ('x', 'y'), 0, 0, tiled=True)  12.1 us
    pallas_call x1, Pallas kernels, body(): pl.pallas_call(dispatch_kernel, out_shape=[shape((CAP, WIDE), bf16)] * 4...  4.84 us
    pallas_call x1, Pallas kernels, body(): pl.pallas_call(backward_kernel, out_shape=[shape((D, HID_DEV), f32), shap...  4.28 us
  transfers between devices with their start and end apart: 16, of which 7 were waited for; matrix products, arithmetic and copies ran while one was open for 0% of the time, Pallas kernels for 6%

profile of v3, /device:TPU:1, one launch (start us, length us, event | category | flops | bytes accessed | tf_op | source)
XLA Modules:
  0.0 204.2 jit_solution(2151571454077580802)
XLA Ops:
  0.6 0.6 stack.23.info_ref
  1.2 0.0 copy-start.9
  1.2 4.8 %dispatch.1 = (bf16[48,2176]{1,0:T(8,128)(2,1)}, bf16[48,2176]{1,0:T(8,128)(2,1)}, bf16[48,2176]{1,0:T(8,128)(2,1)}, bf16[48,2176]{1,0:T(8,128)(2,1)}, f32[8,256...) custom-call(s32[64]{0:T(128)} %group_ref.1, s32[4]{0:T(128)} %mask_ref.1, s32[5]{0:T(128)} %stack.23.info_ref, ...), custom_call_target="tpu_custom_call" | custom-call | tf_op jit(solution)/shard_map/dispatch/pallas_call | solution.py:308
  6.1 3.9 %collective-permute-start = (bf16[2064,128]{1,0:T(8,128)(2,1)}, bf16[2064,128]{1,0:T(8,128)(2,1)S(1)}, u32[]{:S(2)}, u32[]{:S(2)}) collective-permute-start(bf16[2064,128]{1,0:T(8,128)(2,1)} %get-tuple-element.23.refs_1_), channel_id=1, source_target_pairs={{0,128},{128,0},{256,384},{384,256},{1,129},{129,1},{257,385},{385... | collective-permute-start | bytes 1585160 | tf_op jit(solution)/shard_map/ppermute | solution.py:264
  10.0 8.8 %collective-permute-start.4 = (bf16[48,2176]{1,0:T(8,128)(2,1)}, bf16[48,2176]{1,0:T(8,128)(2,1)}, u32[]{:S(2)}, u32[]{:S(2)}) collective-permute-start(bf16[48,2176]{1,0:T(8,128)(2,1)} %get-tuple-element.26), channel_id=1, source_target_pairs={{0,8},{8,0},{16,24},{24,16},{1,9},{9,1},{17,25},{25,17},{2,10},{10... | collective-permute-start | bytes 626696 | tf_op jit(solution)/shard_map/ppermute | solution.py:264
  18.9 10.6 %collective-permute-start.5 = (bf16[48,2176]{1,0:T(8,128)(2,1)}, bf16[48,2176]{1,0:T(8,128)(2,1)}, u32[]{:S(2)}, u32[]{:S(2)}) collective-permute-start(bf16[48,2176]{1,0:T(8,128)(2,1)} %get-tuple-element.27), channel_id=1, source_target_pairs={{0,16},{8,24},{16,0},{24,8},{1,17},{9,25},{17,1},{25,9},{2,18},{10... | collective-permute-start | bytes 626696 | tf_op jit(solution)/shard_map/ppermute | solution.py:264
  29.5 1.9 collective-permute-start.6
  31.4 2.2 %collective-permute-start.2 = (bf16[4096,128]{1,0:T(8,128)(2,1)}, bf16[4096,128]{1,0:T(8,128)(2,1)S(1)}, u32[]{:S(2)}, u32[]{:S(2)}) collective-permute-start(bf16[4096,128]{1,0:T(8,128)(2,1)} %get-tuple-element.24.refs_1_), channel_id=1, source_target_pairs={{0,128},{128,0},{256,384},{384,256},{1,129},{129,1},{257,385},{385... | collective-permute-start | bytes 3145736 | tf_op jit(solution)/shard_map/ppermute | solution.py:264
  33.6 0.0 copy-done.9
  33.6 0.7 fusion
  36.9 0.0 collective-permute-done.refs_0_
  36.9 0.0 copy-start.7
  36.9 1.0 copy-done.7
  37.9 0.0 copy-start.6
  37.9 4.5 %collective-permute-start.1 = (bf16[2064,128]{1,0:T(8,128)(2,1)S(1)}, bf16[2064,128]{1,0:T(8,128)(2,1)S(1)}, u32[]{:S(2)}, u32[]{:S(2)}) collective-permute-start(bf16[2064,128]{1,0:T(8,128)(2,1)S(1)} %pick.7.refs_2_.refs_1_), channel_id=1, source_target_pairs={{0,384},{128,256},{256,128},{384,0},{1,385},{129,257},{257,129},{3... | collective-permute-start | bytes 1585160 | tf_op jit(solution)/shard_map/ppermute | solution.py:264
  42.5 14.3 %collective-permute-done.2.refs_0_ = bf16[4096,128]{1,0:T(8,128)(2,1)S(1)} collective-permute-done((bf16[4096,128]{1,0:T(8,128)(2,1)}, bf16[4096,128]{1,0:T(8,128)(2,1)S(1)}, u32[]{:S(2)}, u32[]{:S(2)}) %collective-permute-start.2) | collective-permute-done | bytes 1048608 | tf_op jit(solution)/shard_map/ppermute | solution.py:264
  56.8 0.0 copy-done.6
  56.8 1.1 pick.8.refs_2_.refs_1_
  57.8 3.7 %collective-permute-start.8 = (bf16[4096,128]{1,0:T(8,128)(2,1)}, bf16[4096,128]{1,0:T(8,128)(2,1)}, u32[]{:S(2)}, u32[]{:S(2)}) collective-permute-start(bf16[4096,128]{1,0:T(8,128)(2,1)} %pick.8.refs_2_.refs_1_), channel_id=1, source_target_pairs={{0,384},{128,256},{256,128},{384,0},{1,385},{129,257},{257,129},{3... | collective-permute-start | bytes 3145736 | tf_op jit(solution)/shard_map/ppermute | solution.py:264
  61.5 0.0 collective-permute-done.1.refs_0_
  61.6 0.0 copy-start.8
  61.6 2.8 %collective-permute-start.3 = (bf16[2064,128]{1,0:T(8,128)(2,1)S(1)}, bf16[2064,128]{1,0:T(8,128)(2,1)S(1)}, u32[]{:S(2)}, u32[]{:S(2)}) collective-permute-start(bf16[2064,128]{1,0:T(8,128)(2,1)S(1)} %pick.9.refs_4_.refs_1_), channel_id=1, source_target_pairs={{0,32},{32,0},{64,96},{96,64},{1,33},{33,1},{65,97},{97,65},{2,34}... | collective-permute-start | bytes 1585160 | tf_op jit(solution)/shard_map/ppermute | solution.py:264
  64.4 0.0 collective-permute-done.4.refs_1_
  64.4 0.0 collective-permute-done.5.refs_2_
  64.4 1.9 collective-permute-done.6.refs_3_
  66.4 0.0 copy-done.8
  66.4 2.1 %join.1.refs_2_.refs_0_ = bf16[192,2176]{1,0:T(8,128)(2,1)} custom-call(bf16[48,2176]{1,0:T(8,128)(2,1)S(1)} %copy-done.8, bf16[48,2176]{1,0:T(8,128)(2,1)} %collective-permute-done.4.refs_1_, bf16[48,2176]{1,0:T(8,128)(2,1)} %collective-permute-done.5.refs_2_, bf16[48,2176]{1,0:T(8,128)(2,1)} %collective-permute-done.6.refs_3_, ...), custom_call_target="tpu_custom_call" | custom-call | flops 99999997952 | tf_op jit(solution)/shard_map/join/pallas_call | solution.py:285
  68.5 4.6 %collective-permute-start.12 = (bf16[192,2176]{1,0:T(8,128)(2,1)}, bf16[192,2176]{1,0:T(8,128)(2,1)}, u32[]{:S(2)}, u32[]{:S(2)}) collective-permute-start(bf16[192,2176]{1,0:T(8,128)(2,1)} %join.1.refs_2_.refs_0_), channel_id=1, source_target_pairs={{0,6},{2,4},{4,2},{6,0},{1,7},{3,5},{5,3},{7,1},{8,14},{10,12},{12... | collective-permute-start | bytes 2506760 | tf_op jit(solution)/shard_map/ppermute | solution.py:264
  73.1 2.3 %collective-permute-start.11 = (bf16[192,2176]{1,0:T(8,128)(2,1)}, bf16[192,2176]{1,0:T(8,128)(2,1)}, u32[]{:S(2)}, u32[]{:S(2)}) collective-permute-start(bf16[192,2176]{1,0:T(8,128)(2,1)} %join.1.refs_2_.refs_0_), channel_id=1, source_target_pairs={{0,4},{2,6},{4,0},{6,2},{1,5},{3,7},{5,1},{7,3},{8,12},{10,14},{12... | collective-permute-start | bytes 2506760 | tf_op jit(solution)/shard_map/ppermute | solution.py:264
  75.4 2.1 %collective-permute-start.10 = (bf16[192,2176]{1,0:T(8,128)(2,1)}, bf16[192,2176]{1,0:T(8,128)(2,1)}, u32[]{:S(2)}, u32[]{:S(2)}) collective-permute-start(bf16[192,2176]{1,0:T(8,128)(2,1)} %join.1.refs_2_.refs_0_), channel_id=1, source_target_pairs={{0,2},{2,0},{4,6},{6,4},{1,3},{3,1},{5,7},{7,5},{8,10},{10,8},{12,... | collective-permute-start | bytes 2506760 | tf_op jit(solution)/shard_map/ppermute | solution.py:264
  77.5 0.0 collective-permute-done.3.refs_0_
  77.6 1.9 collective-permute-start.7
  79.5 4.0 %collective-permute-done.8.refs_0_ = bf16[4096,128]{1,0:T(8,128)(2,1)} collective-permute-done((bf16[4096,128]{1,0:T(8,128)(2,1)}, bf16[4096,128]{1,0:T(8,128)(2,1)}, u32[]{:S(2)}, u32[]{:S(2)}) %collective-permute-start.8) | collective-permute-done | bytes 1048608 | tf_op jit(solution)/shard_map/ppermute | solution.py:264
  83.6 1.6 pick.11.refs_2_.refs_1_
  85.2 2.6 %collective-permute-start.13 = (bf16[4096,128]{1,0:T(8,128)(2,1)S(1)}, bf16[4096,128]{1,0:T(8,128)(2,1)S(1)}, u32[]{:S(2)}, u32[]{:S(2)}) collective-permute-start(bf16[4096,128]{1,0:T(8,128)(2,1)S(1)} %pick.11.refs_2_.refs_1_), channel_id=1, source_target_pairs={{0,32},{32,0},{64,96},{96,64},{1,33},{33,1},{65,97},{97,65},{2,34}... | collective-permute-start | bytes 3145736 | tf_op jit(solution)/shard_map/ppermute | solution.py:264
  87.8 16.6 %collective-permute-done.7.refs_0_ = bf16[2064,128]{1,0:T(8,128)(2,1)S(1)} collective-permute-done((bf16[2064,128]{1,0:T(8,128)(2,1)S(1)}, bf16[2064,128]{1,0:T(8,128)(2,1)S(1)}, u32[]{:S(2)}, u32[]{:S(2)}) %collective-permute-start.7) | collective-permute-done | bytes 528416 | tf_op jit(solution)/shard_map/ppermute | solution.py:264
  104.4 0.0 copy-start.2
  104.4 0.0 copy-start.3
  104.4 2.4 %collective-permute-start.9 = (bf16[2064,128]{1,0:T(8,128)(2,1)S(1)}, bf16[2064,128]{1,0:T(8,128)(2,1)S(1)}, u32[]{:S(2)}, u32[]{:S(2)}) collective-permute-start(bf16[2064,128]{1,0:T(8,128)(2,1)S(1)} %pick.12.own_w_ref), channel_id=1, source_target_pairs={{0,1},{1,0},{2,3},{3,2},{4,5},{5,4},{6,7},{7,6},{8,9},{9,8},{10,11... | collective-permute-start | bytes 1585160 | tf_op jit(solution)/shard_map/ppermute | solution.py:264
  106.8 2.2 %collective-permute-done.12.refs_3_ = bf16[192,2176]{1,0:T(8,128)(2,1)} collective-permute-done((bf16[192,2176]{1,0:T(8,128)(2,1)}, bf16[192,2176]{1,0:T(8,128)(2,1)}, u32[]{:S(2)}, u32[]{:S(2)}) %collective-permute-start.12) | collective-permute-done | bytes 835616 | tf_op jit(solution)/shard_map/ppermute | solution.py:264
  109.0 0.0 collective-permute-done.11.refs_2_
  109.0 2.3 %collective-permute-done.10.refs_1_ = bf16[192,2176]{1,0:T(8,128)(2,1)} collective-permute-done((bf16[192,2176]{1,0:T(8,128)(2,1)}, bf16[192,2176]{1,0:T(8,128)(2,1)}, u32[]{:S(2)}, u32[]{:S(2)}) %collective-permute-start.10) | collective-permute-done | bytes 835616 | tf_op jit(solution)/shard_map/ppermute | solution.py:264
  111.3 0.0 collective-permute-done.9.other_w_ref
  111.3 0.0 copy-done.2
  111.3 0.0 copy-done.3
  111.3 3.3 %forward.1 = (bf16[768,2048]{1,0:T(8,128)(2,1)S(1)}, f32[776,384]{1,0:T(8,128)S(1)}, f32[16,256]{1,0:T(8,128)S(1)}) custom-call(s32[5]{0:T(128)S(1)} %copy-done.3, f32[8,256]{1,0:T(8,128)S(1)} %copy-done.2, bf16[2064,128]{1,0:T(8,128)(2,1)S(1)} %pick.12.own_w_ref, bf16[2064,128]{1,0:T(8,128)(2,1)S(1)} %collective-permute-done.9.other_w_ref, ...), custom_call_target="tpu_custom_call" | custom-call | tf_op jit(solution)/shard_map/forward/pallas_call | solution.py:347
  114.6 0.0 copy-start.4
  114.6 6.3 %collective-permute-done.13.refs_0_ = bf16[4096,128]{1,0:T(8,128)(2,1)S(1)} collective-permute-done((bf16[4096,128]{1,0:T(8,128)(2,1)S(1)}, bf16[4096,128]{1,0:T(8,128)(2,1)S(1)}, u32[]{:S(2)}, u32[]{:S(2)}) %collective-permute-start.13) | collective-permute-done | bytes 1048608 | tf_op jit(solution)/shard_map/ppermute | solution.py:264
  121.0 0.1 pick.13.acc_ref
  121.1 0.0 copy-done.4
  121.1 1.9 collective-permute-start.14
  123.0 12.1 %all_to_all.24 = f32[16,1,256]{2,1,0:T(1,128)S(1)} all-to-all(f32[16,1,256]{2,1,0:T(1,128)S(1)} %copy.16), channel_id=1, replica_groups=mesh['x'=4,'zl'=4,'zh'=4,'y'=4,'c'=2] {'x','y'}, dimensions={0} | all-to-all | bytes 32768 | tf_op jit(solution)/shard_map/all_to_all | solution.py:364
  135.2 41.7 %all_to_all.25 = f32[16,1,256]{2,1,0:T(1,128)S(1)} all-to-all(f32[16,1,256]{2,1,0:T(1,128)S(1)} %broadcast_in_dim.23), channel_id=1, replica_groups=mesh['x'=4,'zl'=4,'zh'=4,'y'=4,'c'=2] {'zl','zh'}, dimensions={0} | all-to-all | bytes 32768 | tf_op jit(solution)/shard_map/all_to_all | solution.py:366
  176.9 14.1 %all_to_all.26 = f32[32,1,256]{2,1,0:T(1,128)S(1)} all-to-all(f32[32,1,256]{2,1,0:T(1,128)S(1)} %broadcast_in_dim.24), channel_id=1, replica_groups=mesh['x'=4,'zl'=4,'zh'=4,'y'=4,'c'=2] {'x','y','c'}, dimensions={0} | all-to-all | bytes 65536 | tf_op jit(solution)/shard_map/all_to_all | solution.py:368
  190.9 0.0 collective-permute-done.14.got_ref
  190.9 1.9 copy-done.5
  192.8 4.3 %backward.1 = (f32[2048,128]{1,0:T(8,128)S(1)}, f32[2056,128]{1,0:T(8,128)S(1)}, f32[8,128]{1,0:T(8,128)S(1)}) custom-call(s32[5]{0:T(128)S(1)} %copy-done.3, f32[32,256]{1,0:T(8,128)S(1)} %bitcast.27, bf16[768,2048]{1,0:T(8,128)(2,1)S(1)} %copy-done.5, f32[776,384]{1,0:T(8,128)S(1)} %get-tuple-element.35.keep_ref), custom_call_target="tpu_custom_call" | custom-call | flops 99999997952 | tf_op jit(solution)/shard_map/backward/pallas_call | solution.py:371
  197.1 0.0 copy-start.1
  197.1 2.3 %collective-permute-start.15 = (f32[2056,128]{1,0:T(8,128)S(1)}, f32[2056,128]{1,0:T(8,128)S(1)}, u32[]{:S(2)}, u32[]{:S(2)}) collective-permute-start(f32[2056,128]{1,0:T(8,128)S(1)} %get-tuple-element.37), channel_id=1, source_target_pairs={{0,1},{1,0},{2,3},{3,2},{4,5},{5,4},{6,7},{7,6},{8,9},{9,8},{10,11... | collective-permute-start | bytes 3158024 | tf_op jit(solution)/shard_map/ppermute | solution.py:264
  199.4 0.0 copy-done
  199.5 3.4 %loss.1 = f32[1,128]{1,0:T(1,128)} custom-call(f32[32,256]{1,0:T(8,128)S(1)} %bitcast.28, s32[64,128]{1,0:T(8,128)S(1)} %bitcast.26), custom_call_target="tpu_custom_call" | custom-call | flops 99999997952 | tf_op jit(solution)/shard_map/loss/pallas_call | solution.py:381
  202.8 0.0 collective-permute-done.15.recv_ref
  202.8 0.0 copy-done.1
  202.8 1.4 final.1
  (12 shorter events, 0.3 us)
Async XLA Ops:
  1.2 32.4 %copy-start.9 = (s32[4]{0:T(128)S(1)}, s32[4]{0:T(128)}, u32[]{:S(2)}) copy-start(s32[4]{0:T(128)} %mask_ref.1) | copy-start | bytes 52
  6.1 30.8 %collective-permute-start = (bf16[2064,128]{1,0:T(8,128)(2,1)}, bf16[2064,128]{1,0:T(8,128)(2,1)S(1)}, u32[]{:S(2)}, u32[]{:S(2)}) collective-permute-start(bf16[2064,128]{1,0:T(8,128)(2,1)} %get-tuple-element.23.refs_1_), channel_id=1, source_target_pairs={{0,128},{128,0},{256,384},{384,256},{1,129},{129,1},{257,385},{385... | collective-permute-start | bytes 1585160 | tf_op jit(solution)/shard_map/ppermute | solution.py:264
  10.0 54.4 %collective-permute-start.4 = (bf16[48,2176]{1,0:T(8,128)(2,1)}, bf16[48,2176]{1,0:T(8,128)(2,1)}, u32[]{:S(2)}, u32[]{:S(2)}) collective-permute-start(bf16[48,2176]{1,0:T(8,128)(2,1)} %get-tuple-element.26), channel_id=1, source_target_pairs={{0,8},{8,0},{16,24},{24,16},{1,9},{9,1},{17,25},{25,17},{2,10},{10... | collective-permute-start | bytes 626696 | tf_op jit(solution)/shard_map/ppermute | solution.py:264
  18.9 45.6 %collective-permute-start.5 = (bf16[48,2176]{1,0:T(8,128)(2,1)}, bf16[48,2176]{1,0:T(8,128)(2,1)}, u32[]{:S(2)}, u32[]{:S(2)}) collective-permute-start(bf16[48,2176]{1,0:T(8,128)(2,1)} %get-tuple-element.27), channel_id=1, source_target_pairs={{0,16},{8,24},{16,0},{24,8},{1,17},{9,25},{17,1},{25,9},{2,18},{10... | collective-permute-start | bytes 626696 | tf_op jit(solution)/shard_map/ppermute | solution.py:264
  29.5 36.9 %collective-permute-start.6 = (bf16[48,2176]{1,0:T(8,128)(2,1)}, bf16[48,2176]{1,0:T(8,128)(2,1)}, u32[]{:S(2)}, u32[]{:S(2)}) collective-permute-start(bf16[48,2176]{1,0:T(8,128)(2,1)} %get-tuple-element.28), channel_id=1, source_target_pairs={{0,24},{8,16},{16,8},{24,0},{1,25},{9,17},{17,9},{25,1},{2,26},{10... | collective-permute-start | bytes 626696 | tf_op jit(solution)/shard_map/ppermute | solution.py:264
  31.4 25.3 %collective-permute-start.2 = (bf16[4096,128]{1,0:T(8,128)(2,1)}, bf16[4096,128]{1,0:T(8,128)(2,1)S(1)}, u32[]{:S(2)}, u32[]{:S(2)}) collective-permute-start(bf16[4096,128]{1,0:T(8,128)(2,1)} %get-tuple-element.24.refs_1_), channel_id=1, source_target_pairs={{0,128},{128,0},{256,384},{384,256},{1,129},{129,1},{257,385},{385... | collective-permute-start | bytes 3145736 | tf_op jit(solution)/shard_map/ppermute | solution.py:264
  36.9 1.0 copy-start.7
  37.9 18.9 %copy-start.6 = (bf16[4096,128]{1,0:T(8,128)(2,1)S(1)}, bf16[4096,128]{1,0:T(8,128)(2,1)}, u32[]{:S(2)}) copy-start(bf16[4096,128]{1,0:T(8,128)(2,1)} %get-tuple-element.24.refs_1_) | copy-start | bytes 3145732
  37.9 23.6 %collective-permute-start.1 = (bf16[2064,128]{1,0:T(8,128)(2,1)S(1)}, bf16[2064,128]{1,0:T(8,128)(2,1)S(1)}, u32[]{:S(2)}, u32[]{:S(2)}) collective-permute-start(bf16[2064,128]{1,0:T(8,128)(2,1)S(1)} %pick.7.refs_2_.refs_1_), channel_id=1, source_target_pairs={{0,384},{128,256},{256,128},{384,0},{1,385},{129,257},{257,129},{3... | collective-permute-start | bytes 1585160 | tf_op jit(solution)/shard_map/ppermute | solution.py:264
  57.8 25.7 %collective-permute-start.8 = (bf16[4096,128]{1,0:T(8,128)(2,1)}, bf16[4096,128]{1,0:T(8,128)(2,1)}, u32[]{:S(2)}, u32[]{:S(2)}) collective-permute-start(bf16[4096,128]{1,0:T(8,128)(2,1)} %pick.8.refs_2_.refs_1_), channel_id=1, source_target_pairs={{0,384},{128,256},{256,128},{384,0},{1,385},{129,257},{257,129},{3... | collective-permute-start | bytes 3145736 | tf_op jit(solution)/shard_map/ppermute | solution.py:264
  61.6 4.8 %copy-start.8 = (bf16[48,2176]{1,0:T(8,128)(2,1)S(1)}, bf16[48,2176]{1,0:T(8,128)(2,1)}, u32[]{:S(2)}) copy-start(bf16[48,2176]{1,0:T(8,128)(2,1)} %get-tuple-element.25.refs_0_) | copy-start | bytes 626692
  61.6 15.9 %collective-permute-start.3 = (bf16[2064,128]{1,0:T(8,128)(2,1)S(1)}, bf16[2064,128]{1,0:T(8,128)(2,1)S(1)}, u32[]{:S(2)}, u32[]{:S(2)}) collective-permute-start(bf16[2064,128]{1,0:T(8,128)(2,1)S(1)} %pick.9.refs_4_.refs_1_), channel_id=1, source_target_pairs={{0,32},{32,0},{64,96},{96,64},{1,33},{33,1},{65,97},{97,65},{2,34}... | collective-permute-start | bytes 1585160 | tf_op jit(solution)/shard_map/ppermute | solution.py:264
  68.5 40.6 %collective-permute-start.12 = (bf16[192,2176]{1,0:T(8,128)(2,1)}, bf16[192,2176]{1,0:T(8,128)(2,1)}, u32[]{:S(2)}, u32[]{:S(2)}) collective-permute-start(bf16[192,2176]{1,0:T(8,128)(2,1)} %join.1.refs_2_.refs_0_), channel_id=1, source_target_pairs={{0,6},{2,4},{4,2},{6,0},{1,7},{3,5},{5,3},{7,1},{8,14},{10,12},{12... | collective-permute-start | bytes 2506760 | tf_op jit(solution)/shard_map/ppermute | solution.py:264
  73.1 35.9 %collective-permute-start.11 = (bf16[192,2176]{1,0:T(8,128)(2,1)}, bf16[192,2176]{1,0:T(8,128)(2,1)}, u32[]{:S(2)}, u32[]{:S(2)}) collective-permute-start(bf16[192,2176]{1,0:T(8,128)(2,1)} %join.1.refs_2_.refs_0_), channel_id=1, source_target_pairs={{0,4},{2,6},{4,0},{6,2},{1,5},{3,7},{5,1},{7,3},{8,12},{10,14},{12... | collective-permute-start | bytes 2506760 | tf_op jit(solution)/shard_map/ppermute | solution.py:264
  75.4 36.0 %collective-permute-start.10 = (bf16[192,2176]{1,0:T(8,128)(2,1)}, bf16[192,2176]{1,0:T(8,128)(2,1)}, u32[]{:S(2)}, u32[]{:S(2)}) collective-permute-start(bf16[192,2176]{1,0:T(8,128)(2,1)} %join.1.refs_2_.refs_0_), channel_id=1, source_target_pairs={{0,2},{2,0},{4,6},{6,4},{1,3},{3,1},{5,7},{7,5},{8,10},{10,8},{12,... | collective-permute-start | bytes 2506760 | tf_op jit(solution)/shard_map/ppermute | solution.py:264
  77.6 26.8 %collective-permute-start.7 = (bf16[2064,128]{1,0:T(8,128)(2,1)S(1)}, bf16[2064,128]{1,0:T(8,128)(2,1)S(1)}, u32[]{:S(2)}, u32[]{:S(2)}) collective-permute-start(bf16[2064,128]{1,0:T(8,128)(2,1)S(1)} %pick.10.refs_2_.refs_1_), channel_id=1, source_target_pairs={{0,64},{32,96},{64,0},{96,32},{1,65},{33,97},{65,1},{97,33},{2,66}... | collective-permute-start | bytes 1585160 | tf_op jit(solution)/shard_map/ppermute | solution.py:264
  85.2 35.8 %collective-permute-start.13 = (bf16[4096,128]{1,0:T(8,128)(2,1)S(1)}, bf16[4096,128]{1,0:T(8,128)(2,1)S(1)}, u32[]{:S(2)}, u32[]{:S(2)}) collective-permute-start(bf16[4096,128]{1,0:T(8,128)(2,1)S(1)} %pick.11.refs_2_.refs_1_), channel_id=1, source_target_pairs={{0,32},{32,0},{64,96},{96,64},{1,33},{33,1},{65,97},{97,65},{2,34}... | collective-permute-start | bytes 3145736 | tf_op jit(solution)/shard_map/ppermute | solution.py:264
  104.4 6.9 %copy-start.2 = (f32[8,256]{1,0:T(8,128)S(1)}, f32[8,256]{1,0:T(8,128)}, u32[]{:S(2)}) copy-start(f32[8,256]{1,0:T(8,128)} %get-tuple-element.22.base_ref) | copy-start | bytes 24580
  104.4 6.9 %copy-start.3 = (s32[5]{0:T(128)S(1)}, s32[5]{0:T(128)}, u32[]{:S(2)}) copy-start(s32[5]{0:T(128)} %stack.23.info_ref) | copy-start | bytes 64
  104.4 6.9 %collective-permute-start.9 = (bf16[2064,128]{1,0:T(8,128)(2,1)S(1)}, bf16[2064,128]{1,0:T(8,128)(2,1)S(1)}, u32[]{:S(2)}, u32[]{:S(2)}) collective-permute-start(bf16[2064,128]{1,0:T(8,128)(2,1)S(1)} %pick.12.own_w_ref), channel_id=1, source_target_pairs={{0,1},{1,0},{2,3},{3,2},{4,5},{5,4},{6,7},{7,6},{8,9},{9,8},{10,11... | collective-permute-start | bytes 1585160 | tf_op jit(solution)/shard_map/ppermute | solution.py:264
  114.6 6.4 %copy-start.4 = (bf16[768,2048]{1,0:T(8,128)(2,1)}, bf16[768,2048]{1,0:T(8,128)(2,1)S(1)}, u32[]{:S(2)}) copy-start(bf16[768,2048]{1,0:T(8,128)(2,1)S(1)} %get-tuple-element.34.x_ref) | copy-start | bytes 9437188
  121.1 69.9 %collective-permute-start.14 = (bf16[4096,128]{1,0:T(8,128)(2,1)S(1)}, bf16[4096,128]{1,0:T(8,128)(2,1)S(1)}, u32[]{:S(2)}, u32[]{:S(2)}) collective-permute-start(bf16[4096,128]{1,0:T(8,128)(2,1)S(1)} %pick.13.acc_ref), channel_id=1, source_target_pairs={{0,64},{32,96},{64,0},{96,32},{1,65},{33,97},{65,1},{97,33},{2,66}... | collective-permute-start | bytes 3145736 | tf_op jit(solution)/shard_map/ppermute | solution.py:264
  190.9 1.9 copy-start.5
  192.8 6.6 %copy-start = (s32[8192]{0:T(1024)S(1)}, s32[8192]{0:T(1024)}, u32[]{:S(2)}) copy-start(s32[8192]{0:T(1024)} %param.16) | copy-start | bytes 98308
  197.1 5.7 %copy-start.1 = (bf16[2048]{0:T(1024)(128)(2,1)S(1)}, bf16[2048]{0:T(1024)(128)(2,1)}, u32[]{:S(2)}) copy-start(bf16[2048]{0:T(1024)(128)(2,1)} %param.17) | copy-start | bytes 12292
  197.1 5.7 %collective-permute-start.15 = (f32[2056,128]{1,0:T(8,128)S(1)}, f32[2056,128]{1,0:T(8,128)S(1)}, u32[]{:S(2)}, u32[]{:S(2)}) collective-permute-start(f32[2056,128]{1,0:T(8,128)S(1)} %get-tuple-element.37), channel_id=1, source_target_pairs={{0,1},{1,0},{2,3},{3,2},{4,5},{5,4},{6,7},{7,6},{8,9},{9,8},{10,11... | collective-permute-start | bytes 3158024 | tf_op jit(solution)/shard_map/ppermute | solution.py:264

commit v4 on v3

--- a/solution.py
+++ b/solution.py
@@ -224,20 +224,27 @@
     out_ref[...] = jnp.broadcast_to(jnp.sum(total, axis=1, keepdims=True) * (1.0 / PAIRS), (1, 128))
 
 
-def final_kernel(take_ref, acc_ref, got_ref, own_ref, recv_ref, own_head_ref, head_ref, new_up_ref, new_down_ref):
+def final_kernel(
+    take_ref, up_ref, up_got_ref, down_ref, down_got_ref, own_ref, recv_ref, own_head_ref, head_ref, new_up_ref, new_down_ref
+):
     step = own_ref[...] + recv_ref[:D, :]
     grad = own_head_ref[0:1] + recv_ref[D : D + 1, :]
     square = (HID_DEV, HID_DEV)
     column = jnp.sum(jnp.where(iota(square, 0) == iota(square, 1), grad, 0.0), axis=1, keepdims=True)
     head = head_ref[...].astype(f32)
-    for wanted, ref in ((1, got_ref), (0, acc_ref)):
+    for wanted, ref in ((1, up_got_ref), (0, up_ref)):
 
         @pl.when(take_ref[0] == wanted)
         def _(ref=ref):
-            new_up_ref[...] = (ref[:D, :].astype(f32) + step).astype(bf16)
+            new_up_ref[...] = (ref[...].astype(f32) + step).astype(bf16)
+
+    for wanted, ref in ((1, down_got_ref), (0, down_ref)):
+
+        @pl.when(take_ref[1] == wanted)
+        def _(ref=ref):
             for j in range(D // HID_DEV):
                 at = j * HID_DEV
-                old = ref[D + at : D + at + HID_DEV, :].astype(f32)
+                old = ref[at : at + HID_DEV, :].astype(f32)
                 new_down_ref[:, at : at + HID_DEV] = (old + column * head[j : j + 1]).astype(bf16)
 
 
@@ -252,6 +259,15 @@
         @pl.when(take_ref[i] == 0)
         def _(i=i):
             out_refs[i][...] = own_refs[i][...]
+
+
+def split_kernel(take_ref, got_ref, own_ref, earlier_ref, up_ref, down_ref):
+    for wanted, ref in ((1, got_ref), (0, own_ref)):
+
+        @pl.when(take_ref[0] == wanted)
+        def _(ref=ref):
+            up_ref[...] = ref[:D, :]
+            down_ref[...] = ref[D:, :]
 
 
 def join_kernel(*refs):
@@ -339,10 +355,20 @@
     held = [rows] + [swap(rows, "y", d) for d in (1, 2, 3)]
     weights = pick(z1, got, weights, rows)
     got = swap(weights, *z2[:2])
-    accums = pick(x3, acc_got, accums, weights)
-    acc_got = swap(accums, *z1[:2])
-    weights = pick(z2, got, weights, accums)
+    up, down = pl.pallas_call(
+        split_kernel,
+        out_shape=[shape((D, HID_DEV), bf16)] * 2,
+        in_specs=[SMEM, VMEM, VMEM, ANY],
+        out_specs=[VMEM] * 2,
+        compiler_params=PARAMS,
+        cost_estimate=SPACED,
+        name="pick_split",
+    )(x3[2], acc_got, accums, weights)
+    weights = pick(z2, got, weights, up)
+    weights, up, down = lax.optimization_barrier((weights, up, down))
     other_weights = swap(weights, "c", 1)
+    up_got = swap(up, *z1[:2])
+    down_got = swap(down, *z2[:2])
 
     xs, keep, part = pl.pallas_call(
         forward_kernel,
@@ -358,16 +384,16 @@
         name="forward",
     )(info, base, weights, other_weights, *held)
 
-    accums = pick(z1, acc_got, accums, part)
-    part, accums = lax.optimization_barrier((part, accums))
-    acc_got = swap(accums, *z2[:2])
     mine = lax.all_to_all(part, ("x", "y"), 0, 0, tiled=True)
     mine = jnp.broadcast_to(jnp.sum(mine, axis=0, keepdims=True), (16, TOK_DEV))
     mine = lax.all_to_all(mine, ("zl", "zh"), 0, 0, tiled=True)
     mine = jnp.broadcast_to(jnp.sum(mine, axis=0, keepdims=True), (32, TOK_DEV))
+    up, down = picks([z1, z2], [up_got, down_got], [up, down], mine)
+    mine, up, down = lax.optimization_barrier((mine, up, down))
+    up_got = swap(up, *z2[:2])
+    down_got = swap(down, *z1[:2])
     table = lax.all_to_all(mine, ("x", "y", "c"), 0, 0, tiled=True)
 
-    table, acc_got = lax.optimization_barrier((table, acc_got))
     own, send, own_head = pl.pallas_call(
         backward_kernel,
         out_shape=[shape((D, HID_DEV), f32), shape((D + 8, HID_DEV), f32), shape((8, HID_DEV), f32)],
@@ -390,11 +416,11 @@
     new_up, new_down = pl.pallas_call(
         final_kernel,
         out_shape=[shape((D, HID_DEV), bf16), shape((HID_DEV, D), bf16)],
-        in_specs=[SMEM] + [VMEM] * 6,
+        in_specs=[SMEM] + [VMEM] * 8,
         out_specs=[VMEM] * 2,
         compiler_params=PARAMS,
         name="final",
-    )(z2[2], accums, acc_got, own, recv, own_head, head)
+    )(jnp.concatenate([z2[2], z1[2]]), up, up_got, down, down_got, own, recv, own_head, head)
     return new_up[None], new_down[None], loss[0, 0]
 
 

time: 205 us -> 199 us (0.971)
  blocking collectives: 67.8 us -> 10.4 us
  starting transfers between devices: 58.7 us -> 84.3 us
  waiting for transfers between devices: 47.7 us -> 66.2 us
  Pallas kernels: 22.2 us -> 27.2 us
    all_to_all x2 -> x0, blocking collectives: 55.7 us -> none  [the longest x1 41.7 us: body(): mine = lax.all_to_all(mine, ('zl', 'zh'), 0, 0, tiled=True)]
    all_to_all x0 -> x2, starting transfers between devices: none -> 17.8 us  [the longest x1 9.21 us: body(): mine = lax.all_to_all(mine, ('zl', 'zh'), 0, 0, tiled=True)]
    all_to_all x0 -> x2, waiting for transfers between devices: none -> 13.8 us  [the longest x1 11.2 us: body(): mine = lax.all_to_all(mine, ('zl', 'zh'), 0, 0, tiled=True)]
    ppermute x16 -> x18, starting transfers between devices: 58.7 us -> 66.6 us  [swap(): return lax.ppermute(block, axis, [(i, i ^ mask) for i in range(count)])]
    ppermute x16 -> x18, waiting for transfers between devices: 47.7 us -> 52.4 us  [swap(): return lax.ppermute(block, axis, [(i, i ^ mask) for i in range(count)])]
    pallas_call x0 -> x1, Pallas kernels: none -> 2.58 us  [body(): pl.pallas_call(split_kernel, out_shape=[shape((D, HID_DEV), bf16)] * 2, i...]
  transfers between devices with their start and end apart: 16 -> 20, of which waited for: 7 -> 8; matrix products, arithmetic and copies ran while one was open for 0% -> 1% of each run, Pallas kernels for 6% -> 9%
where the time goes in v4:
time: 199 us; the launch traced here: 198 us
  starting transfers between devices  84.3 us (42%)
  waiting for transfers between devices  66.2 us (33%)
  Pallas kernels  27.2 us (14%)
  blocking collectives  10.4 us (5%)
  local copies, waits for them, and re-layouts  5.25 us (3%)
  between operations  3.49 us (2%)
    ppermute x18, starting transfers between devices, swap(): return lax.ppermute(block, axis, [(i, i ^ mask) for i in range(count)])  66.6 us
    ppermute x18, waiting for transfers between devices, swap(): return lax.ppermute(block, axis, [(i, i ^ mask) for i in range(count)])  52.4 us
    all_to_all x1, waiting for transfers between devices, body(): mine = lax.all_to_all(mine, ('zl', 'zh'), 0, 0, tiled=True)  11.2 us
    all_to_all x1, blocking collectives, body(): mine = lax.all_to_all(part, ('x', 'y'), 0, 0, tiled=True)  10.4 us
    all_to_all x1, starting transfers between devices, body(): mine = lax.all_to_all(mine, ('zl', 'zh'), 0, 0, tiled=True)  9.21 us
    all_to_all x1, starting transfers between devices, body(): table = lax.all_to_all(mine, ('x', 'y', 'c'), 0, 0, tiled=True)  8.55 us
    pallas_call x1, Pallas kernels, body(): pl.pallas_call(dispatch_kernel, out_shape=[shape((CAP, WIDE), bf16)] * 4...  4.82 us
    pallas_call x1, Pallas kernels, body(): pl.pallas_call(backward_kernel, out_shape=[shape((D, HID_DEV), f32), shap...  4.3 us
  transfers between devices with their start and end apart: 20, of which 8 were waited for; matrix products, arithmetic and copies ran while one was open for 1% of the time, Pallas kernels for 9%

profile of v4, /device:TPU:1, one launch (start us, length us, event | category | flops | bytes accessed | tf_op | source)
XLA Modules:
  0.0 197.8 jit_solution(3453339132915956800)
XLA Ops:
  0.6 0.6 stack.23.info_ref
  1.3 4.8 %dispatch.1 = (bf16[48,2176]{1,0:T(8,128)(2,1)}, bf16[48,2176]{1,0:T(8,128)(2,1)}, bf16[48,2176]{1,0:T(8,128)(2,1)}, bf16[48,2176]{1,0:T(8,128)(2,1)}, f32[8,256...) custom-call(s32[64]{0:T(128)} %group_ref.1, s32[4]{0:T(128)} %mask_ref.1, s32[5]{0:T(128)} %stack.23.info_ref, ...), custom_call_target="tpu_custom_call" | custom-call | tf_op jit(solution)/shard_map/dispatch/pallas_call | solution.py:324
  6.1 3.9 %collective-permute-start = (bf16[2064,128]{1,0:T(8,128)(2,1)}, bf16[2064,128]{1,0:T(8,128)(2,1)S(1)}, u32[]{:S(2)}, u32[]{:S(2)}) collective-permute-start(bf16[2064,128]{1,0:T(8,128)(2,1)} %get-tuple-element.29.refs_1_), channel_id=1, source_target_pairs={{0,128},{128,0},{256,384},{384,256},{1,129},{129,1},{257,385},{385... | collective-permute-start | bytes 1585160 | tf_op jit(solution)/shard_map/ppermute | solution.py:280
  10.0 1.9 collective-permute-start.2
  12.0 9.1 %collective-permute-start.4 = (bf16[48,2176]{1,0:T(8,128)(2,1)}, bf16[48,2176]{1,0:T(8,128)(2,1)}, u32[]{:S(2)}, u32[]{:S(2)}) collective-permute-start(bf16[48,2176]{1,0:T(8,128)(2,1)} %get-tuple-element.32), channel_id=1, source_target_pairs={{0,8},{8,0},{16,24},{24,16},{1,9},{9,1},{17,25},{25,17},{2,10},{10... | collective-permute-start | bytes 626696 | tf_op jit(solution)/shard_map/ppermute | solution.py:280
  21.0 10.6 %collective-permute-start.5 = (bf16[48,2176]{1,0:T(8,128)(2,1)}, bf16[48,2176]{1,0:T(8,128)(2,1)}, u32[]{:S(2)}, u32[]{:S(2)}) collective-permute-start(bf16[48,2176]{1,0:T(8,128)(2,1)} %get-tuple-element.33), channel_id=1, source_target_pairs={{0,16},{8,24},{16,0},{24,8},{1,17},{9,25},{17,1},{25,9},{2,18},{10... | collective-permute-start | bytes 626696 | tf_op jit(solution)/shard_map/ppermute | solution.py:280
  31.7 1.9 collective-permute-start.6
  33.6 0.0 copy-done.9
  33.6 0.7 fusion
  36.8 0.0 collective-permute-done.refs_0_
  36.8 0.0 copy-start.7
  36.8 1.0 copy-done.7
  37.9 4.5 %collective-permute-start.1 = (bf16[2064,128]{1,0:T(8,128)(2,1)S(1)}, bf16[2064,128]{1,0:T(8,128)(2,1)S(1)}, u32[]{:S(2)}, u32[]{:S(2)}) collective-permute-start(bf16[2064,128]{1,0:T(8,128)(2,1)S(1)} %pick.6.refs_2_.refs_1_), channel_id=1, source_target_pairs={{0,384},{128,256},{256,128},{384,0},{1,385},{129,257},{257,129},{3... | collective-permute-start | bytes 1585160 | tf_op jit(solution)/shard_map/ppermute | solution.py:280
  42.4 0.0 collective-permute-done.2.refs_0_
  42.4 0.0 copy-done.6
  42.4 1.1 pick.7.refs_2_.own_ref
  43.5 6.4 %collective-permute-start.8 = (bf16[4096,128]{1,0:T(8,128)(2,1)}, bf16[4096,128]{1,0:T(8,128)(2,1)}, u32[]{:S(2)}, u32[]{:S(2)}) collective-permute-start(bf16[4096,128]{1,0:T(8,128)(2,1)} %pick.7.refs_2_.own_ref), channel_id=1, source_target_pairs={{0,384},{128,256},{256,128},{384,0},{1,385},{129,257},{257,129},{3... | collective-permute-start | bytes 3145736 | tf_op jit(solution)/shard_map/ppermute | solution.py:280
  49.9 2.6 %collective-permute-done.1.refs_0_ = bf16[2064,128]{1,0:T(8,128)(2,1)S(1)} collective-permute-done((bf16[2064,128]{1,0:T(8,128)(2,1)S(1)}, bf16[2064,128]{1,0:T(8,128)(2,1)S(1)}, u32[]{:S(2)}, u32[]{:S(2)}) %collective-permute-start.1) | collective-permute-done | bytes 528416 | tf_op jit(solution)/shard_map/ppermute | solution.py:280
  52.5 3.2 %collective-permute-start.3 = (bf16[2064,128]{1,0:T(8,128)(2,1)S(1)}, bf16[2064,128]{1,0:T(8,128)(2,1)S(1)}, u32[]{:S(2)}, u32[]{:S(2)}) collective-permute-start(bf16[2064,128]{1,0:T(8,128)(2,1)S(1)} %pick.8.refs_4_.refs_1_), channel_id=1, source_target_pairs={{0,32},{32,0},{64,96},{96,64},{1,33},{33,1},{65,97},{97,65},{2,34}... | collective-permute-start | bytes 1585160 | tf_op jit(solution)/shard_map/ppermute | solution.py:280
  55.8 0.0 collective-permute-done.4.refs_1_
  55.8 0.0 collective-permute-done.5.refs_2_
  55.8 12.7 %collective-permute-done.6.refs_3_ = bf16[48,2176]{1,0:T(8,128)(2,1)} collective-permute-done((bf16[48,2176]{1,0:T(8,128)(2,1)}, bf16[48,2176]{1,0:T(8,128)(2,1)}, u32[]{:S(2)}, u32[]{:S(2)}) %collective-permute-start.6) | collective-permute-done | bytes 208928 | tf_op jit(solution)/shard_map/ppermute | solution.py:280
  68.5 2.1 %join.1.refs_2_.refs_0_ = bf16[192,2176]{1,0:T(8,128)(2,1)} custom-call(bf16[48,2176]{1,0:T(8,128)(2,1)S(1)} %copy-done.8, bf16[48,2176]{1,0:T(8,128)(2,1)} %collective-permute-done.4.refs_1_, bf16[48,2176]{1,0:T(8,128)(2,1)} %collective-permute-done.5.refs_2_, bf16[48,2176]{1,0:T(8,128)(2,1)} %collective-permute-done.6.refs_3_, ...), custom_call_target="tpu_custom_call" | custom-call | flops 99999997952 | tf_op jit(solution)/shard_map/join/pallas_call | solution.py:301
  70.6 3.2 %collective-permute-start.10 = (bf16[192,2176]{1,0:T(8,128)(2,1)}, bf16[192,2176]{1,0:T(8,128)(2,1)}, u32[]{:S(2)}, u32[]{:S(2)}) collective-permute-start(bf16[192,2176]{1,0:T(8,128)(2,1)} %join.1.refs_2_.refs_0_), channel_id=1, source_target_pairs={{0,2},{2,0},{4,6},{6,4},{1,3},{3,1},{5,7},{7,5},{8,10},{10,8},{12,... | collective-permute-start | bytes 2506760 | tf_op jit(solution)/shard_map/ppermute | solution.py:280
  73.8 4.5 %collective-permute-start.11 = (bf16[192,2176]{1,0:T(8,128)(2,1)}, bf16[192,2176]{1,0:T(8,128)(2,1)}, u32[]{:S(2)}, u32[]{:S(2)}) collective-permute-start(bf16[192,2176]{1,0:T(8,128)(2,1)} %join.1.refs_2_.refs_0_), channel_id=1, source_target_pairs={{0,4},{2,6},{4,0},{6,2},{1,5},{3,7},{5,1},{7,3},{8,12},{10,14},{12... | collective-permute-start | bytes 2506760 | tf_op jit(solution)/shard_map/ppermute | solution.py:280
  78.4 1.9 collective-permute-start.12
  80.3 0.0 collective-permute-done.3.refs_0_
  80.3 1.9 collective-permute-start.7
  82.3 0.0 collective-permute-done.8.got_ref
  82.3 2.6 %pick_split.1 = (bf16[2048,128]{1,0:T(8,128)(2,1)}, bf16[2048,128]{1,0:T(8,128)(2,1)}) custom-call(s32[1]{0:T(128)} %bitcast.15.take_ref, bf16[4096,128]{1,0:T(8,128)(2,1)} %collective-permute-done.8.got_ref, bf16[4096,128]{1,0:T(8,128)(2,1)} %pick.7.refs_2_.own_ref, bf16[2064,128]{1,0:T(8,128)(2,1)S(1)} %pick.9.earlier_ref.refs_1_), custom_call_target="tpu_custom_call" | custom-call | flops 99999997952 | tf_op jit(solution)/shard_map/pick_split/pallas_call | solution.py:358
  84.9 23.1 %collective-permute-done.7.refs_0_ = bf16[2064,128]{1,0:T(8,128)(2,1)S(1)} collective-permute-done((bf16[2064,128]{1,0:T(8,128)(2,1)S(1)}, bf16[2064,128]{1,0:T(8,128)(2,1)S(1)}, u32[]{:S(2)}, u32[]{:S(2)}) %collective-permute-start.7) | collective-permute-done | bytes 528416 | tf_op jit(solution)/shard_map/ppermute | solution.py:280
  108.0 2.3 %collective-permute-start.9 = (bf16[2064,128]{1,0:T(8,128)(2,1)S(1)}, bf16[2064,128]{1,0:T(8,128)(2,1)S(1)}, u32[]{:S(2)}, u32[]{:S(2)}) collective-permute-start(bf16[2064,128]{1,0:T(8,128)(2,1)S(1)} %pick.10.own_w_ref), channel_id=1, source_target_pairs={{0,1},{1,0},{2,3},{3,2},{4,5},{5,4},{6,7},{7,6},{8,9},{9,8},{10,11... | collective-permute-start | bytes 1585160 | tf_op jit(solution)/shard_map/ppermute | solution.py:280
  110.3 1.9 collective-permute-start.13
  112.2 0.0 collective-permute-done.10.refs_1_
  112.2 2.2 %collective-permute-start.14 = (bf16[2048,128]{1,0:T(8,128)(2,1)}, bf16[2048,128]{1,0:T(8,128)(2,1)}, u32[]{:S(2)}, u32[]{:S(2)}) collective-permute-start(bf16[2048,128]{1,0:T(8,128)(2,1)} %get-tuple-element.40.refs_3_), channel_id=1, source_target_pairs={{0,64},{32,96},{64,0},{96,32},{1,65},{33,97},{65,1},{97,33},{2,66}... | collective-permute-start | bytes 1572872 | tf_op jit(solution)/shard_map/ppermute | solution.py:280
  114.4 0.0 collective-permute-done.11.refs_2_
  114.4 4.0 %collective-permute-done.12.refs_3_ = bf16[192,2176]{1,0:T(8,128)(2,1)} collective-permute-done((bf16[192,2176]{1,0:T(8,128)(2,1)}, bf16[192,2176]{1,0:T(8,128)(2,1)}, u32[]{:S(2)}, u32[]{:S(2)}) %collective-permute-start.12) | collective-permute-done | bytes 835616 | tf_op jit(solution)/shard_map/ppermute | solution.py:280
  118.5 0.0 collective-permute-done.9.other_w_ref
  118.5 0.0 copy-done.3
  118.5 3.3 %forward.1 = (bf16[768,2048]{1,0:T(8,128)(2,1)S(1)}, f32[776,384]{1,0:T(8,128)S(1)}, f32[16,256]{1,0:T(8,128)S(1)}) custom-call(s32[5]{0:T(128)S(1)} %copy-done.3, f32[8,256]{1,0:T(8,128)S(1)} %copy-done.2, bf16[2064,128]{1,0:T(8,128)(2,1)S(1)} %pick.10.own_w_ref, bf16[2064,128]{1,0:T(8,128)(2,1)S(1)} %collective-permute-done.9.other_w_ref, ...), custom_call_target="tpu_custom_call" | custom-call | tf_op jit(solution)/shard_map/forward/pallas_call | solution.py:373
  121.8 1.0 copy-done.4
  122.8 10.4 %all_to_all.26 = f32[16,1,256]{2,1,0:T(1,128)S(1)} all-to-all(f32[16,1,256]{2,1,0:T(1,128)S(1)} %copy.18), channel_id=1, replica_groups=mesh['x'=4,'zl'=4,'zh'=4,'y'=4,'c'=2] {'x','y'}, dimensions={0} | all-to-all | bytes 32768 | tf_op jit(solution)/shard_map/all_to_all | solution.py:387
  133.2 0.6 broadcast_in_dim.23
  133.8 9.2 %all-to-all-start.1 = ((f32[16,1,256]{2,1,0:T(1,128)}), f32[16,1,256]{2,1,0:T(1,128)S(1)}, u32[]{:S(2)}, u32[]{:S(2)}) async-start(f32[16,1,256]{2,1,0:T(1,128)} %broadcast_in_dim.23), calls=%async_computation.1 | async-start | bytes 32768 | tf_op jit(solution)/shard_map/all_to_all | solution.py:389
  143.1 0.1 pad_add_fusion.1.take_ref
  143.1 11.2 %all-to-all-done.1 = f32[16,1,256]{2,1,0:T(1,128)S(1)} async-done(((f32[16,1,256]{2,1,0:T(1,128)}), f32[16,1,256]{2,1,0:T(1,128)S(1)}, u32[]{:S(2)}, u32[]{:S(2)}) %all-to-all-start.1) | async-done | bytes 16416 | tf_op jit(solution)/shard_map/all_to_all | solution.py:389
  154.4 0.0 collective-permute-done.13.refs_0_
  154.4 0.0 collective-permute-done.14.refs_1_
  154.4 2.6 %pick.11 = (bf16[2048,128]{1,0:T(8,128)(2,1)}, bf16[2048,128]{1,0:T(8,128)(2,1)}) custom-call(s32[2]{0:T(128)S(1)} %pad_add_fusion.1.take_ref, bf16[2048,128]{1,0:T(8,128)(2,1)} %collective-permute-done.13.refs_0_, bf16[2048,128]{1,0:T(8,128)(2,1)} %collective-permute-done.14.refs_1_, bf16[2048,128]{1,0:T(8,128)(2,1)} %get-tuple-element.39.refs_2_, ...), custom_call_target="tpu_custom_call" | custom-call | flops 99999997952 | tf_op jit(solution)/shard_map/pick/pallas_call | solution.py:285
  157.0 0.6 copy.20
  157.7 8.6 %all-to-all-start.2 = ((f32[32,1,256]{2,1,0:T(1,128)}), f32[32,1,256]{2,1,0:T(1,128)S(1)}, u32[]{:S(2)}, u32[]{:S(2)}) async-start(f32[32,1,256]{2,1,0:T(1,128)} %copy.20), calls=%async_computation.2 | async-start | bytes 65536 | tf_op jit(solution)/shard_map/all_to_all | solution.py:395
  166.2 0.1 pad_add_fusion.take_ref
  166.3 2.5 %collective-permute-start.15 = (bf16[2048,128]{1,0:T(8,128)(2,1)}, bf16[2048,128]{1,0:T(8,128)(2,1)}, u32[]{:S(2)}, u32[]{:S(2)}) collective-permute-start(bf16[2048,128]{1,0:T(8,128)(2,1)} %get-tuple-element.43.up_ref), channel_id=1, source_target_pairs={{0,64},{32,96},{64,0},{96,32},{1,65},{33,97},{65,1},{97,33},{2,66}... | collective-permute-start | bytes 1572872 | tf_op jit(solution)/shard_map/ppermute | solution.py:280
  168.8 2.2 %collective-permute-start.16 = (bf16[2048,128]{1,0:T(8,128)(2,1)}, bf16[2048,128]{1,0:T(8,128)(2,1)}, u32[]{:S(2)}, u32[]{:S(2)}) collective-permute-start(bf16[2048,128]{1,0:T(8,128)(2,1)} %get-tuple-element.44.down_ref), channel_id=1, source_target_pairs={{0,32},{32,0},{64,96},{96,64},{1,33},{33,1},{65,97},{97,65},{2,34}... | collective-permute-start | bytes 1572872 | tf_op jit(solution)/shard_map/ppermute | solution.py:280
  171.0 2.6 %all-to-all-done.2 = f32[32,1,256]{2,1,0:T(1,128)S(1)} async-done(((f32[32,1,256]{2,1,0:T(1,128)}), f32[32,1,256]{2,1,0:T(1,128)S(1)}, u32[]{:S(2)}, u32[]{:S(2)}) %all-to-all-start.2) | async-done | bytes 32800 | tf_op jit(solution)/shard_map/all_to_all | solution.py:395
  173.6 1.3 copy-done.5
  174.9 4.3 %backward.1 = (f32[2048,128]{1,0:T(8,128)S(1)}, f32[2056,128]{1,0:T(8,128)S(1)}, f32[8,128]{1,0:T(8,128)S(1)}) custom-call(s32[5]{0:T(128)S(1)} %copy-done.3, f32[32,256]{1,0:T(8,128)S(1)} %bitcast.29, bf16[768,2048]{1,0:T(8,128)(2,1)S(1)} %get-tuple-element.46.x_ref, f32[776,384]{1,0:T(8,128)S(1)} %copy-done.5), custom_call_target="tpu_custom_call" | custom-call | flops 99999997952 | tf_op jit(solution)/shard_map/backward/pallas_call | solution.py:397
  179.2 0.0 copy-start.1
  179.2 2.3 %collective-permute-start.17 = (f32[2056,128]{1,0:T(8,128)S(1)}, f32[2056,128]{1,0:T(8,128)S(1)}, u32[]{:S(2)}, u32[]{:S(2)}) collective-permute-start(f32[2056,128]{1,0:T(8,128)S(1)} %get-tuple-element.49), channel_id=1, source_target_pairs={{0,1},{1,0},{2,3},{3,2},{4,5},{5,4},{6,7},{7,6},{8,9},{9,8},{10,11... | collective-permute-start | bytes 3158024 | tf_op jit(solution)/shard_map/ppermute | solution.py:280
  181.5 3.4 %loss.1 = f32[1,128]{1,0:T(1,128)} custom-call(f32[32,256]{1,0:T(8,128)S(1)} %bitcast.30, s32[64,128]{1,0:T(8,128)S(1)} %bitcast.28), custom_call_target="tpu_custom_call" | custom-call | flops 99999997952 | tf_op jit(solution)/shard_map/loss/pallas_call | solution.py:407
  184.9 9.5 %collective-permute-done.15.up_got_ref = bf16[2048,128]{1,0:T(8,128)(2,1)} collective-permute-done((bf16[2048,128]{1,0:T(8,128)(2,1)}, bf16[2048,128]{1,0:T(8,128)(2,1)}, u32[]{:S(2)}, u32[]{:S(2)}) %collective-permute-start.15) | collective-permute-done | bytes 524320 | tf_op jit(solution)/shard_map/ppermute | solution.py:280
  194.4 0.5 collective-permute-done.16.down_got_ref
  194.9 0.0 collective-permute-done.17.recv_ref
  194.9 2.9 %final.1 = (bf16[2048,128]{1,0:T(8,128)(2,1)}, bf16[128,2048]{1,0:T(8,128)(2,1)}) custom-call(s32[2]{0:T(128)S(1)} %pad_add_fusion.take_ref, bf16[2048,128]{1,0:T(8,128)(2,1)} %get-tuple-element.43.up_ref, bf16[2048,128]{1,0:T(8,128)(2,1)} %collective-permute-done.15.up_got_ref, bf16[2048,128]{1,0:T(8,128)(2,1)} %get-tuple-element.44.down_ref, ...), custom_call_target="tpu_custom_call" | custom-call | tf_op jit(solution)/shard_map/final/pallas_call | solution.py:416
  (21 shorter events, 0.3 us)
Async XLA Ops:
  1.3 32.3 %copy-start.9 = (s32[4]{0:T(128)S(1)}, s32[4]{0:T(128)}, u32[]{:S(2)}) copy-start(s32[4]{0:T(128)} %mask_ref.1) | copy-start | bytes 52
  6.1 30.7 %collective-permute-start = (bf16[2064,128]{1,0:T(8,128)(2,1)}, bf16[2064,128]{1,0:T(8,128)(2,1)S(1)}, u32[]{:S(2)}, u32[]{:S(2)}) collective-permute-start(bf16[2064,128]{1,0:T(8,128)(2,1)} %get-tuple-element.29.refs_1_), channel_id=1, source_target_pairs={{0,128},{128,0},{256,384},{384,256},{1,129},{129,1},{257,385},{385... | collective-permute-start | bytes 1585160 | tf_op jit(solution)/shard_map/ppermute | solution.py:280
  10.0 32.4 %collective-permute-start.2 = (bf16[4096,128]{1,0:T(8,128)(2,1)}, bf16[4096,128]{1,0:T(8,128)(2,1)S(1)}, u32[]{:S(2)}, u32[]{:S(2)}) collective-permute-start(bf16[4096,128]{1,0:T(8,128)(2,1)} %get-tuple-element.30.refs_1_), channel_id=1, source_target_pairs={{0,128},{128,0},{256,384},{384,256},{1,129},{129,1},{257,385},{385... | collective-permute-start | bytes 3145736 | tf_op jit(solution)/shard_map/ppermute | solution.py:280
  12.0 43.8 %collective-permute-start.4 = (bf16[48,2176]{1,0:T(8,128)(2,1)}, bf16[48,2176]{1,0:T(8,128)(2,1)}, u32[]{:S(2)}, u32[]{:S(2)}) collective-permute-start(bf16[48,2176]{1,0:T(8,128)(2,1)} %get-tuple-element.32), channel_id=1, source_target_pairs={{0,8},{8,0},{16,24},{24,16},{1,9},{9,1},{17,25},{25,17},{2,10},{10... | collective-permute-start | bytes 626696 | tf_op jit(solution)/shard_map/ppermute | solution.py:280
  21.0 34.8 %collective-permute-start.5 = (bf16[48,2176]{1,0:T(8,128)(2,1)}, bf16[48,2176]{1,0:T(8,128)(2,1)}, u32[]{:S(2)}, u32[]{:S(2)}) collective-permute-start(bf16[48,2176]{1,0:T(8,128)(2,1)} %get-tuple-element.33), channel_id=1, source_target_pairs={{0,16},{8,24},{16,0},{24,8},{1,17},{9,25},{17,1},{25,9},{2,18},{10... | collective-permute-start | bytes 626696 | tf_op jit(solution)/shard_map/ppermute | solution.py:280
  31.7 36.8 %collective-permute-start.6 = (bf16[48,2176]{1,0:T(8,128)(2,1)}, bf16[48,2176]{1,0:T(8,128)(2,1)}, u32[]{:S(2)}, u32[]{:S(2)}) collective-permute-start(bf16[48,2176]{1,0:T(8,128)(2,1)} %get-tuple-element.34), channel_id=1, source_target_pairs={{0,24},{8,16},{16,8},{24,0},{1,25},{9,17},{17,9},{25,1},{2,26},{10... | collective-permute-start | bytes 626696 | tf_op jit(solution)/shard_map/ppermute | solution.py:280
  36.8 1.0 copy-start.7
  37.9 4.6 %copy-start.6 = (bf16[4096,128]{1,0:T(8,128)(2,1)S(1)}, bf16[4096,128]{1,0:T(8,128)(2,1)}, u32[]{:S(2)}) copy-start(bf16[4096,128]{1,0:T(8,128)(2,1)} %get-tuple-element.30.refs_1_) | copy-start | bytes 3145732
  37.9 14.6 %collective-permute-start.1 = (bf16[2064,128]{1,0:T(8,128)(2,1)S(1)}, bf16[2064,128]{1,0:T(8,128)(2,1)S(1)}, u32[]{:S(2)}, u32[]{:S(2)}) collective-permute-start(bf16[2064,128]{1,0:T(8,128)(2,1)S(1)} %pick.6.refs_2_.refs_1_), channel_id=1, source_target_pairs={{0,384},{128,256},{256,128},{384,0},{1,385},{129,257},{257,129},{3... | collective-permute-start | bytes 1585160 | tf_op jit(solution)/shard_map/ppermute | solution.py:280
  43.5 38.8 %collective-permute-start.8 = (bf16[4096,128]{1,0:T(8,128)(2,1)}, bf16[4096,128]{1,0:T(8,128)(2,1)}, u32[]{:S(2)}, u32[]{:S(2)}) collective-permute-start(bf16[4096,128]{1,0:T(8,128)(2,1)} %pick.7.refs_2_.own_ref), channel_id=1, source_target_pairs={{0,384},{128,256},{256,128},{384,0},{1,385},{129,257},{257,129},{3... | collective-permute-start | bytes 3145736 | tf_op jit(solution)/shard_map/ppermute | solution.py:280
  52.5 16.0 %copy-start.8 = (bf16[48,2176]{1,0:T(8,128)(2,1)S(1)}, bf16[48,2176]{1,0:T(8,128)(2,1)}, u32[]{:S(2)}) copy-start(bf16[48,2176]{1,0:T(8,128)(2,1)} %get-tuple-element.31.refs_0_) | copy-start | bytes 626692
  52.5 27.8 %collective-permute-start.3 = (bf16[2064,128]{1,0:T(8,128)(2,1)S(1)}, bf16[2064,128]{1,0:T(8,128)(2,1)S(1)}, u32[]{:S(2)}, u32[]{:S(2)}) collective-permute-start(bf16[2064,128]{1,0:T(8,128)(2,1)S(1)} %pick.8.refs_4_.refs_1_), channel_id=1, source_target_pairs={{0,32},{32,0},{64,96},{96,64},{1,33},{33,1},{65,97},{97,65},{2,34}... | collective-permute-start | bytes 1585160 | tf_op jit(solution)/shard_map/ppermute | solution.py:280
  70.6 41.6 %collective-permute-start.10 = (bf16[192,2176]{1,0:T(8,128)(2,1)}, bf16[192,2176]{1,0:T(8,128)(2,1)}, u32[]{:S(2)}, u32[]{:S(2)}) collective-permute-start(bf16[192,2176]{1,0:T(8,128)(2,1)} %join.1.refs_2_.refs_0_), channel_id=1, source_target_pairs={{0,2},{2,0},{4,6},{6,4},{1,3},{3,1},{5,7},{7,5},{8,10},{10,8},{12,... | collective-permute-start | bytes 2506760 | tf_op jit(solution)/shard_map/ppermute | solution.py:280
  73.8 40.6 %collective-permute-start.11 = (bf16[192,2176]{1,0:T(8,128)(2,1)}, bf16[192,2176]{1,0:T(8,128)(2,1)}, u32[]{:S(2)}, u32[]{:S(2)}) collective-permute-start(bf16[192,2176]{1,0:T(8,128)(2,1)} %join.1.refs_2_.refs_0_), channel_id=1, source_target_pairs={{0,4},{2,6},{4,0},{6,2},{1,5},{3,7},{5,1},{7,3},{8,12},{10,14},{12... | collective-permute-start | bytes 2506760 | tf_op jit(solution)/shard_map/ppermute | solution.py:280
  78.4 40.1 %collective-permute-start.12 = (bf16[192,2176]{1,0:T(8,128)(2,1)}, bf16[192,2176]{1,0:T(8,128)(2,1)}, u32[]{:S(2)}, u32[]{:S(2)}) collective-permute-start(bf16[192,2176]{1,0:T(8,128)(2,1)} %join.1.refs_2_.refs_0_), channel_id=1, source_target_pairs={{0,6},{2,4},{4,2},{6,0},{1,7},{3,5},{5,3},{7,1},{8,14},{10,12},{12... | collective-permute-start | bytes 2506760 | tf_op jit(solution)/shard_map/ppermute | solution.py:280
  80.3 27.6 %collective-permute-start.7 = (bf16[2064,128]{1,0:T(8,128)(2,1)S(1)}, bf16[2064,128]{1,0:T(8,128)(2,1)S(1)}, u32[]{:S(2)}, u32[]{:S(2)}) collective-permute-start(bf16[2064,128]{1,0:T(8,128)(2,1)S(1)} %pick.9.earlier_ref.refs_1_), channel_id=1, source_target_pairs={{0,64},{32,96},{64,0},{96,32},{1,65},{33,97},{65,1},{97,33},{2,66}... | collective-permute-start | bytes 1585160 | tf_op jit(solution)/shard_map/ppermute | solution.py:280
  107.9 10.5 %copy-start.2 = (f32[8,256]{1,0:T(8,128)S(1)}, f32[8,256]{1,0:T(8,128)}, u32[]{:S(2)}) copy-start(f32[8,256]{1,0:T(8,128)} %get-tuple-element.28.base_ref) | copy-start | bytes 24580
  107.9 10.5 %copy-start.3 = (s32[5]{0:T(128)S(1)}, s32[5]{0:T(128)}, u32[]{:S(2)}) copy-start(s32[5]{0:T(128)} %stack.23.info_ref) | copy-start | bytes 64
  108.0 10.5 %collective-permute-start.9 = (bf16[2064,128]{1,0:T(8,128)(2,1)S(1)}, bf16[2064,128]{1,0:T(8,128)(2,1)S(1)}, u32[]{:S(2)}, u32[]{:S(2)}) collective-permute-start(bf16[2064,128]{1,0:T(8,128)(2,1)S(1)} %pick.10.own_w_ref), channel_id=1, source_target_pairs={{0,1},{1,0},{2,3},{3,2},{4,5},{5,4},{6,7},{7,6},{8,9},{9,8},{10,11... | collective-permute-start | bytes 1585160 | tf_op jit(solution)/shard_map/ppermute | solution.py:280
  110.3 44.1 %collective-permute-start.13 = (bf16[2048,128]{1,0:T(8,128)(2,1)}, bf16[2048,128]{1,0:T(8,128)(2,1)}, u32[]{:S(2)}, u32[]{:S(2)}) collective-permute-start(bf16[2048,128]{1,0:T(8,128)(2,1)} %get-tuple-element.39.refs_2_), channel_id=1, source_target_pairs={{0,32},{32,0},{64,96},{96,64},{1,33},{33,1},{65,97},{97,65},{2,34}... | collective-permute-start | bytes 1572872 | tf_op jit(solution)/shard_map/ppermute | solution.py:280
  112.2 42.2 %collective-permute-start.14 = (bf16[2048,128]{1,0:T(8,128)(2,1)}, bf16[2048,128]{1,0:T(8,128)(2,1)}, u32[]{:S(2)}, u32[]{:S(2)}) collective-permute-start(bf16[2048,128]{1,0:T(8,128)(2,1)} %get-tuple-element.40.refs_3_), channel_id=1, source_target_pairs={{0,64},{32,96},{64,0},{96,32},{1,65},{33,97},{65,1},{97,33},{2,66}... | collective-permute-start | bytes 1572872 | tf_op jit(solution)/shard_map/ppermute | solution.py:280
  121.8 1.0 copy-start.4
  133.8 20.5 %all-to-all-start.1 = ((f32[16,1,256]{2,1,0:T(1,128)}), f32[16,1,256]{2,1,0:T(1,128)S(1)}, u32[]{:S(2)}, u32[]{:S(2)}) async-start(f32[16,1,256]{2,1,0:T(1,128)} %broadcast_in_dim.23), calls=%async_computation.1 | async-start | bytes 32768 | tf_op jit(solution)/shard_map/all_to_all | solution.py:389
  157.7 15.9 %all-to-all-start.2 = ((f32[32,1,256]{2,1,0:T(1,128)}), f32[32,1,256]{2,1,0:T(1,128)S(1)}, u32[]{:S(2)}, u32[]{:S(2)}) async-start(f32[32,1,256]{2,1,0:T(1,128)} %copy.20), calls=%async_computation.2 | async-start | bytes 65536 | tf_op jit(solution)/shard_map/all_to_all | solution.py:395
  166.3 28.1 %collective-permute-start.15 = (bf16[2048,128]{1,0:T(8,128)(2,1)}, bf16[2048,128]{1,0:T(8,128)(2,1)}, u32[]{:S(2)}, u32[]{:S(2)}) collective-permute-start(bf16[2048,128]{1,0:T(8,128)(2,1)} %get-tuple-element.43.up_ref), channel_id=1, source_target_pairs={{0,64},{32,96},{64,0},{96,32},{1,65},{33,97},{65,1},{97,33},{2,66}... | collective-permute-start | bytes 1572872 | tf_op jit(solution)/shard_map/ppermute | solution.py:280
  168.8 26.1 %collective-permute-start.16 = (bf16[2048,128]{1,0:T(8,128)(2,1)}, bf16[2048,128]{1,0:T(8,128)(2,1)}, u32[]{:S(2)}, u32[]{:S(2)}) collective-permute-start(bf16[2048,128]{1,0:T(8,128)(2,1)} %get-tuple-element.44.down_ref), channel_id=1, source_target_pairs={{0,32},{32,0},{64,96},{96,64},{1,33},{33,1},{65,97},{97,65},{2,34}... | collective-permute-start | bytes 1572872 | tf_op jit(solution)/shard_map/ppermute | solution.py:280
  173.6 1.3 copy-start.5
  174.9 6.6 %copy-start = (s32[8192]{0:T(1024)S(1)}, s32[8192]{0:T(1024)}, u32[]{:S(2)}) copy-start(s32[8192]{0:T(1024)} %param.16) | copy-start | bytes 98308
  179.2 15.7 %copy-start.1 = (bf16[2048]{0:T(1024)(128)(2,1)S(1)}, bf16[2048]{0:T(1024)(128)(2,1)}, u32[]{:S(2)}) copy-start(bf16[2048]{0:T(1024)(128)(2,1)} %param.17) | copy-start | bytes 12292
  179.2 15.7 %collective-permute-start.17 = (f32[2056,128]{1,0:T(8,128)S(1)}, f32[2056,128]{1,0:T(8,128)S(1)}, u32[]{:S(2)}, u32[]{:S(2)}) collective-permute-start(f32[2056,128]{1,0:T(8,128)S(1)} %get-tuple-element.49), channel_id=1, source_target_pairs={{0,1},{1,0},{2,3},{3,2},{4,5},{5,4},{6,7},{7,6},{8,9},{9,8},{10,11... | collective-permute-start | bytes 3158024 | tf_op jit(solution)/shard_map/ppermute | solution.py:280

commit v5 on v4

--- a/solution.py
+++ b/solution.py
@@ -24,7 +24,9 @@
 PARAMS = pltpu.CompilerParams(vmem_limit_bytes=24 * 1024 * 1024)
 NT = (((1,), (1,)), ((), ()))
 
-BLOCKS = [(EXP_GRP * CAP * d + CAP * k, k, d) for d in range(4) for k in range(EXP_GRP)]
+BLOCKS = [(CAP * d, 0, d) for d in range(4)] + [
+    (4 * CAP + 3 * CAP * d + CAP * (k - 1), k, d) for d in range(4) for k in range(1, EXP_GRP)
+]
 SPACED = pl.CostEstimate(flops=10**11, bytes_accessed=0, transcendentals=0)
 ANY = pl.BlockSpec(memory_space=pl.ANY)
 
@@ -59,7 +61,7 @@
     acc_down_ref,
     *outs,
 ):
-    out_refs, (base_ref, weights_ref, acc_ref) = outs[:4], outs[4:]
+    out_ref, own_ref, base_ref, weights_ref, acc_ref = outs
     acc_ref[:D, :] = acc_up_ref[...]
     for j in range(D // HID_DEV):
         at = j * HID_DEV
@@ -78,7 +80,7 @@
     gates = gates_ref[...]
     sel, gate = [], []
     for k in range(EXP_GRP):
-        slot = zh ^ k
+        slot = k
         mask = mask_ref[slot]
         expert = jnp.int32(0)
         for j in range(16):
@@ -124,13 +126,13 @@
         pick, by_slot, NT, preferred_element_type=f32
     )
     wide = jnp.dot(pick, tok_ref[...], preferred_element_type=f32)
-    for k in range(EXP_GRP):
-        out_refs[k][:, :D] = wide[CAP * k : CAP * (k + 1)].astype(bf16)
-        out_refs[k][:, D:] = notes[CAP * k : CAP * (k + 1)].astype(bf16)
+    out_ref[:, :D] = wide.astype(bf16)
+    out_ref[:, D:] = notes.astype(bf16)
+    own_ref[...] = out_ref[pl.ds(pl.multiple_of(zh * CAP, CAP), CAP), :]
 
 
 def forward_kernel(info_ref, base_ref, own_w_ref, other_w_ref, *refs):
-    groups, (x_ref, keep_ref, part_ref, u_ref) = refs[:4], refs[-4:]
+    groups, (x_ref, keep_ref, part_ref, u_ref) = refs[:8], refs[8:]
     grp, zh, y = info_ref[0], info_ref[1], info_ref[3]
     u_ref[:, :HID_DEV] = own_w_ref[:D, :]
     u_ref[:, HID_DEV:] = other_w_ref[:D, :]
@@ -154,7 +156,7 @@
     total = jnp.where((row == zh * 4 + y) & (grp == 0), base_ref[0:1, :], 0.0)
     for at, k, d in BLOCKS:
         note = keep_ref[at : at + CAP, 2 * HID_DEV :]
-        gate = jnp.sum(jnp.where((lane >= 1 + 3 * k) & (lane < 4 + 3 * k), note, 0.0), axis=1, keepdims=True)
+        gate = jnp.sum(jnp.where((lane >= 1 + 3 * zh) & (lane < 4 + 3 * zh), note, 0.0), axis=1, keepdims=True)
         term = gate * value[at : at + CAP]
         spread = jnp.sum(jnp.where(note[:, 0:1] == token, term, 0.0), axis=0, keepdims=True)
         total = total + jnp.where(row == (zh ^ k) * 4 + (y ^ d), spread, 0.0)
@@ -174,7 +176,7 @@
         part = keep_ref[at : at + CAP, 2 * HID_DEV :]
         mine.append(jnp.sum(jnp.where(part[:, 0:1] == token, values, 0.0), axis=1, keepdims=True))
         gates.append(
-            jnp.sum(jnp.where((lane >= 1 + 3 * k) & (lane < 4 + 3 * k), part, 0.0), axis=1, keepdims=True)
+            jnp.sum(jnp.where((lane >= 1 + 3 * zh) & (lane < 4 + 3 * zh), part, 0.0), axis=1, keepdims=True)
         )
     mine = jnp.concatenate(mine, axis=0)
     gate = jnp.concatenate(gates, axis=0)
@@ -270,9 +272,11 @@
             down_ref[...] = ref[D:, :]
 
 
-def join_kernel(*refs):
-    for k in range(EXP_GRP):
-        refs[-1][CAP * k : CAP * (k + 1), :] = refs[k][...]
+def others_kernel(info_ref, rows_ref, *refs):
+    zh = info_ref[1]
+    for k in range(1, EXP_GRP):
+        block = rows_ref[pl.ds(pl.multiple_of((zh ^ k) * CAP, CAP), CAP), :]
+        refs[-1][CAP * (k - 1) : CAP * k, :] = block
 
 
 def swap(block, axis, mask):
@@ -297,16 +301,16 @@
     return picks([stage], [got], [own], *earlier)[0]
 
 
-def join(blocks, *earlier):
+def others(info, rows, *earlier):
     return pl.pallas_call(
-        join_kernel,
-        out_shape=shape((EXP_GRP * CAP, WIDE), bf16),
-        in_specs=[VMEM] * EXP_GRP + [ANY] * len(earlier),
+        others_kernel,
+        out_shape=shape((3 * CAP, WIDE), bf16),
+        in_specs=[SMEM, VMEM] + [ANY] * len(earlier),
         out_specs=VMEM,
         compiler_params=PARAMS,
         cost_estimate=SPACED,
-        name="join",
-    )(*blocks, *earlier)
+        name="others",
+    )(info, rows, *earlier)
 
 
 def body(tokens, routes, gate_values, old_group, move_mask, pair_index, reward_head, w_up, w_down, acc_up, acc_down):
@@ -321,11 +325,17 @@
     z1 = ("zl", 1, bit[0].reshape(1))
     z2 = ("zl", 2, bit[1].reshape(1))
 
-    *sent, base, weights, accums = pl.pallas_call(
+    sent, own_rows, base, weights, accums = pl.pallas_call(
         dispatch_kernel,
-        out_shape=[shape((CAP, WIDE), bf16)] * 4 + [shape((8, TOK_DEV), f32), shape((D + 16, HID_DEV), bf16), shape((2 * D, HID_DEV), bf16)],
+        out_shape=[
+            shape((EXP_GRP * CAP, WIDE), bf16),
+            shape((CAP, WIDE), bf16),
+            shape((8, TOK_DEV), f32),
+            shape((D + 16, HID_DEV), bf16),
+            shape((2 * D, HID_DEV), bf16),
+        ],
         in_specs=[SMEM] * 3 + [VMEM] * 9,
-        out_specs=[VMEM] * 7,
+        out_specs=[VMEM] * 5,
         compiler_params=pltpu.CompilerParams(vmem_limit_bytes=63 * 1024 * 1024),
         name="dispatch",
     )(
@@ -342,7 +352,8 @@
         acc_up[0],
         acc_down[0],
     )
-    blocks = [sent[0], swap(sent[1], "zh", 1), swap(sent[2], "zh", 2), swap(sent[3], "zh", 3)]
+    arrived = lax.all_to_all(sent, "zh", 0, 0, tiled=True)
+    held = [own_rows] + [swap(own_rows, "y", d) for d in (1, 2, 3)]
     got = swap(weights, *x1[:2])
     acc_got = swap(accums, *x1[:2])
     weights = pick(x1, got, weights)
@@ -351,8 +362,8 @@
     acc_got = swap(accums, *x3[:2])
     weights = pick(x3, got, weights, accums)
     got = swap(weights, *z1[:2])
-    rows = join(blocks, weights)
-    held = [rows] + [swap(rows, "y", d) for d in (1, 2, 3)]
+    rows = others(info, arrived, weights, *held[1:])
+    held += [rows] + [swap(rows, "y", d) for d in (1, 2, 3)]
     weights = pick(z1, got, weights, rows)
     got = swap(weights, *z2[:2])
     up, down = pl.pallas_call(
@@ -377,7 +388,7 @@
             shape((ROWS + 8, 2 * HID_DEV + 128), f32),
             shape((16, TOK_DEV), f32),
         ],
-        in_specs=[SMEM] + [VMEM] * 7,
+        in_specs=[SMEM] + [VMEM] * 11,
         out_specs=[VMEM] * 3,
         scratch_shapes=[pltpu.VMEM((D, 2 * HID_DEV), bf16)],
         compiler_params=PARAMS,

time: 199 us -> 206 us (1.035)
  waiting for transfers between devices: 66.2 us -> 71.2 us
  blocking collectives: 10.4 us -> 12.7 us
    all_to_all x0 -> x1, waiting for transfers between devices: none -> 20.7 us  [body(): arrived = lax.all_to_all(sent, 'zh', 0, 0, tiled=True)]
    ppermute x18, waiting for transfers between devices: 52.4 us -> 36.7 us  [swap(): return lax.ppermute(block, axis, [(i, i ^ mask) for i in range(count)])]
    all_to_all x0 -> x1, starting transfers between devices: none -> 14.8 us  [body(): arrived = lax.all_to_all(sent, 'zh', 0, 0, tiled=True)]
    ppermute x18, starting transfers between devices: 66.6 us -> 55.3 us  [swap(): return lax.ppermute(block, axis, [(i, i ^ mask) for i in range(count)])]
    all_to_all x1, blocking collectives: 10.4 us -> 12.7 us  [body(): mine = lax.all_to_all(part, ('x', 'y'), 0, 0, tiled=True)]
  transfers between devices with their start and end apart: 20 -> 21, of which waited for: 8 -> 7; matrix products, arithmetic and copies ran while one was open for 1% -> 1% of each run, Pallas kernels for 9% -> 8%
where the time goes in v5:
time: 206 us; the launch traced here: 204 us
  starting transfers between devices  84.4 us (41%)
  waiting for transfers between devices  71.2 us (35%)
  Pallas kernels  27.4 us (13%)
  blocking collectives  12.7 us (6%)
  local copies, waits for them, and re-layouts  4.23 us (2%)
  between operations  3.63 us (2%)
    ppermute x18, starting transfers between devices, swap(): return lax.ppermute(block, axis, [(i, i ^ mask) for i in range(count)])  55.3 us
    ppermute x18, waiting for transfers between devices, swap(): return lax.ppermute(block, axis, [(i, i ^ mask) for i in range(count)])  36.7 us
    all_to_all x1, waiting for transfers between devices, body(): arrived = lax.all_to_all(sent, 'zh', 0, 0, tiled=True)  20.7 us
    all_to_all x1, starting transfers between devices, body(): arrived = lax.all_to_all(sent, 'zh', 0, 0, tiled=True)  14.8 us
    all_to_all x1, blocking collectives, body(): mine = lax.all_to_all(part, ('x', 'y'), 0, 0, tiled=True)  12.7 us
    all_to_all x1, waiting for transfers between devices, body(): mine = lax.all_to_all(mine, ('zl', 'zh'), 0, 0, tiled=True)  11.2 us
    all_to_all x1, starting transfers between devices, body(): mine = lax.all_to_all(mine, ('zl', 'zh'), 0, 0, tiled=True)  7.33 us
    all_to_all x1, starting transfers between devices, body(): table = lax.all_to_all(mine, ('x', 'y', 'c'), 0, 0, tiled=True)  6.94 us
  transfers between devices with their start and end apart: 21, of which 7 were waited for; matrix products, arithmetic and copies ran while one was open for 1% of the time, Pallas kernels for 8%

profile of v5, /device:TPU:1, one launch (start us, length us, event | category | flops | bytes accessed | tf_op | source)
XLA Modules:
  0.0 204.4 jit_solution(3997142977084858954)
XLA Ops:
  0.6 0.6 stack.23.info_ref
  1.3 5.0 %dispatch.1 = (bf16[192,2176]{1,0:T(8,128)(2,1)}, bf16[48,2176]{1,0:T(8,128)(2,1)}, f32[8,256]{1,0:T(8,128)}, bf16[2064,128]{1,0:T(8,128)(2,1)}, bf16[4096,128]{1,0:T(8,128)(2,1)}) custom-call(s32[64]{0:T(128)} %group_ref.1, s32[4]{0:T(128)} %mask_ref.1, s32[5]{0:T(128)} %stack.23.info_ref, bf16[256,2048]{1,0:T(8,128)(2,1)} %tok_ref.1, s32[8,256]{1,0:T(8,128)} %bitcast.41, ...), custom_call_target="tpu_custom_call" | custom-call | tf_op jit(solution)/shard_map/dispatch/pallas_call | solution.py:328
  6.3 4.1 %collective-permute-start = (bf16[2064,128]{1,0:T(8,128)(2,1)}, bf16[2064,128]{1,0:T(8,128)(2,1)S(1)}, u32[]{:S(2)}, u32[]{:S(2)}) collective-permute-start(bf16[2064,128]{1,0:T(8,128)(2,1)} %get-tuple-element.27.refs_1_), channel_id=1, source_target_pairs={{0,128},{128,0},{256,384},{384,256},{1,129},{129,1},{257,385},{385... | collective-permute-start | bytes 1585160 | tf_op jit(solution)/shard_map/ppermute | solution.py:284
  10.4 3.2 %collective-permute-start.4 = (bf16[48,2176]{1,0:T(8,128)(2,1)}, bf16[48,2176]{1,0:T(8,128)(2,1)}, u32[]{:S(2)}, u32[]{:S(2)}) collective-permute-start(bf16[48,2176]{1,0:T(8,128)(2,1)} %get-tuple-element.30.refs_0_), channel_id=1, source_target_pairs={{0,2},{2,0},{4,6},{6,4},{1,3},{3,1},{5,7},{7,5},{8,10},{10,8},{12,... | collective-permute-start | bytes 626696 | tf_op jit(solution)/shard_map/ppermute | solution.py:284
  13.6 4.5 %collective-permute-start.5 = (bf16[48,2176]{1,0:T(8,128)(2,1)}, bf16[48,2176]{1,0:T(8,128)(2,1)}, u32[]{:S(2)}, u32[]{:S(2)}) collective-permute-start(bf16[48,2176]{1,0:T(8,128)(2,1)} %get-tuple-element.30.refs_0_), channel_id=1, source_target_pairs={{0,4},{2,6},{4,0},{6,2},{1,5},{3,7},{5,1},{7,3},{8,12},{10,14},{12... | collective-permute-start | bytes 626696 | tf_op jit(solution)/shard_map/ppermute | solution.py:284
  18.1 1.9 collective-permute-start.6
  20.1 2.2 %collective-permute-start.2 = (bf16[4096,128]{1,0:T(8,128)(2,1)}, bf16[4096,128]{1,0:T(8,128)(2,1)S(1)}, u32[]{:S(2)}, u32[]{:S(2)}) collective-permute-start(bf16[4096,128]{1,0:T(8,128)(2,1)} %get-tuple-element.28.refs_1_), channel_id=1, source_target_pairs={{0,128},{128,0},{256,384},{384,256},{1,129},{129,1},{257,385},{385... | collective-permute-start | bytes 3145736 | tf_op jit(solution)/shard_map/ppermute | solution.py:284
  22.2 14.8 %all-to-all-start = ((bf16[4,48,2176]{2,1,0:T(8,128)(2,1)}), bf16[4,48,2176]{2,1,0:T(8,128)(2,1)}, u32[]{:S(2)}, u32[]{:S(2)}) async-start(bf16[4,48,2176]{2,1,0:T(8,128)(2,1)} %bitcast.36), calls=%async_computation | async-start | bytes 1671168 | tf_op jit(solution)/shard_map/all_to_all | solution.py:355
  37.1 0.6 fusion
  40.3 0.0 collective-permute-done.refs_0_
  40.4 4.5 %collective-permute-start.1 = (bf16[2064,128]{1,0:T(8,128)(2,1)S(1)}, bf16[2064,128]{1,0:T(8,128)(2,1)S(1)}, u32[]{:S(2)}, u32[]{:S(2)}) collective-permute-start(bf16[2064,128]{1,0:T(8,128)(2,1)S(1)} %pick.6.refs_2_.refs_1_), channel_id=1, source_target_pairs={{0,384},{128,256},{256,128},{384,0},{1,385},{129,257},{257,129},{3... | collective-permute-start | bytes 1585160 | tf_op jit(solution)/shard_map/ppermute | solution.py:284
  44.9 0.0 collective-permute-done.2.refs_0_
  44.9 0.0 copy-done.7
  44.9 1.1 pick.7.refs_2_.own_ref
  46.0 3.9 %collective-permute-start.8 = (bf16[4096,128]{1,0:T(8,128)(2,1)}, bf16[4096,128]{1,0:T(8,128)(2,1)}, u32[]{:S(2)}, u32[]{:S(2)}) collective-permute-start(bf16[4096,128]{1,0:T(8,128)(2,1)} %pick.7.refs_2_.own_ref), channel_id=1, source_target_pairs={{0,384},{128,256},{256,128},{384,0},{1,385},{129,257},{257,129},{3... | collective-permute-start | bytes 3145736 | tf_op jit(solution)/shard_map/ppermute | solution.py:284
  49.9 5.1 %collective-permute-done.1.refs_0_ = bf16[2064,128]{1,0:T(8,128)(2,1)S(1)} collective-permute-done((bf16[2064,128]{1,0:T(8,128)(2,1)S(1)}, bf16[2064,128]{1,0:T(8,128)(2,1)S(1)}, u32[]{:S(2)}, u32[]{:S(2)}) %collective-permute-start.1) | collective-permute-done | bytes 528416 | tf_op jit(solution)/shard_map/ppermute | solution.py:284
  55.0 2.6 %collective-permute-start.3 = (bf16[2064,128]{1,0:T(8,128)(2,1)S(1)}, bf16[2064,128]{1,0:T(8,128)(2,1)S(1)}, u32[]{:S(2)}, u32[]{:S(2)}) collective-permute-start(bf16[2064,128]{1,0:T(8,128)(2,1)S(1)} %pick.8.refs_0_.refs_1_), channel_id=1, source_target_pairs={{0,32},{32,0},{64,96},{96,64},{1,33},{33,1},{65,97},{97,65},{2,34}... | collective-permute-start | bytes 1585160 | tf_op jit(solution)/shard_map/ppermute | solution.py:284
  57.6 0.0 collective-permute-done.4.refs_1_
  57.6 0.0 collective-permute-done.5.refs_2_
  57.6 0.0 collective-permute-done.6.refs_3_
  57.7 20.7 %all-to-all-done = bf16[4,48,2176]{2,1,0:T(8,128)(2,1)} async-done(((bf16[4,48,2176]{2,1,0:T(8,128)(2,1)}), bf16[4,48,2176]{2,1,0:T(8,128)(2,1)}, u32[]{:S(2)}, u32[]{:S(2)}) %all-to-all-start) | async-done | bytes 835616 | tf_op jit(solution)/shard_map/all_to_all | solution.py:355
  78.3 0.0 copy-done.4
  78.3 2.1 %others.1.refs_2_.refs_4_ = bf16[144,2176]{1,0:T(8,128)(2,1)} custom-call(s32[5]{0:T(128)S(1)} %copy-done.4, bf16[192,2176]{1,0:T(8,128)(2,1)} %bitcast.18.rows_ref, bf16[2064,128]{1,0:T(8,128)(2,1)S(1)} %pick.8.refs_0_.refs_1_, bf16[48,2176]{1,0:T(8,128)(2,1)} %collective-permute-done.4.refs_1_, bf16[48,2176]{1,0:T(8,128)(2,1)} %collective-permute-done.5.refs_2_, ...), custom_call_target="tpu_custom_call" | custom-call | flops 99999997952 | tf_op jit(solution)/shard_map/others/pallas_call | solution.py:305
  80.4 1.9 collective-permute-start.10
  82.3 5.6 %collective-permute-start.11 = (bf16[144,2176]{1,0:T(8,128)(2,1)}, bf16[144,2176]{1,0:T(8,128)(2,1)}, u32[]{:S(2)}, u32[]{:S(2)}) collective-permute-start(bf16[144,2176]{1,0:T(8,128)(2,1)} %others.1.refs_2_.refs_4_), channel_id=1, source_target_pairs={{0,4},{2,6},{4,0},{6,2},{1,5},{3,7},{5,1},{7,3},{8,12},{10,14},{12... | collective-permute-start | bytes 1880072 | tf_op jit(solution)/shard_map/ppermute | solution.py:284
  88.0 2.0 collective-permute-start.12
  90.0 0.0 collective-permute-done.3.refs_0_
  90.1 2.3 %collective-permute-start.7 = (bf16[2064,128]{1,0:T(8,128)(2,1)S(1)}, bf16[2064,128]{1,0:T(8,128)(2,1)S(1)}, u32[]{:S(2)}, u32[]{:S(2)}) collective-permute-start(bf16[2064,128]{1,0:T(8,128)(2,1)S(1)} %pick.9.earlier_ref.refs_1_), channel_id=1, source_target_pairs={{0,64},{32,96},{64,0},{96,32},{1,65},{33,97},{65,1},{97,33},{2,66}... | collective-permute-start | bytes 1585160 | tf_op jit(solution)/shard_map/ppermute | solution.py:284
  92.4 0.0 collective-permute-done.8.got_ref
  92.4 2.6 %pick_split.1 = (bf16[2048,128]{1,0:T(8,128)(2,1)}, bf16[2048,128]{1,0:T(8,128)(2,1)}) custom-call(s32[1]{0:T(128)} %bitcast.15.take_ref, bf16[4096,128]{1,0:T(8,128)(2,1)} %collective-permute-done.8.got_ref, bf16[4096,128]{1,0:T(8,128)(2,1)} %pick.7.refs_2_.own_ref, bf16[2064,128]{1,0:T(8,128)(2,1)S(1)} %pick.9.earlier_ref.refs_1_), custom_call_target="tpu_custom_call" | custom-call | flops 99999997952 | tf_op jit(solution)/shard_map/pick_split/pallas_call | solution.py:369
  95.0 21.6 %collective-permute-done.7.refs_0_ = bf16[2064,128]{1,0:T(8,128)(2,1)S(1)} collective-permute-done((bf16[2064,128]{1,0:T(8,128)(2,1)S(1)}, bf16[2064,128]{1,0:T(8,128)(2,1)S(1)}, u32[]{:S(2)}, u32[]{:S(2)}) %collective-permute-start.7) | collective-permute-done | bytes 528416 | tf_op jit(solution)/shard_map/ppermute | solution.py:284
  116.6 3.8 %collective-permute-start.9 = (bf16[2064,128]{1,0:T(8,128)(2,1)S(1)}, bf16[2064,128]{1,0:T(8,128)(2,1)S(1)}, u32[]{:S(2)}, u32[]{:S(2)}) collective-permute-start(bf16[2064,128]{1,0:T(8,128)(2,1)S(1)} %pick.10.own_w_ref), channel_id=1, source_target_pairs={{0,1},{1,0},{2,3},{3,2},{4,5},{5,4},{6,7},{7,6},{8,9},{9,8},{10,11... | collective-permute-start | bytes 1585160 | tf_op jit(solution)/shard_map/ppermute | solution.py:284
  120.4 1.9 collective-permute-start.13
  122.3 0.0 collective-permute-done.10.refs_5_
  122.3 3.8 %collective-permute-start.14 = (bf16[2048,128]{1,0:T(8,128)(2,1)}, bf16[2048,128]{1,0:T(8,128)(2,1)}, u32[]{:S(2)}, u32[]{:S(2)}) collective-permute-start(bf16[2048,128]{1,0:T(8,128)(2,1)} %get-tuple-element.36.refs_3_), channel_id=1, source_target_pairs={{0,64},{32,96},{64,0},{96,32},{1,65},{33,97},{65,1},{97,33},{2,66}... | collective-permute-start | bytes 1572872 | tf_op jit(solution)/shard_map/ppermute | solution.py:284
  126.1 0.0 collective-permute-done.11.refs_6_
  126.1 0.0 collective-permute-done.12.refs_7_
  126.1 0.0 collective-permute-done.9.other_w_ref
  126.2 0.0 copy-done
  126.2 3.3 %forward.1 = (bf16[768,2048]{1,0:T(8,128)(2,1)S(1)}, f32[776,384]{1,0:T(8,128)S(1)}, f32[16,256]{1,0:T(8,128)S(1)}) custom-call(s32[5]{0:T(128)S(1)} %copy-done.4, f32[8,256]{1,0:T(8,128)S(1)} %copy-done.3, bf16[2064,128]{1,0:T(8,128)(2,1)S(1)} %pick.10.own_w_ref, bf16[2064,128]{1,0:T(8,128)(2,1)S(1)} %collective-permute-done.9.other_w_ref, ...), custom_call_target="tpu_custom_call" | custom-call | tf_op jit(solution)/shard_map/forward/pallas_call | solution.py:384
  129.5 1.0 copy-done.5
  130.5 12.7 %all_to_all.37 = f32[16,1,256]{2,1,0:T(1,128)S(1)} all-to-all(f32[16,1,256]{2,1,0:T(1,128)S(1)} %copy.18), channel_id=1, replica_groups=mesh['x'=4,'zl'=4,'zh'=4,'y'=4,'c'=2] {'x','y'}, dimensions={0} | all-to-all | bytes 32768 | tf_op jit(solution)/shard_map/all_to_all | solution.py:398
  143.3 0.6 broadcast_in_dim.23
  143.9 7.3 %all-to-all-start.2 = ((f32[16,1,256]{2,1,0:T(1,128)}), f32[16,1,256]{2,1,0:T(1,128)S(1)}, u32[]{:S(2)}, u32[]{:S(2)}) async-start(f32[16,1,256]{2,1,0:T(1,128)} %broadcast_in_dim.23), calls=%async_computation.2 | async-start | bytes 32768 | tf_op jit(solution)/shard_map/all_to_all | solution.py:400
  151.2 0.1 pad_add_fusion.1.take_ref
  151.3 11.2 %all-to-all-done.2 = f32[16,1,256]{2,1,0:T(1,128)S(1)} async-done(((f32[16,1,256]{2,1,0:T(1,128)}), f32[16,1,256]{2,1,0:T(1,128)S(1)}, u32[]{:S(2)}, u32[]{:S(2)}) %all-to-all-start.2) | async-done | bytes 16416 | tf_op jit(solution)/shard_map/all_to_all | solution.py:400
  162.6 0.0 collective-permute-done.13.refs_0_
  162.6 0.0 collective-permute-done.14.refs_1_
  162.6 2.6 %pick.11 = (bf16[2048,128]{1,0:T(8,128)(2,1)}, bf16[2048,128]{1,0:T(8,128)(2,1)}) custom-call(s32[2]{0:T(128)S(1)} %pad_add_fusion.1.take_ref, bf16[2048,128]{1,0:T(8,128)(2,1)} %collective-permute-done.13.refs_0_, bf16[2048,128]{1,0:T(8,128)(2,1)} %collective-permute-done.14.refs_1_, bf16[2048,128]{1,0:T(8,128)(2,1)} %get-tuple-element.35.refs_2_, ...), custom_call_target="tpu_custom_call" | custom-call | flops 99999997952 | tf_op jit(solution)/shard_map/pick/pallas_call | solution.py:289
  165.2 0.6 copy.20
  165.8 6.9 %all-to-all-start.3 = ((f32[32,1,256]{2,1,0:T(1,128)}), f32[32,1,256]{2,1,0:T(1,128)S(1)}, u32[]{:S(2)}, u32[]{:S(2)}) async-start(f32[32,1,256]{2,1,0:T(1,128)} %copy.20), calls=%async_computation.3 | async-start | bytes 65536 | tf_op jit(solution)/shard_map/all_to_all | solution.py:406
  172.8 0.1 pad_add_fusion.take_ref
  172.9 2.5 %collective-permute-start.15 = (bf16[2048,128]{1,0:T(8,128)(2,1)}, bf16[2048,128]{1,0:T(8,128)(2,1)}, u32[]{:S(2)}, u32[]{:S(2)}) collective-permute-start(bf16[2048,128]{1,0:T(8,128)(2,1)} %get-tuple-element.39.up_ref), channel_id=1, source_target_pairs={{0,64},{32,96},{64,0},{96,32},{1,65},{33,97},{65,1},{97,33},{2,66}... | collective-permute-start | bytes 1572872 | tf_op jit(solution)/shard_map/ppermute | solution.py:284
  175.4 2.2 %collective-permute-start.16 = (bf16[2048,128]{1,0:T(8,128)(2,1)}, bf16[2048,128]{1,0:T(8,128)(2,1)}, u32[]{:S(2)}, u32[]{:S(2)}) collective-permute-start(bf16[2048,128]{1,0:T(8,128)(2,1)} %get-tuple-element.40.down_ref), channel_id=1, source_target_pairs={{0,32},{32,0},{64,96},{96,64},{1,33},{33,1},{65,97},{97,65},{2,34}... | collective-permute-start | bytes 1572872 | tf_op jit(solution)/shard_map/ppermute | solution.py:284
  177.5 2.6 %all-to-all-done.3 = f32[32,1,256]{2,1,0:T(1,128)S(1)} async-done(((f32[32,1,256]{2,1,0:T(1,128)}), f32[32,1,256]{2,1,0:T(1,128)S(1)}, u32[]{:S(2)}, u32[]{:S(2)}) %all-to-all-start.3) | async-done | bytes 32800 | tf_op jit(solution)/shard_map/all_to_all | solution.py:406
  180.2 1.3 copy-done.6
  181.5 4.3 %backward.1 = (f32[2048,128]{1,0:T(8,128)S(1)}, f32[2056,128]{1,0:T(8,128)S(1)}, f32[8,128]{1,0:T(8,128)S(1)}) custom-call(s32[5]{0:T(128)S(1)} %copy-done.4, f32[32,256]{1,0:T(8,128)S(1)} %bitcast.31, bf16[768,2048]{1,0:T(8,128)(2,1)S(1)} %get-tuple-element.42.x_ref, f32[776,384]{1,0:T(8,128)S(1)} %copy-done.6), custom_call_target="tpu_custom_call" | custom-call | flops 99999997952 | tf_op jit(solution)/shard_map/backward/pallas_call | solution.py:408
  185.8 0.0 copy-start.2
  185.8 2.3 %collective-permute-start.17 = (f32[2056,128]{1,0:T(8,128)S(1)}, f32[2056,128]{1,0:T(8,128)S(1)}, u32[]{:S(2)}, u32[]{:S(2)}) collective-permute-start(f32[2056,128]{1,0:T(8,128)S(1)} %get-tuple-element.45), channel_id=1, source_target_pairs={{0,1},{1,0},{2,3},{3,2},{4,5},{5,4},{6,7},{7,6},{8,9},{9,8},{10,11... | collective-permute-start | bytes 3158024 | tf_op jit(solution)/shard_map/ppermute | solution.py:284
  188.1 3.4 %loss.1 = f32[1,128]{1,0:T(1,128)} custom-call(f32[32,256]{1,0:T(8,128)S(1)} %bitcast.32, s32[64,128]{1,0:T(8,128)S(1)} %bitcast.30), custom_call_target="tpu_custom_call" | custom-call | flops 99999997952 | tf_op jit(solution)/shard_map/loss/pallas_call | solution.py:418
  191.4 9.5 %collective-permute-done.15.up_got_ref = bf16[2048,128]{1,0:T(8,128)(2,1)} collective-permute-done((bf16[2048,128]{1,0:T(8,128)(2,1)}, bf16[2048,128]{1,0:T(8,128)(2,1)}, u32[]{:S(2)}, u32[]{:S(2)}) %collective-permute-start.15) | collective-permute-done | bytes 524320 | tf_op jit(solution)/shard_map/ppermute | solution.py:284
  201.0 0.4 collective-permute-done.16.down_got_ref
  201.4 0.0 collective-permute-done.17.recv_ref
  201.4 2.9 %final.1 = (bf16[2048,128]{1,0:T(8,128)(2,1)}, bf16[128,2048]{1,0:T(8,128)(2,1)}) custom-call(s32[2]{0:T(128)S(1)} %pad_add_fusion.take_ref, bf16[2048,128]{1,0:T(8,128)(2,1)} %get-tuple-element.39.up_ref, bf16[2048,128]{1,0:T(8,128)(2,1)} %collective-permute-done.15.up_got_ref, bf16[2048,128]{1,0:T(8,128)(2,1)} %get-tuple-element.40.down_ref, ...), custom_call_target="tpu_custom_call" | custom-call | tf_op jit(solution)/shard_map/final/pallas_call | solution.py:427
  (23 shorter events, 0.3 us)
Async XLA Ops:
  6.3 30.8 %copy-start.9 = (s32[4]{0:T(128)S(1)}, s32[4]{0:T(128)}, u32[]{:S(2)}) copy-start(s32[4]{0:T(128)} %mask_ref.1) | copy-start | bytes 52
  6.3 34.0 %copy-start.8 = (bf16[2064,128]{1,0:T(8,128)(2,1)S(1)}, bf16[2064,128]{1,0:T(8,128)(2,1)}, u32[]{:S(2)}) copy-start(bf16[2064,128]{1,0:T(8,128)(2,1)} %get-tuple-element.27.refs_1_) | copy-start | bytes 1585156
  6.3 34.0 %collective-permute-start = (bf16[2064,128]{1,0:T(8,128)(2,1)}, bf16[2064,128]{1,0:T(8,128)(2,1)S(1)}, u32[]{:S(2)}, u32[]{:S(2)}) collective-permute-start(bf16[2064,128]{1,0:T(8,128)(2,1)} %get-tuple-element.27.refs_1_), channel_id=1, source_target_pairs={{0,128},{128,0},{256,384},{384,256},{1,129},{129,1},{257,385},{385... | collective-permute-start | bytes 1585160 | tf_op jit(solution)/shard_map/ppermute | solution.py:284
  10.4 47.2 %collective-permute-start.4 = (bf16[48,2176]{1,0:T(8,128)(2,1)}, bf16[48,2176]{1,0:T(8,128)(2,1)}, u32[]{:S(2)}, u32[]{:S(2)}) collective-permute-start(bf16[48,2176]{1,0:T(8,128)(2,1)} %get-tuple-element.30.refs_0_), channel_id=1, source_target_pairs={{0,2},{2,0},{4,6},{6,4},{1,3},{3,1},{5,7},{7,5},{8,10},{10,8},{12,... | collective-permute-start | bytes 626696 | tf_op jit(solution)/shard_map/ppermute | solution.py:284
  13.6 44.0 %collective-permute-start.5 = (bf16[48,2176]{1,0:T(8,128)(2,1)}, bf16[48,2176]{1,0:T(8,128)(2,1)}, u32[]{:S(2)}, u32[]{:S(2)}) collective-permute-start(bf16[48,2176]{1,0:T(8,128)(2,1)} %get-tuple-element.30.refs_0_), channel_id=1, source_target_pairs={{0,4},{2,6},{4,0},{6,2},{1,5},{3,7},{5,1},{7,3},{8,12},{10,14},{12... | collective-permute-start | bytes 626696 | tf_op jit(solution)/shard_map/ppermute | solution.py:284
  18.1 39.5 %collective-permute-start.6 = (bf16[48,2176]{1,0:T(8,128)(2,1)}, bf16[48,2176]{1,0:T(8,128)(2,1)}, u32[]{:S(2)}, u32[]{:S(2)}) collective-permute-start(bf16[48,2176]{1,0:T(8,128)(2,1)} %get-tuple-element.30.refs_0_), channel_id=1, source_target_pairs={{0,6},{2,4},{4,2},{6,0},{1,7},{3,5},{5,3},{7,1},{8,14},{10,12},{12... | collective-permute-start | bytes 626696 | tf_op jit(solution)/shard_map/ppermute | solution.py:284
  20.1 24.8 %collective-permute-start.2 = (bf16[4096,128]{1,0:T(8,128)(2,1)}, bf16[4096,128]{1,0:T(8,128)(2,1)S(1)}, u32[]{:S(2)}, u32[]{:S(2)}) collective-permute-start(bf16[4096,128]{1,0:T(8,128)(2,1)} %get-tuple-element.28.refs_1_), channel_id=1, source_target_pairs={{0,128},{128,0},{256,384},{384,256},{1,129},{129,1},{257,385},{385... | collective-permute-start | bytes 3145736 | tf_op jit(solution)/shard_map/ppermute | solution.py:284
  22.2 56.1 %all-to-all-start = ((bf16[4,48,2176]{2,1,0:T(8,128)(2,1)}), bf16[4,48,2176]{2,1,0:T(8,128)(2,1)}, u32[]{:S(2)}, u32[]{:S(2)}) async-start(bf16[4,48,2176]{2,1,0:T(8,128)(2,1)} %bitcast.36), calls=%async_computation | async-start | bytes 1671168 | tf_op jit(solution)/shard_map/all_to_all | solution.py:355
  40.3 4.6 %copy-start.7 = (bf16[4096,128]{1,0:T(8,128)(2,1)S(1)}, bf16[4096,128]{1,0:T(8,128)(2,1)}, u32[]{:S(2)}) copy-start(bf16[4096,128]{1,0:T(8,128)(2,1)} %get-tuple-element.28.refs_1_) | copy-start | bytes 3145732
  40.4 14.6 %collective-permute-start.1 = (bf16[2064,128]{1,0:T(8,128)(2,1)S(1)}, bf16[2064,128]{1,0:T(8,128)(2,1)S(1)}, u32[]{:S(2)}, u32[]{:S(2)}) collective-permute-start(bf16[2064,128]{1,0:T(8,128)(2,1)S(1)} %pick.6.refs_2_.refs_1_), channel_id=1, source_target_pairs={{0,384},{128,256},{256,128},{384,0},{1,385},{129,257},{257,129},{3... | collective-permute-start | bytes 1585160 | tf_op jit(solution)/shard_map/ppermute | solution.py:284
  46.0 46.4 %collective-permute-start.8 = (bf16[4096,128]{1,0:T(8,128)(2,1)}, bf16[4096,128]{1,0:T(8,128)(2,1)}, u32[]{:S(2)}, u32[]{:S(2)}) collective-permute-start(bf16[4096,128]{1,0:T(8,128)(2,1)} %pick.7.refs_2_.own_ref), channel_id=1, source_target_pairs={{0,384},{128,256},{256,128},{384,0},{1,385},{129,257},{257,129},{3... | collective-permute-start | bytes 3145736 | tf_op jit(solution)/shard_map/ppermute | solution.py:284
  54.9 23.4 %copy-start.4 = (s32[5]{0:T(128)S(1)}, s32[5]{0:T(128)}, u32[]{:S(2)}) copy-start(s32[5]{0:T(128)} %stack.23.info_ref) | copy-start | bytes 64
  55.0 35.0 %collective-permute-start.3 = (bf16[2064,128]{1,0:T(8,128)(2,1)S(1)}, bf16[2064,128]{1,0:T(8,128)(2,1)S(1)}, u32[]{:S(2)}, u32[]{:S(2)}) collective-permute-start(bf16[2064,128]{1,0:T(8,128)(2,1)S(1)} %pick.8.refs_0_.refs_1_), channel_id=1, source_target_pairs={{0,32},{32,0},{64,96},{96,64},{1,33},{33,1},{65,97},{97,65},{2,34}... | collective-permute-start | bytes 1585160 | tf_op jit(solution)/shard_map/ppermute | solution.py:284
  80.4 41.9 %collective-permute-start.10 = (bf16[144,2176]{1,0:T(8,128)(2,1)}, bf16[144,2176]{1,0:T(8,128)(2,1)}, u32[]{:S(2)}, u32[]{:S(2)}) collective-permute-start(bf16[144,2176]{1,0:T(8,128)(2,1)} %others.1.refs_2_.refs_4_), channel_id=1, source_target_pairs={{0,2},{2,0},{4,6},{6,4},{1,3},{3,1},{5,7},{7,5},{8,10},{10,8},{12,... | collective-permute-start | bytes 1880072 | tf_op jit(solution)/shard_map/ppermute | solution.py:284
  82.3 43.8 %collective-permute-start.11 = (bf16[144,2176]{1,0:T(8,128)(2,1)}, bf16[144,2176]{1,0:T(8,128)(2,1)}, u32[]{:S(2)}, u32[]{:S(2)}) collective-permute-start(bf16[144,2176]{1,0:T(8,128)(2,1)} %others.1.refs_2_.refs_4_), channel_id=1, source_target_pairs={{0,4},{2,6},{4,0},{6,2},{1,5},{3,7},{5,1},{7,3},{8,12},{10,14},{12... | collective-permute-start | bytes 1880072 | tf_op jit(solution)/shard_map/ppermute | solution.py:284
  88.0 38.2 %collective-permute-start.12 = (bf16[144,2176]{1,0:T(8,128)(2,1)}, bf16[144,2176]{1,0:T(8,128)(2,1)}, u32[]{:S(2)}, u32[]{:S(2)}) collective-permute-start(bf16[144,2176]{1,0:T(8,128)(2,1)} %others.1.refs_2_.refs_4_), channel_id=1, source_target_pairs={{0,6},{2,4},{4,2},{6,0},{1,7},{3,5},{5,3},{7,1},{8,14},{10,12},{12... | collective-permute-start | bytes 1880072 | tf_op jit(solution)/shard_map/ppermute | solution.py:284
  90.1 26.5 %collective-permute-start.7 = (bf16[2064,128]{1,0:T(8,128)(2,1)S(1)}, bf16[2064,128]{1,0:T(8,128)(2,1)S(1)}, u32[]{:S(2)}, u32[]{:S(2)}) collective-permute-start(bf16[2064,128]{1,0:T(8,128)(2,1)S(1)} %pick.9.earlier_ref.refs_1_), channel_id=1, source_target_pairs={{0,64},{32,96},{64,0},{96,32},{1,65},{33,97},{65,1},{97,33},{2,66}... | collective-permute-start | bytes 1585160 | tf_op jit(solution)/shard_map/ppermute | solution.py:284
  116.5 9.6 %copy-start = (bf16[48,2176]{1,0:T(8,128)(2,1)S(1)}, bf16[48,2176]{1,0:T(8,128)(2,1)}, u32[]{:S(2)}) copy-start(bf16[48,2176]{1,0:T(8,128)(2,1)} %get-tuple-element.30.refs_0_) | copy-start | bytes 626692
  116.5 9.6 %copy-start.3 = (f32[8,256]{1,0:T(8,128)S(1)}, f32[8,256]{1,0:T(8,128)}, u32[]{:S(2)}) copy-start(f32[8,256]{1,0:T(8,128)} %get-tuple-element.26.base_ref) | copy-start | bytes 24580
  116.6 9.6 %collective-permute-start.9 = (bf16[2064,128]{1,0:T(8,128)(2,1)S(1)}, bf16[2064,128]{1,0:T(8,128)(2,1)S(1)}, u32[]{:S(2)}, u32[]{:S(2)}) collective-permute-start(bf16[2064,128]{1,0:T(8,128)(2,1)S(1)} %pick.10.own_w_ref), channel_id=1, source_target_pairs={{0,1},{1,0},{2,3},{3,2},{4,5},{5,4},{6,7},{7,6},{8,9},{9,8},{10,11... | collective-permute-start | bytes 1585160 | tf_op jit(solution)/shard_map/ppermute | solution.py:284
  120.4 42.2 %collective-permute-start.13 = (bf16[2048,128]{1,0:T(8,128)(2,1)}, bf16[2048,128]{1,0:T(8,128)(2,1)}, u32[]{:S(2)}, u32[]{:S(2)}) collective-permute-start(bf16[2048,128]{1,0:T(8,128)(2,1)} %get-tuple-element.35.refs_2_), channel_id=1, source_target_pairs={{0,32},{32,0},{64,96},{96,64},{1,33},{33,1},{65,97},{97,65},{2,34}... | collective-permute-start | bytes 1572872 | tf_op jit(solution)/shard_map/ppermute | solution.py:284
  122.3 40.3 %collective-permute-start.14 = (bf16[2048,128]{1,0:T(8,128)(2,1)}, bf16[2048,128]{1,0:T(8,128)(2,1)}, u32[]{:S(2)}, u32[]{:S(2)}) collective-permute-start(bf16[2048,128]{1,0:T(8,128)(2,1)} %get-tuple-element.36.refs_3_), channel_id=1, source_target_pairs={{0,64},{32,96},{64,0},{96,32},{1,65},{33,97},{65,1},{97,33},{2,66}... | collective-permute-start | bytes 1572872 | tf_op jit(solution)/shard_map/ppermute | solution.py:284
  129.5 1.0 copy-start.5
  143.9 18.6 %all-to-all-start.2 = ((f32[16,1,256]{2,1,0:T(1,128)}), f32[16,1,256]{2,1,0:T(1,128)S(1)}, u32[]{:S(2)}, u32[]{:S(2)}) async-start(f32[16,1,256]{2,1,0:T(1,128)} %broadcast_in_dim.23), calls=%async_computation.2 | async-start | bytes 32768 | tf_op jit(solution)/shard_map/all_to_all | solution.py:400
  165.8 14.3 %all-to-all-start.3 = ((f32[32,1,256]{2,1,0:T(1,128)}), f32[32,1,256]{2,1,0:T(1,128)S(1)}, u32[]{:S(2)}, u32[]{:S(2)}) async-start(f32[32,1,256]{2,1,0:T(1,128)} %copy.20), calls=%async_computation.3 | async-start | bytes 65536 | tf_op jit(solution)/shard_map/all_to_all | solution.py:406
  172.9 28.1 %collective-permute-start.15 = (bf16[2048,128]{1,0:T(8,128)(2,1)}, bf16[2048,128]{1,0:T(8,128)(2,1)}, u32[]{:S(2)}, u32[]{:S(2)}) collective-permute-start(bf16[2048,128]{1,0:T(8,128)(2,1)} %get-tuple-element.39.up_ref), channel_id=1, source_target_pairs={{0,64},{32,96},{64,0},{96,32},{1,65},{33,97},{65,1},{97,33},{2,66}... | collective-permute-start | bytes 1572872 | tf_op jit(solution)/shard_map/ppermute | solution.py:284
  175.4 26.1 %collective-permute-start.16 = (bf16[2048,128]{1,0:T(8,128)(2,1)}, bf16[2048,128]{1,0:T(8,128)(2,1)}, u32[]{:S(2)}, u32[]{:S(2)}) collective-permute-start(bf16[2048,128]{1,0:T(8,128)(2,1)} %get-tuple-element.40.down_ref), channel_id=1, source_target_pairs={{0,32},{32,0},{64,96},{96,64},{1,33},{33,1},{65,97},{97,65},{2,34}... | collective-permute-start | bytes 1572872 | tf_op jit(solution)/shard_map/ppermute | solution.py:284
  180.2 1.3 copy-start.6
  181.5 6.6 %copy-start.1 = (s32[8192]{0:T(1024)S(1)}, s32[8192]{0:T(1024)}, u32[]{:S(2)}) copy-start(s32[8192]{0:T(1024)} %param.16) | copy-start | bytes 98308
  185.8 15.7 %copy-start.2 = (bf16[2048]{0:T(1024)(128)(2,1)S(1)}, bf16[2048]{0:T(1024)(128)(2,1)}, u32[]{:S(2)}) copy-start(bf16[2048]{0:T(1024)(128)(2,1)} %param.17) | copy-start | bytes 12292
  185.8 15.7 %collective-permute-start.17 = (f32[2056,128]{1,0:T(8,128)S(1)}, f32[2056,128]{1,0:T(8,128)S(1)}, u32[]{:S(2)}, u32[]{:S(2)}) collective-permute-start(f32[2056,128]{1,0:T(8,128)S(1)} %get-tuple-element.45), channel_id=1, source_target_pairs={{0,1},{1,0},{2,3},{3,2},{4,5},{5,4},{6,7},{7,6},{8,9},{9,8},{10,11... | collective-permute-start | bytes 3158024 | tf_op jit(solution)/shard_map/ppermute | solution.py:284

commit v6 on v5

--- a/solution.py
+++ b/solution.py
@@ -27,6 +27,7 @@
 BLOCKS = [(CAP * d, 0, d) for d in range(4)] + [
     (4 * CAP + 3 * CAP * d + CAP * (k - 1), k, d) for d in range(4) for k in range(1, EXP_GRP)
 ]
+LIGHT = pl.CostEstimate(flops=0, bytes_accessed=0, transcendentals=0)
 SPACED = pl.CostEstimate(flops=10**11, bytes_accessed=0, transcendentals=0)
 ANY = pl.BlockSpec(memory_space=pl.ANY)
 
@@ -292,7 +293,7 @@
         in_specs=[SMEM] + [VMEM] * (2 * count) + [ANY] * len(earlier),
         out_specs=[VMEM] * count,
         compiler_params=PARAMS,
-        cost_estimate=SPACED,
+        cost_estimate=LIGHT,
         name="pick",
     )(jnp.concatenate([s[2] for s in stages]), *got, *own, *earlier)
 
@@ -353,19 +354,22 @@
         acc_down[0],
     )
     arrived = lax.all_to_all(sent, "zh", 0, 0, tiled=True)
+    got = swap(weights, *x1[:2])
+    weights = pick(x1, got, weights)
+    weights, own_rows, accums = lax.optimization_barrier((weights, own_rows, accums))
+    got = swap(weights, *x3[:2])
     held = [own_rows] + [swap(own_rows, "y", d) for d in (1, 2, 3)]
-    got = swap(weights, *x1[:2])
     acc_got = swap(accums, *x1[:2])
-    weights = pick(x1, got, weights)
-    got = swap(weights, *x3[:2])
+    weights = pick(x3, got, weights)
+    got = swap(weights, *z1[:2])
     accums = pick(x1, acc_got, accums, weights)
     acc_got = swap(accums, *x3[:2])
-    weights = pick(x3, got, weights, accums)
-    got = swap(weights, *z1[:2])
-    rows = others(info, arrived, weights, *held[1:])
+    weights = pick(z1, got, weights, accums, *held[1:])
+    got = swap(weights, *z2[:2])
+    rows = others(info, arrived, weights)
     held += [rows] + [swap(rows, "y", d) for d in (1, 2, 3)]
-    weights = pick(z1, got, weights, rows)
-    got = swap(weights, *z2[:2])
+    weights = pick(z2, got, weights, rows)
+    other_weights = swap(weights, "c", 1)
     up, down = pl.pallas_call(
         split_kernel,
         out_shape=[shape((D, HID_DEV), bf16)] * 2,
@@ -375,9 +379,6 @@
         cost_estimate=SPACED,
         name="pick_split",
     )(x3[2], acc_got, accums, weights)
-    weights = pick(z2, got, weights, up)
-    weights, up, down = lax.optimization_barrier((weights, up, down))
-    other_weights = swap(weights, "c", 1)
     up_got = swap(up, *z1[:2])
     down_got = swap(down, *z2[:2])
 

time: 206 us -> 193 us (0.937)
  waiting for transfers between devices: 71.2 us -> 57.7 us
  Pallas kernels: 27.4 us -> 22.9 us
  local copies, waits for them, and re-layouts: 4.23 us -> 7.65 us
    all_to_all x1, waiting for transfers between devices: 20.7 us -> 0.01 us  [body(): arrived = lax.all_to_all(sent, 'zh', 0, 0, tiled=True)]
    ppermute x18, waiting for transfers between devices: 36.7 us -> 43.9 us  [swap(): return lax.ppermute(block, axis, [(i, i ^ mask) for i in range(count)])]
    unnamed x21 -> x23, local copies, waits for them, and re-layouts: 2.32 us -> 5.75 us
  transfers between devices with their start and end apart: 21 -> 21, of which waited for: 7 -> 10; matrix products, arithmetic and copies ran while one was open for 1% -> 1% of each run, Pallas kernels for 8% -> 7%
where the time goes in v6:
time: 193 us; the launch traced here: 192 us
  starting transfers between devices  86.2 us (45%)
  waiting for transfers between devices  57.7 us (30%)
  Pallas kernels  22.9 us (12%)
  blocking collectives  12.8 us (7%)
  local copies, waits for them, and re-layouts  7.65 us (4%)
  between operations  3.77 us (2%)
    ppermute x18, starting transfers between devices, swap(): return lax.ppermute(block, axis, [(i, i ^ mask) for i in range(count)])  55.1 us
    ppermute x18, waiting for transfers between devices, swap(): return lax.ppermute(block, axis, [(i, i ^ mask) for i in range(count)])  43.9 us
    all_to_all x1, starting transfers between devices, body(): arrived = lax.all_to_all(sent, 'zh', 0, 0, tiled=True)  15.8 us
    all_to_all x1, blocking collectives, body(): mine = lax.all_to_all(part, ('x', 'y'), 0, 0, tiled=True)  12.8 us
    all_to_all x1, waiting for transfers between devices, body(): mine = lax.all_to_all(mine, ('zl', 'zh'), 0, 0, tiled=True)  11.2 us
    all_to_all x1, starting transfers between devices, body(): table = lax.all_to_all(mine, ('x', 'y', 'c'), 0, 0, tiled=True)  7.97 us
    all_to_all x1, starting transfers between devices, body(): mine = lax.all_to_all(mine, ('zl', 'zh'), 0, 0, tiled=True)  7.26 us
    unnamed x23, local copies, waits for them, and re-layouts  5.75 us
  transfers between devices with their start and end apart: 21, of which 10 were waited for; matrix products, arithmetic and copies ran while one was open for 1% of the time, Pallas kernels for 7%

profile of v6, /device:TPU:1, one launch (start us, length us, event | category | flops | bytes accessed | tf_op | source)
XLA Modules:
  0.0 192.0 jit_solution(14298592526786405116)
XLA Ops:
  0.6 0.6 stack.23.info_ref
  1.3 5.0 %dispatch.1 = (bf16[192,2176]{1,0:T(8,128)(2,1)}, bf16[48,2176]{1,0:T(8,128)(2,1)}, f32[8,256]{1,0:T(8,128)}, bf16[2064,128]{1,0:T(8,128)(2,1)}, bf16[4096,128]{1,0:T(8,128)(2,1)}) custom-call(s32[64]{0:T(128)} %group_ref.1, s32[4]{0:T(128)} %mask_ref.1, s32[5]{0:T(128)} %stack.23.info_ref, bf16[256,2048]{1,0:T(8,128)(2,1)} %tok_ref.1, s32[8,256]{1,0:T(8,128)} %bitcast.42, ...), custom_call_target="tpu_custom_call" | custom-call | tf_op jit(solution)/shard_map/dispatch/pallas_call | solution.py:329
  6.2 15.8 %all-to-all-start = ((bf16[4,48,2176]{2,1,0:T(8,128)(2,1)}), bf16[4,48,2176]{2,1,0:T(8,128)(2,1)S(1)}, u32[]{:S(2)}, u32[]{:S(2)}) async-start(bf16[4,48,2176]{2,1,0:T(8,128)(2,1)} %bitcast.37), calls=%async_computation | async-start | bytes 1671168 | tf_op jit(solution)/shard_map/all_to_all | solution.py:356
  22.0 3.2 %collective-permute-start = (bf16[2064,128]{1,0:T(8,128)(2,1)S(1)}, bf16[2064,128]{1,0:T(8,128)(2,1)S(1)}, u32[]{:S(2)}, u32[]{:S(2)}) collective-permute-start(bf16[2064,128]{1,0:T(8,128)(2,1)S(1)} %copy-done.3), channel_id=1, source_target_pairs={{0,128},{128,0},{256,384},{384,256},{1,129},{129,1},{257,385},{385... | collective-permute-start | bytes 1585160 | tf_op jit(solution)/shard_map/ppermute | solution.py:285
  25.3 0.7 fusion
  27.4 9.2 %collective-permute-done.refs_0_ = bf16[2064,128]{1,0:T(8,128)(2,1)S(1)} collective-permute-done((bf16[2064,128]{1,0:T(8,128)(2,1)S(1)}, bf16[2064,128]{1,0:T(8,128)(2,1)S(1)}, u32[]{:S(2)}, u32[]{:S(2)}) %collective-permute-start) | collective-permute-done | bytes 528416 | tf_op jit(solution)/shard_map/ppermute | solution.py:285
  36.6 4.4 %collective-permute-start.1 = (bf16[2064,128]{1,0:T(8,128)(2,1)S(1)}, bf16[2064,128]{1,0:T(8,128)(2,1)S(1)}, u32[]{:S(2)}, u32[]{:S(2)}) collective-permute-start(bf16[2064,128]{1,0:T(8,128)(2,1)S(1)} %pick.6.refs_1_), channel_id=1, source_target_pairs={{0,384},{128,256},{256,128},{384,0},{1,385},{129,257},{257,129},{3... | collective-permute-start | bytes 1585160 | tf_op jit(solution)/shard_map/ppermute | solution.py:285
  41.0 1.9 %collective-permute-start.3 = (bf16[4096,128]{1,0:T(8,128)(2,1)S(1)}, bf16[4096,128]{1,0:T(8,128)(2,1)S(1)}, u32[]{:S(2)}, u32[]{:S(2)}) collective-permute-start(bf16[4096,128]{1,0:T(8,128)(2,1)S(1)} %copy-done), channel_id=1, source_target_pairs={{0,128},{128,0},{256,384},{384,256},{1,129},{129,1},{257,385},{385... | collective-permute-start | bytes 3145736 | tf_op jit(solution)/shard_map/ppermute | solution.py:285
  43.0 8.4 %collective-permute-done.1.refs_0_ = bf16[2064,128]{1,0:T(8,128)(2,1)S(1)} collective-permute-done((bf16[2064,128]{1,0:T(8,128)(2,1)S(1)}, bf16[2064,128]{1,0:T(8,128)(2,1)S(1)}, u32[]{:S(2)}, u32[]{:S(2)}) %collective-permute-start.1) | collective-permute-done | bytes 528416 | tf_op jit(solution)/shard_map/ppermute | solution.py:285
  51.4 2.6 %collective-permute-start.2 = (bf16[2064,128]{1,0:T(8,128)(2,1)S(1)}, bf16[2064,128]{1,0:T(8,128)(2,1)}, u32[]{:S(2)}, u32[]{:S(2)}) collective-permute-start(bf16[2064,128]{1,0:T(8,128)(2,1)S(1)} %pick.7.refs_2_.refs_1_), channel_id=1, source_target_pairs={{0,32},{32,0},{64,96},{96,64},{1,33},{33,1},{65,97},{97,65},{2,34}... | collective-permute-start | bytes 1585160 | tf_op jit(solution)/shard_map/ppermute | solution.py:285
  54.1 4.6 %collective-permute-start.6 = (bf16[48,2176]{1,0:T(8,128)(2,1)}, bf16[48,2176]{1,0:T(8,128)(2,1)}, u32[]{:S(2)}, u32[]{:S(2)}) collective-permute-start(bf16[48,2176]{1,0:T(8,128)(2,1)} %get-tuple-element.32.refs_0_), channel_id=1, source_target_pairs={{0,6},{2,4},{4,2},{6,0},{1,7},{3,5},{5,3},{7,1},{8,14},{10,12},{12... | collective-permute-start | bytes 626696 | tf_op jit(solution)/shard_map/ppermute | solution.py:285
  58.7 2.2 %collective-permute-start.5 = (bf16[48,2176]{1,0:T(8,128)(2,1)}, bf16[48,2176]{1,0:T(8,128)(2,1)}, u32[]{:S(2)}, u32[]{:S(2)}) collective-permute-start(bf16[48,2176]{1,0:T(8,128)(2,1)} %get-tuple-element.32.refs_0_), channel_id=1, source_target_pairs={{0,4},{2,6},{4,0},{6,2},{1,5},{3,7},{5,1},{7,3},{8,12},{10,14},{12... | collective-permute-start | bytes 626696 | tf_op jit(solution)/shard_map/ppermute | solution.py:285
  61.0 2.2 %collective-permute-start.4 = (bf16[48,2176]{1,0:T(8,128)(2,1)}, bf16[48,2176]{1,0:T(8,128)(2,1)}, u32[]{:S(2)}, u32[]{:S(2)}) collective-permute-start(bf16[48,2176]{1,0:T(8,128)(2,1)} %get-tuple-element.32.refs_0_), channel_id=1, source_target_pairs={{0,2},{2,0},{4,6},{6,4},{1,3},{3,1},{5,7},{7,5},{8,10},{10,8},{12,... | collective-permute-start | bytes 626696 | tf_op jit(solution)/shard_map/ppermute | solution.py:285
  64.5 1.0 collective-permute-done.3.refs_0_
  65.5 1.0 copy-done.1
  66.5 1.2 copy-done.2
  67.7 0.1 pick.8.refs_2_.own_ref
  67.8 3.4 %collective-permute-start.12 = (bf16[4096,128]{1,0:T(8,128)(2,1)S(1)}, bf16[4096,128]{1,0:T(8,128)(2,1)}, u32[]{:S(2)}, u32[]{:S(2)}) collective-permute-start(bf16[4096,128]{1,0:T(8,128)(2,1)S(1)} %pick.8.refs_2_.own_ref), channel_id=1, source_target_pairs={{0,384},{128,256},{256,128},{384,0},{1,385},{129,257},{257,129},{3... | collective-permute-start | bytes 3145736 | tf_op jit(solution)/shard_map/ppermute | solution.py:285
  71.2 0.0 collective-permute-done.6.refs_5_.refs_3_
  71.2 0.0 collective-permute-done.5.refs_4_.refs_2_
  71.2 0.0 collective-permute-done.4.refs_3_.refs_1_
  71.2 2.3 %collective-permute-done.2.refs_0_ = bf16[2064,128]{1,0:T(8,128)(2,1)} collective-permute-done((bf16[2064,128]{1,0:T(8,128)(2,1)S(1)}, bf16[2064,128]{1,0:T(8,128)(2,1)}, u32[]{:S(2)}, u32[]{:S(2)}) %collective-permute-start.2) | collective-permute-done | bytes 528416 | tf_op jit(solution)/shard_map/ppermute | solution.py:285
  73.5 1.1 pick.9.refs_0_.refs_1_
  74.6 4.6 %collective-permute-start.7 = (bf16[2064,128]{1,0:T(8,128)(2,1)S(1)}, bf16[2064,128]{1,0:T(8,128)(2,1)S(1)}, u32[]{:S(2)}, u32[]{:S(2)}) collective-permute-start(bf16[2064,128]{1,0:T(8,128)(2,1)S(1)} %pick.9.refs_0_.refs_1_), channel_id=1, source_target_pairs={{0,64},{32,96},{64,0},{96,32},{1,65},{33,97},{65,1},{97,33},{2,66}... | collective-permute-start | bytes 1585160 | tf_op jit(solution)/shard_map/ppermute | solution.py:285
  79.3 0.0 all-to-all-done
  79.3 0.6 others.1.refs_2_.refs_4_
  79.9 4.6 %collective-permute-start.11 = (bf16[144,2176]{1,0:T(8,128)(2,1)S(1)}, bf16[144,2176]{1,0:T(8,128)(2,1)S(1)}, u32[]{:S(2)}, u32[]{:S(2)}) collective-permute-start(bf16[144,2176]{1,0:T(8,128)(2,1)S(1)} %others.1.refs_2_.refs_4_), channel_id=1, source_target_pairs={{0,6},{2,4},{4,2},{6,0},{1,7},{3,5},{5,3},{7,1},{8,14},{10,12},{12... | collective-permute-start | bytes 1880072 | tf_op jit(solution)/shard_map/ppermute | solution.py:285
  84.5 2.3 %collective-permute-start.10 = (bf16[144,2176]{1,0:T(8,128)(2,1)S(1)}, bf16[144,2176]{1,0:T(8,128)(2,1)S(1)}, u32[]{:S(2)}, u32[]{:S(2)}) collective-permute-start(bf16[144,2176]{1,0:T(8,128)(2,1)S(1)} %others.1.refs_2_.refs_4_), channel_id=1, source_target_pairs={{0,4},{2,6},{4,0},{6,2},{1,5},{3,7},{5,1},{7,3},{8,12},{10,14},{12... | collective-permute-start | bytes 1880072 | tf_op jit(solution)/shard_map/ppermute | solution.py:285
  86.8 2.1 %collective-permute-start.9 = (bf16[144,2176]{1,0:T(8,128)(2,1)S(1)}, bf16[144,2176]{1,0:T(8,128)(2,1)S(1)}, u32[]{:S(2)}, u32[]{:S(2)}) collective-permute-start(bf16[144,2176]{1,0:T(8,128)(2,1)S(1)} %others.1.refs_2_.refs_4_), channel_id=1, source_target_pairs={{0,2},{2,0},{4,6},{6,4},{1,3},{3,1},{5,7},{7,5},{8,10},{10,8},{12,... | collective-permute-start | bytes 1880072 | tf_op jit(solution)/shard_map/ppermute | solution.py:285
  89.0 12.4 %collective-permute-done.7.refs_0_ = bf16[2064,128]{1,0:T(8,128)(2,1)S(1)} collective-permute-done((bf16[2064,128]{1,0:T(8,128)(2,1)S(1)}, bf16[2064,128]{1,0:T(8,128)(2,1)S(1)}, u32[]{:S(2)}, u32[]{:S(2)}) %collective-permute-start.7) | collective-permute-done | bytes 528416 | tf_op jit(solution)/shard_map/ppermute | solution.py:285
  101.4 0.0 copy-start.6
  101.4 4.1 %collective-permute-start.8 = (bf16[2064,128]{1,0:T(8,128)(2,1)S(1)}, bf16[2064,128]{1,0:T(8,128)(2,1)S(1)}, u32[]{:S(2)}, u32[]{:S(2)}) collective-permute-start(bf16[2064,128]{1,0:T(8,128)(2,1)S(1)} %pick.10.own_w_ref.earlier_ref), channel_id=1, source_target_pairs={{0,1},{1,0},{2,3},{3,2},{4,5},{5,4},{6,7},{7,6},{8,9},{9,8},{10,11... | collective-permute-start | bytes 1585160 | tf_op jit(solution)/shard_map/ppermute | solution.py:285
  105.5 0.0 collective-permute-done.12.got_ref
  105.5 1.3 pick_split.1
  106.8 1.9 %collective-permute-start.13 = (bf16[2048,128]{1,0:T(8,128)(2,1)S(1)}, bf16[2048,128]{1,0:T(8,128)(2,1)S(1)}, u32[]{:S(2)}, u32[]{:S(2)}) collective-permute-start(bf16[2048,128]{1,0:T(8,128)(2,1)S(1)} %get-tuple-element.35.refs_2_), channel_id=1, source_target_pairs={{0,32},{32,0},{64,96},{96,64},{1,33},{33,1},{65,97},{97,65},{2,34}... | collective-permute-start | bytes 1572872 | tf_op jit(solution)/shard_map/ppermute | solution.py:285
  108.7 0.0 collective-permute-done.8.other_w_ref
  108.8 3.8 %collective-permute-start.14 = (bf16[2048,128]{1,0:T(8,128)(2,1)S(1)}, bf16[2048,128]{1,0:T(8,128)(2,1)S(1)}, u32[]{:S(2)}, u32[]{:S(2)}) collective-permute-start(bf16[2048,128]{1,0:T(8,128)(2,1)S(1)} %get-tuple-element.36.refs_3_), channel_id=1, source_target_pairs={{0,64},{32,96},{64,0},{96,32},{1,65},{33,97},{65,1},{97,33},{2,66}... | collective-permute-start | bytes 1572872 | tf_op jit(solution)/shard_map/ppermute | solution.py:285
  112.6 0.0 collective-permute-done.11.refs_7_
  112.6 0.0 collective-permute-done.10.refs_6_
  112.6 1.1 collective-permute-done.9.refs_5_
  113.8 2.6 %forward.1 = (bf16[768,2048]{1,0:T(8,128)(2,1)S(1)}, f32[776,384]{1,0:T(8,128)S(1)}, f32[16,256]{1,0:T(8,128)S(1)}) custom-call(s32[5]{0:T(128)S(1)} %copy-done.7, f32[8,256]{1,0:T(8,128)S(1)} %copy-done.6, bf16[2064,128]{1,0:T(8,128)(2,1)S(1)} %pick.10.own_w_ref.earlier_ref, bf16[2064,128]{1,0:T(8,128)(2,1)S(1)} %collective-permute-done.8.other_w_ref, ...), custom_call_target="tpu_custom_call" | custom-call | tf_op jit(solution)/shard_map/forward/pallas_call | solution.py:385
  116.4 1.6 copy-done.8
  118.1 12.8 %all_to_all.37 = f32[16,1,256]{2,1,0:T(1,128)S(1)} all-to-all(f32[16,1,256]{2,1,0:T(1,128)S(1)} %copy.18), channel_id=1, replica_groups=mesh['x'=4,'zl'=4,'zh'=4,'y'=4,'c'=2] {'x','y'}, dimensions={0} | all-to-all | bytes 32768 | tf_op jit(solution)/shard_map/all_to_all | solution.py:399
  130.9 0.6 broadcast_in_dim.23
  131.6 7.3 %all-to-all-start.2 = ((f32[16,1,256]{2,1,0:T(1,128)}), f32[16,1,256]{2,1,0:T(1,128)S(1)}, u32[]{:S(2)}, u32[]{:S(2)}) async-start(f32[16,1,256]{2,1,0:T(1,128)} %broadcast_in_dim.23), calls=%async_computation.2 | async-start | bytes 32768 | tf_op jit(solution)/shard_map/all_to_all | solution.py:401
  138.8 0.1 pad_add_fusion.1.take_ref
  138.9 11.2 %all-to-all-done.2 = f32[16,1,256]{2,1,0:T(1,128)S(1)} async-done(((f32[16,1,256]{2,1,0:T(1,128)}), f32[16,1,256]{2,1,0:T(1,128)S(1)}, u32[]{:S(2)}, u32[]{:S(2)}) %all-to-all-start.2) | async-done | bytes 16416 | tf_op jit(solution)/shard_map/all_to_all | solution.py:401
  150.2 0.0 collective-permute-done.13.refs_0_
  150.2 1.6 pick.11
  151.8 0.6 copy.20
  152.4 8.0 %all-to-all-start.3 = ((f32[32,1,256]{2,1,0:T(1,128)}), f32[32,1,256]{2,1,0:T(1,128)S(1)}, u32[]{:S(2)}, u32[]{:S(2)}) async-start(f32[32,1,256]{2,1,0:T(1,128)} %copy.20), calls=%async_computation.3 | async-start | bytes 65536 | tf_op jit(solution)/shard_map/all_to_all | solution.py:407
  160.4 0.1 pad_add_fusion.take_ref
  160.5 2.5 %collective-permute-start.15 = (bf16[2048,128]{1,0:T(8,128)(2,1)}, bf16[2048,128]{1,0:T(8,128)(2,1)}, u32[]{:S(2)}, u32[]{:S(2)}) collective-permute-start(bf16[2048,128]{1,0:T(8,128)(2,1)} %get-tuple-element.39.up_ref), channel_id=1, source_target_pairs={{0,64},{32,96},{64,0},{96,32},{1,65},{33,97},{65,1},{97,33},{2,66}... | collective-permute-start | bytes 1572872 | tf_op jit(solution)/shard_map/ppermute | solution.py:285
  163.0 2.2 %collective-permute-start.16 = (bf16[2048,128]{1,0:T(8,128)(2,1)}, bf16[2048,128]{1,0:T(8,128)(2,1)}, u32[]{:S(2)}, u32[]{:S(2)}) collective-permute-start(bf16[2048,128]{1,0:T(8,128)(2,1)} %get-tuple-element.40.down_ref), channel_id=1, source_target_pairs={{0,32},{32,0},{64,96},{96,64},{1,33},{33,1},{65,97},{97,65},{2,34}... | collective-permute-start | bytes 1572872 | tf_op jit(solution)/shard_map/ppermute | solution.py:285
  165.2 2.6 %all-to-all-done.3 = f32[32,1,256]{2,1,0:T(1,128)S(1)} async-done(((f32[32,1,256]{2,1,0:T(1,128)}), f32[32,1,256]{2,1,0:T(1,128)S(1)}, u32[]{:S(2)}, u32[]{:S(2)}) %all-to-all-start.3) | async-done | bytes 32800 | tf_op jit(solution)/shard_map/all_to_all | solution.py:407
  167.8 1.9 copy-done.9
  169.7 4.3 %backward.1 = (f32[2048,128]{1,0:T(8,128)S(1)}, f32[2056,128]{1,0:T(8,128)S(1)}, f32[8,128]{1,0:T(8,128)S(1)}) custom-call(s32[5]{0:T(128)S(1)} %copy-done.7, f32[32,256]{1,0:T(8,128)S(1)} %bitcast.32, bf16[768,2048]{1,0:T(8,128)(2,1)S(1)} %copy-done.9, f32[776,384]{1,0:T(8,128)S(1)} %get-tuple-element.43.keep_ref), custom_call_target="tpu_custom_call" | custom-call | flops 99999997952 | tf_op jit(solution)/shard_map/backward/pallas_call | solution.py:409
  174.0 0.0 copy-start.5
  174.0 2.3 %collective-permute-start.17 = (f32[2056,128]{1,0:T(8,128)S(1)}, f32[2056,128]{1,0:T(8,128)S(1)}, u32[]{:S(2)}, u32[]{:S(2)}) collective-permute-start(f32[2056,128]{1,0:T(8,128)S(1)} %get-tuple-element.45), channel_id=1, source_target_pairs={{0,1},{1,0},{2,3},{3,2},{4,5},{5,4},{6,7},{7,6},{8,9},{9,8},{10,11... | collective-permute-start | bytes 3158024 | tf_op jit(solution)/shard_map/ppermute | solution.py:285
  176.3 3.4 %loss.1 = f32[1,128]{1,0:T(1,128)} custom-call(f32[32,256]{1,0:T(8,128)S(1)} %bitcast.33, s32[64,128]{1,0:T(8,128)S(1)} %bitcast.31), custom_call_target="tpu_custom_call" | custom-call | flops 99999997952 | tf_op jit(solution)/shard_map/loss/pallas_call | solution.py:419
  179.7 8.9 %collective-permute-done.15.up_got_ref = bf16[2048,128]{1,0:T(8,128)(2,1)} collective-permute-done((bf16[2048,128]{1,0:T(8,128)(2,1)}, bf16[2048,128]{1,0:T(8,128)(2,1)}, u32[]{:S(2)}, u32[]{:S(2)}) %collective-permute-start.15) | collective-permute-done | bytes 524320 | tf_op jit(solution)/shard_map/ppermute | solution.py:285
  188.6 0.5 collective-permute-done.16.down_got_ref
  189.1 0.0 collective-permute-done.17.recv_ref
  189.1 2.9 %final.1 = (bf16[2048,128]{1,0:T(8,128)(2,1)}, bf16[128,2048]{1,0:T(8,128)(2,1)}) custom-call(s32[2]{0:T(128)S(1)} %pad_add_fusion.take_ref, bf16[2048,128]{1,0:T(8,128)(2,1)} %get-tuple-element.39.up_ref, bf16[2048,128]{1,0:T(8,128)(2,1)} %collective-permute-done.15.up_got_ref, bf16[2048,128]{1,0:T(8,128)(2,1)} %get-tuple-element.40.down_ref, ...), custom_call_target="tpu_custom_call" | custom-call | tf_op jit(solution)/shard_map/final/pallas_call | solution.py:428
  (25 shorter events, 0.2 us)
Async XLA Ops:
  6.2 15.8 %copy-start.3 = (bf16[2064,128]{1,0:T(8,128)(2,1)S(1)}, bf16[2064,128]{1,0:T(8,128)(2,1)}, u32[]{:S(2)}) copy-start(bf16[2064,128]{1,0:T(8,128)(2,1)} %get-tuple-element.27.refs_1_) | copy-start | bytes 1585156
  6.2 19.0 %copy-start.10 = (s32[4]{0:T(128)S(1)}, s32[4]{0:T(128)}, u32[]{:S(2)}) copy-start(s32[4]{0:T(128)} %mask_ref.1) | copy-start | bytes 52
  6.2 73.0 %all-to-all-start = ((bf16[4,48,2176]{2,1,0:T(8,128)(2,1)}), bf16[4,48,2176]{2,1,0:T(8,128)(2,1)S(1)}, u32[]{:S(2)}, u32[]{:S(2)}) async-start(bf16[4,48,2176]{2,1,0:T(8,128)(2,1)} %bitcast.37), calls=%async_computation | async-start | bytes 1671168 | tf_op jit(solution)/shard_map/all_to_all | solution.py:356
  22.0 19.0 %copy-start = (bf16[4096,128]{1,0:T(8,128)(2,1)S(1)}, bf16[4096,128]{1,0:T(8,128)(2,1)}, u32[]{:S(2)}) copy-start(bf16[4096,128]{1,0:T(8,128)(2,1)} %get-tuple-element.31.refs_1_) | copy-start | bytes 3145732
  22.0 14.6 %collective-permute-start = (bf16[2064,128]{1,0:T(8,128)(2,1)S(1)}, bf16[2064,128]{1,0:T(8,128)(2,1)S(1)}, u32[]{:S(2)}, u32[]{:S(2)}) collective-permute-start(bf16[2064,128]{1,0:T(8,128)(2,1)S(1)} %copy-done.3), channel_id=1, source_target_pairs={{0,128},{128,0},{256,384},{384,256},{1,129},{129,1},{257,385},{385... | collective-permute-start | bytes 1585160 | tf_op jit(solution)/shard_map/ppermute | solution.py:285
  36.6 14.7 %collective-permute-start.1 = (bf16[2064,128]{1,0:T(8,128)(2,1)S(1)}, bf16[2064,128]{1,0:T(8,128)(2,1)S(1)}, u32[]{:S(2)}, u32[]{:S(2)}) collective-permute-start(bf16[2064,128]{1,0:T(8,128)(2,1)S(1)} %pick.6.refs_1_), channel_id=1, source_target_pairs={{0,384},{128,256},{256,128},{384,0},{1,385},{129,257},{257,129},{3... | collective-permute-start | bytes 1585160 | tf_op jit(solution)/shard_map/ppermute | solution.py:285
  41.0 24.5 %collective-permute-start.3 = (bf16[4096,128]{1,0:T(8,128)(2,1)S(1)}, bf16[4096,128]{1,0:T(8,128)(2,1)S(1)}, u32[]{:S(2)}, u32[]{:S(2)}) collective-permute-start(bf16[4096,128]{1,0:T(8,128)(2,1)S(1)} %copy-done), channel_id=1, source_target_pairs={{0,128},{128,0},{256,384},{384,256},{1,129},{129,1},{257,385},{385... | collective-permute-start | bytes 3145736 | tf_op jit(solution)/shard_map/ppermute | solution.py:285
  51.4 22.1 %collective-permute-start.2 = (bf16[2064,128]{1,0:T(8,128)(2,1)S(1)}, bf16[2064,128]{1,0:T(8,128)(2,1)}, u32[]{:S(2)}, u32[]{:S(2)}) collective-permute-start(bf16[2064,128]{1,0:T(8,128)(2,1)S(1)} %pick.7.refs_2_.refs_1_), channel_id=1, source_target_pairs={{0,32},{32,0},{64,96},{96,64},{1,33},{33,1},{65,97},{97,65},{2,34}... | collective-permute-start | bytes 1585160 | tf_op jit(solution)/shard_map/ppermute | solution.py:285
  54.1 17.1 %collective-permute-start.6 = (bf16[48,2176]{1,0:T(8,128)(2,1)}, bf16[48,2176]{1,0:T(8,128)(2,1)}, u32[]{:S(2)}, u32[]{:S(2)}) collective-permute-start(bf16[48,2176]{1,0:T(8,128)(2,1)} %get-tuple-element.32.refs_0_), channel_id=1, source_target_pairs={{0,6},{2,4},{4,2},{6,0},{1,7},{3,5},{5,3},{7,1},{8,14},{10,12},{12... | collective-permute-start | bytes 626696 | tf_op jit(solution)/shard_map/ppermute | solution.py:285
  58.7 12.5 %collective-permute-start.5 = (bf16[48,2176]{1,0:T(8,128)(2,1)}, bf16[48,2176]{1,0:T(8,128)(2,1)}, u32[]{:S(2)}, u32[]{:S(2)}) collective-permute-start(bf16[48,2176]{1,0:T(8,128)(2,1)} %get-tuple-element.32.refs_0_), channel_id=1, source_target_pairs={{0,4},{2,6},{4,0},{6,2},{1,5},{3,7},{5,1},{7,3},{8,12},{10,14},{12... | collective-permute-start | bytes 626696 | tf_op jit(solution)/shard_map/ppermute | solution.py:285
  61.0 10.3 %collective-permute-start.4 = (bf16[48,2176]{1,0:T(8,128)(2,1)}, bf16[48,2176]{1,0:T(8,128)(2,1)}, u32[]{:S(2)}, u32[]{:S(2)}) collective-permute-start(bf16[48,2176]{1,0:T(8,128)(2,1)} %get-tuple-element.32.refs_0_), channel_id=1, source_target_pairs={{0,2},{2,0},{4,6},{6,4},{1,3},{3,1},{5,7},{7,5},{8,10},{10,8},{12,... | collective-permute-start | bytes 626696 | tf_op jit(solution)/shard_map/ppermute | solution.py:285
  65.5 1.0 copy-start.1
  66.5 1.2 copy-start.2
  67.8 37.7 %collective-permute-start.12 = (bf16[4096,128]{1,0:T(8,128)(2,1)S(1)}, bf16[4096,128]{1,0:T(8,128)(2,1)}, u32[]{:S(2)}, u32[]{:S(2)}) collective-permute-start(bf16[4096,128]{1,0:T(8,128)(2,1)S(1)} %pick.8.refs_2_.own_ref), channel_id=1, source_target_pairs={{0,384},{128,256},{256,128},{384,0},{1,385},{129,257},{257,129},{3... | collective-permute-start | bytes 3145736 | tf_op jit(solution)/shard_map/ppermute | solution.py:285
  73.5 5.8 %copy-start.7 = (s32[5]{0:T(128)S(1)}, s32[5]{0:T(128)}, u32[]{:S(2)}) copy-start(s32[5]{0:T(128)} %stack.23.info_ref) | copy-start | bytes 64
  74.6 26.7 %collective-permute-start.7 = (bf16[2064,128]{1,0:T(8,128)(2,1)S(1)}, bf16[2064,128]{1,0:T(8,128)(2,1)S(1)}, u32[]{:S(2)}, u32[]{:S(2)}) collective-permute-start(bf16[2064,128]{1,0:T(8,128)(2,1)S(1)} %pick.9.refs_0_.refs_1_), channel_id=1, source_target_pairs={{0,64},{32,96},{64,0},{96,32},{1,65},{33,97},{65,1},{97,33},{2,66}... | collective-permute-start | bytes 1585160 | tf_op jit(solution)/shard_map/ppermute | solution.py:285
  79.9 32.7 %collective-permute-start.11 = (bf16[144,2176]{1,0:T(8,128)(2,1)S(1)}, bf16[144,2176]{1,0:T(8,128)(2,1)S(1)}, u32[]{:S(2)}, u32[]{:S(2)}) collective-permute-start(bf16[144,2176]{1,0:T(8,128)(2,1)S(1)} %others.1.refs_2_.refs_4_), channel_id=1, source_target_pairs={{0,6},{2,4},{4,2},{6,0},{1,7},{3,5},{5,3},{7,1},{8,14},{10,12},{12... | collective-permute-start | bytes 1880072 | tf_op jit(solution)/shard_map/ppermute | solution.py:285
  84.5 28.1 %collective-permute-start.10 = (bf16[144,2176]{1,0:T(8,128)(2,1)S(1)}, bf16[144,2176]{1,0:T(8,128)(2,1)S(1)}, u32[]{:S(2)}, u32[]{:S(2)}) collective-permute-start(bf16[144,2176]{1,0:T(8,128)(2,1)S(1)} %others.1.refs_2_.refs_4_), channel_id=1, source_target_pairs={{0,4},{2,6},{4,0},{6,2},{1,5},{3,7},{5,1},{7,3},{8,12},{10,14},{12... | collective-permute-start | bytes 1880072 | tf_op jit(solution)/shard_map/ppermute | solution.py:285
  86.8 27.0 %collective-permute-start.9 = (bf16[144,2176]{1,0:T(8,128)(2,1)S(1)}, bf16[144,2176]{1,0:T(8,128)(2,1)S(1)}, u32[]{:S(2)}, u32[]{:S(2)}) collective-permute-start(bf16[144,2176]{1,0:T(8,128)(2,1)S(1)} %others.1.refs_2_.refs_4_), channel_id=1, source_target_pairs={{0,2},{2,0},{4,6},{6,4},{1,3},{3,1},{5,7},{7,5},{8,10},{10,8},{12,... | collective-permute-start | bytes 1880072 | tf_op jit(solution)/shard_map/ppermute | solution.py:285
  101.4 12.4 %copy-start.6 = (f32[8,256]{1,0:T(8,128)S(1)}, f32[8,256]{1,0:T(8,128)}, u32[]{:S(2)}) copy-start(f32[8,256]{1,0:T(8,128)} %get-tuple-element.26.base_ref) | copy-start | bytes 24580
  101.4 7.4 %collective-permute-start.8 = (bf16[2064,128]{1,0:T(8,128)(2,1)S(1)}, bf16[2064,128]{1,0:T(8,128)(2,1)S(1)}, u32[]{:S(2)}, u32[]{:S(2)}) collective-permute-start(bf16[2064,128]{1,0:T(8,128)(2,1)S(1)} %pick.10.own_w_ref.earlier_ref), channel_id=1, source_target_pairs={{0,1},{1,0},{2,3},{3,2},{4,5},{5,4},{6,7},{7,6},{8,9},{9,8},{10,11... | collective-permute-start | bytes 1585160 | tf_op jit(solution)/shard_map/ppermute | solution.py:285
  106.8 43.3 %collective-permute-start.13 = (bf16[2048,128]{1,0:T(8,128)(2,1)S(1)}, bf16[2048,128]{1,0:T(8,128)(2,1)S(1)}, u32[]{:S(2)}, u32[]{:S(2)}) collective-permute-start(bf16[2048,128]{1,0:T(8,128)(2,1)S(1)} %get-tuple-element.35.refs_2_), channel_id=1, source_target_pairs={{0,32},{32,0},{64,96},{96,64},{1,33},{33,1},{65,97},{97,65},{2,34}... | collective-permute-start | bytes 1572872 | tf_op jit(solution)/shard_map/ppermute | solution.py:285
  108.8 41.4 %collective-permute-start.14 = (bf16[2048,128]{1,0:T(8,128)(2,1)S(1)}, bf16[2048,128]{1,0:T(8,128)(2,1)S(1)}, u32[]{:S(2)}, u32[]{:S(2)}) collective-permute-start(bf16[2048,128]{1,0:T(8,128)(2,1)S(1)} %get-tuple-element.36.refs_3_), channel_id=1, source_target_pairs={{0,64},{32,96},{64,0},{96,32},{1,65},{33,97},{65,1},{97,33},{2,66}... | collective-permute-start | bytes 1572872 | tf_op jit(solution)/shard_map/ppermute | solution.py:285
  116.4 1.6 copy-start.8
  131.6 18.6 %all-to-all-start.2 = ((f32[16,1,256]{2,1,0:T(1,128)}), f32[16,1,256]{2,1,0:T(1,128)S(1)}, u32[]{:S(2)}, u32[]{:S(2)}) async-start(f32[16,1,256]{2,1,0:T(1,128)} %broadcast_in_dim.23), calls=%async_computation.2 | async-start | bytes 32768 | tf_op jit(solution)/shard_map/all_to_all | solution.py:401
  152.4 15.4 %all-to-all-start.3 = ((f32[32,1,256]{2,1,0:T(1,128)}), f32[32,1,256]{2,1,0:T(1,128)S(1)}, u32[]{:S(2)}, u32[]{:S(2)}) async-start(f32[32,1,256]{2,1,0:T(1,128)} %copy.20), calls=%async_computation.3 | async-start | bytes 65536 | tf_op jit(solution)/shard_map/all_to_all | solution.py:407
  160.5 28.1 %collective-permute-start.15 = (bf16[2048,128]{1,0:T(8,128)(2,1)}, bf16[2048,128]{1,0:T(8,128)(2,1)}, u32[]{:S(2)}, u32[]{:S(2)}) collective-permute-start(bf16[2048,128]{1,0:T(8,128)(2,1)} %get-tuple-element.39.up_ref), channel_id=1, source_target_pairs={{0,64},{32,96},{64,0},{96,32},{1,65},{33,97},{65,1},{97,33},{2,66}... | collective-permute-start | bytes 1572872 | tf_op jit(solution)/shard_map/ppermute | solution.py:285
  163.0 26.1 %collective-permute-start.16 = (bf16[2048,128]{1,0:T(8,128)(2,1)}, bf16[2048,128]{1,0:T(8,128)(2,1)}, u32[]{:S(2)}, u32[]{:S(2)}) collective-permute-start(bf16[2048,128]{1,0:T(8,128)(2,1)} %get-tuple-element.40.down_ref), channel_id=1, source_target_pairs={{0,32},{32,0},{64,96},{96,64},{1,33},{33,1},{65,97},{97,65},{2,34}... | collective-permute-start | bytes 1572872 | tf_op jit(solution)/shard_map/ppermute | solution.py:285
  167.8 1.9 copy-start.9
  169.7 6.6 %copy-start.4 = (s32[8192]{0:T(1024)S(1)}, s32[8192]{0:T(1024)}, u32[]{:S(2)}) copy-start(s32[8192]{0:T(1024)} %param.16) | copy-start | bytes 98308
  174.0 15.1 %copy-start.5 = (bf16[2048]{0:T(1024)(128)(2,1)S(1)}, bf16[2048]{0:T(1024)(128)(2,1)}, u32[]{:S(2)}) copy-start(bf16[2048]{0:T(1024)(128)(2,1)} %param.17) | copy-start | bytes 12292
  174.0 15.1 %collective-permute-start.17 = (f32[2056,128]{1,0:T(8,128)S(1)}, f32[2056,128]{1,0:T(8,128)S(1)}, u32[]{:S(2)}, u32[]{:S(2)}) collective-permute-start(f32[2056,128]{1,0:T(8,128)S(1)} %get-tuple-element.45), channel_id=1, source_target_pairs={{0,1},{1,0},{2,3},{3,2},{4,5},{5,4},{6,7},{7,6},{8,9},{9,8},{10,11... | collective-permute-start | bytes 3158024 | tf_op jit(solution)/shard_map/ppermute | solution.py:285

commit v7 on v6

--- a/solution.py
+++ b/solution.py
@@ -285,7 +285,7 @@
     return lax.ppermute(block, axis, [(i, i ^ mask) for i in range(count)])
 
 
-def picks(stages, got, own, *earlier):
+def picks(stages, got, own, *earlier, cost=LIGHT):
     count = len(stages)
     return pl.pallas_call(
         functools.partial(pick_kernel, count),
@@ -293,13 +293,13 @@
         in_specs=[SMEM] + [VMEM] * (2 * count) + [ANY] * len(earlier),
         out_specs=[VMEM] * count,
         compiler_params=PARAMS,
-        cost_estimate=LIGHT,
+        cost_estimate=cost,
         name="pick",
     )(jnp.concatenate([s[2] for s in stages]), *got, *own, *earlier)
 
 
-def pick(stage, got, own, *earlier):
-    return picks([stage], [got], [own], *earlier)[0]
+def pick(stage, got, own, *earlier, cost=LIGHT):
+    return picks([stage], [got], [own], *earlier, cost=cost)[0]
 
 
 def others(info, rows, *earlier):
@@ -360,15 +360,15 @@
     got = swap(weights, *x3[:2])
     held = [own_rows] + [swap(own_rows, "y", d) for d in (1, 2, 3)]
     acc_got = swap(accums, *x1[:2])
-    weights = pick(x3, got, weights)
+    weights = pick(x3, got, weights, *held[1:])
     got = swap(weights, *z1[:2])
     accums = pick(x1, acc_got, accums, weights)
     acc_got = swap(accums, *x3[:2])
-    weights = pick(z1, got, weights, accums, *held[1:])
+    rows = others(info, arrived, weights, accums)
+    held += [rows] + [swap(rows, "y", d) for d in (1, 2, 3)]
+    weights = pick(z1, got, weights, rows, cost=SPACED)
     got = swap(weights, *z2[:2])
-    rows = others(info, arrived, weights)
-    held += [rows] + [swap(rows, "y", d) for d in (1, 2, 3)]
-    weights = pick(z2, got, weights, rows)
+    weights = pick(z2, got, weights)
     other_weights = swap(weights, "c", 1)
     up, down = pl.pallas_call(
         split_kernel,
@@ -397,15 +397,16 @@
     )(info, base, weights, other_weights, *held)
 
     mine = lax.all_to_all(part, ("x", "y"), 0, 0, tiled=True)
-    mine = jnp.broadcast_to(jnp.sum(mine, axis=0, keepdims=True), (16, TOK_DEV))
-    mine = lax.all_to_all(mine, ("zl", "zh"), 0, 0, tiled=True)
-    mine = jnp.broadcast_to(jnp.sum(mine, axis=0, keepdims=True), (32, TOK_DEV))
     up, down = picks([z1, z2], [up_got, down_got], [up, down], mine)
     mine, up, down = lax.optimization_barrier((mine, up, down))
     up_got = swap(up, *z2[:2])
     down_got = swap(down, *z1[:2])
+    mine = jnp.broadcast_to(jnp.sum(mine, axis=0, keepdims=True), (16, TOK_DEV))
+    mine = lax.all_to_all(mine, ("zl", "zh"), 0, 0, tiled=True)
+    mine = jnp.broadcast_to(jnp.sum(mine, axis=0, keepdims=True), (32, TOK_DEV))
     table = lax.all_to_all(mine, ("x", "y", "c"), 0, 0, tiled=True)
 
+    table, up_got, down_got = lax.optimization_barrier((table, up_got, down_got))
     own, send, own_head = pl.pallas_call(
         backward_kernel,
         out_shape=[shape((D, HID_DEV), f32), shape((D + 8, HID_DEV), f32), shape((8, HID_DEV), f32)],

time: 193 us -> 208 us (1.078)
  blocking collectives: 12.8 us -> 28.8 us
  waiting for transfers between devices: 57.7 us -> 51.6 us
  local copies, waits for them, and re-layouts: 7.65 us -> 12 us
    all_to_all x1, blocking collectives: 12.8 us -> 28.8 us  [body(): mine = lax.all_to_all(mine, ('zl', 'zh'), 0, 0, tiled=True)]
    ppermute x18, waiting for transfers between devices: 43.9 us -> 38.1 us  [swap(): return lax.ppermute(block, axis, [(i, i ^ mask) for i in range(count)])]
    all_to_all x1, waiting for transfers between devices: 11.2 us -> 6.37 us  [body(): mine = lax.all_to_all(part, ('x', 'y'), 0, 0, tiled=True)]
    all_to_all x1, waiting for transfers between devices: 2.63 us -> 7.19 us  [body(): table = lax.all_to_all(mine, ('x', 'y', 'c'), 0, 0, tiled=True)]
    unnamed x23 -> x42, local copies, waits for them, and re-layouts: 5.75 us -> 10.2 us
    all_to_all x1, starting transfers between devices: 7.26 us -> 4.56 us  [body(): mine = lax.all_to_all(part, ('x', 'y'), 0, 0, tiled=True)]
    all_to_all x1, starting transfers between devices: 7.97 us -> 10.7 us  [body(): table = lax.all_to_all(mine, ('x', 'y', 'c'), 0, 0, tiled=True)]
  transfers between devices with their start and end apart: 21 -> 21, of which waited for: 10 -> 9; matrix products, arithmetic and copies ran while one was open for 1% -> 1% of each run, Pallas kernels for 7% -> 6%
where the time goes in v7:
time: 208 us; the launch traced here: 207 us
  starting transfers between devices  85.7 us (41%)
  waiting for transfers between devices  51.6 us (25%)
  blocking collectives  28.8 us (14%)
  Pallas kernels  23.9 us (11%)
  local copies, waits for them, and re-layouts  12 us (6%)
  between operations  3.7 us (2%)
    ppermute x18, starting transfers between devices, swap(): return lax.ppermute(block, axis, [(i, i ^ mask) for i in range(count)])  54.7 us
    ppermute x18, waiting for transfers between devices, swap(): return lax.ppermute(block, axis, [(i, i ^ mask) for i in range(count)])  38.1 us
    all_to_all x1, blocking collectives, body(): mine = lax.all_to_all(mine, ('zl', 'zh'), 0, 0, tiled=True)  28.8 us
    all_to_all x1, starting transfers between devices, body(): arrived = lax.all_to_all(sent, 'zh', 0, 0, tiled=True)  15.8 us
    all_to_all x1, starting transfers between devices, body(): table = lax.all_to_all(mine, ('x', 'y', 'c'), 0, 0, tiled=True)  10.7 us
    unnamed x42, local copies, waits for them, and re-layouts  10.2 us
    all_to_all x1, waiting for transfers between devices, body(): table = lax.all_to_all(mine, ('x', 'y', 'c'), 0, 0, tiled=True)  7.19 us
    all_to_all x1, waiting for transfers between devices, body(): mine = lax.all_to_all(part, ('x', 'y'), 0, 0, tiled=True)  6.37 us
  transfers between devices with their start and end apart: 21, of which 9 were waited for; matrix products, arithmetic and copies ran while one was open for 1% of the time, Pallas kernels for 6%

profile of v7, /device:TPU:1, one launch (start us, length us, event | category | flops | bytes accessed | tf_op | source)
XLA Modules:
  0.0 206.6 jit_solution(578119037843756316)
XLA Ops:
  0.6 0.6 stack.23.info_ref
  1.2 5.0 %dispatch.1 = (bf16[192,2176]{1,0:T(8,128)(2,1)}, bf16[48,2176]{1,0:T(8,128)(2,1)}, f32[8,256]{1,0:T(8,128)}, bf16[2064,128]{1,0:T(8,128)(2,1)}, bf16[4096,128]{1,0:T(8,128)(2,1)}) custom-call(s32[64]{0:T(128)} %group_ref.1, s32[4]{0:T(128)} %mask_ref.1, s32[5]{0:T(128)} %stack.23.info_ref, bf16[256,2048]{1,0:T(8,128)(2,1)} %tok_ref.1, s32[8,256]{1,0:T(8,128)} %bitcast.44, ...), custom_call_target="tpu_custom_call" | custom-call | tf_op jit(solution)/shard_map/dispatch/pallas_call | solution.py:329
  6.2 15.8 %all-to-all-start = ((bf16[4,48,2176]{2,1,0:T(8,128)(2,1)}), bf16[4,48,2176]{2,1,0:T(8,128)(2,1)}, u32[]{:S(2)}, u32[]{:S(2)}) async-start(bf16[4,48,2176]{2,1,0:T(8,128)(2,1)} %bitcast.39), calls=%async_computation | async-start | bytes 1671168 | tf_op jit(solution)/shard_map/all_to_all | solution.py:356
  22.0 3.2 %collective-permute-start = (bf16[2064,128]{1,0:T(8,128)(2,1)S(1)}, bf16[2064,128]{1,0:T(8,128)(2,1)S(1)}, u32[]{:S(2)}, u32[]{:S(2)}) collective-permute-start(bf16[2064,128]{1,0:T(8,128)(2,1)S(1)} %copy-done.7), channel_id=1, source_target_pairs={{0,128},{128,0},{256,384},{384,256},{1,129},{129,1},{257,385},{385... | collective-permute-start | bytes 1585160 | tf_op jit(solution)/shard_map/ppermute | solution.py:285
  25.2 0.6 fusion
  27.2 9.5 %collective-permute-done.refs_0_ = bf16[2064,128]{1,0:T(8,128)(2,1)S(1)} collective-permute-done((bf16[2064,128]{1,0:T(8,128)(2,1)S(1)}, bf16[2064,128]{1,0:T(8,128)(2,1)S(1)}, u32[]{:S(2)}, u32[]{:S(2)}) %collective-permute-start) | collective-permute-done | bytes 528416 | tf_op jit(solution)/shard_map/ppermute | solution.py:285
  36.7 3.1 %collective-permute-start.6 = (bf16[4096,128]{1,0:T(8,128)(2,1)S(1)}, bf16[4096,128]{1,0:T(8,128)(2,1)S(1)}, u32[]{:S(2)}, u32[]{:S(2)}) collective-permute-start(bf16[4096,128]{1,0:T(8,128)(2,1)S(1)} %copy-done), channel_id=1, source_target_pairs={{0,128},{128,0},{256,384},{384,256},{1,129},{129,1},{257,385},{385... | collective-permute-start | bytes 3145736 | tf_op jit(solution)/shard_map/ppermute | solution.py:285
  39.8 3.7 %collective-permute-start.1 = (bf16[2064,128]{1,0:T(8,128)(2,1)S(1)}, bf16[2064,128]{1,0:T(8,128)(2,1)}, u32[]{:S(2)}, u32[]{:S(2)}) collective-permute-start(bf16[2064,128]{1,0:T(8,128)(2,1)S(1)} %pick.6.refs_1_), channel_id=1, source_target_pairs={{0,384},{128,256},{256,128},{384,0},{1,385},{129,257},{257,129},{3... | collective-permute-start | bytes 1585160 | tf_op jit(solution)/shard_map/ppermute | solution.py:285
  43.6 4.6 %collective-permute-start.4 = (bf16[48,2176]{1,0:T(8,128)(2,1)}, bf16[48,2176]{1,0:T(8,128)(2,1)S(1)}, u32[]{:S(2)}, u32[]{:S(2)}) collective-permute-start(bf16[48,2176]{1,0:T(8,128)(2,1)} %get-tuple-element.34.refs_0_), channel_id=1, source_target_pairs={{0,6},{2,4},{4,2},{6,0},{1,7},{3,5},{5,3},{7,1},{8,14},{10,12},{12... | collective-permute-start | bytes 626696 | tf_op jit(solution)/shard_map/ppermute | solution.py:285
  48.2 2.3 %collective-permute-start.3 = (bf16[48,2176]{1,0:T(8,128)(2,1)}, bf16[48,2176]{1,0:T(8,128)(2,1)S(1)}, u32[]{:S(2)}, u32[]{:S(2)}) collective-permute-start(bf16[48,2176]{1,0:T(8,128)(2,1)} %get-tuple-element.34.refs_0_), channel_id=1, source_target_pairs={{0,4},{2,6},{4,0},{6,2},{1,5},{3,7},{5,1},{7,3},{8,12},{10,14},{12... | collective-permute-start | bytes 626696 | tf_op jit(solution)/shard_map/ppermute | solution.py:285
  50.5 2.1 %collective-permute-start.2 = (bf16[48,2176]{1,0:T(8,128)(2,1)}, bf16[48,2176]{1,0:T(8,128)(2,1)S(1)}, u32[]{:S(2)}, u32[]{:S(2)}) collective-permute-start(bf16[48,2176]{1,0:T(8,128)(2,1)} %get-tuple-element.34.refs_0_), channel_id=1, source_target_pairs={{0,2},{2,0},{4,6},{6,4},{1,3},{3,1},{5,7},{7,5},{8,10},{10,8},{12,... | collective-permute-start | bytes 626696 | tf_op jit(solution)/shard_map/ppermute | solution.py:285
  53.3 3.6 %collective-permute-done.3.refs_3_.refs_2_ = bf16[48,2176]{1,0:T(8,128)(2,1)S(1)} collective-permute-done((bf16[48,2176]{1,0:T(8,128)(2,1)}, bf16[48,2176]{1,0:T(8,128)(2,1)S(1)}, u32[]{:S(2)}, u32[]{:S(2)}) %collective-permute-start.3) | collective-permute-done | bytes 208928 | tf_op jit(solution)/shard_map/ppermute | solution.py:285
  56.9 0.7 copy-done.1
  57.6 2.3 %collective-permute-done.2.refs_2_.refs_1_ = bf16[48,2176]{1,0:T(8,128)(2,1)S(1)} collective-permute-done((bf16[48,2176]{1,0:T(8,128)(2,1)}, bf16[48,2176]{1,0:T(8,128)(2,1)S(1)}, u32[]{:S(2)}, u32[]{:S(2)}) %collective-permute-start.2) | collective-permute-done | bytes 208928 | tf_op jit(solution)/shard_map/ppermute | solution.py:285
  59.9 0.7 copy-done.4
  60.6 0.9 copy-done.2
  61.5 0.9 copy-done.5
  62.5 1.1 pick.7.refs_2_.refs_0_.refs_1_
  63.5 2.6 %collective-permute-start.5 = (bf16[2064,128]{1,0:T(8,128)(2,1)S(1)}, bf16[2064,128]{1,0:T(8,128)(2,1)}, u32[]{:S(2)}, u32[]{:S(2)}) collective-permute-start(bf16[2064,128]{1,0:T(8,128)(2,1)S(1)} %pick.7.refs_2_.refs_0_.refs_1_), channel_id=1, source_target_pairs={{0,32},{32,0},{64,96},{96,64},{1,33},{33,1},{65,97},{97,65},{2,34}... | collective-permute-start | bytes 1585160 | tf_op jit(solution)/shard_map/ppermute | solution.py:285
  66.2 1.1 pick.8.refs_1_.own_ref
  67.3 2.7 %collective-permute-start.12 = (bf16[4096,128]{1,0:T(8,128)(2,1)}, bf16[4096,128]{1,0:T(8,128)(2,1)}, u32[]{:S(2)}, u32[]{:S(2)}) collective-permute-start(bf16[4096,128]{1,0:T(8,128)(2,1)} %pick.8.refs_1_.own_ref), channel_id=1, source_target_pairs={{0,384},{128,256},{256,128},{384,0},{1,385},{129,257},{257,129},{3... | collective-permute-start | bytes 3145736 | tf_op jit(solution)/shard_map/ppermute | solution.py:285
  69.9 0.0 all-to-all-done
  70.0 1.2 others.1.refs_2_.refs_4_
  71.2 5.3 %collective-permute-done.5.refs_0_ = bf16[2064,128]{1,0:T(8,128)(2,1)} collective-permute-done((bf16[2064,128]{1,0:T(8,128)(2,1)S(1)}, bf16[2064,128]{1,0:T(8,128)(2,1)}, u32[]{:S(2)}, u32[]{:S(2)}) %collective-permute-start.5) | collective-permute-done | bytes 528416 | tf_op jit(solution)/shard_map/ppermute | solution.py:285
  76.5 1.1 pick.9.refs_1_
  77.5 3.1 %collective-permute-start.7 = (bf16[2064,128]{1,0:T(8,128)(2,1)S(1)}, bf16[2064,128]{1,0:T(8,128)(2,1)S(1)}, u32[]{:S(2)}, u32[]{:S(2)}) collective-permute-start(bf16[2064,128]{1,0:T(8,128)(2,1)S(1)} %pick.9.refs_1_), channel_id=1, source_target_pairs={{0,64},{32,96},{64,0},{96,32},{1,65},{33,97},{65,1},{97,33},{2,66}... | collective-permute-start | bytes 1585160 | tf_op jit(solution)/shard_map/ppermute | solution.py:285
  81.3 2.4 %collective-permute-start.11 = (bf16[144,2176]{1,0:T(8,128)(2,1)S(1)}, bf16[144,2176]{1,0:T(8,128)(2,1)S(1)}, u32[]{:S(2)}, u32[]{:S(2)}) collective-permute-start(bf16[144,2176]{1,0:T(8,128)(2,1)S(1)} %others.1.refs_2_.refs_4_), channel_id=1, source_target_pairs={{0,6},{2,4},{4,2},{6,0},{1,7},{3,5},{5,3},{7,1},{8,14},{10,12},{12... | collective-permute-start | bytes 1880072 | tf_op jit(solution)/shard_map/ppermute | solution.py:285
  83.7 3.8 %collective-permute-start.10 = (bf16[144,2176]{1,0:T(8,128)(2,1)S(1)}, bf16[144,2176]{1,0:T(8,128)(2,1)S(1)}, u32[]{:S(2)}, u32[]{:S(2)}) collective-permute-start(bf16[144,2176]{1,0:T(8,128)(2,1)S(1)} %others.1.refs_2_.refs_4_), channel_id=1, source_target_pairs={{0,4},{2,6},{4,0},{6,2},{1,5},{3,7},{5,1},{7,3},{8,12},{10,14},{12... | collective-permute-start | bytes 1880072 | tf_op jit(solution)/shard_map/ppermute | solution.py:285
  87.6 2.7 %collective-permute-start.9 = (bf16[144,2176]{1,0:T(8,128)(2,1)S(1)}, bf16[144,2176]{1,0:T(8,128)(2,1)S(1)}, u32[]{:S(2)}, u32[]{:S(2)}) collective-permute-start(bf16[144,2176]{1,0:T(8,128)(2,1)S(1)} %others.1.refs_2_.refs_4_), channel_id=1, source_target_pairs={{0,2},{2,0},{4,6},{6,4},{1,3},{3,1},{5,7},{7,5},{8,10},{10,8},{12,... | collective-permute-start | bytes 1880072 | tf_op jit(solution)/shard_map/ppermute | solution.py:285
  90.3 14.8 %collective-permute-done.7.refs_0_ = bf16[2064,128]{1,0:T(8,128)(2,1)S(1)} collective-permute-done((bf16[2064,128]{1,0:T(8,128)(2,1)S(1)}, bf16[2064,128]{1,0:T(8,128)(2,1)S(1)}, u32[]{:S(2)}, u32[]{:S(2)}) %collective-permute-start.7) | collective-permute-done | bytes 528416 | tf_op jit(solution)/shard_map/ppermute | solution.py:285
  105.1 0.0 copy-start.10
  105.2 3.1 %collective-permute-start.8 = (bf16[2064,128]{1,0:T(8,128)(2,1)S(1)}, bf16[2064,128]{1,0:T(8,128)(2,1)S(1)}, u32[]{:S(2)}, u32[]{:S(2)}) collective-permute-start(bf16[2064,128]{1,0:T(8,128)(2,1)S(1)} %pick.10.own_w_ref.earlier_ref), channel_id=1, source_target_pairs={{0,1},{1,0},{2,3},{3,2},{4,5},{5,4},{6,7},{7,6},{8,9},{9,8},{10,11... | collective-permute-start | bytes 1585160 | tf_op jit(solution)/shard_map/ppermute | solution.py:285
  108.2 1.6 pick_split.1
  109.9 0.0 copy-start.8
  109.9 1.9 collective-permute-start.13
  111.8 3.8 %collective-permute-start.14 = (bf16[2048,128]{1,0:T(8,128)(2,1)S(1)}, bf16[2048,128]{1,0:T(8,128)(2,1)}, u32[]{:S(2)}, u32[]{:S(2)}) collective-permute-start(bf16[2048,128]{1,0:T(8,128)(2,1)S(1)} %get-tuple-element.39.refs_3_), channel_id=1, source_target_pairs={{0,64},{32,96},{64,0},{96,32},{1,65},{33,97},{65,1},{97,33},{2,66}... | collective-permute-start | bytes 1572872 | tf_op jit(solution)/shard_map/ppermute | solution.py:285
  115.7 0.0 collective-permute-done.9.refs_5_
  115.7 0.0 collective-permute-done.8.other_w_ref
  115.7 1.9 forward.1
  117.7 1.6 copy-done.15
  119.3 1.0 copy-done.17
  120.4 0.6 copy.16
  121.0 4.6 %all-to-all-start.1 = ((f32[16,1,256]{2,1,0:T(1,128)}), f32[16,1,256]{2,1,0:T(1,128)S(1)}, u32[]{:S(2)}, u32[]{:S(2)}) async-start(f32[16,1,256]{2,1,0:T(1,128)} %copy.16), calls=%async_computation.1 | async-start | bytes 32768 | tf_op jit(solution)/shard_map/all_to_all | solution.py:399
  125.5 0.1 pad_add_fusion.1.take_ref
  125.6 6.4 %all-to-all-done.1 = f32[16,1,256]{2,1,0:T(1,128)S(1)} async-done(((f32[16,1,256]{2,1,0:T(1,128)}), f32[16,1,256]{2,1,0:T(1,128)S(1)}, u32[]{:S(2)}, u32[]{:S(2)}) %all-to-all-start.1) | async-done | bytes 16416 | tf_op jit(solution)/shard_map/all_to_all | solution.py:399
  132.0 2.1 collective-permute-done.13.refs_0_
  134.1 0.5 collective-permute-done.14.refs_1_
  134.6 1.0 copy-done.9
  135.6 1.3 pick.11
  136.9 5.1 %collective-permute-start.15 = (bf16[2048,128]{1,0:T(8,128)(2,1)S(1)}, bf16[2048,128]{1,0:T(8,128)(2,1)S(1)}, u32[]{:S(2)}, u32[]{:S(2)}) collective-permute-start(bf16[2048,128]{1,0:T(8,128)(2,1)S(1)} %get-tuple-element.42.up_ref), channel_id=1, source_target_pairs={{0,64},{32,96},{64,0},{96,32},{1,65},{33,97},{65,1},{97,33},{2,66}... | collective-permute-start | bytes 1572872 | tf_op jit(solution)/shard_map/ppermute | solution.py:285
  142.1 1.9 collective-permute-start.16
  144.0 28.8 %all_to_all.37 = f32[16,1,256]{2,1,0:T(1,128)S(1)} all-to-all(f32[16,1,256]{2,1,0:T(1,128)S(1)} %broadcast_in_dim.23), channel_id=1, replica_groups=mesh['x'=4,'zl'=4,'zh'=4,'y'=4,'c'=2] {'zl','zh'}, dimensions={0} | all-to-all | bytes 32768 | tf_op jit(solution)/shard_map/all_to_all | solution.py:405
  172.9 0.6 broadcast_in_dim.24
  173.5 10.7 %all-to-all-start.3 = ((f32[32,1,256]{2,1,0:T(1,128)}), f32[32,1,256]{2,1,0:T(1,128)S(1)}, u32[]{:S(2)}, u32[]{:S(2)}) async-start(f32[32,1,256]{2,1,0:T(1,128)} %broadcast_in_dim.24), calls=%async_computation.3 | async-start | bytes 65536 | tf_op jit(solution)/shard_map/all_to_all | solution.py:407
  184.2 0.1 pad_add_fusion.take_ref
  184.3 7.2 %all-to-all-done.3 = f32[32,1,256]{2,1,0:T(1,128)S(1)} async-done(((f32[32,1,256]{2,1,0:T(1,128)}), f32[32,1,256]{2,1,0:T(1,128)S(1)}, u32[]{:S(2)}, u32[]{:S(2)}) %all-to-all-start.3) | async-done | bytes 32800 | tf_op jit(solution)/shard_map/all_to_all | solution.py:407
  191.5 0.0 collective-permute-done.15.up_got_ref
  191.5 1.9 copy-done.16
  193.4 1.3 copy-done.18
  194.6 4.2 %backward.1 = (f32[2048,128]{1,0:T(8,128)S(1)}, f32[2056,128]{1,0:T(8,128)S(1)}, f32[8,128]{1,0:T(8,128)S(1)}) custom-call(s32[5]{0:T(128)S(1)} %copy-done.14, f32[32,256]{1,0:T(8,128)S(1)} %bitcast.34, bf16[768,2048]{1,0:T(8,128)(2,1)S(1)} %copy-done.16, f32[776,384]{1,0:T(8,128)S(1)} %copy-done.18), custom_call_target="tpu_custom_call" | custom-call | flops 99999997952 | tf_op jit(solution)/shard_map/backward/pallas_call | solution.py:410
  198.9 0.0 copy-start.12
  198.9 2.3 %collective-permute-start.17 = (f32[2056,128]{1,0:T(8,128)S(1)}, f32[2056,128]{1,0:T(8,128)S(1)}, u32[]{:S(2)}, u32[]{:S(2)}) collective-permute-start(f32[2056,128]{1,0:T(8,128)S(1)} %get-tuple-element.51), channel_id=1, source_target_pairs={{0,1},{1,0},{2,3},{3,2},{4,5},{5,4},{6,7},{7,6},{8,9},{9,8},{10,11... | collective-permute-start | bytes 3158024 | tf_op jit(solution)/shard_map/ppermute | solution.py:285
  201.2 3.4 %loss.1 = f32[1,128]{1,0:T(1,128)} custom-call(f32[32,256]{1,0:T(8,128)S(1)} %bitcast.35, s32[64,128]{1,0:T(8,128)S(1)} %bitcast.33), custom_call_target="tpu_custom_call" | custom-call | flops 99999997952 | tf_op jit(solution)/shard_map/loss/pallas_call | solution.py:420
  204.6 2.0 final.1
  (43 shorter events, 0.2 us)
Async XLA Ops:
  6.2 15.8 %copy-start.7 = (bf16[2064,128]{1,0:T(8,128)(2,1)S(1)}, bf16[2064,128]{1,0:T(8,128)(2,1)}, u32[]{:S(2)}) copy-start(bf16[2064,128]{1,0:T(8,128)(2,1)} %get-tuple-element.30.refs_1_) | copy-start | bytes 1585156
  6.2 19.0 %copy-start.19 = (s32[4]{0:T(128)S(1)}, s32[4]{0:T(128)}, u32[]{:S(2)}) copy-start(s32[4]{0:T(128)} %mask_ref.1) | copy-start | bytes 52
  6.2 63.7 %all-to-all-start = ((bf16[4,48,2176]{2,1,0:T(8,128)(2,1)}), bf16[4,48,2176]{2,1,0:T(8,128)(2,1)}, u32[]{:S(2)}, u32[]{:S(2)}) async-start(bf16[4,48,2176]{2,1,0:T(8,128)(2,1)} %bitcast.39), calls=%async_computation | async-start | bytes 1671168 | tf_op jit(solution)/shard_map/all_to_all | solution.py:356
  22.0 14.7 %copy-start = (bf16[4096,128]{1,0:T(8,128)(2,1)S(1)}, bf16[4096,128]{1,0:T(8,128)(2,1)}, u32[]{:S(2)}) copy-start(bf16[4096,128]{1,0:T(8,128)(2,1)} %get-tuple-element.36.refs_1_) | copy-start | bytes 3145732
  22.0 14.7 %collective-permute-start = (bf16[2064,128]{1,0:T(8,128)(2,1)S(1)}, bf16[2064,128]{1,0:T(8,128)(2,1)S(1)}, u32[]{:S(2)}, u32[]{:S(2)}) collective-permute-start(bf16[2064,128]{1,0:T(8,128)(2,1)S(1)} %copy-done.7), channel_id=1, source_target_pairs={{0,128},{128,0},{256,384},{384,256},{1,129},{129,1},{257,385},{385... | collective-permute-start | bytes 1585160 | tf_op jit(solution)/shard_map/ppermute | solution.py:285
  36.7 29.5 %collective-permute-start.6 = (bf16[4096,128]{1,0:T(8,128)(2,1)S(1)}, bf16[4096,128]{1,0:T(8,128)(2,1)S(1)}, u32[]{:S(2)}, u32[]{:S(2)}) collective-permute-start(bf16[4096,128]{1,0:T(8,128)(2,1)S(1)} %copy-done), channel_id=1, source_target_pairs={{0,128},{128,0},{256,384},{384,256},{1,129},{129,1},{257,385},{385... | collective-permute-start | bytes 3145736 | tf_op jit(solution)/shard_map/ppermute | solution.py:285
  39.8 20.7 %collective-permute-start.1 = (bf16[2064,128]{1,0:T(8,128)(2,1)S(1)}, bf16[2064,128]{1,0:T(8,128)(2,1)}, u32[]{:S(2)}, u32[]{:S(2)}) collective-permute-start(bf16[2064,128]{1,0:T(8,128)(2,1)S(1)} %pick.6.refs_1_), channel_id=1, source_target_pairs={{0,384},{128,256},{256,128},{384,0},{1,385},{129,257},{257,129},{3... | collective-permute-start | bytes 1585160 | tf_op jit(solution)/shard_map/ppermute | solution.py:285
  43.6 9.7 %collective-permute-start.4 = (bf16[48,2176]{1,0:T(8,128)(2,1)}, bf16[48,2176]{1,0:T(8,128)(2,1)S(1)}, u32[]{:S(2)}, u32[]{:S(2)}) collective-permute-start(bf16[48,2176]{1,0:T(8,128)(2,1)} %get-tuple-element.34.refs_0_), channel_id=1, source_target_pairs={{0,6},{2,4},{4,2},{6,0},{1,7},{3,5},{5,3},{7,1},{8,14},{10,12},{12... | collective-permute-start | bytes 626696 | tf_op jit(solution)/shard_map/ppermute | solution.py:285
  48.2 8.7 %collective-permute-start.3 = (bf16[48,2176]{1,0:T(8,128)(2,1)}, bf16[48,2176]{1,0:T(8,128)(2,1)S(1)}, u32[]{:S(2)}, u32[]{:S(2)}) collective-permute-start(bf16[48,2176]{1,0:T(8,128)(2,1)} %get-tuple-element.34.refs_0_), channel_id=1, source_target_pairs={{0,4},{2,6},{4,0},{6,2},{1,5},{3,7},{5,1},{7,3},{8,12},{10,14},{12... | collective-permute-start | bytes 626696 | tf_op jit(solution)/shard_map/ppermute | solution.py:285
  50.5 9.4 %collective-permute-start.2 = (bf16[48,2176]{1,0:T(8,128)(2,1)}, bf16[48,2176]{1,0:T(8,128)(2,1)S(1)}, u32[]{:S(2)}, u32[]{:S(2)}) collective-permute-start(bf16[48,2176]{1,0:T(8,128)(2,1)} %get-tuple-element.34.refs_0_), channel_id=1, source_target_pairs={{0,2},{2,0},{4,6},{6,4},{1,3},{3,1},{5,7},{7,5},{8,10},{10,8},{12,... | collective-permute-start | bytes 626696 | tf_op jit(solution)/shard_map/ppermute | solution.py:285
  56.9 0.7 copy-start.1
  59.9 0.7 copy-start.4
  60.6 0.9 copy-start.2
  61.5 0.9 copy-start.5
  63.5 6.4 %copy-start.14 = (s32[5]{0:T(128)S(1)}, s32[5]{0:T(128)}, u32[]{:S(2)}) copy-start(s32[5]{0:T(128)} %stack.23.info_ref) | copy-start | bytes 64
  63.5 12.9 %collective-permute-start.5 = (bf16[2064,128]{1,0:T(8,128)(2,1)S(1)}, bf16[2064,128]{1,0:T(8,128)(2,1)}, u32[]{:S(2)}, u32[]{:S(2)}) collective-permute-start(bf16[2064,128]{1,0:T(8,128)(2,1)S(1)} %pick.7.refs_2_.refs_0_.refs_1_), channel_id=1, source_target_pairs={{0,32},{32,0},{64,96},{96,64},{1,33},{33,1},{65,97},{97,65},{2,34}... | collective-permute-start | bytes 1585160 | tf_op jit(solution)/shard_map/ppermute | solution.py:285
  67.3 40.9 %collective-permute-start.12 = (bf16[4096,128]{1,0:T(8,128)(2,1)}, bf16[4096,128]{1,0:T(8,128)(2,1)}, u32[]{:S(2)}, u32[]{:S(2)}) collective-permute-start(bf16[4096,128]{1,0:T(8,128)(2,1)} %pick.8.refs_1_.own_ref), channel_id=1, source_target_pairs={{0,384},{128,256},{256,128},{384,0},{1,385},{129,257},{257,129},{3... | collective-permute-start | bytes 3145736 | tf_op jit(solution)/shard_map/ppermute | solution.py:285
  77.5 27.5 %collective-permute-start.7 = (bf16[2064,128]{1,0:T(8,128)(2,1)S(1)}, bf16[2064,128]{1,0:T(8,128)(2,1)S(1)}, u32[]{:S(2)}, u32[]{:S(2)}) collective-permute-start(bf16[2064,128]{1,0:T(8,128)(2,1)S(1)} %pick.9.refs_1_), channel_id=1, source_target_pairs={{0,64},{32,96},{64,0},{96,32},{1,65},{33,97},{65,1},{97,33},{2,66}... | collective-permute-start | bytes 1585160 | tf_op jit(solution)/shard_map/ppermute | solution.py:285
  81.3 30.5 %collective-permute-start.11 = (bf16[144,2176]{1,0:T(8,128)(2,1)S(1)}, bf16[144,2176]{1,0:T(8,128)(2,1)S(1)}, u32[]{:S(2)}, u32[]{:S(2)}) collective-permute-start(bf16[144,2176]{1,0:T(8,128)(2,1)S(1)} %others.1.refs_2_.refs_4_), channel_id=1, source_target_pairs={{0,6},{2,4},{4,2},{6,0},{1,7},{3,5},{5,3},{7,1},{8,14},{10,12},{12... | collective-permute-start | bytes 1880072 | tf_op jit(solution)/shard_map/ppermute | solution.py:285
  83.7 31.9 %collective-permute-start.10 = (bf16[144,2176]{1,0:T(8,128)(2,1)S(1)}, bf16[144,2176]{1,0:T(8,128)(2,1)S(1)}, u32[]{:S(2)}, u32[]{:S(2)}) collective-permute-start(bf16[144,2176]{1,0:T(8,128)(2,1)S(1)} %others.1.refs_2_.refs_4_), channel_id=1, source_target_pairs={{0,4},{2,6},{4,0},{6,2},{1,5},{3,7},{5,1},{7,3},{8,12},{10,14},{12... | collective-permute-start | bytes 1880072 | tf_op jit(solution)/shard_map/ppermute | solution.py:285
  87.6 28.1 %collective-permute-start.9 = (bf16[144,2176]{1,0:T(8,128)(2,1)S(1)}, bf16[144,2176]{1,0:T(8,128)(2,1)S(1)}, u32[]{:S(2)}, u32[]{:S(2)}) collective-permute-start(bf16[144,2176]{1,0:T(8,128)(2,1)S(1)} %others.1.refs_2_.refs_4_), channel_id=1, source_target_pairs={{0,2},{2,0},{4,6},{6,4},{1,3},{3,1},{5,7},{7,5},{8,10},{10,8},{12,... | collective-permute-start | bytes 1880072 | tf_op jit(solution)/shard_map/ppermute | solution.py:285
  105.1 10.6 %copy-start.3 = (bf16[48,2176]{1,0:T(8,128)(2,1)S(1)}, bf16[48,2176]{1,0:T(8,128)(2,1)}, u32[]{:S(2)}) copy-start(bf16[48,2176]{1,0:T(8,128)(2,1)} %copy-done.1) | copy-start | bytes 626692
  105.1 10.6 %copy-start.6 = (bf16[48,2176]{1,0:T(8,128)(2,1)S(1)}, bf16[48,2176]{1,0:T(8,128)(2,1)}, u32[]{:S(2)}) copy-start(bf16[48,2176]{1,0:T(8,128)(2,1)} %copy-done.4) | copy-start | bytes 626692
  105.1 10.6 %copy-start.10 = (bf16[48,2176]{1,0:T(8,128)(2,1)S(1)}, bf16[48,2176]{1,0:T(8,128)(2,1)}, u32[]{:S(2)}) copy-start(bf16[48,2176]{1,0:T(8,128)(2,1)} %get-tuple-element.34.refs_0_) | copy-start | bytes 626692
  105.2 10.6 %copy-start.13 = (f32[8,256]{1,0:T(8,128)S(1)}, f32[8,256]{1,0:T(8,128)}, u32[]{:S(2)}) copy-start(f32[8,256]{1,0:T(8,128)} %get-tuple-element.29.base_ref) | copy-start | bytes 24580
  105.2 10.5 %collective-permute-start.8 = (bf16[2064,128]{1,0:T(8,128)(2,1)S(1)}, bf16[2064,128]{1,0:T(8,128)(2,1)S(1)}, u32[]{:S(2)}, u32[]{:S(2)}) collective-permute-start(bf16[2064,128]{1,0:T(8,128)(2,1)S(1)} %pick.10.own_w_ref.earlier_ref), channel_id=1, source_target_pairs={{0,1},{1,0},{2,3},{3,2},{4,5},{5,4},{6,7},{7,6},{8,9},{9,8},{10,11... | collective-permute-start | bytes 1585160 | tf_op jit(solution)/shard_map/ppermute | solution.py:285
  109.9 7.8 %copy-start.8 = (bf16[2048,128]{1,0:T(8,128)(2,1)}, bf16[2048,128]{1,0:T(8,128)(2,1)S(1)}, u32[]{:S(2)}) copy-start(bf16[2048,128]{1,0:T(8,128)(2,1)S(1)} %get-tuple-element.39.refs_3_) | copy-start | bytes 1572868
  109.9 24.2 %collective-permute-start.13 = (bf16[2048,128]{1,0:T(8,128)(2,1)S(1)}, bf16[2048,128]{1,0:T(8,128)(2,1)}, u32[]{:S(2)}, u32[]{:S(2)}) collective-permute-start(bf16[2048,128]{1,0:T(8,128)(2,1)S(1)} %get-tuple-element.38.refs_2_), channel_id=1, source_target_pairs={{0,32},{32,0},{64,96},{96,64},{1,33},{33,1},{65,97},{97,65},{2,34}... | collective-permute-start | bytes 1572872 | tf_op jit(solution)/shard_map/ppermute | solution.py:285
  111.8 22.8 %collective-permute-start.14 = (bf16[2048,128]{1,0:T(8,128)(2,1)S(1)}, bf16[2048,128]{1,0:T(8,128)(2,1)}, u32[]{:S(2)}, u32[]{:S(2)}) collective-permute-start(bf16[2048,128]{1,0:T(8,128)(2,1)S(1)} %get-tuple-element.39.refs_3_), channel_id=1, source_target_pairs={{0,64},{32,96},{64,0},{96,32},{1,65},{33,97},{65,1},{97,33},{2,66}... | collective-permute-start | bytes 1572872 | tf_op jit(solution)/shard_map/ppermute | solution.py:285
  117.7 1.6 copy-start.15
  119.3 1.0 copy-start.17
  121.0 11.0 %all-to-all-start.1 = ((f32[16,1,256]{2,1,0:T(1,128)}), f32[16,1,256]{2,1,0:T(1,128)S(1)}, u32[]{:S(2)}, u32[]{:S(2)}) async-start(f32[16,1,256]{2,1,0:T(1,128)} %copy.16), calls=%async_computation.1 | async-start | bytes 32768 | tf_op jit(solution)/shard_map/all_to_all | solution.py:399
  134.6 1.0 copy-start.9
  136.9 54.5 %collective-permute-start.15 = (bf16[2048,128]{1,0:T(8,128)(2,1)S(1)}, bf16[2048,128]{1,0:T(8,128)(2,1)S(1)}, u32[]{:S(2)}, u32[]{:S(2)}) collective-permute-start(bf16[2048,128]{1,0:T(8,128)(2,1)S(1)} %get-tuple-element.42.up_ref), channel_id=1, source_target_pairs={{0,64},{32,96},{64,0},{96,32},{1,65},{33,97},{65,1},{97,33},{2,66}... | collective-permute-start | bytes 1572872 | tf_op jit(solution)/shard_map/ppermute | solution.py:285
  142.1 49.4 %collective-permute-start.16 = (bf16[2048,128]{1,0:T(8,128)(2,1)S(1)}, bf16[2048,128]{1,0:T(8,128)(2,1)S(1)}, u32[]{:S(2)}, u32[]{:S(2)}) collective-permute-start(bf16[2048,128]{1,0:T(8,128)(2,1)S(1)} %get-tuple-element.44.down_ref), channel_id=1, source_target_pairs={{0,32},{32,0},{64,96},{96,64},{1,33},{33,1},{65,97},{97,65},{2,34}... | collective-permute-start | bytes 1572872 | tf_op jit(solution)/shard_map/ppermute | solution.py:285
  173.5 17.9 %all-to-all-start.3 = ((f32[32,1,256]{2,1,0:T(1,128)}), f32[32,1,256]{2,1,0:T(1,128)S(1)}, u32[]{:S(2)}, u32[]{:S(2)}) async-start(f32[32,1,256]{2,1,0:T(1,128)} %broadcast_in_dim.24), calls=%async_computation.3 | async-start | bytes 65536 | tf_op jit(solution)/shard_map/all_to_all | solution.py:407
  191.5 1.9 copy-start.16
  193.4 1.3 copy-start.18
  194.6 6.6 %copy-start.11 = (s32[8192]{0:T(1024)S(1)}, s32[8192]{0:T(1024)}, u32[]{:S(2)}) copy-start(s32[8192]{0:T(1024)} %param.16) | copy-start | bytes 98308
  198.9 5.7 %copy-start.12 = (bf16[2048]{0:T(1024)(128)(2,1)S(1)}, bf16[2048]{0:T(1024)(128)(2,1)}, u32[]{:S(2)}) copy-start(bf16[2048]{0:T(1024)(128)(2,1)} %param.17) | copy-start | bytes 12292
  198.9 5.7 %collective-permute-start.17 = (f32[2056,128]{1,0:T(8,128)S(1)}, f32[2056,128]{1,0:T(8,128)S(1)}, u32[]{:S(2)}, u32[]{:S(2)}) collective-permute-start(f32[2056,128]{1,0:T(8,128)S(1)} %get-tuple-element.51), channel_id=1, source_target_pairs={{0,1},{1,0},{2,3},{3,2},{4,5},{5,4},{6,7},{7,6},{8,9},{9,8},{10,11... | collective-permute-start | bytes 3158024 | tf_op jit(solution)/shard_map/ppermute | solution.py:285

commit v8 on v6

--- a/solution.py
+++ b/solution.py
@@ -21,6 +21,7 @@
 bf16 = jnp.bfloat16
 VMEM = pl.BlockSpec(memory_space=pltpu.VMEM)
 SMEM = pl.BlockSpec(memory_space=pltpu.SMEM)
+WHOLE = pltpu.CompilerParams(vmem_limit_bytes=62 * 1024 * 1024)
 PARAMS = pltpu.CompilerParams(vmem_limit_bytes=24 * 1024 * 1024)
 NT = (((1,), (1,)), ((), ()))
 
@@ -285,21 +286,21 @@
     return lax.ppermute(block, axis, [(i, i ^ mask) for i in range(count)])
 
 
-def picks(stages, got, own, *earlier):
+def picks(stages, got, own, *earlier, params=PARAMS):
     count = len(stages)
     return pl.pallas_call(
         functools.partial(pick_kernel, count),
         out_shape=[shape(o.shape, o.dtype) for o in own],
         in_specs=[SMEM] + [VMEM] * (2 * count) + [ANY] * len(earlier),
         out_specs=[VMEM] * count,
-        compiler_params=PARAMS,
+        compiler_params=params,
         cost_estimate=LIGHT,
         name="pick",
     )(jnp.concatenate([s[2] for s in stages]), *got, *own, *earlier)
 
 
-def pick(stage, got, own, *earlier):
-    return picks([stage], [got], [own], *earlier)[0]
+def pick(stage, got, own, *earlier, params=PARAMS):
+    return picks([stage], [got], [own], *earlier, params=params)[0]
 
 
 def others(info, rows, *earlier):
@@ -411,7 +412,7 @@
         out_shape=[shape((D, HID_DEV), f32), shape((D + 8, HID_DEV), f32), shape((8, HID_DEV), f32)],
         in_specs=[SMEM] + [VMEM] * 3,
         out_specs=[VMEM] * 3,
-        compiler_params=PARAMS,
+        compiler_params=WHOLE,
         cost_estimate=SPACED,
         name="backward",
     )(info, table, xs, keep)

time: 193 us -> 194 us (level)
  Pallas kernels: 22.9 us -> 26 us
    pallas_call x1, Pallas kernels: 4.27 us -> 7.31 us  [body(): pl.pallas_call(backward_kernel, out_shape=[shape((D, HID_DEV), f32), shap...]
    unnamed x23 -> x29, local copies, waits for them, and re-layouts: 5.75 us -> 5.51 us
  transfers between devices with their start and end apart: 21 -> 21, of which waited for: 10 -> 10; matrix products, arithmetic and copies ran while one was open for 1% -> 1% of each run, Pallas kernels for 7% -> 9%
where the time goes in v8:
time: 194 us; the launch traced here: 193 us
  starting transfers between devices  86 us (44%)
  waiting for transfers between devices  56.7 us (29%)
  Pallas kernels  26 us (13%)
  blocking collectives  12.8 us (7%)
  local copies, waits for them, and re-layouts  7.37 us (4%)
  between operations  3.28 us (2%)
    ppermute x18, starting transfers between devices, swap(): return lax.ppermute(block, axis, [(i, i ^ mask) for i in range(count)])  55 us
    ppermute x18, waiting for transfers between devices, swap(): return lax.ppermute(block, axis, [(i, i ^ mask) for i in range(count)])  42.9 us
    all_to_all x1, starting transfers between devices, body(): arrived = lax.all_to_all(sent, 'zh', 0, 0, tiled=True)  15.8 us
    all_to_all x1, blocking collectives, body(): mine = lax.all_to_all(part, ('x', 'y'), 0, 0, tiled=True)  12.8 us
    all_to_all x1, waiting for transfers between devices, body(): mine = lax.all_to_all(mine, ('zl', 'zh'), 0, 0, tiled=True)  11.2 us
    all_to_all x1, starting transfers between devices, body(): table = lax.all_to_all(mine, ('x', 'y', 'c'), 0, 0, tiled=True)  7.97 us
    pallas_call x1, Pallas kernels, body(): pl.pallas_call(backward_kernel, out_shape=[shape((D, HID_DEV), f32), shap...  7.31 us
    all_to_all x1, starting transfers between devices, body(): mine = lax.all_to_all(mine, ('zl', 'zh'), 0, 0, tiled=True)  7.25 us
  transfers between devices with their start and end apart: 21, of which 10 were waited for; matrix products, arithmetic and copies ran while one was open for 1% of the time, Pallas kernels for 9%

profile of v8, /device:TPU:1, one launch (start us, length us, event | category | flops | bytes accessed | tf_op | source)
XLA Modules:
  0.0 193.0 jit_solution(13069195757834201296)
XLA Ops:
  0.6 0.6 stack.23.info_ref
  1.2 5.0 %dispatch.1 = (bf16[192,2176]{1,0:T(8,128)(2,1)}, bf16[48,2176]{1,0:T(8,128)(2,1)}, f32[8,256]{1,0:T(8,128)}, bf16[2064,128]{1,0:T(8,128)(2,1)}, bf16[4096,128]{1,0:T(8,128)(2,1)}) custom-call(s32[64]{0:T(128)} %group_ref.1, s32[4]{0:T(128)} %mask_ref.1, s32[5]{0:T(128)} %stack.23.info_ref, bf16[256,2048]{1,0:T(8,128)(2,1)} %tok_ref.1, s32[8,256]{1,0:T(8,128)} %bitcast.42, ...), custom_call_target="tpu_custom_call" | custom-call | tf_op jit(solution)/shard_map/dispatch/pallas_call | solution.py:330
  6.2 15.8 %all-to-all-start = ((bf16[4,48,2176]{2,1,0:T(8,128)(2,1)}), bf16[4,48,2176]{2,1,0:T(8,128)(2,1)S(1)}, u32[]{:S(2)}, u32[]{:S(2)}) async-start(bf16[4,48,2176]{2,1,0:T(8,128)(2,1)} %bitcast.37), calls=%async_computation | async-start | bytes 1671168 | tf_op jit(solution)/shard_map/all_to_all | solution.py:357
  22.0 3.2 %collective-permute-start = (bf16[2064,128]{1,0:T(8,128)(2,1)S(1)}, bf16[2064,128]{1,0:T(8,128)(2,1)S(1)}, u32[]{:S(2)}, u32[]{:S(2)}) collective-permute-start(bf16[2064,128]{1,0:T(8,128)(2,1)S(1)} %copy-done.4), channel_id=1, source_target_pairs={{0,128},{128,0},{256,384},{384,256},{1,129},{129,1},{257,385},{385... | collective-permute-start | bytes 1585160 | tf_op jit(solution)/shard_map/ppermute | solution.py:286
  25.2 0.6 fusion
  27.0 9.6 %collective-permute-done.refs_0_ = bf16[2064,128]{1,0:T(8,128)(2,1)S(1)} collective-permute-done((bf16[2064,128]{1,0:T(8,128)(2,1)S(1)}, bf16[2064,128]{1,0:T(8,128)(2,1)S(1)}, u32[]{:S(2)}, u32[]{:S(2)}) %collective-permute-start) | collective-permute-done | bytes 528416 | tf_op jit(solution)/shard_map/ppermute | solution.py:286
  36.6 4.4 %collective-permute-start.1 = (bf16[2064,128]{1,0:T(8,128)(2,1)S(1)}, bf16[2064,128]{1,0:T(8,128)(2,1)S(1)}, u32[]{:S(2)}, u32[]{:S(2)}) collective-permute-start(bf16[2064,128]{1,0:T(8,128)(2,1)S(1)} %pick.6.refs_1_), channel_id=1, source_target_pairs={{0,384},{128,256},{256,128},{384,0},{1,385},{129,257},{257,129},{3... | collective-permute-start | bytes 1585160 | tf_op jit(solution)/shard_map/ppermute | solution.py:286
  41.0 1.9 collective-permute-start.3
  42.9 8.4 %collective-permute-done.1.refs_0_ = bf16[2064,128]{1,0:T(8,128)(2,1)S(1)} collective-permute-done((bf16[2064,128]{1,0:T(8,128)(2,1)S(1)}, bf16[2064,128]{1,0:T(8,128)(2,1)S(1)}, u32[]{:S(2)}, u32[]{:S(2)}) %collective-permute-start.1) | collective-permute-done | bytes 528416 | tf_op jit(solution)/shard_map/ppermute | solution.py:286
  51.4 2.7 %collective-permute-start.2 = (bf16[2064,128]{1,0:T(8,128)(2,1)S(1)}, bf16[2064,128]{1,0:T(8,128)(2,1)}, u32[]{:S(2)}, u32[]{:S(2)}) collective-permute-start(bf16[2064,128]{1,0:T(8,128)(2,1)S(1)} %pick.7.refs_2_.refs_1_), channel_id=1, source_target_pairs={{0,32},{32,0},{64,96},{96,64},{1,33},{33,1},{65,97},{97,65},{2,34}... | collective-permute-start | bytes 1585160 | tf_op jit(solution)/shard_map/ppermute | solution.py:286
  54.0 4.6 %collective-permute-start.6 = (bf16[48,2176]{1,0:T(8,128)(2,1)}, bf16[48,2176]{1,0:T(8,128)(2,1)}, u32[]{:S(2)}, u32[]{:S(2)}) collective-permute-start(bf16[48,2176]{1,0:T(8,128)(2,1)} %get-tuple-element.32.refs_0_), channel_id=1, source_target_pairs={{0,6},{2,4},{4,2},{6,0},{1,7},{3,5},{5,3},{7,1},{8,14},{10,12},{12... | collective-permute-start | bytes 626696 | tf_op jit(solution)/shard_map/ppermute | solution.py:286
  58.7 2.3 %collective-permute-start.5 = (bf16[48,2176]{1,0:T(8,128)(2,1)}, bf16[48,2176]{1,0:T(8,128)(2,1)}, u32[]{:S(2)}, u32[]{:S(2)}) collective-permute-start(bf16[48,2176]{1,0:T(8,128)(2,1)} %get-tuple-element.32.refs_0_), channel_id=1, source_target_pairs={{0,4},{2,6},{4,0},{6,2},{1,5},{3,7},{5,1},{7,3},{8,12},{10,14},{12... | collective-permute-start | bytes 626696 | tf_op jit(solution)/shard_map/ppermute | solution.py:286
  60.9 2.1 %collective-permute-start.4 = (bf16[48,2176]{1,0:T(8,128)(2,1)}, bf16[48,2176]{1,0:T(8,128)(2,1)}, u32[]{:S(2)}, u32[]{:S(2)}) collective-permute-start(bf16[48,2176]{1,0:T(8,128)(2,1)} %get-tuple-element.32.refs_0_), channel_id=1, source_target_pairs={{0,2},{2,0},{4,6},{6,4},{1,3},{3,1},{5,7},{7,5},{8,10},{10,8},{12,... | collective-permute-start | bytes 626696 | tf_op jit(solution)/shard_map/ppermute | solution.py:286
  64.2 1.3 collective-permute-done.3.refs_0_
  65.5 1.0 copy-done.1
  66.5 1.2 copy-done.2
  67.7 0.1 pick.8.refs_2_.own_ref
  67.8 3.1 %collective-permute-start.12 = (bf16[4096,128]{1,0:T(8,128)(2,1)S(1)}, bf16[4096,128]{1,0:T(8,128)(2,1)}, u32[]{:S(2)}, u32[]{:S(2)}) collective-permute-start(bf16[4096,128]{1,0:T(8,128)(2,1)S(1)} %pick.8.refs_2_.own_ref), channel_id=1, source_target_pairs={{0,384},{128,256},{256,128},{384,0},{1,385},{129,257},{257,129},{3... | collective-permute-start | bytes 3145736 | tf_op jit(solution)/shard_map/ppermute | solution.py:286
  70.9 0.0 collective-permute-done.6.refs_5_.refs_3_
  70.9 0.0 collective-permute-done.5.refs_4_.refs_2_
  70.9 0.0 collective-permute-done.4.refs_3_.refs_1_
  70.9 2.5 %collective-permute-done.2.refs_0_ = bf16[2064,128]{1,0:T(8,128)(2,1)} collective-permute-done((bf16[2064,128]{1,0:T(8,128)(2,1)S(1)}, bf16[2064,128]{1,0:T(8,128)(2,1)}, u32[]{:S(2)}, u32[]{:S(2)}) %collective-permute-start.2) | collective-permute-done | bytes 528416 | tf_op jit(solution)/shard_map/ppermute | solution.py:286
  73.5 1.1 pick.9.refs_0_.refs_1_
  74.6 4.6 %collective-permute-start.7 = (bf16[2064,128]{1,0:T(8,128)(2,1)S(1)}, bf16[2064,128]{1,0:T(8,128)(2,1)S(1)}, u32[]{:S(2)}, u32[]{:S(2)}) collective-permute-start(bf16[2064,128]{1,0:T(8,128)(2,1)S(1)} %pick.9.refs_0_.refs_1_), channel_id=1, source_target_pairs={{0,64},{32,96},{64,0},{96,32},{1,65},{33,97},{65,1},{97,33},{2,66}... | collective-permute-start | bytes 1585160 | tf_op jit(solution)/shard_map/ppermute | solution.py:286
  79.2 0.0 all-to-all-done
  79.2 0.6 others.1.refs_2_.refs_4_
  79.8 4.6 %collective-permute-start.11 = (bf16[144,2176]{1,0:T(8,128)(2,1)S(1)}, bf16[144,2176]{1,0:T(8,128)(2,1)S(1)}, u32[]{:S(2)}, u32[]{:S(2)}) collective-permute-start(bf16[144,2176]{1,0:T(8,128)(2,1)S(1)} %others.1.refs_2_.refs_4_), channel_id=1, source_target_pairs={{0,6},{2,4},{4,2},{6,0},{1,7},{3,5},{5,3},{7,1},{8,14},{10,12},{12... | collective-permute-start | bytes 1880072 | tf_op jit(solution)/shard_map/ppermute | solution.py:286
  84.5 2.3 %collective-permute-start.10 = (bf16[144,2176]{1,0:T(8,128)(2,1)S(1)}, bf16[144,2176]{1,0:T(8,128)(2,1)S(1)}, u32[]{:S(2)}, u32[]{:S(2)}) collective-permute-start(bf16[144,2176]{1,0:T(8,128)(2,1)S(1)} %others.1.refs_2_.refs_4_), channel_id=1, source_target_pairs={{0,4},{2,6},{4,0},{6,2},{1,5},{3,7},{5,1},{7,3},{8,12},{10,14},{12... | collective-permute-start | bytes 1880072 | tf_op jit(solution)/shard_map/ppermute | solution.py:286
  86.8 2.1 %collective-permute-start.9 = (bf16[144,2176]{1,0:T(8,128)(2,1)S(1)}, bf16[144,2176]{1,0:T(8,128)(2,1)S(1)}, u32[]{:S(2)}, u32[]{:S(2)}) collective-permute-start(bf16[144,2176]{1,0:T(8,128)(2,1)S(1)} %others.1.refs_2_.refs_4_), channel_id=1, source_target_pairs={{0,2},{2,0},{4,6},{6,4},{1,3},{3,1},{5,7},{7,5},{8,10},{10,8},{12,... | collective-permute-start | bytes 1880072 | tf_op jit(solution)/shard_map/ppermute | solution.py:286
  88.9 12.4 %collective-permute-done.7.refs_0_ = bf16[2064,128]{1,0:T(8,128)(2,1)S(1)} collective-permute-done((bf16[2064,128]{1,0:T(8,128)(2,1)S(1)}, bf16[2064,128]{1,0:T(8,128)(2,1)S(1)}, u32[]{:S(2)}, u32[]{:S(2)}) %collective-permute-start.7) | collective-permute-done | bytes 528416 | tf_op jit(solution)/shard_map/ppermute | solution.py:286
  101.4 0.0 copy-start.8
  101.4 4.0 %collective-permute-start.8 = (bf16[2064,128]{1,0:T(8,128)(2,1)S(1)}, bf16[2064,128]{1,0:T(8,128)(2,1)S(1)}, u32[]{:S(2)}, u32[]{:S(2)}) collective-permute-start(bf16[2064,128]{1,0:T(8,128)(2,1)S(1)} %pick.10.own_w_ref.earlier_ref), channel_id=1, source_target_pairs={{0,1},{1,0},{2,3},{3,2},{4,5},{5,4},{6,7},{7,6},{8,9},{9,8},{10,11... | collective-permute-start | bytes 1585160 | tf_op jit(solution)/shard_map/ppermute | solution.py:286
  105.5 0.0 collective-permute-done.12.got_ref
  105.5 1.3 pick_split.1
  106.8 1.9 collective-permute-start.13
  108.7 0.0 collective-permute-done.8.other_w_ref
  108.7 3.8 %collective-permute-start.14 = (bf16[2048,128]{1,0:T(8,128)(2,1)S(1)}, bf16[2048,128]{1,0:T(8,128)(2,1)S(1)}, u32[]{:S(2)}, u32[]{:S(2)}) collective-permute-start(bf16[2048,128]{1,0:T(8,128)(2,1)S(1)} %get-tuple-element.36.refs_3_), channel_id=1, source_target_pairs={{0,64},{32,96},{64,0},{96,32},{1,65},{33,97},{65,1},{97,33},{2,66}... | collective-permute-start | bytes 1572872 | tf_op jit(solution)/shard_map/ppermute | solution.py:286
  112.6 0.0 collective-permute-done.11.refs_7_
  112.6 0.0 collective-permute-done.10.refs_6_
  112.6 1.1 collective-permute-done.9.refs_5_
  113.7 2.7 %forward.1 = (bf16[768,2048]{1,0:T(8,128)(2,1)S(1)}, f32[776,384]{1,0:T(8,128)S(1)}, f32[16,256]{1,0:T(8,128)S(1)}) custom-call(s32[5]{0:T(128)S(1)} %copy-done.9, f32[8,256]{1,0:T(8,128)S(1)} %copy-done.8, bf16[2064,128]{1,0:T(8,128)(2,1)S(1)} %pick.10.own_w_ref.earlier_ref, bf16[2064,128]{1,0:T(8,128)(2,1)S(1)} %collective-permute-done.8.other_w_ref, ...), custom_call_target="tpu_custom_call" | custom-call | tf_op jit(solution)/shard_map/forward/pallas_call | solution.py:386
  116.4 1.6 copy-done.11
  118.0 1.0 copy-done.12
  119.1 12.8 %all_to_all.37 = f32[16,1,256]{2,1,0:T(1,128)S(1)} all-to-all(f32[16,1,256]{2,1,0:T(1,128)S(1)} %copy.18), channel_id=1, replica_groups=mesh['x'=4,'zl'=4,'zh'=4,'y'=4,'c'=2] {'x','y'}, dimensions={0} | all-to-all | bytes 32768 | tf_op jit(solution)/shard_map/all_to_all | solution.py:400
  131.9 0.6 broadcast_in_dim.23
  132.6 7.2 %all-to-all-start.2 = ((f32[16,1,256]{2,1,0:T(1,128)}), f32[16,1,256]{2,1,0:T(1,128)S(1)}, u32[]{:S(2)}, u32[]{:S(2)}) async-start(f32[16,1,256]{2,1,0:T(1,128)} %broadcast_in_dim.23), calls=%async_computation.2 | async-start | bytes 32768 | tf_op jit(solution)/shard_map/all_to_all | solution.py:402
  139.8 0.1 pad_add_fusion.1.take_ref
  139.9 11.2 %all-to-all-done.2 = f32[16,1,256]{2,1,0:T(1,128)S(1)} async-done(((f32[16,1,256]{2,1,0:T(1,128)}), f32[16,1,256]{2,1,0:T(1,128)S(1)}, u32[]{:S(2)}, u32[]{:S(2)}) %all-to-all-start.2) | async-done | bytes 16416 | tf_op jit(solution)/shard_map/all_to_all | solution.py:402
  151.1 0.0 collective-permute-done.13.refs_0_
  151.1 0.0 collective-permute-done.14.refs_1_
  151.2 1.6 pick.11
  152.8 0.6 copy.20
  153.4 8.0 %all-to-all-start.3 = ((f32[32,1,256]{2,1,0:T(1,128)}), f32[32,1,256]{2,1,0:T(1,128)S(1)}, u32[]{:S(2)}, u32[]{:S(2)}) async-start(f32[32,1,256]{2,1,0:T(1,128)} %copy.20), calls=%async_computation.3 | async-start | bytes 65536 | tf_op jit(solution)/shard_map/all_to_all | solution.py:408
  161.4 0.1 pad_add_fusion.take_ref
  161.5 2.5 %collective-permute-start.15 = (bf16[2048,128]{1,0:T(8,128)(2,1)}, bf16[2048,128]{1,0:T(8,128)(2,1)}, u32[]{:S(2)}, u32[]{:S(2)}) collective-permute-start(bf16[2048,128]{1,0:T(8,128)(2,1)} %get-tuple-element.39.up_ref), channel_id=1, source_target_pairs={{0,64},{32,96},{64,0},{96,32},{1,65},{33,97},{65,1},{97,33},{2,66}... | collective-permute-start | bytes 1572872 | tf_op jit(solution)/shard_map/ppermute | solution.py:286
  164.0 2.2 %collective-permute-start.16 = (bf16[2048,128]{1,0:T(8,128)(2,1)}, bf16[2048,128]{1,0:T(8,128)(2,1)}, u32[]{:S(2)}, u32[]{:S(2)}) collective-permute-start(bf16[2048,128]{1,0:T(8,128)(2,1)} %get-tuple-element.40.down_ref), channel_id=1, source_target_pairs={{0,32},{32,0},{64,96},{96,64},{1,33},{33,1},{65,97},{97,65},{2,34}... | collective-permute-start | bytes 1572872 | tf_op jit(solution)/shard_map/ppermute | solution.py:286
  166.2 2.6 %all-to-all-done.3 = f32[32,1,256]{2,1,0:T(1,128)S(1)} async-done(((f32[32,1,256]{2,1,0:T(1,128)}), f32[32,1,256]{2,1,0:T(1,128)S(1)}, u32[]{:S(2)}, u32[]{:S(2)}) %all-to-all-start.3) | async-done | bytes 32800 | tf_op jit(solution)/shard_map/all_to_all | solution.py:408
  168.8 0.6 copy.24
  169.4 7.3 %backward.1 = (f32[2048,128]{1,0:T(8,128)}, f32[2056,128]{1,0:T(8,128)}, f32[8,128]{1,0:T(8,128)}) custom-call(s32[5]{0:T(128)} %stack.23.info_ref, f32[32,256]{1,0:T(8,128)} %bitcast.32, bf16[768,2048]{1,0:T(8,128)(2,1)} %copy-done.11, f32[776,384]{1,0:T(8,128)} %copy-done.12), custom_call_target="tpu_custom_call" | custom-call | flops 99999997952 | tf_op jit(solution)/shard_map/backward/pallas_call | solution.py:410
  176.7 2.4 %collective-permute-start.17 = (f32[2056,128]{1,0:T(8,128)}, f32[2056,128]{1,0:T(8,128)S(1)}, u32[]{:S(2)}, u32[]{:S(2)}) collective-permute-start(f32[2056,128]{1,0:T(8,128)} %get-tuple-element.45), channel_id=1, source_target_pairs={{0,1},{1,0},{2,3},{3,2},{4,5},{5,4},{6,7},{7,6},{8,9},{9,8},{10,11... | collective-permute-start | bytes 3158024 | tf_op jit(solution)/shard_map/ppermute | solution.py:286
  179.2 3.4 %loss.1 = f32[1,128]{1,0:T(1,128)} custom-call(f32[32,256]{1,0:T(8,128)S(1)} %bitcast.33, s32[64,128]{1,0:T(8,128)S(1)} %bitcast.31), custom_call_target="tpu_custom_call" | custom-call | flops 99999997952 | tf_op jit(solution)/shard_map/loss/pallas_call | solution.py:420
  182.6 7.0 %collective-permute-done.15.up_got_ref = bf16[2048,128]{1,0:T(8,128)(2,1)} collective-permute-done((bf16[2048,128]{1,0:T(8,128)(2,1)}, bf16[2048,128]{1,0:T(8,128)(2,1)}, u32[]{:S(2)}, u32[]{:S(2)}) %collective-permute-start.15) | collective-permute-done | bytes 524320 | tf_op jit(solution)/shard_map/ppermute | solution.py:286
  189.6 0.5 collective-permute-done.16.down_got_ref
  190.1 2.9 %final.1 = (bf16[2048,128]{1,0:T(8,128)(2,1)}, bf16[128,2048]{1,0:T(8,128)(2,1)}) custom-call(s32[2]{0:T(128)S(1)} %pad_add_fusion.take_ref, bf16[2048,128]{1,0:T(8,128)(2,1)} %get-tuple-element.39.up_ref, bf16[2048,128]{1,0:T(8,128)(2,1)} %collective-permute-done.15.up_got_ref, bf16[2048,128]{1,0:T(8,128)(2,1)} %get-tuple-element.40.down_ref, ...), custom_call_target="tpu_custom_call" | custom-call | tf_op jit(solution)/shard_map/final/pallas_call | solution.py:429
  (31 shorter events, 0.3 us)
Async XLA Ops:
  6.2 15.8 %copy-start.4 = (bf16[2064,128]{1,0:T(8,128)(2,1)S(1)}, bf16[2064,128]{1,0:T(8,128)(2,1)}, u32[]{:S(2)}) copy-start(bf16[2064,128]{1,0:T(8,128)(2,1)} %get-tuple-element.27.refs_1_) | copy-start | bytes 1585156
  6.2 19.0 %copy-start.13 = (s32[4]{0:T(128)S(1)}, s32[4]{0:T(128)}, u32[]{:S(2)}) copy-start(s32[4]{0:T(128)} %mask_ref.1) | copy-start | bytes 52
  6.2 73.0 %all-to-all-start = ((bf16[4,48,2176]{2,1,0:T(8,128)(2,1)}), bf16[4,48,2176]{2,1,0:T(8,128)(2,1)S(1)}, u32[]{:S(2)}, u32[]{:S(2)}) async-start(bf16[4,48,2176]{2,1,0:T(8,128)(2,1)} %bitcast.37), calls=%async_computation | async-start | bytes 1671168 | tf_op jit(solution)/shard_map/all_to_all | solution.py:357
  22.0 19.0 %copy-start = (bf16[4096,128]{1,0:T(8,128)(2,1)S(1)}, bf16[4096,128]{1,0:T(8,128)(2,1)}, u32[]{:S(2)}) copy-start(bf16[4096,128]{1,0:T(8,128)(2,1)} %get-tuple-element.31.refs_1_) | copy-start | bytes 3145732
  22.0 14.6 %collective-permute-start = (bf16[2064,128]{1,0:T(8,128)(2,1)S(1)}, bf16[2064,128]{1,0:T(8,128)(2,1)S(1)}, u32[]{:S(2)}, u32[]{:S(2)}) collective-permute-start(bf16[2064,128]{1,0:T(8,128)(2,1)S(1)} %copy-done.4), channel_id=1, source_target_pairs={{0,128},{128,0},{256,384},{384,256},{1,129},{129,1},{257,385},{385... | collective-permute-start | bytes 1585160 | tf_op jit(solution)/shard_map/ppermute | solution.py:286
  36.6 14.7 %collective-permute-start.1 = (bf16[2064,128]{1,0:T(8,128)(2,1)S(1)}, bf16[2064,128]{1,0:T(8,128)(2,1)S(1)}, u32[]{:S(2)}, u32[]{:S(2)}) collective-permute-start(bf16[2064,128]{1,0:T(8,128)(2,1)S(1)} %pick.6.refs_1_), channel_id=1, source_target_pairs={{0,384},{128,256},{256,128},{384,0},{1,385},{129,257},{257,129},{3... | collective-permute-start | bytes 1585160 | tf_op jit(solution)/shard_map/ppermute | solution.py:286
  41.0 24.5 %collective-permute-start.3 = (bf16[4096,128]{1,0:T(8,128)(2,1)S(1)}, bf16[4096,128]{1,0:T(8,128)(2,1)S(1)}, u32[]{:S(2)}, u32[]{:S(2)}) collective-permute-start(bf16[4096,128]{1,0:T(8,128)(2,1)S(1)} %copy-done), channel_id=1, source_target_pairs={{0,128},{128,0},{256,384},{384,256},{1,129},{129,1},{257,385},{385... | collective-permute-start | bytes 3145736 | tf_op jit(solution)/shard_map/ppermute | solution.py:286
  51.4 22.1 %collective-permute-start.2 = (bf16[2064,128]{1,0:T(8,128)(2,1)S(1)}, bf16[2064,128]{1,0:T(8,128)(2,1)}, u32[]{:S(2)}, u32[]{:S(2)}) collective-permute-start(bf16[2064,128]{1,0:T(8,128)(2,1)S(1)} %pick.7.refs_2_.refs_1_), channel_id=1, source_target_pairs={{0,32},{32,0},{64,96},{96,64},{1,33},{33,1},{65,97},{97,65},{2,34}... | collective-permute-start | bytes 1585160 | tf_op jit(solution)/shard_map/ppermute | solution.py:286
  54.0 16.9 %collective-permute-start.6 = (bf16[48,2176]{1,0:T(8,128)(2,1)}, bf16[48,2176]{1,0:T(8,128)(2,1)}, u32[]{:S(2)}, u32[]{:S(2)}) collective-permute-start(bf16[48,2176]{1,0:T(8,128)(2,1)} %get-tuple-element.32.refs_0_), channel_id=1, source_target_pairs={{0,6},{2,4},{4,2},{6,0},{1,7},{3,5},{5,3},{7,1},{8,14},{10,12},{12... | collective-permute-start | bytes 626696 | tf_op jit(solution)/shard_map/ppermute | solution.py:286
  58.7 12.3 %collective-permute-start.5 = (bf16[48,2176]{1,0:T(8,128)(2,1)}, bf16[48,2176]{1,0:T(8,128)(2,1)}, u32[]{:S(2)}, u32[]{:S(2)}) collective-permute-start(bf16[48,2176]{1,0:T(8,128)(2,1)} %get-tuple-element.32.refs_0_), channel_id=1, source_target_pairs={{0,4},{2,6},{4,0},{6,2},{1,5},{3,7},{5,1},{7,3},{8,12},{10,14},{12... | collective-permute-start | bytes 626696 | tf_op jit(solution)/shard_map/ppermute | solution.py:286
  60.9 10.0 %collective-permute-start.4 = (bf16[48,2176]{1,0:T(8,128)(2,1)}, bf16[48,2176]{1,0:T(8,128)(2,1)}, u32[]{:S(2)}, u32[]{:S(2)}) collective-permute-start(bf16[48,2176]{1,0:T(8,128)(2,1)} %get-tuple-element.32.refs_0_), channel_id=1, source_target_pairs={{0,2},{2,0},{4,6},{6,4},{1,3},{3,1},{5,7},{7,5},{8,10},{10,8},{12,... | collective-permute-start | bytes 626696 | tf_op jit(solution)/shard_map/ppermute | solution.py:286
  65.5 1.0 copy-start.1
  66.5 1.2 copy-start.2
  67.8 37.7 %collective-permute-start.12 = (bf16[4096,128]{1,0:T(8,128)(2,1)S(1)}, bf16[4096,128]{1,0:T(8,128)(2,1)}, u32[]{:S(2)}, u32[]{:S(2)}) collective-permute-start(bf16[4096,128]{1,0:T(8,128)(2,1)S(1)} %pick.8.refs_2_.own_ref), channel_id=1, source_target_pairs={{0,384},{128,256},{256,128},{384,0},{1,385},{129,257},{257,129},{3... | collective-permute-start | bytes 3145736 | tf_op jit(solution)/shard_map/ppermute | solution.py:286
  73.5 5.8 %copy-start.9 = (s32[5]{0:T(128)S(1)}, s32[5]{0:T(128)}, u32[]{:S(2)}) copy-start(s32[5]{0:T(128)} %stack.23.info_ref) | copy-start | bytes 64
  74.6 26.8 %collective-permute-start.7 = (bf16[2064,128]{1,0:T(8,128)(2,1)S(1)}, bf16[2064,128]{1,0:T(8,128)(2,1)S(1)}, u32[]{:S(2)}, u32[]{:S(2)}) collective-permute-start(bf16[2064,128]{1,0:T(8,128)(2,1)S(1)} %pick.9.refs_0_.refs_1_), channel_id=1, source_target_pairs={{0,64},{32,96},{64,0},{96,32},{1,65},{33,97},{65,1},{97,33},{2,66}... | collective-permute-start | bytes 1585160 | tf_op jit(solution)/shard_map/ppermute | solution.py:286
  79.8 32.7 %collective-permute-start.11 = (bf16[144,2176]{1,0:T(8,128)(2,1)S(1)}, bf16[144,2176]{1,0:T(8,128)(2,1)S(1)}, u32[]{:S(2)}, u32[]{:S(2)}) collective-permute-start(bf16[144,2176]{1,0:T(8,128)(2,1)S(1)} %others.1.refs_2_.refs_4_), channel_id=1, source_target_pairs={{0,6},{2,4},{4,2},{6,0},{1,7},{3,5},{5,3},{7,1},{8,14},{10,12},{12... | collective-permute-start | bytes 1880072 | tf_op jit(solution)/shard_map/ppermute | solution.py:286
  84.5 28.1 %collective-permute-start.10 = (bf16[144,2176]{1,0:T(8,128)(2,1)S(1)}, bf16[144,2176]{1,0:T(8,128)(2,1)S(1)}, u32[]{:S(2)}, u32[]{:S(2)}) collective-permute-start(bf16[144,2176]{1,0:T(8,128)(2,1)S(1)} %others.1.refs_2_.refs_4_), channel_id=1, source_target_pairs={{0,4},{2,6},{4,0},{6,2},{1,5},{3,7},{5,1},{7,3},{8,12},{10,14},{12... | collective-permute-start | bytes 1880072 | tf_op jit(solution)/shard_map/ppermute | solution.py:286
  86.8 27.0 %collective-permute-start.9 = (bf16[144,2176]{1,0:T(8,128)(2,1)S(1)}, bf16[144,2176]{1,0:T(8,128)(2,1)S(1)}, u32[]{:S(2)}, u32[]{:S(2)}) collective-permute-start(bf16[144,2176]{1,0:T(8,128)(2,1)S(1)} %others.1.refs_2_.refs_4_), channel_id=1, source_target_pairs={{0,2},{2,0},{4,6},{6,4},{1,3},{3,1},{5,7},{7,5},{8,10},{10,8},{12,... | collective-permute-start | bytes 1880072 | tf_op jit(solution)/shard_map/ppermute | solution.py:286
  101.4 12.3 %copy-start.8 = (f32[8,256]{1,0:T(8,128)S(1)}, f32[8,256]{1,0:T(8,128)}, u32[]{:S(2)}) copy-start(f32[8,256]{1,0:T(8,128)} %get-tuple-element.26.base_ref) | copy-start | bytes 24580
  101.4 7.3 %collective-permute-start.8 = (bf16[2064,128]{1,0:T(8,128)(2,1)S(1)}, bf16[2064,128]{1,0:T(8,128)(2,1)S(1)}, u32[]{:S(2)}, u32[]{:S(2)}) collective-permute-start(bf16[2064,128]{1,0:T(8,128)(2,1)S(1)} %pick.10.own_w_ref.earlier_ref), channel_id=1, source_target_pairs={{0,1},{1,0},{2,3},{3,2},{4,5},{5,4},{6,7},{7,6},{8,9},{9,8},{10,11... | collective-permute-start | bytes 1585160 | tf_op jit(solution)/shard_map/ppermute | solution.py:286
  106.8 44.3 %collective-permute-start.13 = (bf16[2048,128]{1,0:T(8,128)(2,1)S(1)}, bf16[2048,128]{1,0:T(8,128)(2,1)S(1)}, u32[]{:S(2)}, u32[]{:S(2)}) collective-permute-start(bf16[2048,128]{1,0:T(8,128)(2,1)S(1)} %get-tuple-element.35.refs_2_), channel_id=1, source_target_pairs={{0,32},{32,0},{64,96},{96,64},{1,33},{33,1},{65,97},{97,65},{2,34}... | collective-permute-start | bytes 1572872 | tf_op jit(solution)/shard_map/ppermute | solution.py:286
  108.7 42.4 %collective-permute-start.14 = (bf16[2048,128]{1,0:T(8,128)(2,1)S(1)}, bf16[2048,128]{1,0:T(8,128)(2,1)S(1)}, u32[]{:S(2)}, u32[]{:S(2)}) collective-permute-start(bf16[2048,128]{1,0:T(8,128)(2,1)S(1)} %get-tuple-element.36.refs_3_), channel_id=1, source_target_pairs={{0,64},{32,96},{64,0},{96,32},{1,65},{33,97},{65,1},{97,33},{2,66}... | collective-permute-start | bytes 1572872 | tf_op jit(solution)/shard_map/ppermute | solution.py:286
  116.4 1.6 copy-start.11
  118.0 1.0 copy-start.12
  132.6 18.5 %all-to-all-start.2 = ((f32[16,1,256]{2,1,0:T(1,128)}), f32[16,1,256]{2,1,0:T(1,128)S(1)}, u32[]{:S(2)}, u32[]{:S(2)}) async-start(f32[16,1,256]{2,1,0:T(1,128)} %broadcast_in_dim.23), calls=%async_computation.2 | async-start | bytes 32768 | tf_op jit(solution)/shard_map/all_to_all | solution.py:402
  153.4 15.4 %all-to-all-start.3 = ((f32[32,1,256]{2,1,0:T(1,128)}), f32[32,1,256]{2,1,0:T(1,128)S(1)}, u32[]{:S(2)}, u32[]{:S(2)}) async-start(f32[32,1,256]{2,1,0:T(1,128)} %copy.20), calls=%async_computation.3 | async-start | bytes 65536 | tf_op jit(solution)/shard_map/all_to_all | solution.py:408
  161.5 28.1 %collective-permute-start.15 = (bf16[2048,128]{1,0:T(8,128)(2,1)}, bf16[2048,128]{1,0:T(8,128)(2,1)}, u32[]{:S(2)}, u32[]{:S(2)}) collective-permute-start(bf16[2048,128]{1,0:T(8,128)(2,1)} %get-tuple-element.39.up_ref), channel_id=1, source_target_pairs={{0,64},{32,96},{64,0},{96,32},{1,65},{33,97},{65,1},{97,33},{2,66}... | collective-permute-start | bytes 1572872 | tf_op jit(solution)/shard_map/ppermute | solution.py:286
  164.0 26.1 %collective-permute-start.16 = (bf16[2048,128]{1,0:T(8,128)(2,1)}, bf16[2048,128]{1,0:T(8,128)(2,1)}, u32[]{:S(2)}, u32[]{:S(2)}) collective-permute-start(bf16[2048,128]{1,0:T(8,128)(2,1)} %get-tuple-element.40.down_ref), channel_id=1, source_target_pairs={{0,32},{32,0},{64,96},{96,64},{1,33},{33,1},{65,97},{97,65},{2,34}... | collective-permute-start | bytes 1572872 | tf_op jit(solution)/shard_map/ppermute | solution.py:286
  169.4 9.8 %copy-start.5 = (s32[8192]{0:T(1024)S(1)}, s32[8192]{0:T(1024)}, u32[]{:S(2)}) copy-start(s32[8192]{0:T(1024)} %param.16) | copy-start | bytes 98308
  169.4 9.8 %copy-start.6 = (f32[32,1,256]{2,0,1:T(8,128)S(1)}, f32[32,1,256]{2,0,1:T(8,128)}, u32[]{:S(2)}) copy-start(f32[32,1,256]{2,0,1:T(8,128)} %copy.24) | copy-start | bytes 98308
  176.7 13.3 %copy-start.3 = (f32[2048,128]{1,0:T(8,128)S(1)}, f32[2048,128]{1,0:T(8,128)}, u32[]{:S(2)}) copy-start(f32[2048,128]{1,0:T(8,128)} %get-tuple-element.44.own_ref) | copy-start | bytes 3145732
  176.7 13.3 %copy-start.7 = (bf16[2048]{0:T(1024)(128)(2,1)S(1)}, bf16[2048]{0:T(1024)(128)(2,1)}, u32[]{:S(2)}) copy-start(bf16[2048]{0:T(1024)(128)(2,1)} %param.17) | copy-start | bytes 12292
  176.7 13.3 %copy-start.10 = (f32[8,128]{1,0:T(8,128)S(1)}, f32[8,128]{1,0:T(8,128)}, u32[]{:S(2)}) copy-start(f32[8,128]{1,0:T(8,128)} %get-tuple-element.46.own_head_ref) | copy-start | bytes 12292
  176.7 13.3 %collective-permute-start.17 = (f32[2056,128]{1,0:T(8,128)}, f32[2056,128]{1,0:T(8,128)S(1)}, u32[]{:S(2)}, u32[]{:S(2)}) collective-permute-start(f32[2056,128]{1,0:T(8,128)} %get-tuple-element.45), channel_id=1, source_target_pairs={{0,1},{1,0},{2,3},{3,2},{4,5},{5,4},{6,7},{7,6},{8,9},{9,8},{10,11... | collective-permute-start | bytes 3158024 | tf_op jit(solution)/shard_map/ppermute | solution.py:286
